TPU v7x, 32 devices: a whole 2x2x4 slice. The times are simulated.
32 devices in a mesh: grid: 8 (over z, y), blk: 4 (over x, core).
Axes of the slice: x: 2, y: 2, z: 4, core: 2. Of those that a mesh axis runs over, the one named last changes fastest.
Arguments:
- a_slots: bfloat16 [8, 4, 8, 2, 128, 128], P('grid', 'blk'), may hold values from -6 to 6
- a_rows: int32 [8, 4, 8, 2], P('grid', 'blk'), may hold values from 0 to 63, as said below
- a_cols: int32 [8, 4, 8, 2], P('grid', 'blk'), may hold values from 0 to 31
- a_count: int32 [8, 4, 8], P('grid', 'blk'), may hold values from 0 to 2, as said below
- owned_rows: int32 [8, 8], P('grid'), may hold values from 0 to 63, as said below
- b_matrix: bfloat16 [4096, 4096], P('grid', 'blk'), may hold values from -0.1875 to 0.1875
Outputs:
- product: bfloat16 [8192, 4096], P('grid', 'blk')
Inputs may be any that keep to these rules, and one draw needn't show every extreme that they name: `a_rows`: every slot sent to product owner g, live or padded, names one of the block rows owned_rows[g, 0 .. 7]; no two slots of the whole draw name the same block row and block column. `a_count`: some product owner receives 2 live slots from every atom owner and atom column. `owned_rows`: A permutation of the 64 block rows.
All inputs are finite; a program needn't handle non-finite values.
Results may differ from a plain program's by a relative error of at most 0.001.
Values may be sent and summed in bfloat16 or wider, within the bound.
No kernel may reach another device: no remote copies, remote signals or barrier semaphores. Data moves between devices by JAX's collectives and lax.ppermute only.
A program may use at most 128 MiB of HBM per device.

v0:
```python
import jax
import jax.numpy as jnp
from jax import lax
from jax.sharding import PartitionSpec as P

CAP = 2
RB = 8


def body(a_slots, a_rows, a_cols, a_count, owned_rows, b_matrix):
    groups = lax.axis_size("grid")
    columns = lax.axis_size("blk")
    block_size = a_slots.shape[-1]
    landed = (
        lax.all_to_all(
            a_slots.reshape(groups, CAP, block_size, block_size),
            "grid",
            split_axis=0,
            concat_axis=0,
            tiled=True,
        ),
        lax.all_to_all(
            a_rows.reshape(groups, CAP), "grid", split_axis=0, concat_axis=0, tiled=True
        ),
        lax.all_to_all(
            a_cols.reshape(groups, CAP), "grid", split_axis=0, concat_axis=0, tiled=True
        ),
        lax.all_to_all(a_count.reshape(groups, 1), "grid", split_axis=0, concat_axis=0, tiled=True),
    )
    slot_data, slot_rows, slot_cols, slot_count = (
        lax.all_gather(landed[0][None], "blk", axis=0, tiled=True),
        lax.all_gather(landed[1][None], "blk", axis=0, tiled=True),
        lax.all_gather(landed[2][None], "blk", axis=0, tiled=True),
        lax.all_gather(landed[3][None], "blk", axis=0, tiled=True),
    )
    total = columns * groups * CAP
    live = (jnp.arange(CAP, dtype=jnp.int32)[None, None, :] < slot_count).reshape(total)
    slot_rows = slot_rows.reshape(total)
    slot_cols = slot_cols.reshape(total)
    slot_data = slot_data.reshape(total, block_size, block_size)
    owned = owned_rows.reshape(RB)
    row_hit = (slot_rows[:, None] == owned[None, :]) & live[:, None]
    k_blocks = b_matrix.shape[0] * groups // block_size
    col_hit = slot_cols[:, None] == jnp.arange(k_blocks, dtype=jnp.int32)[None, :]
    placing = (
        (row_hit[:, :, None] & col_hit[:, None, :])
        .reshape(total, RB * k_blocks)
        .astype(jnp.bfloat16)
    )
    spread = jnp.einsum(
        "sp,sq->pq",
        placing,
        slot_data.reshape(total, block_size * block_size),
        preferred_element_type=jnp.float32,
    )
    tile = spread.astype(jnp.bfloat16).reshape(RB, k_blocks, block_size, block_size)
    tile = tile.transpose(0, 2, 1, 3).reshape(RB * block_size, k_blocks * block_size)
    result = jnp.dot(
        tile,
        lax.all_gather(b_matrix, "grid", axis=0, tiled=True),
        preferred_element_type=jnp.float32,
    )
    return result.astype(jnp.bfloat16)


def solution(mesh):
    in_specs = (
        P("grid", "blk", None, None, None, None),
        P("grid", "blk", None, None),
        P("grid", "blk", None, None),
        P("grid", "blk", None),
        P("grid", None),
        P("grid", "blk"),
    )
    out_specs = P("grid", "blk")
    return jax.shard_map(body, mesh=mesh, in_specs=in_specs, out_specs=out_specs, check_vma=False)
```

profile of v0, /device:TPU:0, one launch (start us, length us, event | category | flops | bytes accessed | tf_op | source)
XLA Modules:
  0.0 199.3 jit_solution(497381565929349732)
XLA Ops:
  6.5 0.0 all-gather.9.cloned.1.call-start
  6.5 21.9 %all_to_all.32 = bf16[8,2,128,128]{3,2,1,0:T(8,128)(2,1)} all-to-all(bf16[8,2,128,128]{3,2,1,0:T(8,128)(2,1)} %bitcast.29), channel_id=1, replica_groups=mesh['grid'=8,'blk'=4] {'grid'}, dimensions={0} | all-to-all | bytes 1048576 | tf_op jit(solution)/shard_map/all_to_all | solution.py:15
  28.5 0.0 all-gather.9.cloned.1.call-update
  28.5 0.0 all-gather.7.cloned.1.call-start
  28.5 0.7 all-gather.7.cloned.1.call-update
  29.2 1.3 copy.17
  30.6 3.6 %all-to-all-start.1 = ((s32[8,1,1]{2,1,0:T(1,128)}), s32[8,1,1]{2,1,0:T(1,128)S(1)}, u32[]{:S(2)}, u32[]{:S(2)}) async-start(s32[8,1,1]{2,1,0:T(1,128)} %copy.17), calls=%async_computation.1 | async-start | bytes 8192 | tf_op jit(solution)/shard_map/all_to_all | solution.py:28
  34.1 1.3 copy.16
  35.5 1.3 copy.18
  36.8 1.3 dynamic-slice
  38.7 1.9 all-to-all-done.1
  40.6 4.2 %all-to-all-start = ((s32[8,1,2]{2,1,0:T(1,128)}), s32[8,1,2]{2,1,0:T(1,128)S(1)}, u32[]{:S(2)}, u32[]{:S(2)}) async-start(s32[8,1,2]{2,1,0:T(1,128)} %copy.16), calls=%async_computation | async-start | bytes 8192 | tf_op jit(solution)/shard_map/all_to_all | solution.py:22
  44.8 0.2 reduce.1
  45.0 0.2 dynamic-update-slice
  45.2 4.9 %all-reduce = s32[32]{0:T(128)S(1)} all-reduce(s32[32]{0:T(128)S(1)} %dynamic-update-slice), channel_id=3, replica_groups=mesh['grid'=8,'blk'=4] {'blk'}, use_global_device_ids=true, to_apply=%add | all-reduce | flops 32 | bytes 256
  50.1 0.1 lt.23
  50.2 0.1 iota_compare_fusion.1
  50.3 0.1 lt.26
  50.4 0.8 all-to-all-done
  51.2 5.2 %all-to-all-start.2 = ((s32[8,1,2]{2,1,0:T(1,128)}), s32[8,1,2]{2,1,0:T(1,128)S(1)}, u32[]{:S(2)}, u32[]{:S(2)}) async-start(s32[8,1,2]{2,1,0:T(1,128)} %copy.18), calls=%async_computation.2 | async-start | bytes 8192 | tf_op jit(solution)/shard_map/all_to_all | solution.py:25
  56.4 5.2 %all-gather = s32[32,1,2]{2,1,0:T(1,128)S(1)} all-gather(s32[8,1,2]{2,1,0:T(1,128)S(1)} %all-to-all-done), channel_id=2, replica_groups=mesh['grid'=8,'blk'=4] {'blk'}, dimensions={0}, use_global_device_ids=true | all-gather | bytes 320 | tf_op jit(solution)/shard_map/all_gather | solution.py:32
  61.6 0.6 broadcast.56
  62.2 0.7 reduce.8
  62.9 0.1 eq.40
  63.0 0.0 all-to-all-done.2
  63.0 5.2 %all-gather.2 = s32[32,1,2]{2,1,0:T(1,128)S(1)} all-gather(s32[8,1,2]{2,1,0:T(1,128)S(1)} %all-to-all-done.2), channel_id=4, replica_groups=mesh['grid'=8,'blk'=4] {'blk'}, dimensions={0}, use_global_device_ids=true | all-gather | bytes 320 | tf_op jit(solution)/shard_map/all_gather | solution.py:33
  68.2 0.7 reduce.7
  68.8 0.1 eq.45
  68.9 0.7 compare_and_fusion
  69.7 0.0 all-gather.9.cloned.1.call-done
  69.7 7.2 %fusion.3 = bf16[32,8,128,128]{3,1,2,0:T(8,128)(2,1)} fusion(pred[64,256]{0,1:T(32,128)(4,1)S(1)} %bitcast.30, bf16[8,8,128,128]{3,2,1,0:T(8,128)(2,1)} %bitcast.28), kind=kOutput, calls=%fused_computation.4 | convolution fusion | flops 541065216 | bytes 10502144 | tf_op jit(solution)/shard_map/sp,sq->pq/dot_general | solution.py:50
  76.9 9.2 %copy.21 = bf16[32,8,128,128]{3,2,1,0:T(8,128)(2,1)} copy(bf16[32,8,128,128]{3,1,2,0:T(8,128)(2,1)} %fusion.3) | data formatting | bytes 16777216
  86.2 12.0 %copy.19 = bf16[8,32,128,128]{3,1,2,0:T(8,128)(2,1)} copy(bf16[8,32,128,128]{3,2,1,0:T(8,128)(2,1)} %bitcast.26) | data formatting | bytes 16777216 | tf_op jit(solution)/shard_map/reshape | solution.py:56
  98.2 79.1 %all-gather.7.cloned.1.call-done = bf16[4096,1024]{1,0:T(8,128)(2,1)} async-done(((bf16[512,1024]{1,0:T(8,128)(2,1)}), bf16[4096,1024]{1,0:T(8,128)(2,1)}) %all-gather.7.cloned.1.call-update) | async-done | bytes 8388624 | tf_op jit(solution)/shard_map/all_gather | solution.py:60
  177.3 15.2 %fusion.6 = bf16[1024,1024]{1,0:T(8,128)(2,1)} fusion(bf16[4096,1024]{1,0:T(8,128)(2,1)} %all-gather.7.cloned.1.call-done, bf16[128,8,32,128]{3,2,1,0:T(8,128)(2,1)} %bitcast.27), kind=kOutput, calls=%fused_computation.7 | convolution fusion | flops 8590983168 | bytes 18874368 | tf_op jit(solution)/shard_map/dot_general | solution.py:58
  (3 shorter events, 0.0 us)
Async XLA Ops:
  6.5 63.2 %all-gather.9.cloned.1.call-start = ((), (), s32[]{:S(2)}) async-start(), calls=%async_computation.5 | async-start | bytes 2621440 | tf_op jit(solution)/shard_map/all_gather | solution.py:31
  28.5 148.8 %all-gather.7.cloned.1.call-start = ((), (), s32[]{:S(2)}) async-start(), calls=%async_computation.4 | async-start | bytes 9437184 | tf_op jit(solution)/shard_map/all_gather | solution.py:60
  30.6 10.1 %all-to-all-start.1 = ((s32[8,1,1]{2,1,0:T(1,128)}), s32[8,1,1]{2,1,0:T(1,128)S(1)}, u32[]{:S(2)}, u32[]{:S(2)}) async-start(s32[8,1,1]{2,1,0:T(1,128)} %copy.17), calls=%async_computation.1 | async-start | bytes 8192 | tf_op jit(solution)/shard_map/all_to_all | solution.py:28
  40.6 10.6 %all-to-all-start = ((s32[8,1,2]{2,1,0:T(1,128)}), s32[8,1,2]{2,1,0:T(1,128)S(1)}, u32[]{:S(2)}, u32[]{:S(2)}) async-start(s32[8,1,2]{2,1,0:T(1,128)} %copy.16), calls=%async_computation | async-start | bytes 8192 | tf_op jit(solution)/shard_map/all_to_all | solution.py:22
  51.2 11.7 %all-to-all-start.2 = ((s32[8,1,2]{2,1,0:T(1,128)}), s32[8,1,2]{2,1,0:T(1,128)S(1)}, u32[]{:S(2)}, u32[]{:S(2)}) async-start(s32[8,1,2]{2,1,0:T(1,128)} %copy.18), calls=%async_computation.2 | async-start | bytes 8192 | tf_op jit(solution)/shard_map/all_to_all | solution.py:25
Sparse Core Ops, SparseCore 0:
  28.6 21.5 all-gather.8
  52.3 124.9 all-gather.6
where the time goes:
time: 200 us; the launch traced here: 199 us
  waiting for transfers between devices  82.5 us (41%)
  blocking collectives  37.2 us (19%)
  local copies, waits for them, and re-layouts  27.8 us (14%)
  matrix products  22.4 us (11%)
  between operations  14.1 us (7%)
  starting transfers between devices  13 us (6%)
  other arithmetic  2.41 us (1%)
    all_gather x1, waiting for transfers between devices, body(): lax.all_gather(b_matrix, 'grid', axis=0, tiled=True)  79.1 us
    all_to_all x1, blocking collectives, body(): lax.all_to_all(a_slots.reshape(groups, CAP, block_size, block_size), 'gri...  21.9 us
    dot_general x1, matrix products, body(): jnp.dot(tile, lax.all_gather(b_matrix, 'grid', axis=0, tiled=True), prefe...  15.2 us
    reshape x1, local copies, waits for them, and re-layouts, body(): spread.astype(jnp.bfloat16).reshape(RB, k_blocks, block_size, block_size)  12 us
    unnamed x4, local copies, waits for them, and re-layouts  10.7 us
    dot_general x1, matrix products, body(): jnp.einsum('sp,sq->pq', placing, slot_data.reshape(total, block_size * bl...  7.2 us
    all_to_all x1, starting transfers between devices, body(): lax.all_to_all(a_cols.reshape(groups, CAP), 'grid', split_axis=0, concat_...  5.21 us
    all_gather x1, blocking collectives, body(): lax.all_gather(landed[2][None], 'blk', axis=0, tiled=True)  5.19 us
  transfers between devices with their start and end apart: 5, of which 3 were waited for; matrix products, arithmetic and copies ran while one was open for 19% of the time, Pallas kernels for 0%

commit v1 on v0

v1 whole, which is shorter than its diff:
```python
import functools

import jax
import jax.numpy as jnp
import numpy as np
from jax import lax
from jax.experimental import pallas as pl
from jax.experimental.pallas import tpu as pltpu
from jax.sharding import PartitionSpec as P

META = 16


def ring_order(n):
    return list(range(0, n, 2)) + list(range(n - 1, 0, -2))


def build_kernel(n_parts, per_part, cap, bs, dest_ref, *refs):
    parts, tile_ref = refs[:n_parts], refs[n_parts]
    tile_ref[...] = jnp.zeros_like(tile_ref)
    k_blocks = tile_ref.shape[0] * 2
    for q in range(n_parts):
        part = parts[q]

        def place(i, carry):
            for c in range(cap):
                dest = dest_ref[q, i, c]

                @pl.when(dest >= 0)
                def _():
                    row = dest // k_blocks
                    col = dest % k_blocks
                    tile_ref[
                        col // 2,
                        pl.ds(pl.multiple_of(row * bs, bs), bs),
                        pl.ds(pl.multiple_of((col % 2) * bs, bs), bs),
                    ] = part[i, pl.ds(c * bs, bs), :]

            return carry

        lax.fori_loop(0, per_part, place, 0)


def build_tile(dest, parts, rows, k_blocks, bs, cap):
    n_parts, per_part = len(parts), parts[0].shape[0]
    return pl.pallas_call(
        functools.partial(build_kernel, n_parts, per_part, cap, bs),
        out_shape=jax.ShapeDtypeStruct((k_blocks // 2, rows, 2 * bs), jnp.bfloat16),
        in_specs=[pl.BlockSpec(memory_space=pltpu.SMEM)]
        + [pl.BlockSpec(memory_space=pltpu.VMEM)] * n_parts,
        out_specs=pl.BlockSpec(memory_space=pltpu.VMEM),
        compiler_params=pltpu.CompilerParams(vmem_limit_bytes=48 << 20),
        cost_estimate=pl.CostEstimate(
            flops=0, bytes_accessed=rows * k_blocks * bs * 4, transcendentals=0
        ),
    )(dest, *parts)


def mul_kernel(n_pieces, has_acc, idx_ref, *refs):
    tiles = refs[:n_pieces]
    pieces = refs[n_pieces : 2 * n_pieces]
    out_ref = refs[-1]
    total = refs[2 * n_pieces][...] if has_acc else None
    for tile, piece in zip(tiles, pieces):
        term = jnp.dot(tile[0], piece[...], preferred_element_type=jnp.float32)
        total = term if total is None else total + term
    out_ref[...] = total.astype(out_ref.dtype)


def mul(idx, tile, pieces, acc, out_dtype):
    n = len(pieces)
    rows = tile.shape[1]
    depth, cols = pieces[0].shape
    bm = 256
    in_specs = [
        pl.BlockSpec((1, bm, depth), functools.partial(lambda i, m, idx: (idx[i], m, 0), i))
        for i in range(n)
    ]
    in_specs += [pl.BlockSpec((depth, cols), lambda m, idx: (0, 0)) for _ in range(n)]
    args = [tile] * n + list(pieces)
    if acc is not None:
        in_specs.append(pl.BlockSpec((bm, cols), lambda m, idx: (m, 0)))
        args.append(acc)
    return pl.pallas_call(
        functools.partial(mul_kernel, n, acc is not None),
        out_shape=jax.ShapeDtypeStruct((rows, cols), out_dtype),
        grid_spec=pltpu.PrefetchScalarGridSpec(
            num_scalar_prefetch=1,
            grid=(rows // bm,),
            in_specs=in_specs,
            out_specs=pl.BlockSpec((bm, cols), lambda m, idx: (m, 0)),
        ),
        compiler_params=pltpu.CompilerParams(vmem_limit_bytes=56 << 20),
        cost_estimate=pl.CostEstimate(
            flops=2 * n * rows * depth * cols,
            bytes_accessed=n * (rows + cols) * depth * 2 + rows * cols * 8,
            transcendentals=0,
        ),
    )(idx, *args)


def body(a_slots, a_rows, a_cols, a_count, owned_rows, b_matrix):
    groups = lax.axis_size("grid")
    columns = lax.axis_size("blk")
    bs = a_slots.shape[-1]
    cap = a_slots.shape[3]
    rb = owned_rows.shape[-1]
    k_local = b_matrix.shape[0]
    k_blocks = k_local * groups // bs
    depth = 2 * bs
    me = lax.axis_index("grid")

    order = ring_order(groups)
    table = jnp.asarray(np.array(order, np.int32))
    place_of = jnp.asarray(np.argsort(np.array(order)).astype(np.int32))
    pos = place_of[me]
    to_right = [(order[i], order[(i + 1) % groups]) for i in range(groups)]
    to_left = [(order[(i + 1) % groups], order[i]) for i in range(groups)]

    per = k_local // depth
    own = [b_matrix[h * depth : (h + 1) * depth] for h in range(per)]
    events = [[(me * per + h, own[h]) for h in range(per)]]
    from_left, from_right = list(own), list(own)
    half = groups // 2
    for s in range(1, half + 1):
        low = range(per) if s < half else range(per // 2)
        high = range(per) if s < half else range(per // 2, per)
        from_left = {h: lax.ppermute(from_left[h], "grid", to_right) for h in low}
        from_right = {h: lax.ppermute(from_right[h], "grid", to_left) for h in high}
        left_owner = table[(pos - s + groups) % groups]
        right_owner = table[(pos + s) % groups]
        events.append(
            [(left_owner * per + h, from_left[h]) for h in low]
            + [(right_owner * per + h, from_right[h]) for h in high]
        )

    live = jnp.arange(cap, dtype=jnp.int32)[None, :] < a_count.reshape(groups, 1)
    row_code = jnp.where(live, a_rows.reshape(groups, cap) + 1, 0)
    meta = jnp.concatenate([row_code, a_cols.reshape(groups, cap)], axis=1)
    meta = jnp.pad(meta.astype(jnp.bfloat16)[:, None, :], ((0, 0), (0, META - 1), (0, bs - 2 * cap)))
    message = jnp.concatenate([a_slots.reshape(groups, cap * bs, bs), meta], axis=1)
    landed = lax.all_to_all(message, "grid", split_axis=0, concat_axis=0, tiled=True)
    if columns == 4:
        swap_core = [(j, j ^ 1) for j in range(columns)]
        swap_chip = [(j, j ^ 2) for j in range(columns)]
        across = lax.ppermute(landed, "blk", swap_chip)
        parts = [
            landed,
            across,
            lax.ppermute(landed, "blk", swap_core),
            lax.ppermute(across, "blk", swap_core),
        ]
    else:
        gathered = lax.all_gather(landed, "blk", axis=0)
        parts = [gathered[j] for j in range(columns)]
    metas = jnp.stack([p[:, cap * bs, : 2 * cap] for p in parts]).astype(jnp.int32)
    owned = owned_rows.reshape(rb)
    hit = metas[..., :cap, None] == owned + 1
    local_row = jnp.sum(jnp.where(hit, jnp.arange(rb, dtype=jnp.int32), 0), axis=-1)
    dest = jnp.where(jnp.any(hit, axis=-1), local_row * k_blocks + metas[..., cap:], -1)
    tile = build_tile(dest, parts, rb * bs, k_blocks, bs, cap)

    acc = None
    early = sum(events[: half - 1], [])
    stages = [early] + events[half - 1 :]
    for t, stage in enumerate(stages):
        idx = jnp.stack([k for k, _ in stage]).astype(jnp.int32)
        last = t == len(stages) - 1
        acc = mul(idx, tile, [p for _, p in stage], acc, jnp.bfloat16 if last else jnp.float32)
    return acc


def solution(mesh):
    in_specs = (
        P("grid", "blk", None, None, None, None),
        P("grid", "blk", None, None),
        P("grid", "blk", None, None),
        P("grid", "blk", None),
        P("grid", None),
        P("grid", "blk"),
    )
    out_specs = P("grid", "blk")
    return jax.shard_map(body, mesh=mesh, in_specs=in_specs, out_specs=out_specs, check_vma=False)
```

time: 200 us -> 120 us (0.60)
  waiting for transfers between devices: 82.5 us -> 30.7 us
  blocking collectives: 37.2 us -> 0 us
  Pallas kernels: 0 us -> 31.8 us
  starting transfers between devices: 13 us -> 39.6 us
  local copies, waits for them, and re-layouts: 27.8 us -> 3.25 us
  matrix products: 22.4 us -> 0 us
  between operations: 14.1 us -> 9.23 us
  other arithmetic: 2.41 us -> 5.18 us
    all_gather x2 -> x0, waiting for transfers between devices: 79.1 us -> none  [the longest x1 79.1 us: body(): lax.all_gather(b_matrix, 'grid', axis=0, tiled=True)]
    ppermute x0 -> x17, starting transfers between devices: none -> 32.4 us  [the longest x7 20 us: body(): from_left = {h: lax.ppermute(from_left[h], 'grid', to_right) for h in low}]
    pallas_call x0 -> x4, Pallas kernels: none -> 31.8 us  [the longest x3 25.9 us: mul(): pl.pallas_call(functools.partial(mul_kernel, n, acc is not None), out_sha...]
    dot_general x2 -> x0, matrix products: 22.4 us -> none  [the longest x1 15.2 us: body(): jnp.dot(tile, lax.all_gather(b_matrix, 'grid', axis=0, tiled=True), prefe...]
    all_to_all x1 -> x0, blocking collectives: 21.9 us -> none  [body(): lax.all_to_all(a_slots.reshape(groups, CAP, block_size, block_size), 'gri...]
    ppermute x0 -> x17, waiting for transfers between devices: none -> 18.3 us  [the longest x7 18.3 us: body(): from_left = {h: lax.ppermute(from_left[h], 'grid', to_right) for h in low}]
    reshape x1 -> x0, local copies, waits for them, and re-layouts: 12 us -> none  [body(): spread.astype(jnp.bfloat16).reshape(RB, k_blocks, block_size, block_size)]
    unnamed x4 -> x12, local copies, waits for them, and re-layouts: 10.7 us -> 0.03 us
  transfers between devices with their start and end apart: 5 -> 18, of which waited for: 3 -> 5; matrix products, arithmetic and copies ran while one was open for 19% -> 4% of each run, Pallas kernels for 0% -> 21%
where the time goes in v1:
time: 120 us
  starting transfers between devices  39.6 us (33%)
  Pallas kernels  31.8 us (26%)
  waiting for transfers between devices  30.7 us (26%)
  between operations  9.23 us (8%)
  other arithmetic  5.18 us (4%)
  local copies, waits for them, and re-layouts  3.25 us (3%)
    pallas_call x3, Pallas kernels, mul(): pl.pallas_call(functools.partial(mul_kernel, n, acc is not None), out_sha...  25.9 us
    ppermute x7, starting transfers between devices, body(): from_left = {h: lax.ppermute(from_left[h], 'grid', to_right) for h in low}  20 us
    ppermute x7, waiting for transfers between devices, body(): from_left = {h: lax.ppermute(from_left[h], 'grid', to_right) for h in low}  18.3 us
    all_to_all x1, waiting for transfers between devices, body(): lax.all_to_all(message, 'grid', split_axis=0, concat_axis=0, tiled=True)  12.4 us
    ppermute x7, starting transfers between devices, body(): from_right = {h: lax.ppermute(from_right[h], 'grid', to_left) for h in high}  10.3 us
    all_to_all x1, starting transfers between devices, body(): lax.all_to_all(message, 'grid', split_axis=0, concat_axis=0, tiled=True)  7.28 us
    pallas_call x1, Pallas kernels, build_tile(): pl.pallas_call(functools.partial(build_kernel, n_parts, per_part, cap, bs...  5.84 us
  transfers between devices with their start and end apart: 18, of which 5 were waited for; matrix products, arithmetic and copies ran while one was open for 4% of the time, Pallas kernels for 21%

profile of v1, /device:TPU:0, one launch (start us, length us, event | category | flops | bytes accessed | tf_op | source)
XLA Modules:
  0.0 119.8 jit_solution(1215541909820693163)
XLA Ops:
  0.0 0.8 convert_bitcast_fusion
  0.8 0.7 fusion.5
  1.5 0.1 copy.28
  1.6 1.9 %fusion.1 = bf16[8,272,128]{2,1,0:T(8,128)(2,1)} fusion(bf16[8,1,4]{2,1,0:T(2,128)(2,1)S(1)} %copy.28, bf16[8,256,128]{2,1,0:T(8,128)(2,1)} %bitcast.26), kind=kLoop, calls=%fused_computation.2 | loop fusion | flops 1671168 | bytes 1081408 | tf_op jit(solution)/shard_map/concatenate | solution.py:141
  3.5 7.3 %all-to-all-start = ((bf16[8,272,128]{2,1,0:T(8,128)(2,1)}), bf16[8,272,128]{2,1,0:T(8,128)(2,1)S(1)}, u32[]{:S(2)}, u32[]{:S(2)}) async-start(bf16[8,272,128]{2,1,0:T(8,128)(2,1)} %fusion.1), calls=%async_computation | async-start | bytes 1114112 | tf_op jit(solution)/shard_map/all_to_all | solution.py:142
  10.8 0.1 fusion.6
  10.9 2.1 %collective-permute-start.11 = (bf16[256,1024]{1,0:T(8,128)(2,1)S(1)}, bf16[256,1024]{1,0:T(8,128)(2,1)}, u32[]{:S(2)}, u32[]{:S(2)}) collective-permute-start(bf16[256,1024]{1,0:T(8,128)(2,1)S(1)} %get-tuple-element.5.refs_11_), channel_id=1, source_target_pairs={{0,8},{8,16},{16,24},{24,28},{28,20},{20,12},{12,4},{4,0},{1,9},{9... | collective-permute-start | bytes 1572872 | tf_op jit(solution)/shard_map/ppermute | solution.py:128
  12.9 0.1 collective-permute-start.7
  13.0 2.0 %collective-permute-start.3 = (bf16[256,1024]{1,0:T(8,128)(2,1)S(1)}, bf16[256,1024]{1,0:T(8,128)(2,1)}, u32[]{:S(2)}, u32[]{:S(2)}) collective-permute-start(bf16[256,1024]{1,0:T(8,128)(2,1)S(1)} %get-tuple-element.6.refs_10_), channel_id=1, source_target_pairs={{0,8},{8,16},{16,24},{24,28},{28,20},{20,12},{12,4},{4,0},{1,9},{9... | collective-permute-start | bytes 1572872 | tf_op jit(solution)/shard_map/ppermute | solution.py:128
  15.0 12.4 %all-to-all-done.refs_0_ = bf16[8,272,128]{2,1,0:T(8,128)(2,1)S(1)} async-done(((bf16[8,272,128]{2,1,0:T(8,128)(2,1)}), bf16[8,272,128]{2,1,0:T(8,128)(2,1)S(1)}, u32[]{:S(2)}, u32[]{:S(2)}) %all-to-all-start) | async-done | bytes 557088 | tf_op jit(solution)/shard_map/all_to_all | solution.py:142
  27.4 1.5 %collective-permute-start = (bf16[8,272,128]{2,1,0:T(8,128)(2,1)S(1)}, bf16[8,272,128]{2,1,0:T(8,128)(2,1)S(1)}, u32[]{:S(2)}, u32[]{:S(2)}) collective-permute-start(bf16[8,272,128]{2,1,0:T(8,128)(2,1)S(1)} %all-to-all-done.refs_0_), channel_id=1, source_target_pairs={{0,2},{1,3},{2,0},{3,1},{4,6},{5,7},{6,4},{7,5},{8,10},{9,11},{10,... | collective-permute-start | bytes 1671176 | tf_op jit(solution)/shard_map/ppermute | solution.py:146
  28.9 1.1 collective-permute-start.14
  29.9 2.3 %collective-permute-done.11.refs_13_ = bf16[256,1024]{1,0:T(8,128)(2,1)} collective-permute-done((bf16[256,1024]{1,0:T(8,128)(2,1)S(1)}, bf16[256,1024]{1,0:T(8,128)(2,1)}, u32[]{:S(2)}, u32[]{:S(2)}) %collective-permute-start.11) | collective-permute-done | bytes 524320 | tf_op jit(solution)/shard_map/ppermute | solution.py:128
  32.2 4.1 %collective-permute-start.12 = (bf16[256,1024]{1,0:T(8,128)(2,1)}, bf16[256,1024]{1,0:T(8,128)(2,1)}, u32[]{:S(2)}, u32[]{:S(2)}) collective-permute-start(bf16[256,1024]{1,0:T(8,128)(2,1)} %collective-permute-done.11.refs_13_), channel_id=1, source_target_pairs={{0,8},{8,16},{16,24},{24,28},{28,20},{20,12},{12,4},{4,0},{1,9},{9... | collective-permute-start | bytes 1572872 | tf_op jit(solution)/shard_map/ppermute | solution.py:128
  36.3 7.2 %collective-permute-done.3.refs_12_ = bf16[256,1024]{1,0:T(8,128)(2,1)} collective-permute-done((bf16[256,1024]{1,0:T(8,128)(2,1)S(1)}, bf16[256,1024]{1,0:T(8,128)(2,1)}, u32[]{:S(2)}, u32[]{:S(2)}) %collective-permute-start.3) | collective-permute-done | bytes 524320 | tf_op jit(solution)/shard_map/ppermute | solution.py:128
  43.5 4.1 %collective-permute-start.4 = (bf16[256,1024]{1,0:T(8,128)(2,1)}, bf16[256,1024]{1,0:T(8,128)(2,1)}, u32[]{:S(2)}, u32[]{:S(2)}) collective-permute-start(bf16[256,1024]{1,0:T(8,128)(2,1)} %collective-permute-done.3.refs_12_), channel_id=1, source_target_pairs={{0,8},{8,16},{16,24},{24,28},{28,20},{20,12},{12,4},{4,0},{1,9},{9... | collective-permute-start | bytes 1572872 | tf_op jit(solution)/shard_map/ppermute | solution.py:128
  47.5 0.5 collective-permute-start.2
  48.1 6.7 %collective-permute-done.12.refs_17_ = bf16[256,1024]{1,0:T(8,128)(2,1)} collective-permute-done((bf16[256,1024]{1,0:T(8,128)(2,1)}, bf16[256,1024]{1,0:T(8,128)(2,1)}, u32[]{:S(2)}, u32[]{:S(2)}) %collective-permute-start.12) | collective-permute-done | bytes 524320 | tf_op jit(solution)/shard_map/ppermute | solution.py:128
  54.8 3.6 %collective-permute-start.15 = (bf16[256,1024]{1,0:T(8,128)(2,1)}, bf16[256,1024]{1,0:T(8,128)(2,1)}, u32[]{:S(2)}, u32[]{:S(2)}) collective-permute-start(bf16[256,1024]{1,0:T(8,128)(2,1)} %collective-permute-done.14.refs_14_), channel_id=1, source_target_pairs={{8,0},{16,8},{24,16},{28,24},{20,28},{12,20},{4,12},{0,4},{9,1},{1... | collective-permute-start | bytes 1572872 | tf_op jit(solution)/shard_map/ppermute | solution.py:129
  58.4 4.4 %collective-permute-start.9 = (bf16[256,1024]{1,0:T(8,128)(2,1)}, bf16[256,1024]{1,0:T(8,128)(2,1)}, u32[]{:S(2)}, u32[]{:S(2)}) collective-permute-start(bf16[256,1024]{1,0:T(8,128)(2,1)} %collective-permute-done.8.refs_19_), channel_id=1, source_target_pairs={{8,0},{16,8},{24,16},{28,24},{20,28},{12,20},{4,12},{0,4},{9,1},{1... | collective-permute-start | bytes 1572872 | tf_op jit(solution)/shard_map/ppermute | solution.py:129
  62.8 2.1 %collective-permute-done.4.refs_16_ = bf16[256,1024]{1,0:T(8,128)(2,1)} collective-permute-done((bf16[256,1024]{1,0:T(8,128)(2,1)}, bf16[256,1024]{1,0:T(8,128)(2,1)}, u32[]{:S(2)}, u32[]{:S(2)}) %collective-permute-start.4) | collective-permute-done | bytes 524320 | tf_op jit(solution)/shard_map/ppermute | solution.py:128
  64.9 4.5 %collective-permute-start.5 = (bf16[256,1024]{1,0:T(8,128)(2,1)}, bf16[256,1024]{1,0:T(8,128)(2,1)}, u32[]{:S(2)}, u32[]{:S(2)}) collective-permute-start(bf16[256,1024]{1,0:T(8,128)(2,1)} %collective-permute-done.4.refs_16_), channel_id=1, source_target_pairs={{0,8},{8,16},{16,24},{24,28},{28,20},{20,12},{12,4},{4,0},{1,9},{9... | collective-permute-start | bytes 1572872 | tf_op jit(solution)/shard_map/ppermute | solution.py:128
  69.4 0.6 dynamic_slice.25
  74.7 0.7 fusion.7
  79.8 0.7 stack.17.idx_ref
  80.4 0.6 pad_add_fusion.idx_ref
  81.0 0.6 pad_add_fusion.1.idx_ref
  81.6 0.1 copy.29
  81.7 0.1 copy.33
  81.8 0.1 copy.30
  81.9 0.1 copy.34
  82.0 2.5 %collective-permute-start.13 = (bf16[256,1024]{1,0:T(8,128)(2,1)}, bf16[256,1024]{1,0:T(8,128)(2,1)}, u32[]{:S(2)}, u32[]{:S(2)}) collective-permute-start(bf16[256,1024]{1,0:T(8,128)(2,1)} %collective-permute-done.12.refs_17_), channel_id=1, source_target_pairs={{0,8},{8,16},{16,24},{24,28},{28,20},{20,12},{12,4},{4,0},{1,9},{9... | collective-permute-start | bytes 1572872 | tf_op jit(solution)/shard_map/ppermute | solution.py:128
  84.5 0.1 copy.31
  84.6 0.1 copy.35
  84.7 1.2 collective-permute-start.10
  85.9 0.9 collective-permute-start.6
  86.8 0.1 copy.32
  86.9 0.1 copy.36
  87.0 0.1 copy.37
  87.1 0.3 fusion.2
  87.4 0.3 compare_reduce_fusion
  87.7 0.1 copy.38
  87.8 0.1 copy.39
  87.9 0.1 fusion.3.dest_ref
  88.0 5.8 %shard_map.82.refs_0_.refs_1_.refs_2_.refs_3_.refs_4_.refs_5_.refs_6_.refs_7_.refs_8_.refs_9_ = bf16[16,1024,256]{2,1,0:T(8,128)(2,1)} custom-call(s32[4,8,2]{2,1,0:T(8,128)S(1)} %fusion.3.dest_ref, bf16[8,272,128]{2,1,0:T(8,128)(2,1)S(1)} %all-to-all-done.refs_0_, bf16[8,272,128]{2,1,0:T(8,128)(2,1)S(1)} %collective-permute-done.refs_1_, ...), custom_call_target="tpu_custom_call" | custom-call | bytes 16777216 | tf_op jit(solution)/shard_map/pallas_call | solution.py:46
  93.8 11.3 %shard_map.83.refs_8_ = f32[1024,1024]{1,0:T(8,128)} custom-call(s32[10]{0:T(128)} %stack.17.idx_ref, bf16[16,1024,256]{2,1,0:T(8,128)(2,1)} %shard_map.82.refs_0_.refs_1_.refs_2_.refs_3_.refs_4_.refs_5_.refs_6_.refs_7_.refs_8_.refs_9_, bf16[16,1024,256]{2,1,0:T(8,128)(2,1)} %shard_map.82.refs_0_.refs_1_.refs_2_.refs_3_.refs_4_.refs_5_.refs_6_.refs_7_.refs_8_.refs_9_, ...), custom_call_target="tpu_custom_call" | custom-call | flops 5368709120 | bytes 18874368 | tf_op jit(solution)/shard_map/pallas_call | solution.py:84
  105.2 8.3 %shard_map.84.refs_4_ = f32[1024,1024]{1,0:T(8,128)} custom-call(s32[4]{0:T(128)} %pad_add_fusion.1.idx_ref, bf16[16,1024,256]{2,1,0:T(8,128)(2,1)} %shard_map.82.refs_0_.refs_1_.refs_2_.refs_3_.refs_4_.refs_5_.refs_6_.refs_7_.refs_8_.refs_9_, bf16[16,1024,256]{2,1,0:T(8,128)(2,1)} %shard_map.82.refs_0_.refs_1_.refs_2_.refs_3_.refs_4_.refs_5_.refs_6_.refs_7_.refs_8_.refs_9_, ...), custom_call_target="tpu_custom_call" | custom-call | flops 2147483648 | bytes 12582912 | tf_op jit(solution)/shard_map/pallas_call | solution.py:84
  113.5 6.3 %shard_map.85 = bf16[1024,1024]{1,0:T(8,128)(2,1)} custom-call(s32[2]{0:T(128)} %pad_add_fusion.idx_ref, bf16[16,1024,256]{2,1,0:T(8,128)(2,1)} %shard_map.82.refs_0_.refs_1_.refs_2_.refs_3_.refs_4_.refs_5_.refs_6_.refs_7_.refs_8_.refs_9_, bf16[16,1024,256]{2,1,0:T(8,128)(2,1)} %shard_map.82.refs_0_.refs_1_.refs_2_.refs_3_.refs_4_.refs_5_.refs_6_.refs_7_.refs_8_.refs_9_, ...), custom_call_target="tpu_custom_call" | custom-call | flops 1073741824 | bytes 10485760 | tf_op jit(solution)/shard_map/pallas_call | solution.py:84
  (35 shorter events, 0.1 us)
Async XLA Ops:
  0.0 10.7 %copy-start.2 = (bf16[512,1024]{1,0:T(8,128)(2,1)S(1)}, bf16[512,1024]{1,0:T(8,128)(2,1)}, u32[]{:S(2)}) copy-start(bf16[512,1024]{1,0:T(8,128)(2,1)} %param.13) | copy-start | bytes 3145732
  3.5 23.9 %all-to-all-start = ((bf16[8,272,128]{2,1,0:T(8,128)(2,1)}), bf16[8,272,128]{2,1,0:T(8,128)(2,1)S(1)}, u32[]{:S(2)}, u32[]{:S(2)}) async-start(bf16[8,272,128]{2,1,0:T(8,128)(2,1)} %fusion.1), calls=%async_computation | async-start | bytes 1114112 | tf_op jit(solution)/shard_map/all_to_all | solution.py:142
  10.7 58.6 %copy-start.5 = (s32[8]{0:T(128)S(1)}, s32[8]{0:T(128)}, u32[]{:S(2)}) copy-start(s32[8]{0:T(128)} %constant.105.clone) | copy-start | bytes 100
  10.8 63.9 %copy-start.3 = (s32[8]{0:T(128)S(1)}, s32[8]{0:T(128)}, u32[]{:S(2)}) copy-start(s32[8]{0:T(128)} %constant.104.clone) | copy-start | bytes 100
  10.8 70.8 %copy-start.4 = (s32[1,8]{1,0:T(1,128)S(1)}, s32[1,8]{1,0:T(1,128)}, u32[]{:S(2)}) copy-start(s32[1,8]{1,0:T(1,128)} %param.12) | copy-start | bytes 100
  10.9 83.0 %copy-start = (bf16[256,1024]{1,0:T(8,128)(2,1)}, bf16[256,1024]{1,0:T(8,128)(2,1)S(1)}, u32[]{:S(2)}) copy-start(bf16[256,1024]{1,0:T(8,128)(2,1)S(1)} %get-tuple-element.5.refs_11_) | copy-start | bytes 1572868
  10.9 82.9 %copy-start.1 = (bf16[256,1024]{1,0:T(8,128)(2,1)}, bf16[256,1024]{1,0:T(8,128)(2,1)S(1)}, u32[]{:S(2)}) copy-start(bf16[256,1024]{1,0:T(8,128)(2,1)S(1)} %get-tuple-element.6.refs_10_) | copy-start | bytes 1572868
  10.9 21.3 %collective-permute-start.11 = (bf16[256,1024]{1,0:T(8,128)(2,1)S(1)}, bf16[256,1024]{1,0:T(8,128)(2,1)}, u32[]{:S(2)}, u32[]{:S(2)}) collective-permute-start(bf16[256,1024]{1,0:T(8,128)(2,1)S(1)} %get-tuple-element.5.refs_11_), channel_id=1, source_target_pairs={{0,8},{8,16},{16,24},{24,28},{28,20},{20,12},{12,4},{4,0},{1,9},{9... | collective-permute-start | bytes 1572872 | tf_op jit(solution)/shard_map/ppermute | solution.py:128
  12.9 23.4 %collective-permute-start.7 = (bf16[256,1024]{1,0:T(8,128)(2,1)S(1)}, bf16[256,1024]{1,0:T(8,128)(2,1)}, u32[]{:S(2)}, u32[]{:S(2)}) collective-permute-start(bf16[256,1024]{1,0:T(8,128)(2,1)S(1)} %get-tuple-element.5.refs_11_), channel_id=1, source_target_pairs={{8,0},{16,8},{24,16},{28,24},{20,28},{12,20},{4,12},{0,4},{9,1},{1... | collective-permute-start | bytes 1572872 | tf_op jit(solution)/shard_map/ppermute | solution.py:129
  13.0 30.5 %collective-permute-start.3 = (bf16[256,1024]{1,0:T(8,128)(2,1)S(1)}, bf16[256,1024]{1,0:T(8,128)(2,1)}, u32[]{:S(2)}, u32[]{:S(2)}) collective-permute-start(bf16[256,1024]{1,0:T(8,128)(2,1)S(1)} %get-tuple-element.6.refs_10_), channel_id=1, source_target_pairs={{0,8},{8,16},{16,24},{24,28},{28,20},{20,12},{12,4},{4,0},{1,9},{9... | collective-permute-start | bytes 1572872 | tf_op jit(solution)/shard_map/ppermute | solution.py:128
  27.4 20.1 %collective-permute-start = (bf16[8,272,128]{2,1,0:T(8,128)(2,1)S(1)}, bf16[8,272,128]{2,1,0:T(8,128)(2,1)S(1)}, u32[]{:S(2)}, u32[]{:S(2)}) collective-permute-start(bf16[8,272,128]{2,1,0:T(8,128)(2,1)S(1)} %all-to-all-done.refs_0_), channel_id=1, source_target_pairs={{0,2},{1,3},{2,0},{3,1},{4,6},{5,7},{6,4},{7,5},{8,10},{9,11},{10,... | collective-permute-start | bytes 1671176 | tf_op jit(solution)/shard_map/ppermute | solution.py:146
  28.9 18.6 %collective-permute-start.14 = (bf16[256,1024]{1,0:T(8,128)(2,1)S(1)}, bf16[256,1024]{1,0:T(8,128)(2,1)}, u32[]{:S(2)}, u32[]{:S(2)}) collective-permute-start(bf16[256,1024]{1,0:T(8,128)(2,1)S(1)} %get-tuple-element.6.refs_10_), channel_id=1, source_target_pairs={{8,0},{16,8},{24,16},{28,24},{20,28},{12,20},{4,12},{0,4},{9,1},{1... | collective-permute-start | bytes 1572872 | tf_op jit(solution)/shard_map/ppermute | solution.py:129
  32.2 22.6 %collective-permute-start.12 = (bf16[256,1024]{1,0:T(8,128)(2,1)}, bf16[256,1024]{1,0:T(8,128)(2,1)}, u32[]{:S(2)}, u32[]{:S(2)}) collective-permute-start(bf16[256,1024]{1,0:T(8,128)(2,1)} %collective-permute-done.11.refs_13_), channel_id=1, source_target_pairs={{0,8},{8,16},{16,24},{24,28},{28,20},{20,12},{12,4},{4,0},{1,9},{9... | collective-permute-start | bytes 1572872 | tf_op jit(solution)/shard_map/ppermute | solution.py:128
  36.3 22.1 %collective-permute-start.8 = (bf16[256,1024]{1,0:T(8,128)(2,1)}, bf16[256,1024]{1,0:T(8,128)(2,1)}, u32[]{:S(2)}, u32[]{:S(2)}) collective-permute-start(bf16[256,1024]{1,0:T(8,128)(2,1)} %collective-permute-done.7.refs_15_), channel_id=1, source_target_pairs={{8,0},{16,8},{24,16},{28,24},{20,28},{12,20},{4,12},{0,4},{9,1},{1... | collective-permute-start | bytes 1572872 | tf_op jit(solution)/shard_map/ppermute | solution.py:129
  43.5 21.4 %collective-permute-start.4 = (bf16[256,1024]{1,0:T(8,128)(2,1)}, bf16[256,1024]{1,0:T(8,128)(2,1)}, u32[]{:S(2)}, u32[]{:S(2)}) collective-permute-start(bf16[256,1024]{1,0:T(8,128)(2,1)} %collective-permute-done.3.refs_12_), channel_id=1, source_target_pairs={{0,8},{8,16},{16,24},{24,28},{28,20},{20,12},{12,4},{4,0},{1,9},{9... | collective-permute-start | bytes 1572872 | tf_op jit(solution)/shard_map/ppermute | solution.py:128
  47.5 36.9 %collective-permute-start.1 = (bf16[8,272,128]{2,1,0:T(8,128)(2,1)S(1)}, bf16[8,272,128]{2,1,0:T(8,128)(2,1)S(1)}, u32[]{:S(2)}, u32[]{:S(2)}) collective-permute-start(bf16[8,272,128]{2,1,0:T(8,128)(2,1)S(1)} %all-to-all-done.refs_0_), channel_id=1, source_target_pairs={{0,1},{1,0},{2,3},{3,2},{4,5},{5,4},{6,7},{7,6},{8,9},{9,8},{10,11... | collective-permute-start | bytes 1671176 | tf_op jit(solution)/shard_map/ppermute | solution.py:150
  47.5 39.2 %collective-permute-start.2 = (bf16[8,272,128]{2,1,0:T(8,128)(2,1)S(1)}, bf16[8,272,128]{2,1,0:T(8,128)(2,1)S(1)}, u32[]{:S(2)}, u32[]{:S(2)}) collective-permute-start(bf16[8,272,128]{2,1,0:T(8,128)(2,1)S(1)} %collective-permute-done.refs_1_), channel_id=1, source_target_pairs={{0,1},{1,0},{2,3},{3,2},{4,5},{5,4},{6,7},{7,6},{8,9},{9,8},{10,11... | collective-permute-start | bytes 1671176 | tf_op jit(solution)/shard_map/ppermute | solution.py:151
  54.8 27.2 %collective-permute-start.15 = (bf16[256,1024]{1,0:T(8,128)(2,1)}, bf16[256,1024]{1,0:T(8,128)(2,1)}, u32[]{:S(2)}, u32[]{:S(2)}) collective-permute-start(bf16[256,1024]{1,0:T(8,128)(2,1)} %collective-permute-done.14.refs_14_), channel_id=1, source_target_pairs={{8,0},{16,8},{24,16},{28,24},{20,28},{12,20},{4,12},{0,4},{9,1},{1... | collective-permute-start | bytes 1572872 | tf_op jit(solution)/shard_map/ppermute | solution.py:129
  58.4 26.3 %collective-permute-start.9 = (bf16[256,1024]{1,0:T(8,128)(2,1)}, bf16[256,1024]{1,0:T(8,128)(2,1)}, u32[]{:S(2)}, u32[]{:S(2)}) collective-permute-start(bf16[256,1024]{1,0:T(8,128)(2,1)} %collective-permute-done.8.refs_19_), channel_id=1, source_target_pairs={{8,0},{16,8},{24,16},{28,24},{20,28},{12,20},{4,12},{0,4},{9,1},{1... | collective-permute-start | bytes 1572872 | tf_op jit(solution)/shard_map/ppermute | solution.py:129
  64.9 21.0 %collective-permute-start.5 = (bf16[256,1024]{1,0:T(8,128)(2,1)}, bf16[256,1024]{1,0:T(8,128)(2,1)}, u32[]{:S(2)}, u32[]{:S(2)}) collective-permute-start(bf16[256,1024]{1,0:T(8,128)(2,1)} %collective-permute-done.4.refs_16_), channel_id=1, source_target_pairs={{0,8},{8,16},{16,24},{24,28},{28,20},{20,12},{12,4},{4,0},{1,9},{9... | collective-permute-start | bytes 1572872 | tf_op jit(solution)/shard_map/ppermute | solution.py:128
  82.0 23.2 %collective-permute-start.13 = (bf16[256,1024]{1,0:T(8,128)(2,1)}, bf16[256,1024]{1,0:T(8,128)(2,1)}, u32[]{:S(2)}, u32[]{:S(2)}) collective-permute-start(bf16[256,1024]{1,0:T(8,128)(2,1)} %collective-permute-done.12.refs_17_), channel_id=1, source_target_pairs={{0,8},{8,16},{16,24},{24,28},{28,20},{20,12},{12,4},{4,0},{1,9},{9... | collective-permute-start | bytes 1572872 | tf_op jit(solution)/shard_map/ppermute | solution.py:128
  84.5 20.7 %collective-permute-start.16 = (bf16[256,1024]{1,0:T(8,128)(2,1)}, bf16[256,1024]{1,0:T(8,128)(2,1)}, u32[]{:S(2)}, u32[]{:S(2)}) collective-permute-start(bf16[256,1024]{1,0:T(8,128)(2,1)} %collective-permute-done.15.refs_18_), channel_id=1, source_target_pairs={{8,0},{16,8},{24,16},{28,24},{20,28},{12,20},{4,12},{0,4},{9,1},{1... | collective-permute-start | bytes 1572872 | tf_op jit(solution)/shard_map/ppermute | solution.py:129
  84.7 28.8 %collective-permute-start.10 = (bf16[256,1024]{1,0:T(8,128)(2,1)}, bf16[256,1024]{1,0:T(8,128)(2,1)}, u32[]{:S(2)}, u32[]{:S(2)}) collective-permute-start(bf16[256,1024]{1,0:T(8,128)(2,1)} %collective-permute-done.9.refs_7_), channel_id=1, source_target_pairs={{8,0},{16,8},{24,16},{28,24},{20,28},{12,20},{4,12},{0,4},{9,1},{1... | collective-permute-start | bytes 1572872 | tf_op jit(solution)/shard_map/ppermute | solution.py:129
  85.9 27.6 %collective-permute-start.6 = (bf16[256,1024]{1,0:T(8,128)(2,1)}, bf16[256,1024]{1,0:T(8,128)(2,1)}, u32[]{:S(2)}, u32[]{:S(2)}) collective-permute-start(bf16[256,1024]{1,0:T(8,128)(2,1)} %collective-permute-done.5.refs_4_), channel_id=1, source_target_pairs={{0,8},{8,16},{16,24},{24,28},{28,20},{20,12},{12,4},{4,0},{1,9},{9... | collective-permute-start | bytes 1572872 | tf_op jit(solution)/shard_map/ppermute | solution.py:128

commit v2 on v1

v2 whole, which is shorter than its diff:
```python
import functools

import jax
import jax.numpy as jnp
from jax import lax
from jax.experimental import pallas as pl
from jax.experimental.pallas import tpu as pltpu
from jax.sharding import PartitionSpec as P

META = 16


def ring_order(n):
    return list(range(0, n, 2)) + list(range(n - 1, 0, -2))


def ring_place(g, n):
    return jnp.where(g % 2 == 0, g // 2, n - 1 - g // 2)


def build_kernel(dims, bounds, pos_ref, owned_ref, *refs):
    n_parts, per_part, cap, bs, groups, blocks = dims
    metas, parts = refs[:n_parts], refs[n_parts : 2 * n_parts]
    tiles = refs[2 * n_parts :]
    for tile in tiles:
        tile[...] = jnp.zeros_like(tile)
    half, per = groups // 2, blocks // 2
    for meta, part in zip(metas, parts):

        def place(i, carry):
            for c in range(cap):
                code, col = meta[i, c], meta[i, cap + c]
                row, found = jnp.int32(0), jnp.int32(0)
                for r in range(owned_ref.shape[0]):
                    hit = owned_ref[r] + 1 == code
                    row = jnp.where(hit, r, row)
                    found = jnp.where(hit, 1, found)
                owner, local = col // blocks, col % blocks
                ahead = lax.rem(ring_place(owner, groups) - pos_ref[0] + groups, groups)
                hops = jnp.minimum(ahead, groups - ahead)
                first = jnp.where(hops == 0, 0, per * (2 * hops - 1))
                first += jnp.where((ahead > 0) & (ahead < half), per, 0)
                piece = first + local // 2
                for (low, high), tile in zip(bounds, tiles):

                    @pl.when((found == 1) & (piece >= low) & (piece < high))
                    def _():
                        at = ((piece - low) * 2 + local % 2) * bs
                        tile[
                            pl.ds(pl.multiple_of(row * bs, bs), bs),
                            pl.ds(pl.multiple_of(at, bs), bs),
                        ] = part[i, pl.ds(c * bs, bs), :]

            return carry

        lax.fori_loop(0, per_part, place, 0)


def build_tiles(pos, owned, metas, parts, dims, bounds, rows):
    n_parts, _, _, bs, groups, blocks = dims
    smem = pl.BlockSpec(memory_space=pltpu.SMEM)
    vmem = pl.BlockSpec(memory_space=pltpu.VMEM)
    return pl.pallas_call(
        functools.partial(build_kernel, dims, bounds),
        out_shape=[
            jax.ShapeDtypeStruct((rows, (high - low) * 2 * bs), jnp.bfloat16)
            for low, high in bounds
        ],
        in_specs=[smem] * (2 + n_parts) + [vmem] * n_parts,
        out_specs=[vmem] * len(bounds),
        compiler_params=pltpu.CompilerParams(vmem_limit_bytes=48 << 20),
        cost_estimate=pl.CostEstimate(
            flops=0, bytes_accessed=rows * groups * blocks * bs * 4, transcendentals=0
        ),
    )(pos, owned, *metas, *parts)


def mul_kernel(n_pieces, tile_ref, *refs):
    right = jnp.concatenate([piece[...] for piece in refs[:n_pieces]], axis=0)
    total = jnp.dot(tile_ref[...], right, preferred_element_type=jnp.float32)
    if len(refs) == n_pieces + 2:
        total += refs[n_pieces][...]
    refs[-1][...] = total.astype(refs[-1].dtype)


def mul(tile, pieces, acc, out_dtype):
    n = len(pieces)
    rows, inner = tile.shape
    depth, cols = pieces[0].shape
    bn = 256
    in_specs = [pl.BlockSpec((rows, inner), lambda j: (0, 0))]
    in_specs += [pl.BlockSpec((depth, bn), lambda j: (0, j)) for _ in range(n)]
    args = [tile, *pieces]
    if acc is not None:
        in_specs.append(pl.BlockSpec((rows, bn), lambda j: (0, j)))
        args.append(acc)
    return pl.pallas_call(
        functools.partial(mul_kernel, n),
        out_shape=jax.ShapeDtypeStruct((rows, cols), out_dtype),
        grid=(cols // bn,),
        in_specs=in_specs,
        out_specs=pl.BlockSpec((rows, bn), lambda j: (0, j)),
        compiler_params=pltpu.CompilerParams(vmem_limit_bytes=56 << 20),
        cost_estimate=pl.CostEstimate(
            flops=2 * rows * inner * cols,
            bytes_accessed=(rows + cols) * inner * 2 + rows * cols * 8,
            transcendentals=0,
        ),
    )(*args)


def body(a_slots, a_rows, a_cols, a_count, owned_rows, b_matrix):
    groups = lax.axis_size("grid")
    columns = lax.axis_size("blk")
    bs = a_slots.shape[-1]
    cap = a_slots.shape[3]
    rb = owned_rows.shape[-1]
    blocks = b_matrix.shape[0] // bs
    depth = 2 * bs
    per = blocks // 2
    half = groups // 2
    pos = ring_place(lax.axis_index("grid"), groups).reshape(1)

    order = ring_order(groups)
    to_right = [(order[i], order[(i + 1) % groups]) for i in range(groups)]
    to_left = [(order[(i + 1) % groups], order[i]) for i in range(groups)]

    own = [b_matrix[h * depth : (h + 1) * depth] for h in range(per)]
    events = [own]
    from_left, from_right = list(own), list(own)
    for s in range(1, half + 1):
        low = range(per) if s < half else range(per // 2)
        high = range(per) if s < half else range(per // 2, per)
        from_left = {h: lax.ppermute(from_left[h], "grid", to_right) for h in low}
        from_right = {h: lax.ppermute(from_right[h], "grid", to_left) for h in high}
        events.append([from_left[h] for h in low] + [from_right[h] for h in high])

    live = jnp.arange(cap, dtype=jnp.int32)[None, :] < a_count.reshape(groups, 1)
    row_code = jnp.where(live, a_rows.reshape(groups, cap) + 1, 0)
    meta = jnp.concatenate([row_code, a_cols.reshape(groups, cap)], axis=1)
    meta = jnp.pad(meta.astype(jnp.bfloat16)[:, None, :], ((0, 0), (0, META - 1), (0, bs - 2 * cap)))
    message = jnp.concatenate([a_slots.reshape(groups, cap * bs, bs), meta], axis=1)
    landed = lax.all_to_all(message, "grid", split_axis=0, concat_axis=0, tiled=True)
    if columns == 4:
        swap_core = [(j, j ^ 1) for j in range(columns)]
        swap_chip = [(j, j ^ 2) for j in range(columns)]
        across = lax.ppermute(landed, "blk", swap_chip)
        parts = [
            landed,
            across,
            lax.ppermute(landed, "blk", swap_core),
            lax.ppermute(across, "blk", swap_core),
        ]
    else:
        gathered = lax.all_gather(landed, "blk", axis=0)
        parts = [gathered[j] for j in range(columns)]
    metas = [p[:, cap * bs, : 2 * cap].astype(jnp.int32) for p in parts]

    stages = [sum(events[: half - 1], []), events[half - 1], events[half]]
    bounds, start = [], 0
    for stage in stages:
        bounds.append((start, start + len(stage)))
        start += len(stage)
    dims = (columns, groups, cap, bs, groups, blocks)
    tiles = build_tiles(pos, owned_rows.reshape(rb), metas, parts, dims, bounds, rb * bs)

    acc = None
    for t, (tile, stage) in enumerate(zip(tiles, stages)):
        acc = mul(tile, stage, acc, jnp.bfloat16 if t == len(stages) - 1 else jnp.float32)
    return acc


def solution(mesh):
    in_specs = (
        P("grid", "blk", None, None, None, None),
        P("grid", "blk", None, None),
        P("grid", "blk", None, None),
        P("grid", "blk", None),
        P("grid", None),
        P("grid", "blk"),
    )
    out_specs = P("grid", "blk")
    return jax.shard_map(body, mesh=mesh, in_specs=in_specs, out_specs=out_specs, check_vma=False)
```

time: 120 us -> 124 us (1.033)
  waiting for transfers between devices: 30.7 us -> 49.8 us
  between operations: 9.23 us -> 0.17 us
  starting transfers between devices: 39.6 us -> 33.5 us
  other arithmetic: 5.18 us -> 3.39 us
  local copies, waits for them, and re-layouts: 3.25 us -> 4.52 us
    ppermute x7, waiting for transfers between devices: 18.3 us -> 36.4 us  [body(): from_left = {h: lax.ppermute(from_left[h], 'grid', to_right) for h in low}]
    ppermute x7, waiting for transfers between devices: 0.02 us -> 13.4 us  [body(): from_right = {h: lax.ppermute(from_right[h], 'grid', to_left) for h in high}]
    all_to_all x1, waiting for transfers between devices: 12.4 us -> 0.01 us  [body(): lax.all_to_all(message, 'grid', split_axis=0, concat_axis=0, tiled=True)]
    ppermute x7, starting transfers between devices: 10.3 us -> 5.41 us  [body(): from_right = {h: lax.ppermute(from_right[h], 'grid', to_left) for h in high}]
    unnamed x12 -> x26, local copies, waits for them, and re-layouts: 0.03 us -> 4.35 us
    dynamic_slice x2 -> x0, local copies, waits for them, and re-layouts: 1.27 us -> none  [the longest x1 0.68 us: body(): right_owner = table[(pos + s) % groups]]
  transfers between devices with their start and end apart: 18 -> 18, of which waited for: 5 -> 6; matrix products, arithmetic and copies ran while one was open for 4% -> 0% of each run, Pallas kernels for 21% -> 21%
where the time goes in v2:
time: 124 us; the launch traced here: 123 us
  waiting for transfers between devices  49.8 us (40%)
  starting transfers between devices  33.5 us (27%)
  Pallas kernels  31.8 us (26%)
  local copies, waits for them, and re-layouts  4.52 us (4%)
  other arithmetic  3.39 us (3%)
    ppermute x7, waiting for transfers between devices, body(): from_left = {h: lax.ppermute(from_left[h], 'grid', to_right) for h in low}  36.4 us
    pallas_call x3, Pallas kernels, mul(): pl.pallas_call(functools.partial(mul_kernel, n), out_shape=jax.ShapeDtype...  24.1 us
    ppermute x7, starting transfers between devices, body(): from_left = {h: lax.ppermute(from_left[h], 'grid', to_right) for h in low}  19.2 us
    ppermute x7, waiting for transfers between devices, body(): from_right = {h: lax.ppermute(from_right[h], 'grid', to_left) for h in high}  13.4 us
    pallas_call x1, Pallas kernels, build_tiles(): pl.pallas_call(functools.partial(build_kernel, dims, bounds), out_shape=[...  7.7 us
    all_to_all x1, starting transfers between devices, body(): lax.all_to_all(message, 'grid', split_axis=0, concat_axis=0, tiled=True)  7.28 us
    ppermute x7, starting transfers between devices, body(): from_right = {h: lax.ppermute(from_right[h], 'grid', to_left) for h in high}  5.41 us
    unnamed x26, local copies, waits for them, and re-layouts  4.35 us
  transfers between devices with their start and end apart: 18, of which 6 were waited for; matrix products, arithmetic and copies ran while one was open for 0% of the time, Pallas kernels for 21%

profile of v2, /device:TPU:0, one launch (start us, length us, event | category | flops | bytes accessed | tf_op | source)
XLA Modules:
  0.0 123.3 jit_solution(4079531954643542515)
XLA Ops:
  0.0 0.8 convert_bitcast_fusion
  0.8 0.7 fusion.3
  1.5 0.1 copy.26
  1.6 1.9 %fusion.1 = bf16[8,272,128]{2,1,0:T(8,128)(2,1)} fusion(bf16[8,1,4]{2,1,0:T(2,128)(2,1)S(1)} %copy.26, bf16[8,256,128]{2,1,0:T(8,128)(2,1)} %bitcast.21), kind=kLoop, calls=%fused_computation.2 | loop fusion | flops 1671168 | bytes 1081408 | tf_op jit(solution)/shard_map/concatenate | solution.py:142
  3.5 7.3 %all-to-all-start = ((bf16[8,272,128]{2,1,0:T(8,128)(2,1)}), bf16[8,272,128]{2,1,0:T(8,128)(2,1)S(1)}, u32[]{:S(2)}, u32[]{:S(2)}) async-start(bf16[8,272,128]{2,1,0:T(8,128)(2,1)} %fusion.1), calls=%async_computation | async-start | bytes 1114112 | tf_op jit(solution)/shard_map/all_to_all | solution.py:143
  10.8 0.1 fusion.4
  10.9 2.1 %collective-permute-start.11 = (bf16[256,1024]{1,0:T(8,128)(2,1)S(1)}, bf16[256,1024]{1,0:T(8,128)(2,1)S(1)}, u32[]{:S(2)}, u32[]{:S(2)}) collective-permute-start(bf16[256,1024]{1,0:T(8,128)(2,1)S(1)} %get-tuple-element.11.refs_1_), channel_id=1, source_target_pairs={{0,8},{8,16},{16,24},{24,28},{28,20},{20,12},{12,4},{4,0},{1,9},{9... | collective-permute-start | bytes 1572872 | tf_op jit(solution)/shard_map/ppermute | solution.py:134
  12.9 1.5 %collective-permute-start.3 = (bf16[256,1024]{1,0:T(8,128)(2,1)S(1)}, bf16[256,1024]{1,0:T(8,128)(2,1)}, u32[]{:S(2)}, u32[]{:S(2)}) collective-permute-start(bf16[256,1024]{1,0:T(8,128)(2,1)S(1)} %get-tuple-element.12.refs_0_), channel_id=1, source_target_pairs={{0,8},{8,16},{16,24},{24,28},{28,20},{20,12},{12,4},{4,0},{1,9},{9... | collective-permute-start | bytes 1572872 | tf_op jit(solution)/shard_map/ppermute | solution.py:134
  14.4 0.6 collective-permute-start.7
  15.0 0.1 collective-permute-start.14
  15.0 17.2 %collective-permute-done.11.refs_3_ = bf16[256,1024]{1,0:T(8,128)(2,1)S(1)} collective-permute-done((bf16[256,1024]{1,0:T(8,128)(2,1)S(1)}, bf16[256,1024]{1,0:T(8,128)(2,1)S(1)}, u32[]{:S(2)}, u32[]{:S(2)}) %collective-permute-start.11) | collective-permute-done | bytes 524320 | tf_op jit(solution)/shard_map/ppermute | solution.py:134
  32.2 4.1 %collective-permute-start.12 = (bf16[256,1024]{1,0:T(8,128)(2,1)S(1)}, bf16[256,1024]{1,0:T(8,128)(2,1)}, u32[]{:S(2)}, u32[]{:S(2)}) collective-permute-start(bf16[256,1024]{1,0:T(8,128)(2,1)S(1)} %collective-permute-done.11.refs_3_), channel_id=1, source_target_pairs={{0,8},{8,16},{16,24},{24,28},{28,20},{20,12},{12,4},{4,0},{1,9},{9... | collective-permute-start | bytes 1572872 | tf_op jit(solution)/shard_map/ppermute | solution.py:134
  36.3 0.0 all-to-all-done.refs_4_
  36.3 1.5 %collective-permute-start = (bf16[8,272,128]{2,1,0:T(8,128)(2,1)S(1)}, bf16[8,272,128]{2,1,0:T(8,128)(2,1)S(1)}, u32[]{:S(2)}, u32[]{:S(2)}) collective-permute-start(bf16[8,272,128]{2,1,0:T(8,128)(2,1)S(1)} %all-to-all-done.refs_4_), channel_id=1, source_target_pairs={{0,2},{1,3},{2,0},{3,1},{4,6},{5,7},{6,4},{7,5},{8,10},{9,11},{10,... | collective-permute-start | bytes 1671176 | tf_op jit(solution)/shard_map/ppermute | solution.py:147
  37.8 5.7 %collective-permute-done.3.refs_2_ = bf16[256,1024]{1,0:T(8,128)(2,1)} collective-permute-done((bf16[256,1024]{1,0:T(8,128)(2,1)S(1)}, bf16[256,1024]{1,0:T(8,128)(2,1)}, u32[]{:S(2)}, u32[]{:S(2)}) %collective-permute-start.3) | collective-permute-done | bytes 524320 | tf_op jit(solution)/shard_map/ppermute | solution.py:134
  43.5 4.1 %collective-permute-start.4 = (bf16[256,1024]{1,0:T(8,128)(2,1)}, bf16[256,1024]{1,0:T(8,128)(2,1)}, u32[]{:S(2)}, u32[]{:S(2)}) collective-permute-start(bf16[256,1024]{1,0:T(8,128)(2,1)} %collective-permute-done.3.refs_2_), channel_id=1, source_target_pairs={{0,8},{8,16},{16,24},{24,28},{28,20},{20,12},{12,4},{4,0},{1,9},{9... | collective-permute-start | bytes 1572872 | tf_op jit(solution)/shard_map/ppermute | solution.py:134
  47.6 0.0 collective-permute-done.7.refs_5_
  47.6 0.0 collective-permute-start.8
  47.6 0.0 collective-permute-done.14.refs_4_
  47.6 0.1 collective-permute-start.1
  47.6 7.1 %collective-permute-done.12.refs_7_ = bf16[256,1024]{1,0:T(8,128)(2,1)} collective-permute-done((bf16[256,1024]{1,0:T(8,128)(2,1)S(1)}, bf16[256,1024]{1,0:T(8,128)(2,1)}, u32[]{:S(2)}, u32[]{:S(2)}) %collective-permute-start.12) | collective-permute-done | bytes 524320 | tf_op jit(solution)/shard_map/ppermute | solution.py:134
  54.7 3.7 %collective-permute-start.15 = (bf16[256,1024]{1,0:T(8,128)(2,1)}, bf16[256,1024]{1,0:T(8,128)(2,1)}, u32[]{:S(2)}, u32[]{:S(2)}) collective-permute-start(bf16[256,1024]{1,0:T(8,128)(2,1)} %collective-permute-done.14.refs_4_), channel_id=1, source_target_pairs={{8,0},{16,8},{24,16},{28,24},{20,28},{12,20},{4,12},{0,4},{9,1},{1... | collective-permute-start | bytes 1572872 | tf_op jit(solution)/shard_map/ppermute | solution.py:135
  58.4 6.5 %collective-permute-done.4.refs_6_ = bf16[256,1024]{1,0:T(8,128)(2,1)} collective-permute-done((bf16[256,1024]{1,0:T(8,128)(2,1)}, bf16[256,1024]{1,0:T(8,128)(2,1)}, u32[]{:S(2)}, u32[]{:S(2)}) %collective-permute-start.4) | collective-permute-done | bytes 524320 | tf_op jit(solution)/shard_map/ppermute | solution.py:134
  64.9 4.5 %collective-permute-start.5 = (bf16[256,1024]{1,0:T(8,128)(2,1)}, bf16[256,1024]{1,0:T(8,128)(2,1)S(1)}, u32[]{:S(2)}, u32[]{:S(2)}) collective-permute-start(bf16[256,1024]{1,0:T(8,128)(2,1)} %collective-permute-done.4.refs_6_), channel_id=1, source_target_pairs={{0,8},{8,16},{16,24},{24,28},{28,20},{20,12},{12,4},{4,0},{1,9},{9... | collective-permute-start | bytes 1572872 | tf_op jit(solution)/shard_map/ppermute | solution.py:134
  69.4 0.0 collective-permute-done.8.refs_9_
  69.4 0.0 collective-permute-start.9
  69.4 0.0 collective-permute-done.refs_5_
  69.4 0.1 collective-permute-start.2
  69.5 2.6 %collective-permute-done.15.refs_8_ = bf16[256,1024]{1,0:T(8,128)(2,1)} collective-permute-done((bf16[256,1024]{1,0:T(8,128)(2,1)}, bf16[256,1024]{1,0:T(8,128)(2,1)}, u32[]{:S(2)}, u32[]{:S(2)}) %collective-permute-start.15) | collective-permute-done | bytes 524320 | tf_op jit(solution)/shard_map/ppermute | solution.py:135
  72.2 1.7 %collective-permute-start.13 = (bf16[256,1024]{1,0:T(8,128)(2,1)}, bf16[256,1024]{1,0:T(8,128)(2,1)S(1)}, u32[]{:S(2)}, u32[]{:S(2)}) collective-permute-start(bf16[256,1024]{1,0:T(8,128)(2,1)} %collective-permute-done.12.refs_7_), channel_id=1, source_target_pairs={{0,8},{8,16},{16,24},{24,28},{28,20},{20,12},{12,4},{4,0},{1,9},{9... | collective-permute-start | bytes 1572872 | tf_op jit(solution)/shard_map/ppermute | solution.py:134
  73.9 0.3 collective-permute-start.16
  74.2 10.7 %collective-permute-done.9.refs_3_ = bf16[256,1024]{1,0:T(8,128)(2,1)S(1)} collective-permute-done((bf16[256,1024]{1,0:T(8,128)(2,1)}, bf16[256,1024]{1,0:T(8,128)(2,1)S(1)}, u32[]{:S(2)}, u32[]{:S(2)}) %collective-permute-start.9) | collective-permute-done | bytes 524320 | tf_op jit(solution)/shard_map/ppermute | solution.py:135
  84.9 0.8 collective-permute-start.10
  85.7 0.0 collective-permute-done.5.refs_0_
  85.7 1.3 %collective-permute-start.6 = (bf16[256,1024]{1,0:T(8,128)(2,1)S(1)}, bf16[256,1024]{1,0:T(8,128)(2,1)S(1)}, u32[]{:S(2)}, u32[]{:S(2)}) collective-permute-start(bf16[256,1024]{1,0:T(8,128)(2,1)S(1)} %collective-permute-done.5.refs_0_), channel_id=1, source_target_pairs={{0,8},{8,16},{16,24},{24,28},{28,20},{20,12},{12,4},{4,0},{1,9},{9... | collective-permute-start | bytes 1572872 | tf_op jit(solution)/shard_map/ppermute | solution.py:134
  87.0 0.0 collective-permute-done.2.refs_7_
  87.1 7.7 %shard_map.64 = (bf16[1024,2560]{1,0:T(8,128)(2,1)}, bf16[1024,1024]{1,0:T(8,128)(2,1)S(1)}, bf16[1024,512]{1,0:T(8,128)(2,1)S(1)}) custom-call(s32[1]{0:T(128)} %bitcast.pos_ref, s32[8]{0:T(128)S(1)} %bitcast.20, s32[8,4]{1,0:T(8,128)S(1)} %bitcast.16, s32[8,4]{1,0:T(8,128)S(1)} %bitcast.17, s32[8,4]{1,0:T(8,128)S(1)} %bitcast.18, s32[8,4]{1,0:T(8,128)S(1)} %bitcast.19, ...), custom_call_target="tpu_custom_call" | custom-call | bytes 16777216 | tf_op jit(solution)/shard_map/pallas_call | solution.py:63
  94.8 1.3 %copy-done = bf16[1024,1024]{1,0:T(8,128)(2,1)} copy-done((bf16[1024,1024]{1,0:T(8,128)(2,1)}, bf16[1024,1024]{1,0:T(8,128)(2,1)S(1)}, u32[]{:S(2)}) %copy-start) | copy-done | bytes 2097176
  96.1 1.0 copy-done.1
  97.1 10.7 %shard_map.65.refs_4_ = f32[1024,1024]{1,0:T(8,128)} custom-call(bf16[1024,2560]{1,0:T(8,128)(2,1)} %get-tuple-element.10.tile_ref, bf16[256,1024]{1,0:T(8,128)(2,1)} %copy-done.11, bf16[256,1024]{1,0:T(8,128)(2,1)} %copy-done.10, bf16[256,1024]{1,0:T(8,128)(2,1)} %collective-permute-done.3.refs_2_, bf16[256,1024]{1,0:T(8,128)(2,1)} %copy-done.12, ...), custom_call_target="tpu_custom_call" | custom-call | flops 5368709120 | bytes 18874368 | tf_op jit(solution)/shard_map/pallas_call | solution.py:97
  107.8 0.0 collective-permute-done.13.refs_1_
  107.8 0.0 collective-permute-done.16.refs_2_
  107.8 0.8 copy-done.6
  108.6 0.2 copy-done.8
  108.8 7.8 %shard_map.66.refs_2_ = f32[1024,1024]{1,0:T(8,128)} custom-call(bf16[1024,1024]{1,0:T(8,128)(2,1)} %copy-done, bf16[256,1024]{1,0:T(8,128)(2,1)} %copy-done.4, bf16[256,1024]{1,0:T(8,128)(2,1)} %copy-done.6, bf16[256,1024]{1,0:T(8,128)(2,1)} %copy-done.8, bf16[256,1024]{1,0:T(8,128)(2,1)} %copy-done.5, f32[1024,1024]{1,0:T(8,128)} %shard_map.65.refs_4_), custom_call_target="tpu_custom_call" | custom-call | flops 2147483648 | bytes 12582912 | tf_op jit(solution)/shard_map/pallas_call | solution.py:97
  116.6 0.8 copy-done.7
  117.4 0.2 copy-done.9
  117.6 5.7 %shard_map.67 = bf16[1024,1024]{1,0:T(8,128)(2,1)} custom-call(bf16[1024,512]{1,0:T(8,128)(2,1)} %copy-done.1, bf16[256,1024]{1,0:T(8,128)(2,1)} %copy-done.9, bf16[256,1024]{1,0:T(8,128)(2,1)} %copy-done.7, f32[1024,1024]{1,0:T(8,128)} %shard_map.66.refs_2_), custom_call_target="tpu_custom_call" | custom-call | flops 1073741824 | bytes 10485760 | tf_op jit(solution)/shard_map/pallas_call | solution.py:97
  (28 shorter events, 0.1 us)
Async XLA Ops:
  0.0 10.8 %copy-start.3 = (bf16[512,1024]{1,0:T(8,128)(2,1)S(1)}, bf16[512,1024]{1,0:T(8,128)(2,1)}, u32[]{:S(2)}) copy-start(bf16[512,1024]{1,0:T(8,128)(2,1)} %param.11) | copy-start | bytes 3145732
  1.6 85.5 %copy-start.2 = (s32[1,8]{1,0:T(1,128)S(1)}, s32[1,8]{1,0:T(1,128)}, u32[]{:S(2)}) copy-start(s32[1,8]{1,0:T(1,128)} %param.10) | copy-start | bytes 100
  3.5 32.8 %all-to-all-start = ((bf16[8,272,128]{2,1,0:T(8,128)(2,1)}), bf16[8,272,128]{2,1,0:T(8,128)(2,1)S(1)}, u32[]{:S(2)}, u32[]{:S(2)}) async-start(bf16[8,272,128]{2,1,0:T(8,128)(2,1)} %fusion.1), calls=%async_computation | async-start | bytes 1114112 | tf_op jit(solution)/shard_map/all_to_all | solution.py:143
  10.8 86.3 %copy-start.10 = (bf16[256,1024]{1,0:T(8,128)(2,1)}, bf16[256,1024]{1,0:T(8,128)(2,1)S(1)}, u32[]{:S(2)}) copy-start(bf16[256,1024]{1,0:T(8,128)(2,1)S(1)} %get-tuple-element.11.refs_1_) | copy-start | bytes 1572868
  10.8 86.3 %copy-start.11 = (bf16[256,1024]{1,0:T(8,128)(2,1)}, bf16[256,1024]{1,0:T(8,128)(2,1)S(1)}, u32[]{:S(2)}) copy-start(bf16[256,1024]{1,0:T(8,128)(2,1)S(1)} %get-tuple-element.12.refs_0_) | copy-start | bytes 1572868
  10.9 21.4 %collective-permute-start.11 = (bf16[256,1024]{1,0:T(8,128)(2,1)S(1)}, bf16[256,1024]{1,0:T(8,128)(2,1)S(1)}, u32[]{:S(2)}, u32[]{:S(2)}) collective-permute-start(bf16[256,1024]{1,0:T(8,128)(2,1)S(1)} %get-tuple-element.11.refs_1_), channel_id=1, source_target_pairs={{0,8},{8,16},{16,24},{24,28},{28,20},{20,12},{12,4},{4,0},{1,9},{9... | collective-permute-start | bytes 1572872 | tf_op jit(solution)/shard_map/ppermute | solution.py:134
  12.9 30.6 %collective-permute-start.3 = (bf16[256,1024]{1,0:T(8,128)(2,1)S(1)}, bf16[256,1024]{1,0:T(8,128)(2,1)}, u32[]{:S(2)}, u32[]{:S(2)}) collective-permute-start(bf16[256,1024]{1,0:T(8,128)(2,1)S(1)} %get-tuple-element.12.refs_0_), channel_id=1, source_target_pairs={{0,8},{8,16},{16,24},{24,28},{28,20},{20,12},{12,4},{4,0},{1,9},{9... | collective-permute-start | bytes 1572872 | tf_op jit(solution)/shard_map/ppermute | solution.py:134
  14.4 33.2 %collective-permute-start.7 = (bf16[256,1024]{1,0:T(8,128)(2,1)S(1)}, bf16[256,1024]{1,0:T(8,128)(2,1)}, u32[]{:S(2)}, u32[]{:S(2)}) collective-permute-start(bf16[256,1024]{1,0:T(8,128)(2,1)S(1)} %get-tuple-element.11.refs_1_), channel_id=1, source_target_pairs={{8,0},{16,8},{24,16},{28,24},{20,28},{12,20},{4,12},{0,4},{9,1},{1... | collective-permute-start | bytes 1572872 | tf_op jit(solution)/shard_map/ppermute | solution.py:135
  15.0 32.6 %collective-permute-start.14 = (bf16[256,1024]{1,0:T(8,128)(2,1)S(1)}, bf16[256,1024]{1,0:T(8,128)(2,1)}, u32[]{:S(2)}, u32[]{:S(2)}) collective-permute-start(bf16[256,1024]{1,0:T(8,128)(2,1)S(1)} %get-tuple-element.12.refs_0_), channel_id=1, source_target_pairs={{8,0},{16,8},{24,16},{28,24},{20,28},{12,20},{4,12},{0,4},{9,1},{1... | collective-permute-start | bytes 1572872 | tf_op jit(solution)/shard_map/ppermute | solution.py:135
  32.2 64.9 %copy-start.12 = (bf16[256,1024]{1,0:T(8,128)(2,1)}, bf16[256,1024]{1,0:T(8,128)(2,1)S(1)}, u32[]{:S(2)}) copy-start(bf16[256,1024]{1,0:T(8,128)(2,1)S(1)} %collective-permute-done.11.refs_3_) | copy-start | bytes 1572868
  32.2 22.5 %collective-permute-start.12 = (bf16[256,1024]{1,0:T(8,128)(2,1)S(1)}, bf16[256,1024]{1,0:T(8,128)(2,1)}, u32[]{:S(2)}, u32[]{:S(2)}) collective-permute-start(bf16[256,1024]{1,0:T(8,128)(2,1)S(1)} %collective-permute-done.11.refs_3_), channel_id=1, source_target_pairs={{0,8},{8,16},{16,24},{24,28},{28,20},{20,12},{12,4},{4,0},{1,9},{9... | collective-permute-start | bytes 1572872 | tf_op jit(solution)/shard_map/ppermute | solution.py:134
  36.3 33.1 %collective-permute-start = (bf16[8,272,128]{2,1,0:T(8,128)(2,1)S(1)}, bf16[8,272,128]{2,1,0:T(8,128)(2,1)S(1)}, u32[]{:S(2)}, u32[]{:S(2)}) collective-permute-start(bf16[8,272,128]{2,1,0:T(8,128)(2,1)S(1)} %all-to-all-done.refs_4_), channel_id=1, source_target_pairs={{0,2},{1,3},{2,0},{3,1},{4,6},{5,7},{6,4},{7,5},{8,10},{9,11},{10,... | collective-permute-start | bytes 1671176 | tf_op jit(solution)/shard_map/ppermute | solution.py:147
  43.5 21.4 %collective-permute-start.4 = (bf16[256,1024]{1,0:T(8,128)(2,1)}, bf16[256,1024]{1,0:T(8,128)(2,1)}, u32[]{:S(2)}, u32[]{:S(2)}) collective-permute-start(bf16[256,1024]{1,0:T(8,128)(2,1)} %collective-permute-done.3.refs_2_), channel_id=1, source_target_pairs={{0,8},{8,16},{16,24},{24,28},{28,20},{20,12},{12,4},{4,0},{1,9},{9... | collective-permute-start | bytes 1572872 | tf_op jit(solution)/shard_map/ppermute | solution.py:134
  47.6 21.9 %collective-permute-start.8 = (bf16[256,1024]{1,0:T(8,128)(2,1)}, bf16[256,1024]{1,0:T(8,128)(2,1)}, u32[]{:S(2)}, u32[]{:S(2)}) collective-permute-start(bf16[256,1024]{1,0:T(8,128)(2,1)} %collective-permute-done.7.refs_5_), channel_id=1, source_target_pairs={{8,0},{16,8},{24,16},{28,24},{20,28},{12,20},{4,12},{0,4},{9,1},{1... | collective-permute-start | bytes 1572872 | tf_op jit(solution)/shard_map/ppermute | solution.py:135
  47.6 26.3 %collective-permute-start.1 = (bf16[8,272,128]{2,1,0:T(8,128)(2,1)S(1)}, bf16[8,272,128]{2,1,0:T(8,128)(2,1)S(1)}, u32[]{:S(2)}, u32[]{:S(2)}) collective-permute-start(bf16[8,272,128]{2,1,0:T(8,128)(2,1)S(1)} %all-to-all-done.refs_4_), channel_id=1, source_target_pairs={{0,1},{1,0},{2,3},{3,2},{4,5},{5,4},{6,7},{7,6},{8,9},{9,8},{10,11... | collective-permute-start | bytes 1671176 | tf_op jit(solution)/shard_map/ppermute | solution.py:151
  54.7 17.4 %collective-permute-start.15 = (bf16[256,1024]{1,0:T(8,128)(2,1)}, bf16[256,1024]{1,0:T(8,128)(2,1)}, u32[]{:S(2)}, u32[]{:S(2)}) collective-permute-start(bf16[256,1024]{1,0:T(8,128)(2,1)} %collective-permute-done.14.refs_4_), channel_id=1, source_target_pairs={{8,0},{16,8},{24,16},{28,24},{20,28},{12,20},{4,12},{0,4},{9,1},{1... | collective-permute-start | bytes 1572872 | tf_op jit(solution)/shard_map/ppermute | solution.py:135
  64.9 20.8 %collective-permute-start.5 = (bf16[256,1024]{1,0:T(8,128)(2,1)}, bf16[256,1024]{1,0:T(8,128)(2,1)S(1)}, u32[]{:S(2)}, u32[]{:S(2)}) collective-permute-start(bf16[256,1024]{1,0:T(8,128)(2,1)} %collective-permute-done.4.refs_6_), channel_id=1, source_target_pairs={{0,8},{8,16},{16,24},{24,28},{28,20},{20,12},{12,4},{4,0},{1,9},{9... | collective-permute-start | bytes 1572872 | tf_op jit(solution)/shard_map/ppermute | solution.py:134
  69.4 15.5 %collective-permute-start.9 = (bf16[256,1024]{1,0:T(8,128)(2,1)}, bf16[256,1024]{1,0:T(8,128)(2,1)S(1)}, u32[]{:S(2)}, u32[]{:S(2)}) collective-permute-start(bf16[256,1024]{1,0:T(8,128)(2,1)} %collective-permute-done.8.refs_9_), channel_id=1, source_target_pairs={{8,0},{16,8},{24,16},{28,24},{20,28},{12,20},{4,12},{0,4},{9,1},{1... | collective-permute-start | bytes 1572872 | tf_op jit(solution)/shard_map/ppermute | solution.py:135
  69.4 17.6 %collective-permute-start.2 = (bf16[8,272,128]{2,1,0:T(8,128)(2,1)S(1)}, bf16[8,272,128]{2,1,0:T(8,128)(2,1)S(1)}, u32[]{:S(2)}, u32[]{:S(2)}) collective-permute-start(bf16[8,272,128]{2,1,0:T(8,128)(2,1)S(1)} %collective-permute-done.refs_5_), channel_id=1, source_target_pairs={{0,1},{1,0},{2,3},{3,2},{4,5},{5,4},{6,7},{7,6},{8,9},{9,8},{10,11... | collective-permute-start | bytes 1671176 | tf_op jit(solution)/shard_map/ppermute | solution.py:152
  72.2 35.6 %collective-permute-start.13 = (bf16[256,1024]{1,0:T(8,128)(2,1)}, bf16[256,1024]{1,0:T(8,128)(2,1)S(1)}, u32[]{:S(2)}, u32[]{:S(2)}) collective-permute-start(bf16[256,1024]{1,0:T(8,128)(2,1)} %collective-permute-done.12.refs_7_), channel_id=1, source_target_pairs={{0,8},{8,16},{16,24},{24,28},{28,20},{20,12},{12,4},{4,0},{1,9},{9... | collective-permute-start | bytes 1572872 | tf_op jit(solution)/shard_map/ppermute | solution.py:134
  73.9 33.9 %collective-permute-start.16 = (bf16[256,1024]{1,0:T(8,128)(2,1)}, bf16[256,1024]{1,0:T(8,128)(2,1)S(1)}, u32[]{:S(2)}, u32[]{:S(2)}) collective-permute-start(bf16[256,1024]{1,0:T(8,128)(2,1)} %collective-permute-done.15.refs_8_), channel_id=1, source_target_pairs={{8,0},{16,8},{24,16},{28,24},{20,28},{12,20},{4,12},{0,4},{9,1},{1... | collective-permute-start | bytes 1572872 | tf_op jit(solution)/shard_map/ppermute | solution.py:135
  84.9 22.9 %copy-start.5 = (bf16[256,1024]{1,0:T(8,128)(2,1)}, bf16[256,1024]{1,0:T(8,128)(2,1)S(1)}, u32[]{:S(2)}) copy-start(bf16[256,1024]{1,0:T(8,128)(2,1)S(1)} %collective-permute-done.9.refs_3_) | copy-start | bytes 1572868
  84.9 31.7 %collective-permute-start.10 = (bf16[256,1024]{1,0:T(8,128)(2,1)S(1)}, bf16[256,1024]{1,0:T(8,128)(2,1)S(1)}, u32[]{:S(2)}, u32[]{:S(2)}) collective-permute-start(bf16[256,1024]{1,0:T(8,128)(2,1)S(1)} %collective-permute-done.9.refs_3_), channel_id=1, source_target_pairs={{8,0},{16,8},{24,16},{28,24},{20,28},{12,20},{4,12},{0,4},{9,1},{1... | collective-permute-start | bytes 1572872 | tf_op jit(solution)/shard_map/ppermute | solution.py:135
  85.7 22.1 %copy-start.4 = (bf16[256,1024]{1,0:T(8,128)(2,1)}, bf16[256,1024]{1,0:T(8,128)(2,1)S(1)}, u32[]{:S(2)}) copy-start(bf16[256,1024]{1,0:T(8,128)(2,1)S(1)} %collective-permute-done.5.refs_0_) | copy-start | bytes 1572868
  85.7 30.9 %collective-permute-start.6 = (bf16[256,1024]{1,0:T(8,128)(2,1)S(1)}, bf16[256,1024]{1,0:T(8,128)(2,1)S(1)}, u32[]{:S(2)}, u32[]{:S(2)}) collective-permute-start(bf16[256,1024]{1,0:T(8,128)(2,1)S(1)} %collective-permute-done.5.refs_0_), channel_id=1, source_target_pairs={{0,8},{8,16},{16,24},{24,28},{28,20},{20,12},{12,4},{4,0},{1,9},{9... | collective-permute-start | bytes 1572872 | tf_op jit(solution)/shard_map/ppermute | solution.py:134
  94.8 1.3 %copy-start = (bf16[1024,1024]{1,0:T(8,128)(2,1)}, bf16[1024,1024]{1,0:T(8,128)(2,1)S(1)}, u32[]{:S(2)}) copy-start(bf16[1024,1024]{1,0:T(8,128)(2,1)S(1)} %get-tuple-element.9.tile_ref) | copy-start | bytes 6291460
  96.1 1.0 copy-start.1
  107.8 0.8 copy-start.6
  107.8 1.0 copy-start.8
  116.6 0.8 copy-start.7
  116.6 1.0 copy-start.9

commit v3 on v2

--- a/solution.py
+++ b/solution.py
@@ -73,6 +73,22 @@
             flops=0, bytes_accessed=rows * groups * blocks * bs * 4, transcendentals=0
         ),
     )(pos, owned, *metas, *parts)
+
+
+def after_kernel(*refs):
+    pass
+
+
+def after(values, others):
+    anywhere = pl.BlockSpec(memory_space=pl.ANY)
+    return pl.pallas_call(
+        after_kernel,
+        out_shape=[jax.ShapeDtypeStruct(v.shape, v.dtype) for v in values],
+        in_specs=[anywhere] * (len(values) + len(others)),
+        out_specs=[anywhere] * len(values),
+        input_output_aliases={i: i for i in range(len(values))},
+        cost_estimate=pl.CostEstimate(flops=0, bytes_accessed=0, transcendentals=0),
+    )(*values, *others)
 
 
 def mul_kernel(n_pieces, tile_ref, *refs):
@@ -109,6 +125,17 @@
     )(*args)
 
 
+def across_row(landed, columns):
+    if columns != 4:
+        gathered = lax.all_gather(landed, "blk", axis=0)
+        return [gathered[j] for j in range(columns)]
+    swap_core = [(j, j ^ 1) for j in range(columns)]
+    swap_chip = [(j, j ^ 2) for j in range(columns)]
+    across = lax.ppermute(landed, "blk", swap_chip)
+    near = lax.ppermute(landed, "blk", swap_core)
+    return [landed, across, near, lax.ppermute(across, "blk", swap_core)]
+
+
 def body(a_slots, a_rows, a_cols, a_count, owned_rows, b_matrix):
     groups = lax.axis_size("grid")
     columns = lax.axis_size("blk")
@@ -125,6 +152,12 @@
     to_right = [(order[i], order[(i + 1) % groups]) for i in range(groups)]
     to_left = [(order[(i + 1) % groups], order[i]) for i in range(groups)]
 
+    live = jnp.arange(cap, dtype=jnp.int32)[None, :] < a_count.reshape(groups, 1)
+    row_code = jnp.where(live, a_rows.reshape(groups, cap) + 1, 0)
+    meta = jnp.concatenate([row_code, a_cols.reshape(groups, cap)], axis=1)
+    meta = jnp.pad(meta.astype(jnp.bfloat16)[:, None, :], ((0, 0), (0, META - 1), (0, bs - 2 * cap)))
+    message = jnp.concatenate([a_slots.reshape(groups, cap * bs, bs), meta], axis=1)
+
     own = [b_matrix[h * depth : (h + 1) * depth] for h in range(per)]
     events = [own]
     from_left, from_right = list(own), list(own)
@@ -133,27 +166,17 @@
         high = range(per) if s < half else range(per // 2, per)
         from_left = {h: lax.ppermute(from_left[h], "grid", to_right) for h in low}
         from_right = {h: lax.ppermute(from_right[h], "grid", to_left) for h in high}
+        if s == 1:
+            (message,) = after([message], [from_left[0], from_right[0]])
+            landed = lax.all_to_all(message, "grid", split_axis=0, concat_axis=0, tiled=True)
+        if s == 2:
+            from_left[0], from_right[0] = after([from_left[0], from_right[0]], [landed])
+            parts = across_row(landed, columns)
+        if s == half - 1:
+            from_left[0], from_right[per - 1] = after(
+                [from_left[0], from_right[per - 1]], parts[1:]
+            )
         events.append([from_left[h] for h in low] + [from_right[h] for h in high])
-
-    live = jnp.arange(cap, dtype=jnp.int32)[None, :] < a_count.reshape(groups, 1)
-    row_code = jnp.where(live, a_rows.reshape(groups, cap) + 1, 0)
-    meta = jnp.concatenate([row_code, a_cols.reshape(groups, cap)], axis=1)
-    meta = jnp.pad(meta.astype(jnp.bfloat16)[:, None, :], ((0, 0), (0, META - 1), (0, bs - 2 * cap)))
-    message = jnp.concatenate([a_slots.reshape(groups, cap * bs, bs), meta], axis=1)
-    landed = lax.all_to_all(message, "grid", split_axis=0, concat_axis=0, tiled=True)
-    if columns == 4:
-        swap_core = [(j, j ^ 1) for j in range(columns)]
-        swap_chip = [(j, j ^ 2) for j in range(columns)]
-        across = lax.ppermute(landed, "blk", swap_chip)
-        parts = [
-            landed,
-            across,
-            lax.ppermute(landed, "blk", swap_core),
-            lax.ppermute(across, "blk", swap_core),
-        ]
-    else:
-        gathered = lax.all_gather(landed, "blk", axis=0)
-        parts = [gathered[j] for j in range(columns)]
     metas = [p[:, cap * bs, : 2 * cap].astype(jnp.int32) for p in parts]
 
     stages = [sum(events[: half - 1], []), events[half - 1], events[half]]

time: 124 us -> 138 us (1.11)
  waiting for transfers between devices: 49.8 us -> 62.5 us
  local copies, waits for them, and re-layouts: 4.52 us -> 11.1 us
  starting transfers between devices: 33.5 us -> 28.8 us
    all_to_all x1, waiting for transfers between devices: 0.01 us -> 12.2 us  [body(): lax.all_to_all(message, 'grid', split_axis=0, concat_axis=0, tiled=True)]
    ppermute x7, waiting for transfers between devices: 13.4 us -> 22.2 us  [body(): from_right = {h: lax.ppermute(from_right[h], 'grid', to_left) for h in high}]
    ppermute x7, waiting for transfers between devices: 36.4 us -> 28.1 us  [body(): from_left = {h: lax.ppermute(from_left[h], 'grid', to_right) for h in low}]
    unnamed x26 -> x50, local copies, waits for them, and re-layouts: 4.35 us -> 9.66 us
    ppermute x7, starting transfers between devices: 5.41 us -> 3.22 us  [body(): from_right = {h: lax.ppermute(from_right[h], 'grid', to_left) for h in high}]
    all_to_all x1, starting transfers between devices: 7.28 us -> 5.33 us  [body(): lax.all_to_all(message, 'grid', split_axis=0, concat_axis=0, tiled=True)]
    convert_element_type x4, other arithmetic: 0.03 us -> 1.5 us  [body(): metas = [p[:, cap * bs, :2 * cap].astype(jnp.int32) for p in parts]]
    concatenate x3, other arithmetic: 1.47 us -> 0.02 us  [body(): meta = jnp.concatenate([row_code, a_cols.reshape(groups, cap)], axis=1)]
  transfers between devices with their start and end apart: 18 -> 18, of which waited for: 6 -> 10; matrix products, arithmetic and copies ran while one was open for 0% -> 2% of each run, Pallas kernels for 21% -> 19%
where the time goes in v3:
time: 138 us; the launch traced here: 137 us
  waiting for transfers between devices  62.5 us (45%)
  Pallas kernels  32.1 us (23%)
  starting transfers between devices  28.8 us (21%)
  local copies, waits for them, and re-layouts  11.1 us (8%)
  other arithmetic  2.36 us (2%)
    ppermute x7, waiting for transfers between devices, body(): from_left = {h: lax.ppermute(from_left[h], 'grid', to_right) for h in low}  28.1 us
    pallas_call x3, Pallas kernels, mul(): pl.pallas_call(functools.partial(mul_kernel, n), out_shape=jax.ShapeDtype...  24.1 us
    ppermute x7, waiting for transfers between devices, body(): from_right = {h: lax.ppermute(from_right[h], 'grid', to_left) for h in high}  22.2 us
    ppermute x7, starting transfers between devices, body(): from_left = {h: lax.ppermute(from_left[h], 'grid', to_right) for h in low}  18.7 us
    all_to_all x1, waiting for transfers between devices, body(): lax.all_to_all(message, 'grid', split_axis=0, concat_axis=0, tiled=True)  12.2 us
    unnamed x50, local copies, waits for them, and re-layouts  9.66 us
    pallas_call x1, Pallas kernels, build_tiles(): pl.pallas_call(functools.partial(build_kernel, dims, bounds), out_shape=[...  7.97 us
    all_to_all x1, starting transfers between devices, body(): lax.all_to_all(message, 'grid', split_axis=0, concat_axis=0, tiled=True)  5.33 us
  transfers between devices with their start and end apart: 18, of which 10 were waited for; matrix products, arithmetic and copies ran while one was open for 2% of the time, Pallas kernels for 19%

profile of v3, /device:TPU:0, one launch (start us, length us, event | category | flops | bytes accessed | tf_op | source)
XLA Modules:
  0.0 137.1 jit_solution(15051264885752971433)
XLA Ops:
  0.0 1.3 fusion.4
  1.4 3.1 %collective-permute-start = (bf16[256,1024]{1,0:T(8,128)(2,1)S(1)}, bf16[256,1024]{1,0:T(8,128)(2,1)S(1)}, u32[]{:S(2)}, u32[]{:S(2)}) collective-permute-start(bf16[256,1024]{1,0:T(8,128)(2,1)S(1)} %get-tuple-element.20.refs_0_), channel_id=1, source_target_pairs={{0,8},{8,16},{16,24},{24,28},{28,20},{20,12},{12,4},{4,0},{1,9},{9... | collective-permute-start | bytes 1572872 | tf_op jit(solution)/shard_map/ppermute | solution.py:167
  4.4 0.0 collective-permute-start.1
  4.5 0.1 copy.31
  4.6 0.8 fusion.1.refs_0_
  5.5 10.9 %collective-permute-done.refs_1_.refs_2_ = bf16[256,1024]{1,0:T(8,128)(2,1)S(1)} collective-permute-done((bf16[256,1024]{1,0:T(8,128)(2,1)S(1)}, bf16[256,1024]{1,0:T(8,128)(2,1)S(1)}, u32[]{:S(2)}, u32[]{:S(2)}) %collective-permute-start) | collective-permute-done | bytes 524320 | tf_op jit(solution)/shard_map/ppermute | solution.py:167
  16.3 1.5 %collective-permute-done.1.refs_2_.refs_4_ = bf16[256,1024]{1,0:T(8,128)(2,1)S(1)} collective-permute-done((bf16[256,1024]{1,0:T(8,128)(2,1)S(1)}, bf16[256,1024]{1,0:T(8,128)(2,1)S(1)}, u32[]{:S(2)}, u32[]{:S(2)}) %collective-permute-start.1) | collective-permute-done | bytes 524320 | tf_op jit(solution)/shard_map/ppermute | solution.py:168
  17.8 0.8 copy-done.19
  18.7 5.3 %all-to-all-start = ((bf16[8,272,128]{2,1,0:T(8,128)(2,1)}), bf16[8,272,128]{2,1,0:T(8,128)(2,1)}, u32[]{:S(2)}, u32[]{:S(2)}) async-start(bf16[8,272,128]{2,1,0:T(8,128)(2,1)} %shard_map.64), calls=%async_computation | async-start | bytes 1114112 | tf_op jit(solution)/shard_map/all_to_all | solution.py:171
  24.0 2.0 %collective-permute-start.8 = (bf16[256,1024]{1,0:T(8,128)(2,1)S(1)}, bf16[256,1024]{1,0:T(8,128)(2,1)S(1)}, u32[]{:S(2)}, u32[]{:S(2)}) collective-permute-start(bf16[256,1024]{1,0:T(8,128)(2,1)S(1)} %get-tuple-element.19.refs_1_), channel_id=1, source_target_pairs={{8,0},{16,8},{24,16},{28,24},{20,28},{12,20},{4,12},{0,4},{9,1},{1... | collective-permute-start | bytes 1572872 | tf_op jit(solution)/shard_map/ppermute | solution.py:168
  26.0 0.1 collective-permute-start.13
  26.1 2.0 %collective-permute-start.5 = (bf16[256,1024]{1,0:T(8,128)(2,1)}, bf16[256,1024]{1,0:T(8,128)(2,1)S(1)}, u32[]{:S(2)}, u32[]{:S(2)}) collective-permute-start(bf16[256,1024]{1,0:T(8,128)(2,1)} %copy-done.18), channel_id=1, source_target_pairs={{0,8},{8,16},{16,24},{24,28},{28,20},{20,12},{12,4},{4,0},{1,9},{9... | collective-permute-start | bytes 1572872 | tf_op jit(solution)/shard_map/ppermute | solution.py:167
  28.0 12.2 %all-to-all-done.refs_4_.refs_2_ = bf16[8,272,128]{2,1,0:T(8,128)(2,1)} async-done(((bf16[8,272,128]{2,1,0:T(8,128)(2,1)}), bf16[8,272,128]{2,1,0:T(8,128)(2,1)}, u32[]{:S(2)}, u32[]{:S(2)}) %all-to-all-start) | async-done | bytes 557088 | tf_op jit(solution)/shard_map/all_to_all | solution.py:171
  40.3 1.5 %collective-permute-start.2 = (bf16[8,272,128]{2,1,0:T(8,128)(2,1)}, bf16[8,272,128]{2,1,0:T(8,128)(2,1)S(1)}, u32[]{:S(2)}, u32[]{:S(2)}) collective-permute-start(bf16[8,272,128]{2,1,0:T(8,128)(2,1)} %all-to-all-done.refs_4_.refs_2_), channel_id=1, source_target_pairs={{0,2},{1,3},{2,0},{3,1},{4,6},{5,7},{6,4},{7,5},{8,10},{9,11},{10,... | collective-permute-start | bytes 1671176 | tf_op jit(solution)/shard_map/ppermute | solution.py:134
  41.8 3.9 %collective-permute-done.8.refs_5_ = bf16[256,1024]{1,0:T(8,128)(2,1)S(1)} collective-permute-done((bf16[256,1024]{1,0:T(8,128)(2,1)S(1)}, bf16[256,1024]{1,0:T(8,128)(2,1)S(1)}, u32[]{:S(2)}, u32[]{:S(2)}) %collective-permute-start.8) | collective-permute-done | bytes 524320 | tf_op jit(solution)/shard_map/ppermute | solution.py:168
  45.7 0.0 collective-permute-start.9
  45.7 0.0 collective-permute-done.13.refs_3_
  45.7 4.5 %collective-permute-start.14 = (bf16[256,1024]{1,0:T(8,128)(2,1)S(1)}, bf16[256,1024]{1,0:T(8,128)(2,1)}, u32[]{:S(2)}, u32[]{:S(2)}) collective-permute-start(bf16[256,1024]{1,0:T(8,128)(2,1)S(1)} %collective-permute-done.13.refs_3_), channel_id=1, source_target_pairs={{0,8},{8,16},{16,24},{24,28},{28,20},{20,12},{12,4},{4,0},{1,9},{9... | collective-permute-start | bytes 1572872 | tf_op jit(solution)/shard_map/ppermute | solution.py:167
  50.2 0.0 collective-permute-start.6
  50.2 6.6 %collective-permute-done.5.refs_0_ = bf16[256,1024]{1,0:T(8,128)(2,1)S(1)} collective-permute-done((bf16[256,1024]{1,0:T(8,128)(2,1)}, bf16[256,1024]{1,0:T(8,128)(2,1)S(1)}, u32[]{:S(2)}, u32[]{:S(2)}) %collective-permute-start.5) | collective-permute-done | bytes 524320 | tf_op jit(solution)/shard_map/ppermute | solution.py:167
  56.9 6.2 %collective-permute-done.9.refs_9_ = bf16[256,1024]{1,0:T(8,128)(2,1)} collective-permute-done((bf16[256,1024]{1,0:T(8,128)(2,1)S(1)}, bf16[256,1024]{1,0:T(8,128)(2,1)}, u32[]{:S(2)}, u32[]{:S(2)}) %collective-permute-start.9) | collective-permute-done | bytes 524320 | tf_op jit(solution)/shard_map/ppermute | solution.py:168
  63.1 0.0 collective-permute-start.10
  63.1 2.8 %collective-permute-done.14.refs_7_ = bf16[256,1024]{1,0:T(8,128)(2,1)} collective-permute-done((bf16[256,1024]{1,0:T(8,128)(2,1)S(1)}, bf16[256,1024]{1,0:T(8,128)(2,1)}, u32[]{:S(2)}, u32[]{:S(2)}) %collective-permute-start.14) | collective-permute-done | bytes 524320 | tf_op jit(solution)/shard_map/ppermute | solution.py:167
  65.9 4.4 %collective-permute-start.15 = (bf16[256,1024]{1,0:T(8,128)(2,1)}, bf16[256,1024]{1,0:T(8,128)(2,1)}, u32[]{:S(2)}, u32[]{:S(2)}) collective-permute-start(bf16[256,1024]{1,0:T(8,128)(2,1)} %collective-permute-done.14.refs_7_), channel_id=1, source_target_pairs={{0,8},{8,16},{16,24},{24,28},{28,20},{20,12},{12,4},{4,0},{1,9},{9... | collective-permute-start | bytes 1572872 | tf_op jit(solution)/shard_map/ppermute | solution.py:167
  70.4 3.9 %collective-permute-done.6.refs_1_ = bf16[256,1024]{1,0:T(8,128)(2,1)S(1)} collective-permute-done((bf16[256,1024]{1,0:T(8,128)(2,1)}, bf16[256,1024]{1,0:T(8,128)(2,1)S(1)}, u32[]{:S(2)}, u32[]{:S(2)}) %collective-permute-start.6) | collective-permute-done | bytes 524320 | tf_op jit(solution)/shard_map/ppermute | solution.py:168
  74.2 0.8 copy-done.12
  75.0 2.0 %collective-permute-start.7 = (bf16[256,1024]{1,0:T(8,128)(2,1)}, bf16[256,1024]{1,0:T(8,128)(2,1)S(1)}, u32[]{:S(2)}, u32[]{:S(2)}) collective-permute-start(bf16[256,1024]{1,0:T(8,128)(2,1)} %get-tuple-element.13.refs_6_), channel_id=1, source_target_pairs={{0,8},{8,16},{16,24},{24,28},{28,20},{20,12},{12,4},{4,0},{1,9},{9... | collective-permute-start | bytes 1572872 | tf_op jit(solution)/shard_map/ppermute | solution.py:167
  77.1 0.1 collective-permute-start.4
  77.1 0.8 slice_convert_fusion.3
  77.9 0.1 collective-permute-start.16
  78.0 6.7 %collective-permute-done.10.refs_1_ = bf16[256,1024]{1,0:T(8,128)(2,1)S(1)} collective-permute-done((bf16[256,1024]{1,0:T(8,128)(2,1)}, bf16[256,1024]{1,0:T(8,128)(2,1)S(1)}, u32[]{:S(2)}, u32[]{:S(2)}) %collective-permute-start.10) | collective-permute-done | bytes 524320 | tf_op jit(solution)/shard_map/ppermute | solution.py:168
  84.7 7.8 %collective-permute-done.7.refs_0_ = bf16[256,1024]{1,0:T(8,128)(2,1)S(1)} collective-permute-done((bf16[256,1024]{1,0:T(8,128)(2,1)}, bf16[256,1024]{1,0:T(8,128)(2,1)S(1)}, u32[]{:S(2)}, u32[]{:S(2)}) %collective-permute-start.7) | collective-permute-done | bytes 524320 | tf_op jit(solution)/shard_map/ppermute | solution.py:167
  92.5 0.8 copy-done.10
  93.3 0.8 copy-done.4
  94.1 2.6 %collective-permute-start.11 = (bf16[256,1024]{1,0:T(8,128)(2,1)}, bf16[256,1024]{1,0:T(8,128)(2,1)S(1)}, u32[]{:S(2)}, u32[]{:S(2)}) collective-permute-start(bf16[256,1024]{1,0:T(8,128)(2,1)} %get-tuple-element.14.refs_0_), channel_id=1, source_target_pairs={{0,8},{8,16},{16,24},{24,28},{28,20},{20,12},{12,4},{4,0},{1,9},{9... | collective-permute-start | bytes 1572872 | tf_op jit(solution)/shard_map/ppermute | solution.py:167
  96.7 1.1 collective-permute-start.12
  97.8 0.7 slice_convert_fusion
  98.5 1.0 copy-done.1
  99.6 1.1 copy-done.3
  100.6 1.1 copy-done.5
  101.7 8.0 %shard_map.65 = (bf16[1024,2560]{1,0:T(8,128)(2,1)}, bf16[1024,1024]{1,0:T(8,128)(2,1)S(1)}, bf16[1024,512]{1,0:T(8,128)(2,1)S(1)}) custom-call(s32[1]{0:T(128)} %bitcast.pos_ref, s32[8]{0:T(128)S(1)} %bitcast.20, s32[8,4]{1,0:T(8,128)S(1)} %bitcast.16, s32[8,4]{1,0:T(8,128)S(1)} %bitcast.17, s32[8,4]{1,0:T(8,128)S(1)} %bitcast.18, s32[8,4]{1,0:T(8,128)S(1)} %bitcast.19, ...), custom_call_target="tpu_custom_call" | custom-call | bytes 16777216 | tf_op jit(solution)/shard_map/pallas_call | solution.py:63
  109.7 1.3 copy-done.6
  111.0 1.0 copy-done.7
  111.9 10.7 %shard_map.68.refs_4_ = f32[1024,1024]{1,0:T(8,128)} custom-call(bf16[1024,2560]{1,0:T(8,128)(2,1)} %get-tuple-element.18.tile_ref, bf16[256,1024]{1,0:T(8,128)(2,1)} %copy-done.17, bf16[256,1024]{1,0:T(8,128)(2,1)} %copy-done.16, bf16[256,1024]{1,0:T(8,128)(2,1)} %copy-done.18, bf16[256,1024]{1,0:T(8,128)(2,1)} %copy-done.23, bf16[256,1024]{1,0:T(8,128)(2,1)} %copy-done.19, ...), custom_call_target="tpu_custom_call" | custom-call | flops 5368709120 | bytes 18874368 | tf_op jit(solution)/shard_map/pallas_call | solution.py:113
  122.6 7.8 %shard_map.69.refs_2_ = f32[1024,1024]{1,0:T(8,128)} custom-call(bf16[1024,1024]{1,0:T(8,128)(2,1)} %copy-done.6, bf16[256,1024]{1,0:T(8,128)(2,1)} %get-tuple-element.14.refs_0_, bf16[256,1024]{1,0:T(8,128)(2,1)} %collective-permute-done.15.refs_1_, bf16[256,1024]{1,0:T(8,128)(2,1)} %collective-permute-done.16.refs_2_, ...), custom_call_target="tpu_custom_call" | custom-call | flops 2147483648 | bytes 12582912 | tf_op jit(solution)/shard_map/pallas_call | solution.py:113
  130.5 0.8 copy-done.13
  131.2 0.2 copy-done.14
  131.4 5.7 %shard_map.70 = bf16[1024,1024]{1,0:T(8,128)(2,1)} custom-call(bf16[1024,512]{1,0:T(8,128)(2,1)} %copy-done.7, bf16[256,1024]{1,0:T(8,128)(2,1)} %copy-done.13, bf16[256,1024]{1,0:T(8,128)(2,1)} %copy-done.14, f32[1024,1024]{1,0:T(8,128)} %shard_map.69.refs_2_), custom_call_target="tpu_custom_call" | custom-call | flops 1073741824 | bytes 10485760 | tf_op jit(solution)/shard_map/pallas_call | solution.py:113
  (55 shorter events, 0.1 us)
Async XLA Ops:
  0.0 4.5 %copy-start.24 = (s32[1,1,8,2]{2,3,1,0:T(2,128)S(1)}, s32[1,1,8,2]{2,3,1,0:T(2,128)}, u32[]{:S(2)}) copy-start(s32[1,1,8,2]{2,3,1,0:T(2,128)} %param.8) | copy-start | bytes 196
  0.0 4.5 %copy-start.21 = (s32[1,1,8]{2,1,0:T(1,128)S(1)}, s32[1,1,8]{2,1,0:T(1,128)}, u32[]{:S(2)}) copy-start(s32[1,1,8]{2,1,0:T(1,128)} %param.9) | copy-start | bytes 100
  0.0 4.5 %copy-start.20 = (s32[1,1,8,2]{2,3,1,0:T(2,128)S(1)}, s32[1,1,8,2]{2,3,1,0:T(2,128)}, u32[]{:S(2)}) copy-start(s32[1,1,8,2]{2,3,1,0:T(2,128)} %param.7) | copy-start | bytes 196
  0.0 4.6 %copy-start.15 = (bf16[1,1,8,2,128,128]{5,4,3,2,1,0:T(8,128)(2,1)S(1)}, bf16[1,1,8,2,128,128]{5,4,3,2,1,0:T(8,128)(2,1)}, u32[]{:S(2)}) copy-start(bf16[1,1,8,2,128,128]{5,4,3,2,1,0:T(8,128)(2,1)} %param.6) | copy-start | bytes 1572868
  1.3 17.3 %copy-start.17 = (bf16[256,1024]{1,0:T(8,128)(2,1)}, bf16[256,1024]{1,0:T(8,128)(2,1)S(1)}, u32[]{:S(2)}) copy-start(bf16[256,1024]{1,0:T(8,128)(2,1)S(1)} %get-tuple-element.20.refs_0_) | copy-start | bytes 1572868
  1.3 24.7 %copy-start.16 = (bf16[256,1024]{1,0:T(8,128)(2,1)}, bf16[256,1024]{1,0:T(8,128)(2,1)S(1)}, u32[]{:S(2)}) copy-start(bf16[256,1024]{1,0:T(8,128)(2,1)S(1)} %get-tuple-element.19.refs_1_) | copy-start | bytes 1572868
  1.4 15.0 %collective-permute-start = (bf16[256,1024]{1,0:T(8,128)(2,1)S(1)}, bf16[256,1024]{1,0:T(8,128)(2,1)S(1)}, u32[]{:S(2)}, u32[]{:S(2)}) collective-permute-start(bf16[256,1024]{1,0:T(8,128)(2,1)S(1)} %get-tuple-element.20.refs_0_), channel_id=1, source_target_pairs={{0,8},{8,16},{16,24},{24,28},{28,20},{20,12},{12,4},{4,0},{1,9},{9... | collective-permute-start | bytes 1572872 | tf_op jit(solution)/shard_map/ppermute | solution.py:167
  4.4 13.4 %collective-permute-start.1 = (bf16[256,1024]{1,0:T(8,128)(2,1)S(1)}, bf16[256,1024]{1,0:T(8,128)(2,1)S(1)}, u32[]{:S(2)}, u32[]{:S(2)}) collective-permute-start(bf16[256,1024]{1,0:T(8,128)(2,1)S(1)} %get-tuple-element.20.refs_0_), channel_id=1, source_target_pairs={{8,0},{16,8},{24,16},{28,24},{20,28},{12,20},{4,12},{0,4},{9,1},{1... | collective-permute-start | bytes 1572872 | tf_op jit(solution)/shard_map/ppermute | solution.py:168
  16.3 1.5 %copy-start.18 = (bf16[256,1024]{1,0:T(8,128)(2,1)}, bf16[256,1024]{1,0:T(8,128)(2,1)S(1)}, u32[]{:S(2)}) copy-start(bf16[256,1024]{1,0:T(8,128)(2,1)S(1)} %collective-permute-done.refs_1_.refs_2_) | copy-start | bytes 1572868
  17.8 0.8 copy-start.19
  18.7 21.6 %all-to-all-start = ((bf16[8,272,128]{2,1,0:T(8,128)(2,1)}), bf16[8,272,128]{2,1,0:T(8,128)(2,1)}, u32[]{:S(2)}, u32[]{:S(2)}) async-start(bf16[8,272,128]{2,1,0:T(8,128)(2,1)} %shard_map.64), calls=%async_computation | async-start | bytes 1114112 | tf_op jit(solution)/shard_map/all_to_all | solution.py:171
  24.0 21.7 %collective-permute-start.8 = (bf16[256,1024]{1,0:T(8,128)(2,1)S(1)}, bf16[256,1024]{1,0:T(8,128)(2,1)S(1)}, u32[]{:S(2)}, u32[]{:S(2)}) collective-permute-start(bf16[256,1024]{1,0:T(8,128)(2,1)S(1)} %get-tuple-element.19.refs_1_), channel_id=1, source_target_pairs={{8,0},{16,8},{24,16},{28,24},{20,28},{12,20},{4,12},{0,4},{9,1},{1... | collective-permute-start | bytes 1572872 | tf_op jit(solution)/shard_map/ppermute | solution.py:168
  26.0 19.7 %collective-permute-start.13 = (bf16[256,1024]{1,0:T(8,128)(2,1)S(1)}, bf16[256,1024]{1,0:T(8,128)(2,1)S(1)}, u32[]{:S(2)}, u32[]{:S(2)}) collective-permute-start(bf16[256,1024]{1,0:T(8,128)(2,1)S(1)} %get-tuple-element.19.refs_1_), channel_id=1, source_target_pairs={{0,8},{8,16},{16,24},{24,28},{28,20},{20,12},{12,4},{4,0},{1,9},{9... | collective-permute-start | bytes 1572872 | tf_op jit(solution)/shard_map/ppermute | solution.py:167
  26.1 30.8 %collective-permute-start.5 = (bf16[256,1024]{1,0:T(8,128)(2,1)}, bf16[256,1024]{1,0:T(8,128)(2,1)S(1)}, u32[]{:S(2)}, u32[]{:S(2)}) collective-permute-start(bf16[256,1024]{1,0:T(8,128)(2,1)} %copy-done.18), channel_id=1, source_target_pairs={{0,8},{8,16},{16,24},{24,28},{28,20},{20,12},{12,4},{4,0},{1,9},{9... | collective-permute-start | bytes 1572872 | tf_op jit(solution)/shard_map/ppermute | solution.py:167
  40.3 36.8 %collective-permute-start.2 = (bf16[8,272,128]{2,1,0:T(8,128)(2,1)}, bf16[8,272,128]{2,1,0:T(8,128)(2,1)S(1)}, u32[]{:S(2)}, u32[]{:S(2)}) collective-permute-start(bf16[8,272,128]{2,1,0:T(8,128)(2,1)} %all-to-all-done.refs_4_.refs_2_), channel_id=1, source_target_pairs={{0,2},{1,3},{2,0},{3,1},{4,6},{5,7},{6,4},{7,5},{8,10},{9,11},{10,... | collective-permute-start | bytes 1671176 | tf_op jit(solution)/shard_map/ppermute | solution.py:134
  45.7 11.2 %copy-start.22 = (bf16[256,1024]{1,0:T(8,128)(2,1)}, bf16[256,1024]{1,0:T(8,128)(2,1)S(1)}, u32[]{:S(2)}) copy-start(bf16[256,1024]{1,0:T(8,128)(2,1)S(1)} %collective-permute-done.8.refs_5_) | copy-start | bytes 1572868
  45.7 17.4 %collective-permute-start.9 = (bf16[256,1024]{1,0:T(8,128)(2,1)S(1)}, bf16[256,1024]{1,0:T(8,128)(2,1)}, u32[]{:S(2)}, u32[]{:S(2)}) collective-permute-start(bf16[256,1024]{1,0:T(8,128)(2,1)S(1)} %collective-permute-done.8.refs_5_), channel_id=1, source_target_pairs={{8,0},{16,8},{24,16},{28,24},{20,28},{12,20},{4,12},{0,4},{9,1},{1... | collective-permute-start | bytes 1572872 | tf_op jit(solution)/shard_map/ppermute | solution.py:168
  45.7 31.4 %copy-start.23 = (bf16[256,1024]{1,0:T(8,128)(2,1)}, bf16[256,1024]{1,0:T(8,128)(2,1)S(1)}, u32[]{:S(2)}) copy-start(bf16[256,1024]{1,0:T(8,128)(2,1)S(1)} %collective-permute-done.13.refs_3_) | copy-start | bytes 1572868
  45.7 20.3 %collective-permute-start.14 = (bf16[256,1024]{1,0:T(8,128)(2,1)S(1)}, bf16[256,1024]{1,0:T(8,128)(2,1)}, u32[]{:S(2)}, u32[]{:S(2)}) collective-permute-start(bf16[256,1024]{1,0:T(8,128)(2,1)S(1)} %collective-permute-done.13.refs_3_), channel_id=1, source_target_pairs={{0,8},{8,16},{16,24},{24,28},{28,20},{20,12},{12,4},{4,0},{1,9},{9... | collective-permute-start | bytes 1572872 | tf_op jit(solution)/shard_map/ppermute | solution.py:167
  50.2 24.0 %collective-permute-start.6 = (bf16[256,1024]{1,0:T(8,128)(2,1)}, bf16[256,1024]{1,0:T(8,128)(2,1)S(1)}, u32[]{:S(2)}, u32[]{:S(2)}) collective-permute-start(bf16[256,1024]{1,0:T(8,128)(2,1)} %copy-done.19), channel_id=1, source_target_pairs={{8,0},{16,8},{24,16},{28,24},{20,28},{12,20},{4,12},{0,4},{9,1},{1... | collective-permute-start | bytes 1572872 | tf_op jit(solution)/shard_map/ppermute | solution.py:168
  56.9 17.4 %copy-start.11 = (bf16[256,1024]{1,0:T(8,128)(2,1)}, bf16[256,1024]{1,0:T(8,128)(2,1)S(1)}, u32[]{:S(2)}) copy-start(bf16[256,1024]{1,0:T(8,128)(2,1)S(1)} %collective-permute-done.5.refs_0_) | copy-start | bytes 1572868
  56.9 21.0 %collective-permute-start.3 = (bf16[8,272,128]{2,1,0:T(8,128)(2,1)}, bf16[8,272,128]{2,1,0:T(8,128)(2,1)S(1)}, u32[]{:S(2)}, u32[]{:S(2)}) collective-permute-start(bf16[8,272,128]{2,1,0:T(8,128)(2,1)} %all-to-all-done.refs_4_.refs_2_), channel_id=1, source_target_pairs={{0,1},{1,0},{2,3},{3,2},{4,5},{5,4},{6,7},{7,6},{8,9},{9,8},{10,11... | collective-permute-start | bytes 1671176 | tf_op jit(solution)/shard_map/ppermute | solution.py:135
  56.9 41.6 %copy-start.8 = (s32[1,8]{1,0:T(1,128)S(1)}, s32[1,8]{1,0:T(1,128)}, u32[]{:S(2)}) copy-start(s32[1,8]{1,0:T(1,128)} %param.10) | copy-start | bytes 100
  63.1 21.6 %collective-permute-start.10 = (bf16[256,1024]{1,0:T(8,128)(2,1)}, bf16[256,1024]{1,0:T(8,128)(2,1)S(1)}, u32[]{:S(2)}, u32[]{:S(2)}) collective-permute-start(bf16[256,1024]{1,0:T(8,128)(2,1)} %collective-permute-done.9.refs_9_), channel_id=1, source_target_pairs={{8,0},{16,8},{24,16},{28,24},{20,28},{12,20},{4,12},{0,4},{9,1},{1... | collective-permute-start | bytes 1572872 | tf_op jit(solution)/shard_map/ppermute | solution.py:168
  65.9 56.7 %collective-permute-start.15 = (bf16[256,1024]{1,0:T(8,128)(2,1)}, bf16[256,1024]{1,0:T(8,128)(2,1)}, u32[]{:S(2)}, u32[]{:S(2)}) collective-permute-start(bf16[256,1024]{1,0:T(8,128)(2,1)} %collective-permute-done.14.refs_7_), channel_id=1, source_target_pairs={{0,8},{8,16},{16,24},{24,28},{28,20},{20,12},{12,4},{4,0},{1,9},{9... | collective-permute-start | bytes 1572872 | tf_op jit(solution)/shard_map/ppermute | solution.py:167
  74.2 0.8 copy-start.12
  75.0 17.5 %collective-permute-start.7 = (bf16[256,1024]{1,0:T(8,128)(2,1)}, bf16[256,1024]{1,0:T(8,128)(2,1)S(1)}, u32[]{:S(2)}, u32[]{:S(2)}) collective-permute-start(bf16[256,1024]{1,0:T(8,128)(2,1)} %get-tuple-element.13.refs_6_), channel_id=1, source_target_pairs={{0,8},{8,16},{16,24},{24,28},{28,20},{20,12},{12,4},{4,0},{1,9},{9... | collective-permute-start | bytes 1572872 | tf_op jit(solution)/shard_map/ppermute | solution.py:167
  77.1 15.4 %copy-start = (bf16[8,272,128]{2,1,0:T(8,128)(2,1)}, bf16[8,272,128]{2,1,0:T(8,128)(2,1)S(1)}, u32[]{:S(2)}) copy-start(bf16[8,272,128]{2,1,0:T(8,128)(2,1)S(1)} %collective-permute-done.2.refs_5_.refs_2_) | copy-start | bytes 1671172
  77.1 15.4 %collective-permute-start.4 = (bf16[8,272,128]{2,1,0:T(8,128)(2,1)S(1)}, bf16[8,272,128]{2,1,0:T(8,128)(2,1)S(1)}, u32[]{:S(2)}, u32[]{:S(2)}) collective-permute-start(bf16[8,272,128]{2,1,0:T(8,128)(2,1)S(1)} %collective-permute-done.2.refs_5_.refs_2_), channel_id=1, source_target_pairs={{0,1},{1,0},{2,3},{3,2},{4,5},{5,4},{6,7},{7,6},{8,9},{9,8},{10,11... | collective-permute-start | bytes 1671176 | tf_op jit(solution)/shard_map/ppermute | solution.py:136
  77.9 14.6 %copy-start.2 = (bf16[8,272,128]{2,1,0:T(8,128)(2,1)}, bf16[8,272,128]{2,1,0:T(8,128)(2,1)S(1)}, u32[]{:S(2)}) copy-start(bf16[8,272,128]{2,1,0:T(8,128)(2,1)S(1)} %collective-permute-done.3.refs_6_.refs_3_) | copy-start | bytes 1671172
  77.9 44.7 %collective-permute-start.16 = (bf16[256,1024]{1,0:T(8,128)(2,1)}, bf16[256,1024]{1,0:T(8,128)(2,1)}, u32[]{:S(2)}, u32[]{:S(2)}) collective-permute-start(bf16[256,1024]{1,0:T(8,128)(2,1)} %get-tuple-element.17.refs_8_), channel_id=1, source_target_pairs={{8,0},{16,8},{24,16},{28,24},{20,28},{12,20},{4,12},{0,4},{9,1},{1... | collective-permute-start | bytes 1572872 | tf_op jit(solution)/shard_map/ppermute | solution.py:168
  84.7 7.8 %copy-start.9 = (bf16[256,1024]{1,0:T(8,128)(2,1)}, bf16[256,1024]{1,0:T(8,128)(2,1)S(1)}, u32[]{:S(2)}) copy-start(bf16[256,1024]{1,0:T(8,128)(2,1)S(1)} %collective-permute-done.10.refs_1_) | copy-start | bytes 1572868
  92.5 0.8 copy-start.10
  93.3 0.8 copy-start.4
  94.1 36.3 %collective-permute-start.11 = (bf16[256,1024]{1,0:T(8,128)(2,1)}, bf16[256,1024]{1,0:T(8,128)(2,1)S(1)}, u32[]{:S(2)}, u32[]{:S(2)}) collective-permute-start(bf16[256,1024]{1,0:T(8,128)(2,1)} %get-tuple-element.14.refs_0_), channel_id=1, source_target_pairs={{0,8},{8,16},{16,24},{24,28},{28,20},{20,12},{12,4},{4,0},{1,9},{9... | collective-permute-start | bytes 1572872 | tf_op jit(solution)/shard_map/ppermute | solution.py:167
  96.7 33.8 %collective-permute-start.12 = (bf16[256,1024]{1,0:T(8,128)(2,1)}, bf16[256,1024]{1,0:T(8,128)(2,1)S(1)}, u32[]{:S(2)}, u32[]{:S(2)}) collective-permute-start(bf16[256,1024]{1,0:T(8,128)(2,1)} %get-tuple-element.15.refs_3_), channel_id=1, source_target_pairs={{8,0},{16,8},{24,16},{28,24},{20,28},{12,20},{4,12},{0,4},{9,1},{1... | collective-permute-start | bytes 1572872 | tf_op jit(solution)/shard_map/ppermute | solution.py:168
  98.5 1.1 copy-start.1
  99.6 1.1 copy-start.3
  100.6 1.1 copy-start.5
  109.7 1.3 copy-start.6
  111.0 1.0 copy-start.7
  130.4 0.8 copy-start.13
  130.4 1.0 copy-start.14

commit v4 on v3

--- a/solution.py
+++ b/solution.py
@@ -8,6 +8,7 @@
 from jax.sharding import PartitionSpec as P
 
 META = 16
+VMEM_BYTES = 62 << 20
 
 
 def ring_order(n):
@@ -68,7 +69,7 @@
         ],
         in_specs=[smem] * (2 + n_parts) + [vmem] * n_parts,
         out_specs=[vmem] * len(bounds),
-        compiler_params=pltpu.CompilerParams(vmem_limit_bytes=48 << 20),
+        compiler_params=pltpu.CompilerParams(vmem_limit_bytes=VMEM_BYTES),
         cost_estimate=pl.CostEstimate(
             flops=0, bytes_accessed=rows * groups * blocks * bs * 4, transcendentals=0
         ),
@@ -116,7 +117,7 @@
         grid=(cols // bn,),
         in_specs=in_specs,
         out_specs=pl.BlockSpec((rows, bn), lambda j: (0, j)),
-        compiler_params=pltpu.CompilerParams(vmem_limit_bytes=56 << 20),
+        compiler_params=pltpu.CompilerParams(vmem_limit_bytes=VMEM_BYTES),
         cost_estimate=pl.CostEstimate(
             flops=2 * rows * inner * cols,
             bytes_accessed=(rows + cols) * inner * 2 + rows * cols * 8,
@@ -167,15 +168,15 @@
         from_left = {h: lax.ppermute(from_left[h], "grid", to_right) for h in low}
         from_right = {h: lax.ppermute(from_right[h], "grid", to_left) for h in high}
         if s == 1:
-            (message,) = after([message], [from_left[0], from_right[0]])
+            first = list(from_left.values()) + list(from_right.values())
+            (message,) = after([message], first)
             landed = lax.all_to_all(message, "grid", split_axis=0, concat_axis=0, tiled=True)
         if s == 2:
-            from_left[0], from_right[0] = after([from_left[0], from_right[0]], [landed])
+            from_left[per - 1], from_right[0] = after([from_left[per - 1], from_right[0]], [landed])
             parts = across_row(landed, columns)
         if s == half - 1:
-            from_left[0], from_right[per - 1] = after(
-                [from_left[0], from_right[per - 1]], parts[1:]
-            )
+            (from_left[0],) = after([from_left[0]], parts[1:2])
+            (from_right[per - 1],) = after([from_right[per - 1]], parts[2:])
         events.append([from_left[h] for h in low] + [from_right[h] for h in high])
     metas = [p[:, cap * bs, : 2 * cap].astype(jnp.int32) for p in parts]
 

time: 138 us -> 128 us (0.928)
  waiting for transfers between devices: 62.5 us -> 51.6 us
  local copies, waits for them, and re-layouts: 11.1 us -> 5.68 us
  other arithmetic: 2.36 us -> 5.46 us
  starting transfers between devices: 28.8 us -> 31.1 us
  Pallas kernels: 32.1 us -> 33.7 us
    ppermute x7, waiting for transfers between devices: 22.2 us -> 7.7 us  [body(): from_right = {h: lax.ppermute(from_right[h], 'grid', to_left) for h in high}]
    ppermute x7, starting transfers between devices: 3.22 us -> 11.2 us  [body(): from_right = {h: lax.ppermute(from_right[h], 'grid', to_left) for h in high}]
    unnamed x50 -> x36, local copies, waits for them, and re-layouts: 9.66 us -> 3.46 us
    ppermute x7, starting transfers between devices: 18.7 us -> 12.8 us  [body(): from_left = {h: lax.ppermute(from_left[h], 'grid', to_right) for h in low}]
    ppermute x7, waiting for transfers between devices: 28.1 us -> 33 us  [body(): from_left = {h: lax.ppermute(from_left[h], 'grid', to_right) for h in low}]
    convert_element_type x4, other arithmetic: 1.5 us -> 4.59 us  [body(): metas = [p[:, cap * bs, :2 * cap].astype(jnp.int32) for p in parts]]
    pallas_call x1, Pallas kernels: 7.97 us -> 9.54 us  [build_tiles(): pl.pallas_call(functools.partial(build_kernel, dims, bounds), out_shape=[...]
  transfers between devices with their start and end apart: 18 -> 18, of which waited for: 10 -> 9; matrix products, arithmetic and copies ran while one was open for 2% -> 4% of each run, Pallas kernels for 19% -> 22%
where the time goes in v4:
time: 128 us
  waiting for transfers between devices  51.6 us (40%)
  Pallas kernels  33.7 us (26%)
  starting transfers between devices  31.1 us (24%)
  local copies, waits for them, and re-layouts  5.68 us (4%)
  other arithmetic  5.46 us (4%)
    ppermute x7, waiting for transfers between devices, body(): from_left = {h: lax.ppermute(from_left[h], 'grid', to_right) for h in low}  33 us
    pallas_call x3, Pallas kernels, mul(): pl.pallas_call(functools.partial(mul_kernel, n), out_shape=jax.ShapeDtype...  24.1 us
    ppermute x7, starting transfers between devices, body(): from_left = {h: lax.ppermute(from_left[h], 'grid', to_right) for h in low}  12.8 us
    ppermute x7, starting transfers between devices, body(): from_right = {h: lax.ppermute(from_right[h], 'grid', to_left) for h in high}  11.2 us
    all_to_all x1, waiting for transfers between devices, body(): lax.all_to_all(message, 'grid', split_axis=0, concat_axis=0, tiled=True)  10.9 us
    pallas_call x1, Pallas kernels, build_tiles(): pl.pallas_call(functools.partial(build_kernel, dims, bounds), out_shape=[...  9.54 us
    ppermute x7, waiting for transfers between devices, body(): from_right = {h: lax.ppermute(from_right[h], 'grid', to_left) for h in high}  7.7 us
    all_to_all x1, starting transfers between devices, body(): lax.all_to_all(message, 'grid', split_axis=0, concat_axis=0, tiled=True)  5.55 us
  transfers between devices with their start and end apart: 18, of which 9 were waited for; matrix products, arithmetic and copies ran while one was open for 4% of the time, Pallas kernels for 22%

profile of v4, /device:TPU:0, one launch (start us, length us, event | category | flops | bytes accessed | tf_op | source)
XLA Modules:
  0.0 127.7 jit_solution(7403103855534274899)
XLA Ops:
  0.0 2.1 %fusion.4 = (bf16[256,1024]{1,0:T(8,128)(2,1)S(1)}, bf16[256,1024]{1,0:T(8,128)(2,1)}) fusion(bf16[512,1024]{1,0:T(8,128)(2,1)} %param.11), kind=kLoop, calls=%fused_computation.12 | loop fusion | bytes 2097152 | tf_op jit(solution)/shard_map/slice | solution.py:162
  2.1 3.0 %collective-permute-start = (bf16[256,1024]{1,0:T(8,128)(2,1)}, bf16[256,1024]{1,0:T(8,128)(2,1)S(1)}, u32[]{:S(2)}, u32[]{:S(2)}) collective-permute-start(bf16[256,1024]{1,0:T(8,128)(2,1)} %get-tuple-element.16.refs_0_), channel_id=1, source_target_pairs={{0,8},{8,16},{16,24},{24,28},{28,20},{20,12},{12,4},{4,0},{1,9},{9... | collective-permute-start | bytes 1572872 | tf_op jit(solution)/shard_map/ppermute | solution.py:168
  5.2 0.0 collective-permute-start.2
  5.2 2.0 %collective-permute-start.1 = (bf16[256,1024]{1,0:T(8,128)(2,1)S(1)}, bf16[256,1024]{1,0:T(8,128)(2,1)S(1)}, u32[]{:S(2)}, u32[]{:S(2)}) collective-permute-start(bf16[256,1024]{1,0:T(8,128)(2,1)S(1)} %get-tuple-element.15.refs_1_), channel_id=1, source_target_pairs={{0,8},{8,16},{16,24},{24,28},{28,20},{20,12},{12,4},{4,0},{1,9},{9... | collective-permute-start | bytes 1572872 | tf_op jit(solution)/shard_map/ppermute | solution.py:168
  7.2 0.0 collective-permute-start.3
  7.3 0.1 copy.31
  7.4 0.8 fusion.1.refs_0_
  8.2 9.9 %collective-permute-done.refs_1_.refs_2_ = bf16[256,1024]{1,0:T(8,128)(2,1)S(1)} collective-permute-done((bf16[256,1024]{1,0:T(8,128)(2,1)}, bf16[256,1024]{1,0:T(8,128)(2,1)S(1)}, u32[]{:S(2)}, u32[]{:S(2)}) %collective-permute-start) | collective-permute-done | bytes 524320 | tf_op jit(solution)/shard_map/ppermute | solution.py:168
  18.1 10.4 %collective-permute-done.1.refs_2_.refs_3_ = bf16[256,1024]{1,0:T(8,128)(2,1)S(1)} collective-permute-done((bf16[256,1024]{1,0:T(8,128)(2,1)S(1)}, bf16[256,1024]{1,0:T(8,128)(2,1)S(1)}, u32[]{:S(2)}, u32[]{:S(2)}) %collective-permute-start.1) | collective-permute-done | bytes 524320 | tf_op jit(solution)/shard_map/ppermute | solution.py:168
  28.5 1.5 %collective-permute-done.3.refs_4_.refs_5_ = bf16[256,1024]{1,0:T(8,128)(2,1)S(1)} collective-permute-done((bf16[256,1024]{1,0:T(8,128)(2,1)S(1)}, bf16[256,1024]{1,0:T(8,128)(2,1)S(1)}, u32[]{:S(2)}, u32[]{:S(2)}) %collective-permute-start.3) | collective-permute-done | bytes 524320 | tf_op jit(solution)/shard_map/ppermute | solution.py:169
  30.0 0.8 copy-done.9
  30.8 5.6 %all-to-all-start = ((bf16[8,272,128]{2,1,0:T(8,128)(2,1)}), bf16[8,272,128]{2,1,0:T(8,128)(2,1)S(1)}, u32[]{:S(2)}, u32[]{:S(2)}) async-start(bf16[8,272,128]{2,1,0:T(8,128)(2,1)} %shard_map.64), calls=%async_computation | async-start | bytes 1114112 | tf_op jit(solution)/shard_map/all_to_all | solution.py:173
  36.4 2.0 %collective-permute-start.7 = (bf16[256,1024]{1,0:T(8,128)(2,1)}, bf16[256,1024]{1,0:T(8,128)(2,1)}, u32[]{:S(2)}, u32[]{:S(2)}) collective-permute-start(bf16[256,1024]{1,0:T(8,128)(2,1)} %copy-done.6), channel_id=1, source_target_pairs={{0,8},{8,16},{16,24},{24,28},{28,20},{20,12},{12,4},{4,0},{1,9},{9... | collective-permute-start | bytes 1572872 | tf_op jit(solution)/shard_map/ppermute | solution.py:168
  38.4 1.5 %collective-permute-start.13 = (bf16[256,1024]{1,0:T(8,128)(2,1)}, bf16[256,1024]{1,0:T(8,128)(2,1)S(1)}, u32[]{:S(2)}, u32[]{:S(2)}) collective-permute-start(bf16[256,1024]{1,0:T(8,128)(2,1)} %copy-done.8), channel_id=1, source_target_pairs={{0,8},{8,16},{16,24},{24,28},{28,20},{20,12},{12,4},{4,0},{1,9},{9... | collective-permute-start | bytes 1572872 | tf_op jit(solution)/shard_map/ppermute | solution.py:168
  39.9 10.9 %all-to-all-done.refs_4_.refs_2_ = bf16[8,272,128]{2,1,0:T(8,128)(2,1)S(1)} async-done(((bf16[8,272,128]{2,1,0:T(8,128)(2,1)}), bf16[8,272,128]{2,1,0:T(8,128)(2,1)S(1)}, u32[]{:S(2)}, u32[]{:S(2)}) %all-to-all-start) | async-done | bytes 557088 | tf_op jit(solution)/shard_map/all_to_all | solution.py:173
  50.8 1.5 %collective-permute-start.4 = (bf16[8,272,128]{2,1,0:T(8,128)(2,1)S(1)}, bf16[8,272,128]{2,1,0:T(8,128)(2,1)S(1)}, u32[]{:S(2)}, u32[]{:S(2)}) collective-permute-start(bf16[8,272,128]{2,1,0:T(8,128)(2,1)S(1)} %all-to-all-done.refs_4_.refs_2_), channel_id=1, source_target_pairs={{0,2},{1,3},{2,0},{3,1},{4,6},{5,7},{6,4},{7,5},{8,10},{9,11},{10,... | collective-permute-start | bytes 1671176 | tf_op jit(solution)/shard_map/ppermute | solution.py:135
  52.2 3.0 %collective-permute-start.10 = (bf16[256,1024]{1,0:T(8,128)(2,1)}, bf16[256,1024]{1,0:T(8,128)(2,1)}, u32[]{:S(2)}, u32[]{:S(2)}) collective-permute-start(bf16[256,1024]{1,0:T(8,128)(2,1)} %copy-done.9), channel_id=1, source_target_pairs={{8,0},{16,8},{24,16},{28,24},{20,28},{12,20},{4,12},{0,4},{9,1},{1... | collective-permute-start | bytes 1572872 | tf_op jit(solution)/shard_map/ppermute | solution.py:169
  55.3 0.0 collective-permute-start.14
  55.3 2.7 %collective-permute-done.7.refs_6_ = bf16[256,1024]{1,0:T(8,128)(2,1)} collective-permute-done((bf16[256,1024]{1,0:T(8,128)(2,1)}, bf16[256,1024]{1,0:T(8,128)(2,1)}, u32[]{:S(2)}, u32[]{:S(2)}) %collective-permute-start.7) | collective-permute-done | bytes 524320 | tf_op jit(solution)/shard_map/ppermute | solution.py:168
  58.0 3.3 %collective-permute-start.8 = (bf16[256,1024]{1,0:T(8,128)(2,1)}, bf16[256,1024]{1,0:T(8,128)(2,1)S(1)}, u32[]{:S(2)}, u32[]{:S(2)}) collective-permute-start(bf16[256,1024]{1,0:T(8,128)(2,1)} %collective-permute-done.7.refs_6_), channel_id=1, source_target_pairs={{0,8},{8,16},{16,24},{24,28},{28,20},{20,12},{12,4},{4,0},{1,9},{9... | collective-permute-start | bytes 1572872 | tf_op jit(solution)/shard_map/ppermute | solution.py:168
  61.3 7.9 %collective-permute-done.13.refs_0_ = bf16[256,1024]{1,0:T(8,128)(2,1)S(1)} collective-permute-done((bf16[256,1024]{1,0:T(8,128)(2,1)}, bf16[256,1024]{1,0:T(8,128)(2,1)S(1)}, u32[]{:S(2)}, u32[]{:S(2)}) %collective-permute-start.13) | collective-permute-done | bytes 524320 | tf_op jit(solution)/shard_map/ppermute | solution.py:168
  69.3 0.0 collective-permute-start.5
  69.3 0.0 collective-permute-done.10.refs_9_
  69.3 3.1 %collective-permute-start.11 = (bf16[256,1024]{1,0:T(8,128)(2,1)}, bf16[256,1024]{1,0:T(8,128)(2,1)S(1)}, u32[]{:S(2)}, u32[]{:S(2)}) collective-permute-start(bf16[256,1024]{1,0:T(8,128)(2,1)} %collective-permute-done.10.refs_9_), channel_id=1, source_target_pairs={{8,0},{16,8},{24,16},{28,24},{20,28},{12,20},{4,12},{0,4},{9,1},{1... | collective-permute-start | bytes 1572872 | tf_op jit(solution)/shard_map/ppermute | solution.py:169
  72.4 4.6 %collective-permute-done.14.refs_1_ = bf16[256,1024]{1,0:T(8,128)(2,1)} collective-permute-done((bf16[256,1024]{1,0:T(8,128)(2,1)}, bf16[256,1024]{1,0:T(8,128)(2,1)}, u32[]{:S(2)}, u32[]{:S(2)}) %collective-permute-start.14) | collective-permute-done | bytes 524320 | tf_op jit(solution)/shard_map/ppermute | solution.py:169
  77.0 0.1 collective-permute-start.6
  77.1 1.4 %slice_convert_fusion.3 = s32[8,1,4]{2,1,0:T(1,128)} fusion(bf16[8,272,128]{2,1,0:T(8,128)(2,1)} %copy-done), kind=kLoop, calls=%fused_computation.6 | loop fusion | flops 32 | bytes 192 | tf_op jit(solution)/shard_map/convert_element_type | solution.py:181
  78.5 2.0 %collective-permute-done.8.refs_0_ = bf16[256,1024]{1,0:T(8,128)(2,1)S(1)} collective-permute-done((bf16[256,1024]{1,0:T(8,128)(2,1)}, bf16[256,1024]{1,0:T(8,128)(2,1)S(1)}, u32[]{:S(2)}, u32[]{:S(2)}) %collective-permute-start.8) | collective-permute-done | bytes 524320 | tf_op jit(solution)/shard_map/ppermute | solution.py:168
  80.5 3.1 %collective-permute-start.16 = (bf16[256,1024]{1,0:T(8,128)(2,1)}, bf16[256,1024]{1,0:T(8,128)(2,1)}, u32[]{:S(2)}, u32[]{:S(2)}) collective-permute-start(bf16[256,1024]{1,0:T(8,128)(2,1)} %get-tuple-element.13.refs_8_), channel_id=1, source_target_pairs={{8,0},{16,8},{24,16},{28,24},{20,28},{12,20},{4,12},{0,4},{9,1},{1... | collective-permute-start | bytes 1572872 | tf_op jit(solution)/shard_map/ppermute | solution.py:169
  83.6 1.3 %slice_convert_fusion.2 = s32[8,1,4]{2,1,0:T(1,128)} fusion(bf16[8,272,128]{2,1,0:T(8,128)(2,1)} %copy-done.1), kind=kLoop, calls=%fused_computation.5 | loop fusion | flops 32 | bytes 192 | tf_op jit(solution)/shard_map/convert_element_type | solution.py:181
  84.9 0.0 collective-permute-done.5.refs_6_.refs_1_
  84.9 1.0 collective-permute-start.9
  85.9 0.6 slice_convert_fusion.1
  86.5 1.6 %collective-permute-done.11.refs_0_ = bf16[256,1024]{1,0:T(8,128)(2,1)S(1)} collective-permute-done((bf16[256,1024]{1,0:T(8,128)(2,1)}, bf16[256,1024]{1,0:T(8,128)(2,1)S(1)}, u32[]{:S(2)}, u32[]{:S(2)}) %collective-permute-start.11) | collective-permute-done | bytes 524320 | tf_op jit(solution)/shard_map/ppermute | solution.py:169
  88.1 0.0 collective-permute-done.6.refs_7_.refs_2_
  88.1 0.8 copy-done.5
  88.9 0.8 copy-done.3
  89.7 1.9 %collective-permute-start.12 = (bf16[256,1024]{1,0:T(8,128)(2,1)}, bf16[256,1024]{1,0:T(8,128)(2,1)S(1)}, u32[]{:S(2)}, u32[]{:S(2)}) collective-permute-start(bf16[256,1024]{1,0:T(8,128)(2,1)} %shard_map.67.refs_3_), channel_id=1, source_target_pairs={{8,0},{16,8},{24,16},{28,24},{20,28},{12,20},{4,12},{0,4},{9,1},{1... | collective-permute-start | bytes 1572872 | tf_op jit(solution)/shard_map/ppermute | solution.py:169
  91.6 1.3 %slice_convert_fusion = s32[8,1,4]{2,1,0:T(1,128)} fusion(bf16[8,272,128]{2,1,0:T(8,128)(2,1)} %copy-done.3), kind=kLoop, calls=%fused_computation.3 | loop fusion | flops 32 | bytes 192 | tf_op jit(solution)/shard_map/convert_element_type | solution.py:181
  93.0 9.5 %shard_map.65 = (bf16[1024,2560]{1,0:T(8,128)(2,1)}, bf16[1024,1024]{1,0:T(8,128)(2,1)}, bf16[1024,512]{1,0:T(8,128)(2,1)}) custom-call(s32[1]{0:T(128)} %bitcast.pos_ref, s32[8]{0:T(128)} %bitcast.22, s32[8,4]{1,0:T(8,128)} %bitcast.17, s32[8,4]{1,0:T(8,128)} %bitcast.18, s32[8,4]{1,0:T(8,128)} %bitcast.19, s32[8,4]{1,0:T(8,128)} %bitcast.20, ...), custom_call_target="tpu_custom_call" | custom-call | bytes 16777216 | tf_op jit(solution)/shard_map/pallas_call | solution.py:64
  102.5 10.7 %shard_map.69.refs_4_ = f32[1024,1024]{1,0:T(8,128)} custom-call(bf16[1024,2560]{1,0:T(8,128)(2,1)} %get-tuple-element.14.tile_ref, bf16[256,1024]{1,0:T(8,128)(2,1)} %get-tuple-element.16.refs_0_, bf16[256,1024]{1,0:T(8,128)(2,1)} %copy-done.14, bf16[256,1024]{1,0:T(8,128)(2,1)} %copy-done.6, bf16[256,1024]{1,0:T(8,128)(2,1)} %copy-done.8, ...), custom_call_target="tpu_custom_call" | custom-call | flops 5368709120 | bytes 18874368 | tf_op jit(solution)/shard_map/pallas_call | solution.py:114
  113.2 0.0 collective-permute-done.16.refs_2_
  113.2 7.8 %shard_map.70.refs_2_ = f32[1024,1024]{1,0:T(8,128)} custom-call(bf16[1024,1024]{1,0:T(8,128)(2,1)} %get-tuple-element.11.tile_ref, bf16[256,1024]{1,0:T(8,128)(2,1)} %shard_map.66.refs_0_, bf16[256,1024]{1,0:T(8,128)(2,1)} %collective-permute-done.15.refs_1_, bf16[256,1024]{1,0:T(8,128)(2,1)} %collective-permute-done.16.refs_2_, ...), custom_call_target="tpu_custom_call" | custom-call | flops 2147483648 | bytes 12582912 | tf_op jit(solution)/shard_map/pallas_call | solution.py:114
  121.0 0.0 collective-permute-done.9.refs_0_
  121.0 0.0 collective-permute-done.12.refs_1_
  121.0 0.8 copy-done.11
  121.8 0.2 copy-done.12
  122.0 5.7 %shard_map.71 = bf16[1024,1024]{1,0:T(8,128)(2,1)} custom-call(bf16[1024,512]{1,0:T(8,128)(2,1)} %get-tuple-element.10.tile_ref, bf16[256,1024]{1,0:T(8,128)(2,1)} %copy-done.11, bf16[256,1024]{1,0:T(8,128)(2,1)} %copy-done.12, f32[1024,1024]{1,0:T(8,128)} %shard_map.70.refs_2_), custom_call_target="tpu_custom_call" | custom-call | flops 1073741824 | bytes 10485760 | tf_op jit(solution)/shard_map/pallas_call | solution.py:114
  (42 shorter events, 0.1 us)
Async XLA Ops:
  0.0 7.2 %copy-start.17 = (s32[1,1,8,2]{2,3,1,0:T(2,128)S(1)}, s32[1,1,8,2]{2,3,1,0:T(2,128)}, u32[]{:S(2)}) copy-start(s32[1,1,8,2]{2,3,1,0:T(2,128)} %param.8) | copy-start | bytes 196
  0.0 7.2 %copy-start.16 = (s32[1,1,8]{2,1,0:T(1,128)S(1)}, s32[1,1,8]{2,1,0:T(1,128)}, u32[]{:S(2)}) copy-start(s32[1,1,8]{2,1,0:T(1,128)} %param.9) | copy-start | bytes 100
  0.0 7.2 %copy-start.15 = (s32[1,1,8,2]{2,3,1,0:T(2,128)S(1)}, s32[1,1,8,2]{2,3,1,0:T(2,128)}, u32[]{:S(2)}) copy-start(s32[1,1,8,2]{2,3,1,0:T(2,128)} %param.7) | copy-start | bytes 196
  0.0 7.4 %copy-start.13 = (bf16[1,1,8,2,128,128]{5,4,3,2,1,0:T(8,128)(2,1)S(1)}, bf16[1,1,8,2,128,128]{5,4,3,2,1,0:T(8,128)(2,1)}, u32[]{:S(2)}) copy-start(bf16[1,1,8,2,128,128]{5,4,3,2,1,0:T(8,128)(2,1)} %param.6) | copy-start | bytes 1572868
  2.1 28.7 %copy-start.14 = (bf16[256,1024]{1,0:T(8,128)(2,1)}, bf16[256,1024]{1,0:T(8,128)(2,1)S(1)}, u32[]{:S(2)}) copy-start(bf16[256,1024]{1,0:T(8,128)(2,1)S(1)} %get-tuple-element.15.refs_1_) | copy-start | bytes 1572868
  2.1 15.9 %collective-permute-start = (bf16[256,1024]{1,0:T(8,128)(2,1)}, bf16[256,1024]{1,0:T(8,128)(2,1)S(1)}, u32[]{:S(2)}, u32[]{:S(2)}) collective-permute-start(bf16[256,1024]{1,0:T(8,128)(2,1)} %get-tuple-element.16.refs_0_), channel_id=1, source_target_pairs={{0,8},{8,16},{16,24},{24,28},{28,20},{20,12},{12,4},{4,0},{1,9},{9... | collective-permute-start | bytes 1572872 | tf_op jit(solution)/shard_map/ppermute | solution.py:168
  5.2 23.3 %collective-permute-start.2 = (bf16[256,1024]{1,0:T(8,128)(2,1)}, bf16[256,1024]{1,0:T(8,128)(2,1)S(1)}, u32[]{:S(2)}, u32[]{:S(2)}) collective-permute-start(bf16[256,1024]{1,0:T(8,128)(2,1)} %get-tuple-element.16.refs_0_), channel_id=1, source_target_pairs={{8,0},{16,8},{24,16},{28,24},{20,28},{12,20},{4,12},{0,4},{9,1},{1... | collective-permute-start | bytes 1572872 | tf_op jit(solution)/shard_map/ppermute | solution.py:169
  5.2 23.3 %collective-permute-start.1 = (bf16[256,1024]{1,0:T(8,128)(2,1)S(1)}, bf16[256,1024]{1,0:T(8,128)(2,1)S(1)}, u32[]{:S(2)}, u32[]{:S(2)}) collective-permute-start(bf16[256,1024]{1,0:T(8,128)(2,1)S(1)} %get-tuple-element.15.refs_1_), channel_id=1, source_target_pairs={{0,8},{8,16},{16,24},{24,28},{28,20},{20,12},{12,4},{4,0},{1,9},{9... | collective-permute-start | bytes 1572872 | tf_op jit(solution)/shard_map/ppermute | solution.py:168
  7.2 22.8 %collective-permute-start.3 = (bf16[256,1024]{1,0:T(8,128)(2,1)S(1)}, bf16[256,1024]{1,0:T(8,128)(2,1)S(1)}, u32[]{:S(2)}, u32[]{:S(2)}) collective-permute-start(bf16[256,1024]{1,0:T(8,128)(2,1)S(1)} %get-tuple-element.15.refs_1_), channel_id=1, source_target_pairs={{8,0},{16,8},{24,16},{28,24},{20,28},{12,20},{4,12},{0,4},{9,1},{1... | collective-permute-start | bytes 1572872 | tf_op jit(solution)/shard_map/ppermute | solution.py:169
  18.1 11.9 %copy-start.6 = (bf16[256,1024]{1,0:T(8,128)(2,1)}, bf16[256,1024]{1,0:T(8,128)(2,1)S(1)}, u32[]{:S(2)}) copy-start(bf16[256,1024]{1,0:T(8,128)(2,1)S(1)} %collective-permute-done.refs_1_.refs_2_) | copy-start | bytes 1572868
  28.5 1.5 %copy-start.8 = (bf16[256,1024]{1,0:T(8,128)(2,1)}, bf16[256,1024]{1,0:T(8,128)(2,1)S(1)}, u32[]{:S(2)}) copy-start(bf16[256,1024]{1,0:T(8,128)(2,1)S(1)} %collective-permute-done.1.refs_2_.refs_3_) | copy-start | bytes 1572868
  28.5 1.5 %copy-start.7 = (bf16[256,1024]{1,0:T(8,128)(2,1)}, bf16[256,1024]{1,0:T(8,128)(2,1)S(1)}, u32[]{:S(2)}) copy-start(bf16[256,1024]{1,0:T(8,128)(2,1)S(1)} %collective-permute-done.2.refs_3_.refs_4_) | copy-start | bytes 1572868
  30.0 0.8 copy-start.9
  30.8 19.9 %all-to-all-start = ((bf16[8,272,128]{2,1,0:T(8,128)(2,1)}), bf16[8,272,128]{2,1,0:T(8,128)(2,1)S(1)}, u32[]{:S(2)}, u32[]{:S(2)}) async-start(bf16[8,272,128]{2,1,0:T(8,128)(2,1)} %shard_map.64), calls=%async_computation | async-start | bytes 1114112 | tf_op jit(solution)/shard_map/all_to_all | solution.py:173
  36.4 21.6 %collective-permute-start.7 = (bf16[256,1024]{1,0:T(8,128)(2,1)}, bf16[256,1024]{1,0:T(8,128)(2,1)}, u32[]{:S(2)}, u32[]{:S(2)}) collective-permute-start(bf16[256,1024]{1,0:T(8,128)(2,1)} %copy-done.6), channel_id=1, source_target_pairs={{0,8},{8,16},{16,24},{24,28},{28,20},{20,12},{12,4},{4,0},{1,9},{9... | collective-permute-start | bytes 1572872 | tf_op jit(solution)/shard_map/ppermute | solution.py:168
  38.4 30.9 %collective-permute-start.13 = (bf16[256,1024]{1,0:T(8,128)(2,1)}, bf16[256,1024]{1,0:T(8,128)(2,1)S(1)}, u32[]{:S(2)}, u32[]{:S(2)}) collective-permute-start(bf16[256,1024]{1,0:T(8,128)(2,1)} %copy-done.8), channel_id=1, source_target_pairs={{0,8},{8,16},{16,24},{24,28},{28,20},{20,12},{12,4},{4,0},{1,9},{9... | collective-permute-start | bytes 1572872 | tf_op jit(solution)/shard_map/ppermute | solution.py:168
  50.8 26.2 %copy-start = (bf16[8,272,128]{2,1,0:T(8,128)(2,1)}, bf16[8,272,128]{2,1,0:T(8,128)(2,1)S(1)}, u32[]{:S(2)}) copy-start(bf16[8,272,128]{2,1,0:T(8,128)(2,1)S(1)} %all-to-all-done.refs_4_.refs_2_) | copy-start | bytes 1671172
  50.8 26.2 %collective-permute-start.4 = (bf16[8,272,128]{2,1,0:T(8,128)(2,1)S(1)}, bf16[8,272,128]{2,1,0:T(8,128)(2,1)S(1)}, u32[]{:S(2)}, u32[]{:S(2)}) collective-permute-start(bf16[8,272,128]{2,1,0:T(8,128)(2,1)S(1)} %all-to-all-done.refs_4_.refs_2_), channel_id=1, source_target_pairs={{0,2},{1,3},{2,0},{3,1},{4,6},{5,7},{6,4},{7,5},{8,10},{9,11},{10,... | collective-permute-start | bytes 1671176 | tf_op jit(solution)/shard_map/ppermute | solution.py:135
  52.2 17.0 %collective-permute-start.10 = (bf16[256,1024]{1,0:T(8,128)(2,1)}, bf16[256,1024]{1,0:T(8,128)(2,1)}, u32[]{:S(2)}, u32[]{:S(2)}) collective-permute-start(bf16[256,1024]{1,0:T(8,128)(2,1)} %copy-done.9), channel_id=1, source_target_pairs={{8,0},{16,8},{24,16},{28,24},{20,28},{12,20},{4,12},{0,4},{9,1},{1... | collective-permute-start | bytes 1572872 | tf_op jit(solution)/shard_map/ppermute | solution.py:169
  55.3 21.7 %collective-permute-start.14 = (bf16[256,1024]{1,0:T(8,128)(2,1)}, bf16[256,1024]{1,0:T(8,128)(2,1)}, u32[]{:S(2)}, u32[]{:S(2)}) collective-permute-start(bf16[256,1024]{1,0:T(8,128)(2,1)} %copy-done.7), channel_id=1, source_target_pairs={{8,0},{16,8},{24,16},{28,24},{20,28},{12,20},{4,12},{0,4},{9,1},{1... | collective-permute-start | bytes 1572872 | tf_op jit(solution)/shard_map/ppermute | solution.py:169
  58.0 22.5 %collective-permute-start.8 = (bf16[256,1024]{1,0:T(8,128)(2,1)}, bf16[256,1024]{1,0:T(8,128)(2,1)S(1)}, u32[]{:S(2)}, u32[]{:S(2)}) collective-permute-start(bf16[256,1024]{1,0:T(8,128)(2,1)} %collective-permute-done.7.refs_6_), channel_id=1, source_target_pairs={{0,8},{8,16},{16,24},{24,28},{28,20},{20,12},{12,4},{4,0},{1,9},{9... | collective-permute-start | bytes 1572872 | tf_op jit(solution)/shard_map/ppermute | solution.py:168
  69.3 7.7 %copy-start.10 = (bf16[256,1024]{1,0:T(8,128)(2,1)}, bf16[256,1024]{1,0:T(8,128)(2,1)S(1)}, u32[]{:S(2)}) copy-start(bf16[256,1024]{1,0:T(8,128)(2,1)S(1)} %collective-permute-done.13.refs_0_) | copy-start | bytes 1572868
  69.3 15.7 %collective-permute-start.5 = (bf16[8,272,128]{2,1,0:T(8,128)(2,1)S(1)}, bf16[8,272,128]{2,1,0:T(8,128)(2,1)S(1)}, u32[]{:S(2)}, u32[]{:S(2)}) collective-permute-start(bf16[8,272,128]{2,1,0:T(8,128)(2,1)S(1)} %all-to-all-done.refs_4_.refs_2_), channel_id=1, source_target_pairs={{0,1},{1,0},{2,3},{3,2},{4,5},{5,4},{6,7},{7,6},{8,9},{9,8},{10,11... | collective-permute-start | bytes 1671176 | tf_op jit(solution)/shard_map/ppermute | solution.py:136
  69.3 18.8 %collective-permute-start.11 = (bf16[256,1024]{1,0:T(8,128)(2,1)}, bf16[256,1024]{1,0:T(8,128)(2,1)S(1)}, u32[]{:S(2)}, u32[]{:S(2)}) collective-permute-start(bf16[256,1024]{1,0:T(8,128)(2,1)} %collective-permute-done.10.refs_9_), channel_id=1, source_target_pairs={{8,0},{16,8},{24,16},{28,24},{20,28},{12,20},{4,12},{0,4},{9,1},{1... | collective-permute-start | bytes 1572872 | tf_op jit(solution)/shard_map/ppermute | solution.py:169
  77.0 36.2 %collective-permute-start.15 = (bf16[256,1024]{1,0:T(8,128)(2,1)}, bf16[256,1024]{1,0:T(8,128)(2,1)}, u32[]{:S(2)}, u32[]{:S(2)}) collective-permute-start(bf16[256,1024]{1,0:T(8,128)(2,1)} %get-tuple-element.12.refs_7_), channel_id=1, source_target_pairs={{0,8},{8,16},{16,24},{24,28},{28,20},{20,12},{12,4},{4,0},{1,9},{9... | collective-permute-start | bytes 1572872 | tf_op jit(solution)/shard_map/ppermute | solution.py:168
  77.0 6.6 %copy-start.1 = (bf16[8,272,128]{2,1,0:T(8,128)(2,1)}, bf16[8,272,128]{2,1,0:T(8,128)(2,1)S(1)}, u32[]{:S(2)}) copy-start(bf16[8,272,128]{2,1,0:T(8,128)(2,1)S(1)} %collective-permute-done.4.refs_5_.refs_1_) | copy-start | bytes 1671172
  77.0 11.1 %collective-permute-start.6 = (bf16[8,272,128]{2,1,0:T(8,128)(2,1)S(1)}, bf16[8,272,128]{2,1,0:T(8,128)(2,1)S(1)}, u32[]{:S(2)}, u32[]{:S(2)}) collective-permute-start(bf16[8,272,128]{2,1,0:T(8,128)(2,1)S(1)} %collective-permute-done.4.refs_5_.refs_1_), channel_id=1, source_target_pairs={{0,1},{1,0},{2,3},{3,2},{4,5},{5,4},{6,7},{7,6},{8,9},{9,8},{10,11... | collective-permute-start | bytes 1671176 | tf_op jit(solution)/shard_map/ppermute | solution.py:137
  80.5 3.1 %copy-start.4 = (bf16[256,1024]{1,0:T(8,128)(2,1)}, bf16[256,1024]{1,0:T(8,128)(2,1)S(1)}, u32[]{:S(2)}) copy-start(bf16[256,1024]{1,0:T(8,128)(2,1)S(1)} %collective-permute-done.8.refs_0_) | copy-start | bytes 1572868
  80.5 32.7 %collective-permute-start.16 = (bf16[256,1024]{1,0:T(8,128)(2,1)}, bf16[256,1024]{1,0:T(8,128)(2,1)}, u32[]{:S(2)}, u32[]{:S(2)}) collective-permute-start(bf16[256,1024]{1,0:T(8,128)(2,1)} %get-tuple-element.13.refs_8_), channel_id=1, source_target_pairs={{8,0},{16,8},{24,16},{28,24},{20,28},{12,20},{4,12},{0,4},{9,1},{1... | collective-permute-start | bytes 1572872 | tf_op jit(solution)/shard_map/ppermute | solution.py:169
  84.9 3.2 %copy-start.2 = (bf16[8,272,128]{2,1,0:T(8,128)(2,1)}, bf16[8,272,128]{2,1,0:T(8,128)(2,1)S(1)}, u32[]{:S(2)}) copy-start(bf16[8,272,128]{2,1,0:T(8,128)(2,1)S(1)} %collective-permute-done.5.refs_6_.refs_1_) | copy-start | bytes 1671172
  84.9 36.0 %collective-permute-start.9 = (bf16[256,1024]{1,0:T(8,128)(2,1)}, bf16[256,1024]{1,0:T(8,128)(2,1)S(1)}, u32[]{:S(2)}, u32[]{:S(2)}) collective-permute-start(bf16[256,1024]{1,0:T(8,128)(2,1)} %shard_map.66.refs_0_), channel_id=1, source_target_pairs={{0,8},{8,16},{16,24},{24,28},{28,20},{20,12},{12,4},{4,0},{1,9},{9... | collective-permute-start | bytes 1572872 | tf_op jit(solution)/shard_map/ppermute | solution.py:168
  88.1 0.8 copy-start.5
  88.9 0.8 copy-start.3
  89.7 31.3 %collective-permute-start.12 = (bf16[256,1024]{1,0:T(8,128)(2,1)}, bf16[256,1024]{1,0:T(8,128)(2,1)S(1)}, u32[]{:S(2)}, u32[]{:S(2)}) collective-permute-start(bf16[256,1024]{1,0:T(8,128)(2,1)} %shard_map.67.refs_3_), channel_id=1, source_target_pairs={{8,0},{16,8},{24,16},{28,24},{20,28},{12,20},{4,12},{0,4},{9,1},{1... | collective-permute-start | bytes 1572872 | tf_op jit(solution)/shard_map/ppermute | solution.py:169
  121.0 0.8 copy-start.11
  121.0 1.0 copy-start.12

commit v5 on v4

--- a/solution.py
+++ b/solution.py
@@ -88,6 +88,7 @@
         in_specs=[anywhere] * (len(values) + len(others)),
         out_specs=[anywhere] * len(values),
         input_output_aliases={i: i for i in range(len(values))},
+        compiler_params=pltpu.CompilerParams(vmem_limit_bytes=VMEM_BYTES),
         cost_estimate=pl.CostEstimate(flops=0, bytes_accessed=0, transcendentals=0),
     )(*values, *others)
 
@@ -159,34 +160,33 @@
     meta = jnp.pad(meta.astype(jnp.bfloat16)[:, None, :], ((0, 0), (0, META - 1), (0, bs - 2 * cap)))
     message = jnp.concatenate([a_slots.reshape(groups, cap * bs, bs), meta], axis=1)
 
+    landed = lax.all_to_all(message, "grid", split_axis=0, concat_axis=0, tiled=True)
+    parts = across_row(landed, columns)
+    metas = [p[:, cap * bs, : 2 * cap].astype(jnp.int32) for p in parts]
+    bounds, start = [], 0
+    for count in (per * (half - 1) * 2 - per, per * 2, per):
+        bounds.append((start, start + count))
+        start += count
+    dims = (columns, groups, cap, bs, groups, blocks)
+    tiles = build_tiles(pos, owned_rows.reshape(rb), metas, parts, dims, bounds, rb * bs)
+
     own = [b_matrix[h * depth : (h + 1) * depth] for h in range(per)]
     events = [own]
-    from_left, from_right = list(own), list(own)
+    from_left, from_right = dict(enumerate(own)), dict(enumerate(own))
     for s in range(1, half + 1):
         low = range(per) if s < half else range(per // 2)
         high = range(per) if s < half else range(per // 2, per)
         from_left = {h: lax.ppermute(from_left[h], "grid", to_right) for h in low}
         from_right = {h: lax.ppermute(from_right[h], "grid", to_left) for h in high}
-        if s == 1:
-            first = list(from_left.values()) + list(from_right.values())
-            (message,) = after([message], first)
-            landed = lax.all_to_all(message, "grid", split_axis=0, concat_axis=0, tiled=True)
-        if s == 2:
-            from_left[per - 1], from_right[0] = after([from_left[per - 1], from_right[0]], [landed])
-            parts = across_row(landed, columns)
+        if s == half - 2:
+            from_left[0], from_right[0] = after([from_left[0], from_right[0]], parts[1:2])
+            from_left[per - 1], from_right[per - 1] = after(
+                [from_left[per - 1], from_right[per - 1]], parts[2:]
+            )
         if s == half - 1:
-            (from_left[0],) = after([from_left[0]], parts[1:2])
-            (from_right[per - 1],) = after([from_right[per - 1]], parts[2:])
+            from_left[0], from_right[0] = after([from_left[0], from_right[0]], tiles)
         events.append([from_left[h] for h in low] + [from_right[h] for h in high])
-    metas = [p[:, cap * bs, : 2 * cap].astype(jnp.int32) for p in parts]
-
     stages = [sum(events[: half - 1], []), events[half - 1], events[half]]
-    bounds, start = [], 0
-    for stage in stages:
-        bounds.append((start, start + len(stage)))
-        start += len(stage)
-    dims = (columns, groups, cap, bs, groups, blocks)
-    tiles = build_tiles(pos, owned_rows.reshape(rb), metas, parts, dims, bounds, rb * bs)
 
     acc = None
     for t, (tile, stage) in enumerate(zip(tiles, stages)):

time: 128 us -> 124 us (0.969)
  waiting for transfers between devices: 51.6 us -> 39.9 us
  starting transfers between devices: 31.1 us -> 37.6 us
  other arithmetic: 5.46 us -> 7.88 us
  local copies, waits for them, and re-layouts: 5.68 us -> 4.38 us
    ppermute x7, waiting for transfers between devices: 33 us -> 9.52 us  [body(): from_left = {h: lax.ppermute(from_left[h], 'grid', to_right) for h in low}]
    ppermute x7, waiting for transfers between devices: 7.7 us -> 18.2 us  [body(): from_right = {h: lax.ppermute(from_right[h], 'grid', to_left) for h in high}]
    ppermute x7, starting transfers between devices: 11.2 us -> 19.1 us  [body(): from_right = {h: lax.ppermute(from_right[h], 'grid', to_left) for h in high}]
    ppermute x7, starting transfers between devices: 12.8 us -> 9.25 us  [body(): from_left = {h: lax.ppermute(from_left[h], 'grid', to_right) for h in low}]
    all_to_all x1, starting transfers between devices: 5.55 us -> 7.28 us  [body(): lax.all_to_all(message, 'grid', split_axis=0, concat_axis=0, tiled=True)]
    concatenate x3, other arithmetic: 0.02 us -> 1.47 us  [body(): meta = jnp.concatenate([row_code, a_cols.reshape(groups, cap)], axis=1)]
    unnamed x36 -> x18, local copies, waits for them, and re-layouts: 3.46 us -> 3.23 us
  transfers between devices with their start and end apart: 18 -> 18, of which waited for: 9 -> 9; matrix products, arithmetic and copies ran while one was open for 4% -> 5% of each run, Pallas kernels for 22% -> 23%
where the time goes in v5:
time: 124 us
  waiting for transfers between devices  39.9 us (32%)
  starting transfers between devices  37.6 us (30%)
  Pallas kernels  33.7 us (27%)
  other arithmetic  7.88 us (6%)
  local copies, waits for them, and re-layouts  4.38 us (4%)
    pallas_call x3, Pallas kernels, mul(): pl.pallas_call(functools.partial(mul_kernel, n), out_shape=jax.ShapeDtype...  24.1 us
    ppermute x7, starting transfers between devices, body(): from_right = {h: lax.ppermute(from_right[h], 'grid', to_left) for h in high}  19.1 us
    ppermute x7, waiting for transfers between devices, body(): from_right = {h: lax.ppermute(from_right[h], 'grid', to_left) for h in high}  18.2 us
    all_to_all x1, waiting for transfers between devices, body(): lax.all_to_all(message, 'grid', split_axis=0, concat_axis=0, tiled=True)  12.1 us
    pallas_call x1, Pallas kernels, build_tiles(): pl.pallas_call(functools.partial(build_kernel, dims, bounds), out_shape=[...  9.58 us
    ppermute x7, waiting for transfers between devices, body(): from_left = {h: lax.ppermute(from_left[h], 'grid', to_right) for h in low}  9.52 us
    ppermute x7, starting transfers between devices, body(): from_left = {h: lax.ppermute(from_left[h], 'grid', to_right) for h in low}  9.25 us
    all_to_all x1, starting transfers between devices, body(): lax.all_to_all(message, 'grid', split_axis=0, concat_axis=0, tiled=True)  7.28 us
  transfers between devices with their start and end apart: 18, of which 9 were waited for; matrix products, arithmetic and copies ran while one was open for 5% of the time, Pallas kernels for 23%

profile of v5, /device:TPU:0, one launch (start us, length us, event | category | flops | bytes accessed | tf_op | source)
XLA Modules:
  0.0 123.5 jit_solution(11959954307451226777)
XLA Ops:
  0.0 0.8 convert_bitcast_fusion
  0.8 0.7 fusion.3
  1.5 0.1 copy.32
  1.6 1.9 %fusion.1 = bf16[8,272,128]{2,1,0:T(8,128)(2,1)} fusion(bf16[8,1,4]{2,1,0:T(2,128)(2,1)S(1)} %copy.32, bf16[8,256,128]{2,1,0:T(8,128)(2,1)} %bitcast.16), kind=kLoop, calls=%fused_computation.2 | loop fusion | flops 1671168 | bytes 1081408 | tf_op jit(solution)/shard_map/concatenate | solution.py:161
  3.5 7.3 %all-to-all-start = ((bf16[8,272,128]{2,1,0:T(8,128)(2,1)}), bf16[8,272,128]{2,1,0:T(8,128)(2,1)S(1)}, u32[]{:S(2)}, u32[]{:S(2)}) async-start(bf16[8,272,128]{2,1,0:T(8,128)(2,1)} %fusion.1), calls=%async_computation | async-start | bytes 1114112 | tf_op jit(solution)/shard_map/all_to_all | solution.py:163
  10.7 1.1 fusion.4
  11.8 2.0 %collective-permute-start.3 = (bf16[256,1024]{1,0:T(8,128)(2,1)}, bf16[256,1024]{1,0:T(8,128)(2,1)S(1)}, u32[]{:S(2)}, u32[]{:S(2)}) collective-permute-start(bf16[256,1024]{1,0:T(8,128)(2,1)} %get-tuple-element.24.refs_0_), channel_id=1, source_target_pairs={{0,8},{8,16},{16,24},{24,28},{28,20},{20,12},{12,4},{4,0},{1,9},{9... | collective-permute-start | bytes 1572872 | tf_op jit(solution)/shard_map/ppermute | solution.py:179
  13.8 12.1 %all-to-all-done.refs_4_ = bf16[8,272,128]{2,1,0:T(8,128)(2,1)S(1)} async-done(((bf16[8,272,128]{2,1,0:T(8,128)(2,1)}), bf16[8,272,128]{2,1,0:T(8,128)(2,1)S(1)}, u32[]{:S(2)}, u32[]{:S(2)}) %all-to-all-start) | async-done | bytes 557088 | tf_op jit(solution)/shard_map/all_to_all | solution.py:163
  25.9 1.5 %collective-permute-start = (bf16[8,272,128]{2,1,0:T(8,128)(2,1)S(1)}, bf16[8,272,128]{2,1,0:T(8,128)(2,1)}, u32[]{:S(2)}, u32[]{:S(2)}) collective-permute-start(bf16[8,272,128]{2,1,0:T(8,128)(2,1)S(1)} %all-to-all-done.refs_4_), channel_id=1, source_target_pairs={{0,2},{1,3},{2,0},{3,1},{4,6},{5,7},{6,4},{7,5},{8,10},{9,11},{10,... | collective-permute-start | bytes 1671176 | tf_op jit(solution)/shard_map/ppermute | solution.py:136
  27.4 1.0 collective-permute-start.10
  28.4 1.5 %collective-permute-start.5 = (bf16[256,1024]{1,0:T(8,128)(2,1)}, bf16[256,1024]{1,0:T(8,128)(2,1)S(1)}, u32[]{:S(2)}, u32[]{:S(2)}) collective-permute-start(bf16[256,1024]{1,0:T(8,128)(2,1)} %get-tuple-element.24.refs_0_), channel_id=1, source_target_pairs={{8,0},{16,8},{24,16},{28,24},{20,28},{12,20},{4,12},{0,4},{9,1},{1... | collective-permute-start | bytes 1572872 | tf_op jit(solution)/shard_map/ppermute | solution.py:180
  29.9 2.0 %collective-permute-start.12 = (bf16[256,1024]{1,0:T(8,128)(2,1)}, bf16[256,1024]{1,0:T(8,128)(2,1)}, u32[]{:S(2)}, u32[]{:S(2)}) collective-permute-start(bf16[256,1024]{1,0:T(8,128)(2,1)} %get-tuple-element.23.refs_1_), channel_id=1, source_target_pairs={{8,0},{16,8},{24,16},{28,24},{20,28},{12,20},{4,12},{0,4},{9,1},{1... | collective-permute-start | bytes 1572872 | tf_op jit(solution)/shard_map/ppermute | solution.py:180
  32.0 0.4 collective-permute-done.3.refs_2_
  32.3 4.1 %collective-permute-start.4 = (bf16[256,1024]{1,0:T(8,128)(2,1)S(1)}, bf16[256,1024]{1,0:T(8,128)(2,1)}, u32[]{:S(2)}, u32[]{:S(2)}) collective-permute-start(bf16[256,1024]{1,0:T(8,128)(2,1)S(1)} %collective-permute-done.3.refs_2_), channel_id=1, source_target_pairs={{0,8},{8,16},{16,24},{24,28},{28,20},{20,12},{12,4},{4,0},{1,9},{9... | collective-permute-start | bytes 1572872 | tf_op jit(solution)/shard_map/ppermute | solution.py:179
  36.4 7.2 %collective-permute-done.10.refs_3_ = bf16[256,1024]{1,0:T(8,128)(2,1)} collective-permute-done((bf16[256,1024]{1,0:T(8,128)(2,1)}, bf16[256,1024]{1,0:T(8,128)(2,1)}, u32[]{:S(2)}, u32[]{:S(2)}) %collective-permute-start.10) | collective-permute-done | bytes 524320 | tf_op jit(solution)/shard_map/ppermute | solution.py:179
  43.6 0.0 collective-permute-start.1
  43.6 0.0 collective-permute-done.refs_5_.refs_2_
  43.6 0.5 collective-permute-start.2
  44.1 0.0 collective-permute-done.5.refs_4_
  44.1 3.6 %collective-permute-start.6 = (bf16[256,1024]{1,0:T(8,128)(2,1)S(1)}, bf16[256,1024]{1,0:T(8,128)(2,1)}, u32[]{:S(2)}, u32[]{:S(2)}) collective-permute-start(bf16[256,1024]{1,0:T(8,128)(2,1)S(1)} %collective-permute-done.5.refs_4_), channel_id=1, source_target_pairs={{8,0},{16,8},{24,16},{28,24},{20,28},{12,20},{4,12},{0,4},{9,1},{1... | collective-permute-start | bytes 1572872 | tf_op jit(solution)/shard_map/ppermute | solution.py:180
  47.7 5.4 %collective-permute-done.12.refs_5_ = bf16[256,1024]{1,0:T(8,128)(2,1)} collective-permute-done((bf16[256,1024]{1,0:T(8,128)(2,1)}, bf16[256,1024]{1,0:T(8,128)(2,1)}, u32[]{:S(2)}, u32[]{:S(2)}) %collective-permute-start.12) | collective-permute-done | bytes 524320 | tf_op jit(solution)/shard_map/ppermute | solution.py:180
  53.1 0.8 collective-permute-start.11
  53.8 0.9 collective-permute-done.4.refs_0_
  54.7 3.7 %collective-permute-start.13 = (bf16[256,1024]{1,0:T(8,128)(2,1)}, bf16[256,1024]{1,0:T(8,128)(2,1)}, u32[]{:S(2)}, u32[]{:S(2)}) collective-permute-start(bf16[256,1024]{1,0:T(8,128)(2,1)} %collective-permute-done.12.refs_5_), channel_id=1, source_target_pairs={{8,0},{16,8},{24,16},{28,24},{20,28},{12,20},{4,12},{0,4},{9,1},{1... | collective-permute-start | bytes 1572872 | tf_op jit(solution)/shard_map/ppermute | solution.py:180
  58.4 0.6 slice_convert_fusion.3
  59.0 5.3 %collective-permute-done.6.refs_1_ = bf16[256,1024]{1,0:T(8,128)(2,1)} collective-permute-done((bf16[256,1024]{1,0:T(8,128)(2,1)S(1)}, bf16[256,1024]{1,0:T(8,128)(2,1)}, u32[]{:S(2)}, u32[]{:S(2)}) %collective-permute-start.6) | collective-permute-done | bytes 524320 | tf_op jit(solution)/shard_map/ppermute | solution.py:180
  64.3 0.8 collective-permute-start.7
  65.1 1.1 collective-permute-done.11.refs_0_
  66.2 4.3 %collective-permute-start.8 = (bf16[256,1024]{1,0:T(8,128)(2,1)}, bf16[256,1024]{1,0:T(8,128)(2,1)}, u32[]{:S(2)}, u32[]{:S(2)}) collective-permute-start(bf16[256,1024]{1,0:T(8,128)(2,1)} %get-tuple-element.16.refs_8_), channel_id=1, source_target_pairs={{8,0},{16,8},{24,16},{28,24},{20,28},{12,20},{4,12},{0,4},{9,1},{1... | collective-permute-start | bytes 1572872 | tf_op jit(solution)/shard_map/ppermute | solution.py:180
  70.5 5.1 %collective-permute-done.13.refs_1_ = bf16[256,1024]{1,0:T(8,128)(2,1)} collective-permute-done((bf16[256,1024]{1,0:T(8,128)(2,1)}, bf16[256,1024]{1,0:T(8,128)(2,1)}, u32[]{:S(2)}, u32[]{:S(2)}) %collective-permute-start.13) | collective-permute-done | bytes 524320 | tf_op jit(solution)/shard_map/ppermute | solution.py:180
  75.5 0.0 collective-permute-done.1.refs_6_.refs_2_
  75.5 0.0 collective-permute-done.2.refs_7_.refs_3_
  75.6 0.8 copy-done.1
  76.4 0.8 copy-done.2
  77.2 2.2 %collective-permute-start.14 = (bf16[256,1024]{1,0:T(8,128)(2,1)}, bf16[256,1024]{1,0:T(8,128)(2,1)S(1)}, u32[]{:S(2)}, u32[]{:S(2)}) collective-permute-start(bf16[256,1024]{1,0:T(8,128)(2,1)} %get-tuple-element.20.refs_9_), channel_id=1, source_target_pairs={{8,0},{16,8},{24,16},{28,24},{20,28},{12,20},{4,12},{0,4},{9,1},{1... | collective-permute-start | bytes 1572872 | tf_op jit(solution)/shard_map/ppermute | solution.py:180
  79.4 1.3 %slice_convert_fusion.2 = s32[8,1,4]{2,1,0:T(1,128)} fusion(bf16[8,272,128]{2,1,0:T(8,128)(2,1)} %collective-permute-done.refs_5_.refs_2_), kind=kLoop, calls=%fused_computation.5 | loop fusion | flops 32 | bytes 192 | tf_op jit(solution)/shard_map/convert_element_type | solution.py:165
  80.7 1.3 %slice_convert_fusion.1 = s32[8,1,4]{2,1,0:T(1,128)} fusion(bf16[8,272,128]{2,1,0:T(8,128)(2,1)} %copy-done.1), kind=kLoop, calls=%fused_computation.4 | loop fusion | flops 32 | bytes 192 | tf_op jit(solution)/shard_map/convert_element_type | solution.py:165
  82.0 0.0 collective-permute-start.16
  82.0 1.3 %slice_convert_fusion = s32[8,1,4]{2,1,0:T(1,128)} fusion(bf16[8,272,128]{2,1,0:T(8,128)(2,1)} %copy-done.2), kind=kLoop, calls=%fused_computation.3 | loop fusion | flops 32 | bytes 192 | tf_op jit(solution)/shard_map/convert_element_type | solution.py:165
  83.3 9.6 %shard_map.64 = (bf16[1024,2560]{1,0:T(8,128)(2,1)}, bf16[1024,1024]{1,0:T(8,128)(2,1)}, bf16[1024,512]{1,0:T(8,128)(2,1)}) custom-call(s32[1]{0:T(128)} %bitcast.pos_ref, s32[8]{0:T(128)} %bitcast.22, s32[8,4]{1,0:T(8,128)} %bitcast.17, s32[8,4]{1,0:T(8,128)} %bitcast.18, s32[8,4]{1,0:T(8,128)} %bitcast.19, s32[8,4]{1,0:T(8,128)} %bitcast.20, ...), custom_call_target="tpu_custom_call" | custom-call | bytes 16777216 | tf_op jit(solution)/shard_map/pallas_call | solution.py:64
  92.9 0.6 collective-permute-start.9
  93.5 2.5 %collective-permute-done.14.refs_3_ = bf16[256,1024]{1,0:T(8,128)(2,1)S(1)} collective-permute-done((bf16[256,1024]{1,0:T(8,128)(2,1)}, bf16[256,1024]{1,0:T(8,128)(2,1)S(1)}, u32[]{:S(2)}, u32[]{:S(2)}) %collective-permute-start.14) | collective-permute-done | bytes 524320 | tf_op jit(solution)/shard_map/ppermute | solution.py:180
  96.0 1.7 %collective-permute-start.15 = (bf16[256,1024]{1,0:T(8,128)(2,1)S(1)}, bf16[256,1024]{1,0:T(8,128)(2,1)}, u32[]{:S(2)}, u32[]{:S(2)}) collective-permute-start(bf16[256,1024]{1,0:T(8,128)(2,1)S(1)} %collective-permute-done.14.refs_3_), channel_id=1, source_target_pairs={{8,0},{16,8},{24,16},{28,24},{20,28},{12,20},{4,12},{0,4},{9,1},{1... | collective-permute-start | bytes 1572872 | tf_op jit(solution)/shard_map/ppermute | solution.py:180
  97.8 10.7 %shard_map.68.refs_4_ = f32[1024,1024]{1,0:T(8,128)} custom-call(bf16[1024,2560]{1,0:T(8,128)(2,1)} %get-tuple-element.17.refs_2_.tile_ref, bf16[256,1024]{1,0:T(8,128)(2,1)} %get-tuple-element.24.refs_0_, bf16[256,1024]{1,0:T(8,128)(2,1)} %get-tuple-element.23.refs_1_, bf16[256,1024]{1,0:T(8,128)(2,1)} %copy-done.7, ...), custom_call_target="tpu_custom_call" | custom-call | flops 5368709120 | bytes 18874368 | tf_op jit(solution)/shard_map/pallas_call | solution.py:115
  108.5 0.8 copy-done.5
  109.3 7.8 %shard_map.69.refs_2_ = f32[1024,1024]{1,0:T(8,128)} custom-call(bf16[1024,1024]{1,0:T(8,128)(2,1)} %get-tuple-element.18.refs_3_.tile_ref, bf16[256,1024]{1,0:T(8,128)(2,1)} %get-tuple-element.19.refs_0_, bf16[256,1024]{1,0:T(8,128)(2,1)} %copy-done.5, bf16[256,1024]{1,0:T(8,128)(2,1)} %get-tuple-element.22.refs_2_, bf16[256,1024]{1,0:T(8,128)(2,1)} %copy-done.4, ...), custom_call_target="tpu_custom_call" | custom-call | flops 2147483648 | bytes 12582912 | tf_op jit(solution)/shard_map/pallas_call | solution.py:115
  117.1 0.8 copy-done.6
  117.9 5.7 %shard_map.70 = bf16[1024,1024]{1,0:T(8,128)(2,1)} custom-call(bf16[1024,512]{1,0:T(8,128)(2,1)} %get-tuple-element.14.refs_4_.tile_ref, bf16[256,1024]{1,0:T(8,128)(2,1)} %copy-done.6, bf16[256,1024]{1,0:T(8,128)(2,1)} %collective-permute-done.15.refs_1_, f32[1024,1024]{1,0:T(8,128)} %shard_map.69.refs_2_), custom_call_target="tpu_custom_call" | custom-call | flops 1073741824 | bytes 10485760 | tf_op jit(solution)/shard_map/pallas_call | solution.py:115
  (23 shorter events, 0.1 us)
Async XLA Ops:
  0.0 10.7 %copy-start.3 = (bf16[512,1024]{1,0:T(8,128)(2,1)S(1)}, bf16[512,1024]{1,0:T(8,128)(2,1)}, u32[]{:S(2)}) copy-start(bf16[512,1024]{1,0:T(8,128)(2,1)} %param.11) | copy-start | bytes 3145732
  3.5 22.5 %all-to-all-start = ((bf16[8,272,128]{2,1,0:T(8,128)(2,1)}), bf16[8,272,128]{2,1,0:T(8,128)(2,1)S(1)}, u32[]{:S(2)}, u32[]{:S(2)}) async-start(bf16[8,272,128]{2,1,0:T(8,128)(2,1)} %fusion.1), calls=%async_computation | async-start | bytes 1114112 | tf_op jit(solution)/shard_map/all_to_all | solution.py:163
  11.8 20.5 %collective-permute-start.3 = (bf16[256,1024]{1,0:T(8,128)(2,1)}, bf16[256,1024]{1,0:T(8,128)(2,1)S(1)}, u32[]{:S(2)}, u32[]{:S(2)}) collective-permute-start(bf16[256,1024]{1,0:T(8,128)(2,1)} %get-tuple-element.24.refs_0_), channel_id=1, source_target_pairs={{0,8},{8,16},{16,24},{24,28},{28,20},{20,12},{12,4},{4,0},{1,9},{9... | collective-permute-start | bytes 1572872 | tf_op jit(solution)/shard_map/ppermute | solution.py:179
  25.9 57.4 %copy-start = (bf16[8,272,128]{2,1,0:T(8,128)(2,1)}, bf16[8,272,128]{2,1,0:T(8,128)(2,1)S(1)}, u32[]{:S(2)}) copy-start(bf16[8,272,128]{2,1,0:T(8,128)(2,1)S(1)} %all-to-all-done.refs_4_) | copy-start | bytes 1671172
  25.9 17.6 %collective-permute-start = (bf16[8,272,128]{2,1,0:T(8,128)(2,1)S(1)}, bf16[8,272,128]{2,1,0:T(8,128)(2,1)}, u32[]{:S(2)}, u32[]{:S(2)}) collective-permute-start(bf16[8,272,128]{2,1,0:T(8,128)(2,1)S(1)} %all-to-all-done.refs_4_), channel_id=1, source_target_pairs={{0,2},{1,3},{2,0},{3,1},{4,6},{5,7},{6,4},{7,5},{8,10},{9,11},{10,... | collective-permute-start | bytes 1671176 | tf_op jit(solution)/shard_map/ppermute | solution.py:136
  27.4 16.1 %collective-permute-start.10 = (bf16[256,1024]{1,0:T(8,128)(2,1)}, bf16[256,1024]{1,0:T(8,128)(2,1)}, u32[]{:S(2)}, u32[]{:S(2)}) collective-permute-start(bf16[256,1024]{1,0:T(8,128)(2,1)} %get-tuple-element.23.refs_1_), channel_id=1, source_target_pairs={{0,8},{8,16},{16,24},{24,28},{28,20},{20,12},{12,4},{4,0},{1,9},{9... | collective-permute-start | bytes 1572872 | tf_op jit(solution)/shard_map/ppermute | solution.py:179
  28.4 15.6 %collective-permute-start.5 = (bf16[256,1024]{1,0:T(8,128)(2,1)}, bf16[256,1024]{1,0:T(8,128)(2,1)S(1)}, u32[]{:S(2)}, u32[]{:S(2)}) collective-permute-start(bf16[256,1024]{1,0:T(8,128)(2,1)} %get-tuple-element.24.refs_0_), channel_id=1, source_target_pairs={{8,0},{16,8},{24,16},{28,24},{20,28},{12,20},{4,12},{0,4},{9,1},{1... | collective-permute-start | bytes 1572872 | tf_op jit(solution)/shard_map/ppermute | solution.py:180
  29.9 23.1 %collective-permute-start.12 = (bf16[256,1024]{1,0:T(8,128)(2,1)}, bf16[256,1024]{1,0:T(8,128)(2,1)}, u32[]{:S(2)}, u32[]{:S(2)}) collective-permute-start(bf16[256,1024]{1,0:T(8,128)(2,1)} %get-tuple-element.23.refs_1_), channel_id=1, source_target_pairs={{8,0},{16,8},{24,16},{28,24},{20,28},{12,20},{4,12},{0,4},{9,1},{1... | collective-permute-start | bytes 1572872 | tf_op jit(solution)/shard_map/ppermute | solution.py:180
  32.3 11.2 %copy-start.7 = (bf16[256,1024]{1,0:T(8,128)(2,1)}, bf16[256,1024]{1,0:T(8,128)(2,1)S(1)}, u32[]{:S(2)}) copy-start(bf16[256,1024]{1,0:T(8,128)(2,1)S(1)} %collective-permute-done.3.refs_2_) | copy-start | bytes 1572868
  32.3 22.4 %collective-permute-start.4 = (bf16[256,1024]{1,0:T(8,128)(2,1)S(1)}, bf16[256,1024]{1,0:T(8,128)(2,1)}, u32[]{:S(2)}, u32[]{:S(2)}) collective-permute-start(bf16[256,1024]{1,0:T(8,128)(2,1)S(1)} %collective-permute-done.3.refs_2_), channel_id=1, source_target_pairs={{0,8},{8,16},{16,24},{24,28},{28,20},{20,12},{12,4},{4,0},{1,9},{9... | collective-permute-start | bytes 1572872 | tf_op jit(solution)/shard_map/ppermute | solution.py:179
  43.6 32.0 %collective-permute-start.1 = (bf16[8,272,128]{2,1,0:T(8,128)(2,1)S(1)}, bf16[8,272,128]{2,1,0:T(8,128)(2,1)S(1)}, u32[]{:S(2)}, u32[]{:S(2)}) collective-permute-start(bf16[8,272,128]{2,1,0:T(8,128)(2,1)S(1)} %all-to-all-done.refs_4_), channel_id=1, source_target_pairs={{0,1},{1,0},{2,3},{3,2},{4,5},{5,4},{6,7},{7,6},{8,9},{9,8},{10,11... | collective-permute-start | bytes 1671176 | tf_op jit(solution)/shard_map/ppermute | solution.py:137
  43.6 32.0 %collective-permute-start.2 = (bf16[8,272,128]{2,1,0:T(8,128)(2,1)}, bf16[8,272,128]{2,1,0:T(8,128)(2,1)S(1)}, u32[]{:S(2)}, u32[]{:S(2)}) collective-permute-start(bf16[8,272,128]{2,1,0:T(8,128)(2,1)} %collective-permute-done.refs_5_.refs_2_), channel_id=1, source_target_pairs={{0,1},{1,0},{2,3},{3,2},{4,5},{5,4},{6,7},{7,6},{8,9},{9,8},{10,11... | collective-permute-start | bytes 1671176 | tf_op jit(solution)/shard_map/ppermute | solution.py:138
  44.1 10.6 %copy-start.8 = (bf16[256,1024]{1,0:T(8,128)(2,1)}, bf16[256,1024]{1,0:T(8,128)(2,1)S(1)}, u32[]{:S(2)}) copy-start(bf16[256,1024]{1,0:T(8,128)(2,1)S(1)} %collective-permute-done.5.refs_4_) | copy-start | bytes 1572868
  44.1 20.2 %collective-permute-start.6 = (bf16[256,1024]{1,0:T(8,128)(2,1)S(1)}, bf16[256,1024]{1,0:T(8,128)(2,1)}, u32[]{:S(2)}, u32[]{:S(2)}) collective-permute-start(bf16[256,1024]{1,0:T(8,128)(2,1)S(1)} %collective-permute-done.5.refs_4_), channel_id=1, source_target_pairs={{8,0},{16,8},{24,16},{28,24},{20,28},{12,20},{4,12},{0,4},{9,1},{1... | collective-permute-start | bytes 1572872 | tf_op jit(solution)/shard_map/ppermute | solution.py:180
  53.1 13.1 %collective-permute-start.11 = (bf16[256,1024]{1,0:T(8,128)(2,1)}, bf16[256,1024]{1,0:T(8,128)(2,1)}, u32[]{:S(2)}, u32[]{:S(2)}) collective-permute-start(bf16[256,1024]{1,0:T(8,128)(2,1)} %collective-permute-done.10.refs_3_), channel_id=1, source_target_pairs={{0,8},{8,16},{16,24},{24,28},{28,20},{20,12},{12,4},{4,0},{1,9},{9... | collective-permute-start | bytes 1572872 | tf_op jit(solution)/shard_map/ppermute | solution.py:179
  54.7 20.8 %collective-permute-start.13 = (bf16[256,1024]{1,0:T(8,128)(2,1)}, bf16[256,1024]{1,0:T(8,128)(2,1)}, u32[]{:S(2)}, u32[]{:S(2)}) collective-permute-start(bf16[256,1024]{1,0:T(8,128)(2,1)} %collective-permute-done.12.refs_5_), channel_id=1, source_target_pairs={{8,0},{16,8},{24,16},{28,24},{20,28},{12,20},{4,12},{0,4},{9,1},{1... | collective-permute-start | bytes 1572872 | tf_op jit(solution)/shard_map/ppermute | solution.py:180
  64.3 28.6 %collective-permute-start.7 = (bf16[256,1024]{1,0:T(8,128)(2,1)}, bf16[256,1024]{1,0:T(8,128)(2,1)}, u32[]{:S(2)}, u32[]{:S(2)}) collective-permute-start(bf16[256,1024]{1,0:T(8,128)(2,1)} %get-tuple-element.15.refs_6_), channel_id=1, source_target_pairs={{0,8},{8,16},{16,24},{24,28},{28,20},{20,12},{12,4},{4,0},{1,9},{9... | collective-permute-start | bytes 1572872 | tf_op jit(solution)/shard_map/ppermute | solution.py:179
  66.2 26.7 %collective-permute-start.8 = (bf16[256,1024]{1,0:T(8,128)(2,1)}, bf16[256,1024]{1,0:T(8,128)(2,1)}, u32[]{:S(2)}, u32[]{:S(2)}) collective-permute-start(bf16[256,1024]{1,0:T(8,128)(2,1)} %get-tuple-element.16.refs_8_), channel_id=1, source_target_pairs={{8,0},{16,8},{24,16},{28,24},{20,28},{12,20},{4,12},{0,4},{9,1},{1... | collective-permute-start | bytes 1572872 | tf_op jit(solution)/shard_map/ppermute | solution.py:180
  75.5 0.8 copy-start.1
  76.4 0.8 copy-start.2
  77.2 18.8 %collective-permute-start.14 = (bf16[256,1024]{1,0:T(8,128)(2,1)}, bf16[256,1024]{1,0:T(8,128)(2,1)S(1)}, u32[]{:S(2)}, u32[]{:S(2)}) collective-permute-start(bf16[256,1024]{1,0:T(8,128)(2,1)} %get-tuple-element.20.refs_9_), channel_id=1, source_target_pairs={{8,0},{16,8},{24,16},{28,24},{20,28},{12,20},{4,12},{0,4},{9,1},{1... | collective-permute-start | bytes 1572872 | tf_op jit(solution)/shard_map/ppermute | solution.py:180
  82.0 26.5 %collective-permute-start.16 = (bf16[256,1024]{1,0:T(8,128)(2,1)}, bf16[256,1024]{1,0:T(8,128)(2,1)S(1)}, u32[]{:S(2)}, u32[]{:S(2)}) collective-permute-start(bf16[256,1024]{1,0:T(8,128)(2,1)} %get-tuple-element.21.refs_7_), channel_id=1, source_target_pairs={{0,8},{8,16},{16,24},{24,28},{28,20},{20,12},{12,4},{4,0},{1,9},{9... | collective-permute-start | bytes 1572872 | tf_op jit(solution)/shard_map/ppermute | solution.py:179
  92.9 24.1 %collective-permute-start.9 = (bf16[256,1024]{1,0:T(8,128)(2,1)}, bf16[256,1024]{1,0:T(8,128)(2,1)S(1)}, u32[]{:S(2)}, u32[]{:S(2)}) collective-permute-start(bf16[256,1024]{1,0:T(8,128)(2,1)} %get-tuple-element.19.refs_0_), channel_id=1, source_target_pairs={{0,8},{8,16},{16,24},{24,28},{28,20},{20,12},{12,4},{4,0},{1,9},{9... | collective-permute-start | bytes 1572872 | tf_op jit(solution)/shard_map/ppermute | solution.py:179
  96.0 12.5 %copy-start.4 = (bf16[256,1024]{1,0:T(8,128)(2,1)}, bf16[256,1024]{1,0:T(8,128)(2,1)S(1)}, u32[]{:S(2)}) copy-start(bf16[256,1024]{1,0:T(8,128)(2,1)S(1)} %collective-permute-done.14.refs_3_) | copy-start | bytes 1572868
  96.0 21.1 %collective-permute-start.15 = (bf16[256,1024]{1,0:T(8,128)(2,1)S(1)}, bf16[256,1024]{1,0:T(8,128)(2,1)}, u32[]{:S(2)}, u32[]{:S(2)}) collective-permute-start(bf16[256,1024]{1,0:T(8,128)(2,1)S(1)} %collective-permute-done.14.refs_3_), channel_id=1, source_target_pairs={{8,0},{16,8},{24,16},{28,24},{20,28},{12,20},{4,12},{0,4},{9,1},{1... | collective-permute-start | bytes 1572872 | tf_op jit(solution)/shard_map/ppermute | solution.py:180
  108.5 0.8 copy-start.5
  117.1 0.8 copy-start.6

commit v6 on v0

v6 whole, which is shorter than its diff:
```python
import functools

import jax
import jax.numpy as jnp
from jax import lax
from jax.experimental import pallas as pl
from jax.experimental.pallas import tpu as pltpu
from jax.sharding import PartitionSpec as P

META = 16
VMEM_BYTES = 62 << 20


def ring_order(n):
    return list(range(0, n, 2)) + list(range(n - 1, 0, -2))


def ring_place(g, n):
    return jnp.where(g % 2 == 0, g // 2, n - 1 - g // 2)


def first_kernel(dims, dest_ref, *refs):
    n_parts, n_right, per_part, cap, bs, blocks = dims
    parts = refs[:n_parts]
    rights = refs[n_parts : n_parts + n_right]
    acc_hbm, late_hbm, left, right, acc, right_sem, acc_sem, late_sem = refs[n_parts + n_right :]
    depth = blocks * bs
    inner = n_right * depth
    bn = acc.shape[-1]
    fetches = [
        pltpu.make_async_copy(source, right.at[pl.ds(i * depth, depth)], right_sem.at[i])
        for i, source in enumerate(rights)
    ]
    for fetch in fetches:
        fetch.start()
    left[...] = jnp.zeros_like(left)
    k_blocks = left.shape[1] // bs
    for q, part in enumerate(parts):

        def place(i, carry):
            for c in range(cap):
                dest = dest_ref[q, i, c]

                @pl.when(dest >= 0)
                def _():
                    row, col = dest // k_blocks, dest % k_blocks
                    left[
                        pl.ds(pl.multiple_of(row * bs, bs), bs),
                        pl.ds(pl.multiple_of(col * bs, bs), bs),
                    ] = part[i, pl.ds(c * bs, bs), :]

            return carry

        lax.fori_loop(0, per_part, place, 0)
    late = pltpu.make_async_copy(left.at[:, pl.ds(inner, depth)], late_hbm, late_sem)
    late.start()
    for fetch in fetches:
        fetch.wait()
    stores = []
    for j in range(acc.shape[0]):
        acc[j] = jnp.dot(
            left[:, :inner],
            right[:, j * bn : (j + 1) * bn],
            preferred_element_type=jnp.float32,
        )
        store = pltpu.make_async_copy(acc.at[j], acc_hbm.at[j], acc_sem.at[j])
        store.start()
        stores.append(store)
    late.wait()
    for store in stores:
        store.wait()


def first_product(dest, parts, rights, rows, bs, cap, bn):
    n_parts, n_right = len(parts), len(rights)
    depth, cols = rights[0].shape
    inner = n_right * depth
    anywhere = pl.BlockSpec(memory_space=pl.ANY)
    dims = (n_parts, n_right, parts[0].shape[0], cap, bs, depth // bs)
    return pl.pallas_call(
        functools.partial(first_kernel, dims),
        out_shape=[
            jax.ShapeDtypeStruct((cols // bn, rows, bn), jnp.float32),
            jax.ShapeDtypeStruct((rows, depth), jnp.bfloat16),
        ],
        in_specs=[pl.BlockSpec(memory_space=pltpu.SMEM)]
        + [pl.BlockSpec(memory_space=pltpu.VMEM)] * n_parts
        + [anywhere] * n_right,
        out_specs=[anywhere] * 2,
        scratch_shapes=[
            pltpu.VMEM((rows, inner + depth), jnp.bfloat16),
            pltpu.VMEM((inner, cols), jnp.bfloat16),
            pltpu.VMEM((cols // bn, rows, bn), jnp.float32),
            pltpu.SemaphoreType.DMA((n_right,)),
            pltpu.SemaphoreType.DMA((cols // bn,)),
            pltpu.SemaphoreType.DMA,
        ],
        compiler_params=pltpu.CompilerParams(vmem_limit_bytes=VMEM_BYTES),
        cost_estimate=pl.CostEstimate(
            flops=2 * rows * inner * cols,
            bytes_accessed=inner * cols * 2 + rows * cols * 4,
            transcendentals=0,
        ),
    )(dest, *parts, *rights)


def last_kernel(left_ref, low_ref, high_ref, acc_ref, out_ref):
    right = jnp.concatenate([low_ref[...], high_ref[...]], axis=0)
    total = jnp.dot(left_ref[...], right, preferred_element_type=jnp.float32)
    out_ref[...] = (acc_ref[0] + total).astype(out_ref.dtype)


def last_product(left, low, high, acc):
    rows, inner = left.shape
    steps, _, bn = acc.shape
    return pl.pallas_call(
        last_kernel,
        out_shape=jax.ShapeDtypeStruct((rows, steps * bn), jnp.bfloat16),
        grid=(steps,),
        in_specs=[
            pl.BlockSpec((rows, inner), lambda j: (0, 0)),
            pl.BlockSpec((low.shape[0], bn), lambda j: (0, j)),
            pl.BlockSpec((high.shape[0], bn), lambda j: (0, j)),
            pl.BlockSpec((1, rows, bn), lambda j: (j, 0, 0)),
        ],
        out_specs=pl.BlockSpec((rows, bn), lambda j: (0, j)),
        compiler_params=pltpu.CompilerParams(vmem_limit_bytes=VMEM_BYTES),
        cost_estimate=pl.CostEstimate(
            flops=2 * rows * inner * steps * bn,
            bytes_accessed=(rows + steps * bn) * inner * 2 + rows * steps * bn * 6,
            transcendentals=0,
        ),
    )(left, low, high, acc)


def across_row(landed, columns):
    if columns != 4:
        gathered = lax.all_gather(landed, "blk", axis=0)
        return [gathered[j] for j in range(columns)]
    swap_core = [(j, j ^ 1) for j in range(columns)]
    swap_chip = [(j, j ^ 2) for j in range(columns)]
    across = lax.ppermute(landed, "blk", swap_chip)
    near = lax.ppermute(landed, "blk", swap_core)
    return [landed, across, near, lax.ppermute(across, "blk", swap_core)]


def body(a_slots, a_rows, a_cols, a_count, owned_rows, b_matrix):
    groups = lax.axis_size("grid")
    columns = lax.axis_size("blk")
    bs = a_slots.shape[-1]
    cap = a_slots.shape[3]
    rb = owned_rows.shape[-1]
    k_local, n_local = b_matrix.shape
    blocks = k_local // bs
    half = groups // 2

    order = ring_order(groups)
    to_right = [(order[i], order[(i + 1) % groups]) for i in range(groups)]
    to_left = [(order[(i + 1) % groups], order[i]) for i in range(groups)]
    from_left, from_right, rights = b_matrix, b_matrix, [b_matrix]
    for s in range(1, half):
        from_left = lax.ppermute(from_left, "grid", to_right)
        from_right = lax.ppermute(from_right, "grid", to_left)
        rights += [from_left, from_right]
    low = lax.ppermute(from_left[: k_local // 2], "grid", to_right)
    high = lax.ppermute(from_right[k_local // 2 :], "grid", to_left)

    live = jnp.arange(cap, dtype=jnp.int32)[None, :] < a_count.reshape(groups, 1)
    row_code = jnp.where(live, a_rows.reshape(groups, cap) + 1, 0)
    meta = jnp.concatenate([row_code, a_cols.reshape(groups, cap)], axis=1)
    meta = jnp.pad(meta.astype(jnp.bfloat16)[:, None, :], ((0, 0), (0, META - 1), (0, bs - 2 * cap)))
    message = jnp.concatenate([a_slots.reshape(groups, cap * bs, bs), meta], axis=1)
    landed = lax.all_to_all(message, "grid", split_axis=0, concat_axis=0, tiled=True)
    parts = across_row(landed, columns)

    metas = jnp.stack([p[:, cap * bs, : 2 * cap] for p in parts]).astype(jnp.int32)
    code, col = metas[..., :cap], metas[..., cap:]
    hit = code[..., None] == owned_rows.reshape(rb) + 1
    row = jnp.sum(jnp.where(hit, jnp.arange(rb, dtype=jnp.int32), 0), axis=-1)
    pos = ring_place(lax.axis_index("grid"), groups)
    ahead = (ring_place(col // blocks, groups) - pos + groups) % groups
    hops = jnp.minimum(ahead, groups - ahead)
    first = jnp.where(hops == 0, 0, 2 * hops - 1) + jnp.where((ahead > 0) & (ahead < half), 1, 0)
    dest = row * (blocks * groups) + first * blocks + col % blocks
    dest = jnp.where(jnp.any(hit, axis=-1), dest, -1)

    acc, late = first_product(dest, parts, rights, rb * bs, bs, cap, n_local // 4)
    return last_product(late, low, high, acc)


def solution(mesh):
    in_specs = (
        P("grid", "blk", None, None, None, None),
        P("grid", "blk", None, None),
        P("grid", "blk", None, None),
        P("grid", "blk", None),
        P("grid", None),
        P("grid", "blk"),
    )
    out_specs = P("grid", "blk")
    return jax.shard_map(body, mesh=mesh, in_specs=in_specs, out_specs=out_specs, check_vma=False)
```

time: 200 us -> 112 us (0.56)
  blocking collectives: 37.2 us -> 0 us
  matrix products: 22.4 us -> 0 us
  local copies, waits for them, and re-layouts: 27.8 us -> 5.99 us
  waiting for transfers between devices: 82.5 us -> 62.1 us
  Pallas kernels: 0 us -> 19.9 us
  between operations: 14.1 us -> 0.09 us
  starting transfers between devices: 13 us -> 19.2 us
  other arithmetic: 2.41 us -> 4.66 us
    all_gather x2 -> x0, waiting for transfers between devices: 79.1 us -> none  [the longest x1 79.1 us: body(): lax.all_gather(b_matrix, 'grid', axis=0, tiled=True)]
    ppermute x0 -> x11, waiting for transfers between devices: none -> 51.2 us  [the longest x3 42.1 us: body(): from_right = lax.ppermute(from_right, 'grid', to_left)]
    dot_general x2 -> x0, matrix products: 22.4 us -> none  [the longest x1 15.2 us: body(): jnp.dot(tile, lax.all_gather(b_matrix, 'grid', axis=0, tiled=True), prefe...]
    all_to_all x1 -> x0, blocking collectives: 21.9 us -> none  [body(): lax.all_to_all(a_slots.reshape(groups, CAP, block_size, block_size), 'gri...]
    pallas_call x0 -> x2, Pallas kernels: none -> 19.9 us  [the longest x1 14.3 us: first_product(): pl.pallas_call(functools.partial(first_kernel, dims), out_shape=[jax.Shap...]
    ppermute x0 -> x11, starting transfers between devices: none -> 12.9 us  [the longest x3 9.3 us: body(): from_left = lax.ppermute(from_left, 'grid', to_right)]
    reshape x1 -> x0, local copies, waits for them, and re-layouts: 12 us -> none  [body(): spread.astype(jnp.bfloat16).reshape(RB, k_blocks, block_size, block_size)]
    all_gather x2 -> x0, blocking collectives: 10.4 us -> none  [the longest x1 5.19 us: body(): lax.all_gather(landed[2][None], 'blk', axis=0, tiled=True)]
  transfers between devices with their start and end apart: 5 -> 12, of which waited for: 3 -> 5; matrix products, arithmetic and copies ran while one was open for 19% -> 8% of each run, Pallas kernels for 0% -> 13%
where the time goes in v6:
time: 112 us
  waiting for transfers between devices  62.1 us (55%)
  Pallas kernels  19.9 us (18%)
  starting transfers between devices  19.2 us (17%)
  local copies, waits for them, and re-layouts  5.99 us (5%)
  other arithmetic  4.66 us (4%)
    ppermute x3, waiting for transfers between devices, body(): from_right = lax.ppermute(from_right, 'grid', to_left)  42.1 us
    pallas_call x1, Pallas kernels, first_product(): pl.pallas_call(functools.partial(first_kernel, dims), out_shape=[jax.Shap...  14.3 us
    all_to_all x1, waiting for transfers between devices, body(): lax.all_to_all(message, 'grid', split_axis=0, concat_axis=0, tiled=True)  10.9 us
    ppermute x3, starting transfers between devices, body(): from_left = lax.ppermute(from_left, 'grid', to_right)  9.3 us
    ppermute x1, waiting for transfers between devices, across_row(): across = lax.ppermute(landed, 'blk', swap_chip)  9.03 us
    all_to_all x1, starting transfers between devices, body(): lax.all_to_all(message, 'grid', split_axis=0, concat_axis=0, tiled=True)  6.28 us
    pallas_call x1, Pallas kernels, last_product(): pl.pallas_call(last_kernel, out_shape=jax.ShapeDtypeStruct((rows, steps *...  5.64 us
  transfers between devices with their start and end apart: 12, of which 5 were waited for; matrix products, arithmetic and copies ran while one was open for 8% of the time, Pallas kernels for 13%

profile of v6, /device:TPU:0, one launch (start us, length us, event | category | flops | bytes accessed | tf_op | source)
XLA Modules:
  0.0 111.9 jit_solution(7152890967775671448)
XLA Ops:
  0.0 3.0 %collective-permute-start.3 = (bf16[512,1024]{1,0:T(8,128)(2,1)}, bf16[512,1024]{1,0:T(8,128)(2,1)}, u32[]{:S(2)}, u32[]{:S(2)}) collective-permute-start(bf16[512,1024]{1,0:T(8,128)(2,1)} %refs_4_.1), channel_id=1, source_target_pairs={{0,8},{8,16},{16,24},{24,28},{28,20},{20,12},{12,4},{4,0},{1,9},{9... | collective-permute-start | bytes 3145736 | tf_op jit(solution)/shard_map/ppermute | solution.py:162
  3.0 0.0 collective-permute-start.4
  3.0 0.7 convert_bitcast_fusion
  3.7 0.7 fusion.13
  4.4 0.1 copy.26
  4.5 1.9 %fusion.1 = bf16[8,272,128]{2,1,0:T(8,128)(2,1)} fusion(bf16[8,1,4]{2,1,0:T(2,128)(2,1)S(1)} %copy.26, bf16[8,256,128]{2,1,0:T(8,128)(2,1)} %bitcast.17), kind=kLoop, calls=%fused_computation.2 | loop fusion | flops 1671168 | bytes 1081408 | tf_op jit(solution)/shard_map/concatenate | solution.py:172
  6.4 6.3 %all-to-all-start = ((bf16[8,272,128]{2,1,0:T(8,128)(2,1)}), bf16[8,272,128]{2,1,0:T(8,128)(2,1)S(1)}, u32[]{:S(2)}, u32[]{:S(2)}) async-start(bf16[8,272,128]{2,1,0:T(8,128)(2,1)} %fusion.1), calls=%async_computation | async-start | bytes 1114112 | tf_op jit(solution)/shard_map/all_to_all | solution.py:173
  12.7 16.6 %collective-permute-done.4.refs_6_ = bf16[512,1024]{1,0:T(8,128)(2,1)S(1)} collective-permute-done((bf16[512,1024]{1,0:T(8,128)(2,1)}, bf16[512,1024]{1,0:T(8,128)(2,1)S(1)}, u32[]{:S(2)}, u32[]{:S(2)}) %collective-permute-start.4) | collective-permute-done | bytes 1048608 | tf_op jit(solution)/shard_map/ppermute | solution.py:163
  29.3 0.3 collective-permute-start.6
  29.7 0.0 collective-permute-done.3.refs_5_
  29.7 1.7 %collective-permute-start.5 = (bf16[512,1024]{1,0:T(8,128)(2,1)}, bf16[512,1024]{1,0:T(8,128)(2,1)}, u32[]{:S(2)}, u32[]{:S(2)}) collective-permute-start(bf16[512,1024]{1,0:T(8,128)(2,1)} %collective-permute-done.3.refs_5_), channel_id=1, source_target_pairs={{0,8},{8,16},{16,24},{24,28},{28,20},{20,12},{12,4},{4,0},{1,9},{9... | collective-permute-start | bytes 3145736 | tf_op jit(solution)/shard_map/ppermute | solution.py:162
  31.4 10.9 %all-to-all-done.refs_0_ = bf16[8,272,128]{2,1,0:T(8,128)(2,1)S(1)} async-done(((bf16[8,272,128]{2,1,0:T(8,128)(2,1)}), bf16[8,272,128]{2,1,0:T(8,128)(2,1)S(1)}, u32[]{:S(2)}, u32[]{:S(2)}) %all-to-all-start) | async-done | bytes 557088 | tf_op jit(solution)/shard_map/all_to_all | solution.py:173
  42.3 1.5 %collective-permute-start = (bf16[8,272,128]{2,1,0:T(8,128)(2,1)S(1)}, bf16[8,272,128]{2,1,0:T(8,128)(2,1)S(1)}, u32[]{:S(2)}, u32[]{:S(2)}) collective-permute-start(bf16[8,272,128]{2,1,0:T(8,128)(2,1)S(1)} %all-to-all-done.refs_0_), channel_id=1, source_target_pairs={{0,2},{1,3},{2,0},{3,1},{4,6},{5,7},{6,4},{7,5},{8,10},{9,11},{10,... | collective-permute-start | bytes 1671176 | tf_op jit(solution)/shard_map/ppermute | solution.py:142
  43.8 0.0 collective-permute-start.1
  43.8 9.0 %collective-permute-done.refs_1_ = bf16[8,272,128]{2,1,0:T(8,128)(2,1)S(1)} collective-permute-done((bf16[8,272,128]{2,1,0:T(8,128)(2,1)S(1)}, bf16[8,272,128]{2,1,0:T(8,128)(2,1)S(1)}, u32[]{:S(2)}, u32[]{:S(2)}) %collective-permute-start) | collective-permute-done | bytes 557088 | tf_op jit(solution)/shard_map/ppermute | solution.py:142
  52.8 0.0 collective-permute-start.2
  52.8 6.6 %collective-permute-done.6.refs_8_ = bf16[512,1024]{1,0:T(8,128)(2,1)} collective-permute-done((bf16[512,1024]{1,0:T(8,128)(2,1)S(1)}, bf16[512,1024]{1,0:T(8,128)(2,1)}, u32[]{:S(2)}, u32[]{:S(2)}) %collective-permute-start.6) | collective-permute-done | bytes 1048608 | tf_op jit(solution)/shard_map/ppermute | solution.py:163
  59.4 0.0 collective-permute-start.8
  59.4 4.6 %collective-permute-start.7 = (bf16[512,1024]{1,0:T(8,128)(2,1)}, bf16[512,1024]{1,0:T(8,128)(2,1)}, u32[]{:S(2)}, u32[]{:S(2)}) collective-permute-start(bf16[512,1024]{1,0:T(8,128)(2,1)} %collective-permute-done.5.refs_7_), channel_id=1, source_target_pairs={{0,8},{8,16},{16,24},{24,28},{28,20},{20,12},{12,4},{4,0},{1,9},{9... | collective-permute-start | bytes 3145736 | tf_op jit(solution)/shard_map/ppermute | solution.py:162
  64.0 0.1 copy.27
  64.1 0.1 copy.31
  64.2 0.1 copy.28
  64.3 0.1 copy.32
  64.4 0.0 collective-permute-done.1.refs_2_
  64.4 0.1 copy.29
  64.5 0.1 copy.33
  64.6 0.0 collective-permute-done.2.refs_3_
  64.6 0.7 slice.35
  65.3 0.1 copy.30
  65.4 0.1 copy.34
  65.5 0.1 copy.35
  65.6 0.3 fusion.2
  65.9 0.1 copy.36
  66.0 0.3 compare_reduce_fusion
  66.3 0.1 copy.37
  66.4 0.7 fusion.8.dest_ref
  67.2 19.0 %collective-permute-done.8.refs_10_ = bf16[512,1024]{1,0:T(8,128)(2,1)S(1)} collective-permute-done((bf16[512,1024]{1,0:T(8,128)(2,1)}, bf16[512,1024]{1,0:T(8,128)(2,1)S(1)}, u32[]{:S(2)}, u32[]{:S(2)}) %collective-permute-start.8) | collective-permute-done | bytes 1048608 | tf_op jit(solution)/shard_map/ppermute | solution.py:163
  86.1 0.9 slice.39
  87.0 0.0 collective-permute-start.10
  87.0 0.0 collective-permute-done.7.refs_9_
  87.0 0.3 copy-done.3
  87.3 1.9 %slice.38 = bf16[256,1024]{1,0:T(8,128)(2,1)} slice(bf16[512,1024]{1,0:T(8,128)(2,1)} %collective-permute-done.7.refs_9_), slice={[0:256], [0:1024]} | slice | bytes 1048576 | tf_op jit(solution)/shard_map/slice | solution.py:165
  89.2 1.8 %collective-permute-start.9 = (bf16[256,1024]{1,0:T(8,128)(2,1)}, bf16[256,1024]{1,0:T(8,128)(2,1)S(1)}, u32[]{:S(2)}, u32[]{:S(2)}) collective-permute-start(bf16[256,1024]{1,0:T(8,128)(2,1)} %slice.38), channel_id=1, source_target_pairs={{0,8},{8,16},{16,24},{24,28},{28,20},{20,12},{12,4},{4,0},{1,9},{9... | collective-permute-start | bytes 1572872 | tf_op jit(solution)/shard_map/ppermute | solution.py:165
  91.0 14.3 %shard_map.64 = (f32[4,1024,256]{2,1,0:T(8,128)}, bf16[1024,512]{1,0:T(8,128)(2,1)}) custom-call(s32[4,8,2]{2,1,0:T(8,128)} %fusion.8.dest_ref, bf16[8,272,128]{2,1,0:T(8,128)(2,1)} %copy-done, bf16[8,272,128]{2,1,0:T(8,128)(2,1)} %copy-done.4, bf16[8,272,128]{2,1,0:T(8,128)(2,1)} %copy-done.5, bf16[8,272,128]{2,1,0:T(8,128)(2,1)} %collective-permute-done.2.refs_3_, ...), custom_call_target="tpu_custom_call" | custom-call | flops 7516192768 | bytes 11534336 | tf_op jit(solution)/shard_map/pallas_call | solution.py:80
  105.3 0.0 collective-permute-done.9.low_ref
  105.3 0.8 copy-done.1
  106.1 0.2 copy-done.2
  106.3 5.6 %shard_map.65 = bf16[1024,1024]{1,0:T(8,128)(2,1)} custom-call(bf16[1024,512]{1,0:T(8,128)(2,1)} %get-tuple-element.7.left_ref, bf16[256,1024]{1,0:T(8,128)(2,1)} %copy-done.2, bf16[256,1024]{1,0:T(8,128)(2,1)} %copy-done.1, f32[4,1024,256]{2,1,0:T(8,128)} %get-tuple-element.8.acc_ref), custom_call_target="tpu_custom_call" | custom-call | flops 1073741824 | bytes 8388608 | tf_op jit(solution)/shard_map/pallas_call | solution.py:116
  (21 shorter events, 0.1 us)
Async XLA Ops:
  0.0 29.7 %collective-permute-start.3 = (bf16[512,1024]{1,0:T(8,128)(2,1)}, bf16[512,1024]{1,0:T(8,128)(2,1)}, u32[]{:S(2)}, u32[]{:S(2)}) collective-permute-start(bf16[512,1024]{1,0:T(8,128)(2,1)} %refs_4_.1), channel_id=1, source_target_pairs={{0,8},{8,16},{16,24},{24,28},{28,20},{20,12},{12,4},{4,0},{1,9},{9... | collective-permute-start | bytes 3145736 | tf_op jit(solution)/shard_map/ppermute | solution.py:162
  3.0 26.3 %collective-permute-start.4 = (bf16[512,1024]{1,0:T(8,128)(2,1)}, bf16[512,1024]{1,0:T(8,128)(2,1)S(1)}, u32[]{:S(2)}, u32[]{:S(2)}) collective-permute-start(bf16[512,1024]{1,0:T(8,128)(2,1)} %refs_4_.1), channel_id=1, source_target_pairs={{8,0},{16,8},{24,16},{28,24},{20,28},{12,20},{4,12},{0,4},{9,1},{1... | collective-permute-start | bytes 3145736 | tf_op jit(solution)/shard_map/ppermute | solution.py:163
  4.5 59.4 %copy-start.7 = (s32[1,8]{1,0:T(1,128)S(1)}, s32[1,8]{1,0:T(1,128)}, u32[]{:S(2)}) copy-start(s32[1,8]{1,0:T(1,128)} %param.10) | copy-start | bytes 100
  6.4 35.8 %all-to-all-start = ((bf16[8,272,128]{2,1,0:T(8,128)(2,1)}), bf16[8,272,128]{2,1,0:T(8,128)(2,1)S(1)}, u32[]{:S(2)}, u32[]{:S(2)}) async-start(bf16[8,272,128]{2,1,0:T(8,128)(2,1)} %fusion.1), calls=%async_computation | async-start | bytes 1114112 | tf_op jit(solution)/shard_map/all_to_all | solution.py:173
  29.3 23.5 %copy-start.6 = (bf16[512,1024]{1,0:T(8,128)(2,1)}, bf16[512,1024]{1,0:T(8,128)(2,1)S(1)}, u32[]{:S(2)}) copy-start(bf16[512,1024]{1,0:T(8,128)(2,1)S(1)} %collective-permute-done.4.refs_6_) | copy-start | bytes 3145732
  29.3 30.1 %collective-permute-start.6 = (bf16[512,1024]{1,0:T(8,128)(2,1)S(1)}, bf16[512,1024]{1,0:T(8,128)(2,1)}, u32[]{:S(2)}, u32[]{:S(2)}) collective-permute-start(bf16[512,1024]{1,0:T(8,128)(2,1)S(1)} %collective-permute-done.4.refs_6_), channel_id=1, source_target_pairs={{8,0},{16,8},{24,16},{28,24},{20,28},{12,20},{4,12},{0,4},{9,1},{1... | collective-permute-start | bytes 3145736 | tf_op jit(solution)/shard_map/ppermute | solution.py:163
  29.7 29.7 %collective-permute-start.5 = (bf16[512,1024]{1,0:T(8,128)(2,1)}, bf16[512,1024]{1,0:T(8,128)(2,1)}, u32[]{:S(2)}, u32[]{:S(2)}) collective-permute-start(bf16[512,1024]{1,0:T(8,128)(2,1)} %collective-permute-done.3.refs_5_), channel_id=1, source_target_pairs={{0,8},{8,16},{16,24},{24,28},{28,20},{20,12},{12,4},{4,0},{1,9},{9... | collective-permute-start | bytes 3145736 | tf_op jit(solution)/shard_map/ppermute | solution.py:162
  42.3 47.0 %copy-start = (bf16[8,272,128]{2,1,0:T(8,128)(2,1)}, bf16[8,272,128]{2,1,0:T(8,128)(2,1)S(1)}, u32[]{:S(2)}) copy-start(bf16[8,272,128]{2,1,0:T(8,128)(2,1)S(1)} %all-to-all-done.refs_0_) | copy-start | bytes 1671172
  42.3 10.5 %collective-permute-start = (bf16[8,272,128]{2,1,0:T(8,128)(2,1)S(1)}, bf16[8,272,128]{2,1,0:T(8,128)(2,1)S(1)}, u32[]{:S(2)}, u32[]{:S(2)}) collective-permute-start(bf16[8,272,128]{2,1,0:T(8,128)(2,1)S(1)} %all-to-all-done.refs_0_), channel_id=1, source_target_pairs={{0,2},{1,3},{2,0},{3,1},{4,6},{5,7},{6,4},{7,5},{8,10},{9,11},{10,... | collective-permute-start | bytes 1671176 | tf_op jit(solution)/shard_map/ppermute | solution.py:142
  43.8 20.6 %collective-permute-start.1 = (bf16[8,272,128]{2,1,0:T(8,128)(2,1)S(1)}, bf16[8,272,128]{2,1,0:T(8,128)(2,1)S(1)}, u32[]{:S(2)}, u32[]{:S(2)}) collective-permute-start(bf16[8,272,128]{2,1,0:T(8,128)(2,1)S(1)} %all-to-all-done.refs_0_), channel_id=1, source_target_pairs={{0,1},{1,0},{2,3},{3,2},{4,5},{5,4},{6,7},{7,6},{8,9},{9,8},{10,11... | collective-permute-start | bytes 1671176 | tf_op jit(solution)/shard_map/ppermute | solution.py:143
  52.8 33.3 %copy-start.4 = (bf16[8,272,128]{2,1,0:T(8,128)(2,1)}, bf16[8,272,128]{2,1,0:T(8,128)(2,1)S(1)}, u32[]{:S(2)}) copy-start(bf16[8,272,128]{2,1,0:T(8,128)(2,1)S(1)} %collective-permute-done.refs_1_) | copy-start | bytes 1671172
  52.8 11.8 %collective-permute-start.2 = (bf16[8,272,128]{2,1,0:T(8,128)(2,1)S(1)}, bf16[8,272,128]{2,1,0:T(8,128)(2,1)}, u32[]{:S(2)}, u32[]{:S(2)}) collective-permute-start(bf16[8,272,128]{2,1,0:T(8,128)(2,1)S(1)} %collective-permute-done.refs_1_), channel_id=1, source_target_pairs={{0,1},{1,0},{2,3},{3,2},{4,5},{5,4},{6,7},{7,6},{8,9},{9,8},{10,11... | collective-permute-start | bytes 1671176 | tf_op jit(solution)/shard_map/ppermute | solution.py:144
  59.4 26.7 %collective-permute-start.8 = (bf16[512,1024]{1,0:T(8,128)(2,1)}, bf16[512,1024]{1,0:T(8,128)(2,1)S(1)}, u32[]{:S(2)}, u32[]{:S(2)}) collective-permute-start(bf16[512,1024]{1,0:T(8,128)(2,1)} %collective-permute-done.6.refs_8_), channel_id=1, source_target_pairs={{8,0},{16,8},{24,16},{28,24},{20,28},{12,20},{4,12},{0,4},{9,1},{1... | collective-permute-start | bytes 3145736 | tf_op jit(solution)/shard_map/ppermute | solution.py:163
  59.4 27.6 %collective-permute-start.7 = (bf16[512,1024]{1,0:T(8,128)(2,1)}, bf16[512,1024]{1,0:T(8,128)(2,1)}, u32[]{:S(2)}, u32[]{:S(2)}) collective-permute-start(bf16[512,1024]{1,0:T(8,128)(2,1)} %collective-permute-done.5.refs_7_), channel_id=1, source_target_pairs={{0,8},{8,16},{16,24},{24,28},{28,20},{20,12},{12,4},{4,0},{1,9},{9... | collective-permute-start | bytes 3145736 | tf_op jit(solution)/shard_map/ppermute | solution.py:162
  64.4 22.7 %copy-start.5 = (bf16[8,272,128]{2,1,0:T(8,128)(2,1)}, bf16[8,272,128]{2,1,0:T(8,128)(2,1)S(1)}, u32[]{:S(2)}) copy-start(bf16[8,272,128]{2,1,0:T(8,128)(2,1)S(1)} %collective-permute-done.1.refs_2_) | copy-start | bytes 1671172
  86.1 1.2 %copy-start.3 = (bf16[512,1024]{1,0:T(8,128)(2,1)}, bf16[512,1024]{1,0:T(8,128)(2,1)S(1)}, u32[]{:S(2)}) copy-start(bf16[512,1024]{1,0:T(8,128)(2,1)S(1)} %collective-permute-done.8.refs_10_) | copy-start | bytes 3145732
  87.0 18.3 %collective-permute-start.10 = (bf16[256,1024]{1,0:T(8,128)(2,1)}, bf16[256,1024]{1,0:T(8,128)(2,1)S(1)}, u32[]{:S(2)}, u32[]{:S(2)}) collective-permute-start(bf16[256,1024]{1,0:T(8,128)(2,1)} %slice.39), channel_id=1, source_target_pairs={{8,0},{16,8},{24,16},{28,24},{20,28},{12,20},{4,12},{0,4},{9,1},{1... | collective-permute-start | bytes 1572872 | tf_op jit(solution)/shard_map/ppermute | solution.py:166
  89.2 16.1 %collective-permute-start.9 = (bf16[256,1024]{1,0:T(8,128)(2,1)}, bf16[256,1024]{1,0:T(8,128)(2,1)S(1)}, u32[]{:S(2)}, u32[]{:S(2)}) collective-permute-start(bf16[256,1024]{1,0:T(8,128)(2,1)} %slice.38), channel_id=1, source_target_pairs={{0,8},{8,16},{16,24},{24,28},{28,20},{20,12},{12,4},{4,0},{1,9},{9... | collective-permute-start | bytes 1572872 | tf_op jit(solution)/shard_map/ppermute | solution.py:165
  105.3 0.8 copy-start.1
  105.3 1.0 copy-start.2

commit v7 on v6

--- a/solution.py
+++ b/solution.py
@@ -52,7 +52,9 @@
             return carry
 
         lax.fori_loop(0, per_part, place, 0)
-    late = pltpu.make_async_copy(left.at[:, pl.ds(inner, depth)], late_hbm, late_sem)
+    late = pltpu.make_async_copy(
+        left.at[:, pl.ds(inner, late_hbm.shape[1])], late_hbm, late_sem
+    )
     late.start()
     for fetch in fetches:
         fetch.wait()
@@ -71,7 +73,7 @@
         store.wait()
 
 
-def first_product(dest, parts, rights, rows, bs, cap, bn):
+def first_product(dest, parts, rights, rows, late_width, bs, cap, bn):
     n_parts, n_right = len(parts), len(rights)
     depth, cols = rights[0].shape
     inner = n_right * depth
@@ -81,14 +83,14 @@
         functools.partial(first_kernel, dims),
         out_shape=[
             jax.ShapeDtypeStruct((cols // bn, rows, bn), jnp.float32),
-            jax.ShapeDtypeStruct((rows, depth), jnp.bfloat16),
+            jax.ShapeDtypeStruct((rows, late_width), jnp.bfloat16),
         ],
         in_specs=[pl.BlockSpec(memory_space=pltpu.SMEM)]
         + [pl.BlockSpec(memory_space=pltpu.VMEM)] * n_parts
         + [anywhere] * n_right,
         out_specs=[anywhere] * 2,
         scratch_shapes=[
-            pltpu.VMEM((rows, inner + depth), jnp.bfloat16),
+            pltpu.VMEM((rows, inner + late_width), jnp.bfloat16),
             pltpu.VMEM((inner, cols), jnp.bfloat16),
             pltpu.VMEM((cols // bn, rows, bn), jnp.float32),
             pltpu.SemaphoreType.DMA((n_right,)),
@@ -104,33 +106,34 @@
     )(dest, *parts, *rights)
 
 
-def last_kernel(left_ref, low_ref, high_ref, acc_ref, out_ref):
-    right = jnp.concatenate([low_ref[...], high_ref[...]], axis=0)
+def add_kernel(left_ref, *refs):
+    right = jnp.concatenate([piece[...] for piece in refs[:-2]], axis=0)
     total = jnp.dot(left_ref[...], right, preferred_element_type=jnp.float32)
-    out_ref[...] = (acc_ref[0] + total).astype(out_ref.dtype)
-
-
-def last_product(left, low, high, acc):
-    rows, inner = left.shape
-    steps, _, bn = acc.shape
+    out_ref = refs[-1]
+    out_ref[...] = (refs[-2][0] + total).astype(out_ref.dtype).reshape(out_ref.shape)
+
+
+def add_product(left, place, pieces, acc, last):
+    steps, rows, bn = acc.shape
+    inner = sum(piece.shape[0] for piece in pieces)
+    acc_spec = pl.BlockSpec((1, rows, bn), lambda j: (j, 0, 0))
+    out_spec = pl.BlockSpec((rows, bn), lambda j: (0, j))
+    out_shape = jax.ShapeDtypeStruct((rows, steps * bn), jnp.bfloat16)
     return pl.pallas_call(
-        last_kernel,
-        out_shape=jax.ShapeDtypeStruct((rows, steps * bn), jnp.bfloat16),
+        add_kernel,
+        out_shape=out_shape if last else jax.ShapeDtypeStruct(acc.shape, acc.dtype),
         grid=(steps,),
-        in_specs=[
-            pl.BlockSpec((rows, inner), lambda j: (0, 0)),
-            pl.BlockSpec((low.shape[0], bn), lambda j: (0, j)),
-            pl.BlockSpec((high.shape[0], bn), lambda j: (0, j)),
-            pl.BlockSpec((1, rows, bn), lambda j: (j, 0, 0)),
-        ],
-        out_specs=pl.BlockSpec((rows, bn), lambda j: (0, j)),
+        in_specs=[pl.BlockSpec((rows, inner), lambda j: (0, place))]
+        + [pl.BlockSpec((piece.shape[0], bn), lambda j: (0, j)) for piece in pieces]
+        + [acc_spec],
+        out_specs=out_spec if last else acc_spec,
         compiler_params=pltpu.CompilerParams(vmem_limit_bytes=VMEM_BYTES),
         cost_estimate=pl.CostEstimate(
             flops=2 * rows * inner * steps * bn,
-            bytes_accessed=(rows + steps * bn) * inner * 2 + rows * steps * bn * 6,
+            bytes_accessed=(rows + steps * bn) * inner * 2 + rows * steps * bn * 8,
             transcendentals=0,
         ),
-    )(left, low, high, acc)
+    )(left, *pieces, acc)
 
 
 def across_row(landed, columns):
@@ -157,13 +160,18 @@
     order = ring_order(groups)
     to_right = [(order[i], order[(i + 1) % groups]) for i in range(groups)]
     to_left = [(order[(i + 1) % groups], order[i]) for i in range(groups)]
-    from_left, from_right, rights = b_matrix, b_matrix, [b_matrix]
-    for s in range(1, half):
+    from_left, from_right, early = b_matrix, b_matrix, [b_matrix]
+    for s in range(1, half - 1):
         from_left = lax.ppermute(from_left, "grid", to_right)
         from_right = lax.ppermute(from_right, "grid", to_left)
-        rights += [from_left, from_right]
-    low = lax.ppermute(from_left[: k_local // 2], "grid", to_right)
-    high = lax.ppermute(from_right[k_local // 2 :], "grid", to_left)
+        early += [from_left, from_right]
+    split = k_local // 2
+    left_low = lax.ppermute(from_left[:split], "grid", to_right)
+    right_high = lax.ppermute(from_right[split:], "grid", to_left)
+    left_high = lax.ppermute(from_left[split:], "grid", to_right)
+    right_low = lax.ppermute(from_right[:split], "grid", to_left)
+    low = lax.ppermute(left_low, "grid", to_right)
+    high = lax.ppermute(right_high, "grid", to_left)
 
     live = jnp.arange(cap, dtype=jnp.int32)[None, :] < a_count.reshape(groups, 1)
     row_code = jnp.where(live, a_rows.reshape(groups, cap) + 1, 0)
@@ -184,8 +192,9 @@
     dest = row * (blocks * groups) + first * blocks + col % blocks
     dest = jnp.where(jnp.any(hit, axis=-1), dest, -1)
 
-    acc, late = first_product(dest, parts, rights, rb * bs, bs, cap, n_local // 4)
-    return last_product(late, low, high, acc)
+    acc, late = first_product(dest, parts, early, rb * bs, 3 * k_local, bs, cap, n_local // 4)
+    acc = add_product(late, 0, [left_low, left_high, right_low, right_high], acc, False)
+    return add_product(late, 2, [low, high], acc, True)
 
 
 def solution(mesh):

time: 112 us -> 116 us (1.036)
  Pallas kernels: 19.9 us -> 24.5 us
  waiting for transfers between devices: 62.1 us -> 59.9 us
  local copies, waits for them, and re-layouts: 5.99 us -> 7.29 us
    ppermute x3 -> x2, waiting for transfers between devices: 42.1 us -> 8.37 us  [body(): from_right = lax.ppermute(from_right, 'grid', to_left)]
    all_to_all x1, waiting for transfers between devices: 10.9 us -> 24.5 us  [body(): lax.all_to_all(message, 'grid', split_axis=0, concat_axis=0, tiled=True)]
    ppermute x3 -> x2, waiting for transfers between devices: 0.01 us -> 10.9 us  [body(): from_left = lax.ppermute(from_left, 'grid', to_right)]
    ppermute x2 -> x6, waiting for transfers between devices: 0.01 us -> 10.4 us  [the longest x1 10.3 us: body(): right_high = lax.ppermute(from_right[split:], 'grid', to_left)]
    pallas_call x1 -> x2, Pallas kernels: 5.64 us -> 13.4 us  [add_product(): pl.pallas_call(add_kernel, out_shape=out_shape if last else jax.ShapeDtyp...]
    ppermute x3 -> x2, starting transfers between devices: 9.3 us -> 5.56 us  [body(): from_left = lax.ppermute(from_left, 'grid', to_right)]
    ppermute x2 -> x6, starting transfers between devices: 1.75 us -> 5.37 us  [the longest x1 1.71 us: body(): left_high = lax.ppermute(from_left[split:], 'grid', to_right)]
    ppermute x1, waiting for transfers between devices: 9.03 us -> 5.47 us  [across_row(): across = lax.ppermute(landed, 'blk', swap_chip)]
  transfers between devices with their start and end apart: 12 -> 14, of which waited for: 5 -> 7; matrix products, arithmetic and copies ran while one was open for 8% -> 9% of each run, Pallas kernels for 13% -> 16%
where the time goes in v7:
time: 116 us
  waiting for transfers between devices  59.9 us (52%)
  Pallas kernels  24.5 us (21%)
  starting transfers between devices  19.3 us (17%)
  local copies, waits for them, and re-layouts  7.29 us (6%)
  other arithmetic  4.61 us (4%)
    all_to_all x1, waiting for transfers between devices, body(): lax.all_to_all(message, 'grid', split_axis=0, concat_axis=0, tiled=True)  24.5 us
    pallas_call x2, Pallas kernels, add_product(): pl.pallas_call(add_kernel, out_shape=out_shape if last else jax.ShapeDtyp...  13.4 us
    pallas_call x1, Pallas kernels, first_product(): pl.pallas_call(functools.partial(first_kernel, dims), out_shape=[jax.Shap...  11.1 us
    ppermute x2, waiting for transfers between devices, body(): from_left = lax.ppermute(from_left, 'grid', to_right)  10.9 us
    ppermute x1, waiting for transfers between devices, body(): right_high = lax.ppermute(from_right[split:], 'grid', to_left)  10.3 us
    ppermute x2, waiting for transfers between devices, body(): from_right = lax.ppermute(from_right, 'grid', to_left)  8.37 us
    ppermute x2, starting transfers between devices, body(): from_left = lax.ppermute(from_left, 'grid', to_right)  5.56 us
    ppermute x1, waiting for transfers between devices, across_row(): across = lax.ppermute(landed, 'blk', swap_chip)  5.47 us
  transfers between devices with their start and end apart: 14, of which 7 were waited for; matrix products, arithmetic and copies ran while one was open for 9% of the time, Pallas kernels for 16%

profile of v7, /device:TPU:0, one launch (start us, length us, event | category | flops | bytes accessed | tf_op | source)
XLA Modules:
  0.0 115.6 jit_solution(5779239990154922610)
XLA Ops:
  0.0 3.0 %collective-permute-start.3 = (bf16[512,1024]{1,0:T(8,128)(2,1)}, bf16[512,1024]{1,0:T(8,128)(2,1)}, u32[]{:S(2)}, u32[]{:S(2)}) collective-permute-start(bf16[512,1024]{1,0:T(8,128)(2,1)} %refs_4_.1), channel_id=1, source_target_pairs={{0,8},{8,16},{16,24},{24,28},{28,20},{20,12},{12,4},{4,0},{1,9},{9... | collective-permute-start | bytes 3145736 | tf_op jit(solution)/shard_map/ppermute | solution.py:165
  3.0 0.7 convert_bitcast_fusion
  3.7 0.7 fusion.13
  4.4 0.1 copy.26
  4.5 1.9 %fusion.1 = bf16[8,272,128]{2,1,0:T(8,128)(2,1)} fusion(bf16[8,1,4]{2,1,0:T(2,128)(2,1)S(1)} %copy.26, bf16[8,256,128]{2,1,0:T(8,128)(2,1)} %bitcast.17), kind=kLoop, calls=%fused_computation.2 | loop fusion | flops 1671168 | bytes 1081408 | tf_op jit(solution)/shard_map/concatenate | solution.py:180
  6.4 4.8 %all-to-all-start = ((bf16[8,272,128]{2,1,0:T(8,128)(2,1)}), bf16[8,272,128]{2,1,0:T(8,128)(2,1)S(1)}, u32[]{:S(2)}, u32[]{:S(2)}) async-start(bf16[8,272,128]{2,1,0:T(8,128)(2,1)} %fusion.1), calls=%async_computation | async-start | bytes 1114112 | tf_op jit(solution)/shard_map/all_to_all | solution.py:181
  11.2 2.0 %collective-permute-start.4 = (bf16[512,1024]{1,0:T(8,128)(2,1)S(1)}, bf16[512,1024]{1,0:T(8,128)(2,1)}, u32[]{:S(2)}, u32[]{:S(2)}) collective-permute-start(bf16[512,1024]{1,0:T(8,128)(2,1)S(1)} %copy-done.6), channel_id=1, source_target_pairs={{8,0},{16,8},{24,16},{28,24},{20,28},{12,20},{4,12},{0,4},{9,1},{1... | collective-permute-start | bytes 3145736 | tf_op jit(solution)/shard_map/ppermute | solution.py:166
  13.3 24.5 %all-to-all-done.refs_0_ = bf16[8,272,128]{2,1,0:T(8,128)(2,1)S(1)} async-done(((bf16[8,272,128]{2,1,0:T(8,128)(2,1)}), bf16[8,272,128]{2,1,0:T(8,128)(2,1)S(1)}, u32[]{:S(2)}, u32[]{:S(2)}) %all-to-all-start) | async-done | bytes 557088 | tf_op jit(solution)/shard_map/all_to_all | solution.py:181
  37.8 1.5 %collective-permute-start = (bf16[8,272,128]{2,1,0:T(8,128)(2,1)S(1)}, bf16[8,272,128]{2,1,0:T(8,128)(2,1)}, u32[]{:S(2)}, u32[]{:S(2)}) collective-permute-start(bf16[8,272,128]{2,1,0:T(8,128)(2,1)S(1)} %all-to-all-done.refs_0_), channel_id=1, source_target_pairs={{0,2},{1,3},{2,0},{3,1},{4,6},{5,7},{6,4},{7,5},{8,10},{9,11},{10,... | collective-permute-start | bytes 1671176 | tf_op jit(solution)/shard_map/ppermute | solution.py:145
  39.2 2.5 %collective-permute-start.5 = (bf16[512,1024]{1,0:T(8,128)(2,1)}, bf16[512,1024]{1,0:T(8,128)(2,1)S(1)}, u32[]{:S(2)}, u32[]{:S(2)}) collective-permute-start(bf16[512,1024]{1,0:T(8,128)(2,1)} %collective-permute-done.3.refs_5_), channel_id=1, source_target_pairs={{0,8},{8,16},{16,24},{24,28},{28,20},{20,12},{12,4},{4,0},{1,9},{9... | collective-permute-start | bytes 3145736 | tf_op jit(solution)/shard_map/ppermute | solution.py:165
  41.8 3.0 %collective-permute-done.4.refs_6_ = bf16[512,1024]{1,0:T(8,128)(2,1)} collective-permute-done((bf16[512,1024]{1,0:T(8,128)(2,1)S(1)}, bf16[512,1024]{1,0:T(8,128)(2,1)}, u32[]{:S(2)}, u32[]{:S(2)}) %collective-permute-start.4) | collective-permute-done | bytes 1048608 | tf_op jit(solution)/shard_map/ppermute | solution.py:166
  44.8 0.0 collective-permute-start.6
  44.8 0.0 collective-permute-start.1
  44.8 5.5 %collective-permute-done.refs_1_ = bf16[8,272,128]{2,1,0:T(8,128)(2,1)} collective-permute-done((bf16[8,272,128]{2,1,0:T(8,128)(2,1)S(1)}, bf16[8,272,128]{2,1,0:T(8,128)(2,1)}, u32[]{:S(2)}, u32[]{:S(2)}) %collective-permute-start) | collective-permute-done | bytes 557088 | tf_op jit(solution)/shard_map/ppermute | solution.py:145
  50.3 0.1 copy.27
  50.4 0.1 copy.31
  50.5 0.7 slice.41
  51.3 0.1 copy.28
  51.4 0.1 copy.32
  51.5 0.7 slice.42
  52.2 0.1 copy.29
  52.3 0.1 copy.33
  52.4 0.2 collective-permute-done.2.refs_3_
  52.6 0.7 slice.43
  53.3 0.1 copy.30
  53.4 0.1 copy.34
  53.5 10.9 %collective-permute-done.5.refs_7_ = bf16[512,1024]{1,0:T(8,128)(2,1)S(1)} collective-permute-done((bf16[512,1024]{1,0:T(8,128)(2,1)}, bf16[512,1024]{1,0:T(8,128)(2,1)S(1)}, u32[]{:S(2)}, u32[]{:S(2)}) %collective-permute-start.5) | collective-permute-done | bytes 1048608 | tf_op jit(solution)/shard_map/ppermute | solution.py:165
  64.5 1.2 %fusion.15 = (bf16[256,1024]{1,0:T(8,128)(2,1)}, bf16[256,1024]{1,0:T(8,128)(2,1)}) fusion(bf16[512,1024]{1,0:T(8,128)(2,1)S(1)} %collective-permute-done.5.refs_7_), kind=kLoop, calls=%fused_computation.40 | loop fusion | bytes 2097152 | tf_op jit(solution)/shard_map/slice | solution.py:171
  65.6 0.3 collective-permute-start.7
  65.9 5.3 %collective-permute-done.6.refs_8_ = bf16[512,1024]{1,0:T(8,128)(2,1)S(1)} collective-permute-done((bf16[512,1024]{1,0:T(8,128)(2,1)}, bf16[512,1024]{1,0:T(8,128)(2,1)S(1)}, u32[]{:S(2)}, u32[]{:S(2)}) %collective-permute-start.6) | collective-permute-done | bytes 1048608 | tf_op jit(solution)/shard_map/ppermute | solution.py:166
  71.2 1.2 %fusion.14 = (bf16[256,1024]{1,0:T(8,128)(2,1)}, bf16[256,1024]{1,0:T(8,128)(2,1)}) fusion(bf16[512,1024]{1,0:T(8,128)(2,1)S(1)} %collective-permute-done.6.refs_8_), kind=kLoop, calls=%fused_computation.39 | loop fusion | bytes 2097152 | tf_op jit(solution)/shard_map/slice | solution.py:172
  72.4 0.4 collective-permute-start.9
  72.8 0.1 copy.35
  72.9 0.3 fusion.2
  73.2 0.1 copy.36
  73.3 0.3 compare_reduce_fusion
  73.6 0.1 copy.37
  73.7 1.7 %collective-permute-start.11 = (bf16[256,1024]{1,0:T(8,128)(2,1)}, bf16[256,1024]{1,0:T(8,128)(2,1)}, u32[]{:S(2)}, u32[]{:S(2)}) collective-permute-start(bf16[256,1024]{1,0:T(8,128)(2,1)} %get-tuple-element.11), channel_id=1, source_target_pairs={{0,8},{8,16},{16,24},{24,28},{28,20},{20,12},{12,4},{4,0},{1,9},{9... | collective-permute-start | bytes 1572872 | tf_op jit(solution)/shard_map/ppermute | solution.py:171
  75.4 1.0 collective-permute-start.12
  76.4 0.7 fusion.8.dest_ref
  77.1 10.3 %collective-permute-done.9.refs_3_ = bf16[256,1024]{1,0:T(8,128)(2,1)S(1)} collective-permute-done((bf16[256,1024]{1,0:T(8,128)(2,1)}, bf16[256,1024]{1,0:T(8,128)(2,1)S(1)}, u32[]{:S(2)}, u32[]{:S(2)}) %collective-permute-start.9) | collective-permute-done | bytes 524320 | tf_op jit(solution)/shard_map/ppermute | solution.py:170
  87.5 0.6 collective-permute-start.10
  88.0 1.5 %collective-permute-start.8 = (bf16[256,1024]{1,0:T(8,128)(2,1)}, bf16[256,1024]{1,0:T(8,128)(2,1)S(1)}, u32[]{:S(2)}, u32[]{:S(2)}) collective-permute-start(bf16[256,1024]{1,0:T(8,128)(2,1)} %collective-permute-done.7.refs_0_), channel_id=1, source_target_pairs={{0,8},{8,16},{16,24},{24,28},{28,20},{20,12},{12,4},{4,0},{1,9},{9... | collective-permute-start | bytes 1572872 | tf_op jit(solution)/shard_map/ppermute | solution.py:173
  89.5 11.1 %shard_map.64 = (f32[4,1024,256]{2,1,0:T(8,128)}, bf16[1024,1536]{1,0:T(8,128)(2,1)}) custom-call(s32[4,8,2]{2,1,0:T(8,128)} %fusion.8.dest_ref, bf16[8,272,128]{2,1,0:T(8,128)(2,1)} %copy-done.2, bf16[8,272,128]{2,1,0:T(8,128)(2,1)} %collective-permute-done.refs_1_, bf16[8,272,128]{2,1,0:T(8,128)(2,1)} %collective-permute-done.1.refs_2_, ...), custom_call_target="tpu_custom_call" | custom-call | flops 5368709120 | bytes 9437184 | tf_op jit(solution)/shard_map/pallas_call | solution.py:82
  100.6 7.8 %shard_map.65.refs_2_ = f32[4,1024,256]{2,1,0:T(8,128)} custom-call(bf16[1024,1536]{1,0:T(8,128)(2,1)} %get-tuple-element.7.left_ref, bf16[256,1024]{1,0:T(8,128)(2,1)} %collective-permute-done.7.refs_0_, bf16[256,1024]{1,0:T(8,128)(2,1)} %collective-permute-done.11.refs_1_, bf16[256,1024]{1,0:T(8,128)(2,1)} %collective-permute-done.12.refs_2_, ...), custom_call_target="tpu_custom_call" | custom-call | flops 2147483648 | bytes 12582912 | tf_op jit(solution)/shard_map/pallas_call | solution.py:122
  108.4 0.8 copy-done.3
  109.2 0.8 copy-done.4
  110.0 5.6 %shard_map.66 = bf16[1024,1024]{1,0:T(8,128)(2,1)} custom-call(bf16[1024,1536]{1,0:T(8,128)(2,1)} %get-tuple-element.7.left_ref, bf16[256,1024]{1,0:T(8,128)(2,1)} %copy-done.4, bf16[256,1024]{1,0:T(8,128)(2,1)} %copy-done.3, f32[4,1024,256]{2,1,0:T(8,128)} %shard_map.65.refs_2_), custom_call_target="tpu_custom_call" | custom-call | flops 1073741824 | bytes 10485760 | tf_op jit(solution)/shard_map/pallas_call | solution.py:122
  (26 shorter events, 0.1 us)
Async XLA Ops:
  0.0 11.2 %copy-start.6 = (bf16[512,1024]{1,0:T(8,128)(2,1)S(1)}, bf16[512,1024]{1,0:T(8,128)(2,1)}, u32[]{:S(2)}) copy-start(bf16[512,1024]{1,0:T(8,128)(2,1)} %refs_4_.1) | copy-start | bytes 3145732
  0.0 39.2 %collective-permute-start.3 = (bf16[512,1024]{1,0:T(8,128)(2,1)}, bf16[512,1024]{1,0:T(8,128)(2,1)}, u32[]{:S(2)}, u32[]{:S(2)}) collective-permute-start(bf16[512,1024]{1,0:T(8,128)(2,1)} %refs_4_.1), channel_id=1, source_target_pairs={{0,8},{8,16},{16,24},{24,28},{28,20},{20,12},{12,4},{4,0},{1,9},{9... | collective-permute-start | bytes 3145736 | tf_op jit(solution)/shard_map/ppermute | solution.py:165
  4.5 45.8 %copy-start.7 = (s32[1,8]{1,0:T(1,128)S(1)}, s32[1,8]{1,0:T(1,128)}, u32[]{:S(2)}) copy-start(s32[1,8]{1,0:T(1,128)} %param.10) | copy-start | bytes 100
  6.4 31.3 %all-to-all-start = ((bf16[8,272,128]{2,1,0:T(8,128)(2,1)}), bf16[8,272,128]{2,1,0:T(8,128)(2,1)S(1)}, u32[]{:S(2)}, u32[]{:S(2)}) async-start(bf16[8,272,128]{2,1,0:T(8,128)(2,1)} %fusion.1), calls=%async_computation | async-start | bytes 1114112 | tf_op jit(solution)/shard_map/all_to_all | solution.py:181
  11.2 33.6 %collective-permute-start.4 = (bf16[512,1024]{1,0:T(8,128)(2,1)S(1)}, bf16[512,1024]{1,0:T(8,128)(2,1)}, u32[]{:S(2)}, u32[]{:S(2)}) collective-permute-start(bf16[512,1024]{1,0:T(8,128)(2,1)S(1)} %copy-done.6), channel_id=1, source_target_pairs={{8,0},{16,8},{24,16},{28,24},{20,28},{12,20},{4,12},{0,4},{9,1},{1... | collective-permute-start | bytes 3145736 | tf_op jit(solution)/shard_map/ppermute | solution.py:166
  37.8 34.6 %copy-start.2 = (bf16[8,272,128]{2,1,0:T(8,128)(2,1)}, bf16[8,272,128]{2,1,0:T(8,128)(2,1)S(1)}, u32[]{:S(2)}) copy-start(bf16[8,272,128]{2,1,0:T(8,128)(2,1)S(1)} %all-to-all-done.refs_0_) | copy-start | bytes 1671172
  37.8 12.6 %collective-permute-start = (bf16[8,272,128]{2,1,0:T(8,128)(2,1)S(1)}, bf16[8,272,128]{2,1,0:T(8,128)(2,1)}, u32[]{:S(2)}, u32[]{:S(2)}) collective-permute-start(bf16[8,272,128]{2,1,0:T(8,128)(2,1)S(1)} %all-to-all-done.refs_0_), channel_id=1, source_target_pairs={{0,2},{1,3},{2,0},{3,1},{4,6},{5,7},{6,4},{7,5},{8,10},{9,11},{10,... | collective-permute-start | bytes 1671176 | tf_op jit(solution)/shard_map/ppermute | solution.py:145
  39.2 25.2 %collective-permute-start.5 = (bf16[512,1024]{1,0:T(8,128)(2,1)}, bf16[512,1024]{1,0:T(8,128)(2,1)S(1)}, u32[]{:S(2)}, u32[]{:S(2)}) collective-permute-start(bf16[512,1024]{1,0:T(8,128)(2,1)} %collective-permute-done.3.refs_5_), channel_id=1, source_target_pairs={{0,8},{8,16},{16,24},{24,28},{28,20},{20,12},{12,4},{4,0},{1,9},{9... | collective-permute-start | bytes 3145736 | tf_op jit(solution)/shard_map/ppermute | solution.py:165
  44.8 26.4 %collective-permute-start.6 = (bf16[512,1024]{1,0:T(8,128)(2,1)}, bf16[512,1024]{1,0:T(8,128)(2,1)S(1)}, u32[]{:S(2)}, u32[]{:S(2)}) collective-permute-start(bf16[512,1024]{1,0:T(8,128)(2,1)} %collective-permute-done.4.refs_6_), channel_id=1, source_target_pairs={{8,0},{16,8},{24,16},{28,24},{20,28},{12,20},{4,12},{0,4},{9,1},{1... | collective-permute-start | bytes 3145736 | tf_op jit(solution)/shard_map/ppermute | solution.py:166
  44.8 6.6 %collective-permute-start.1 = (bf16[8,272,128]{2,1,0:T(8,128)(2,1)S(1)}, bf16[8,272,128]{2,1,0:T(8,128)(2,1)}, u32[]{:S(2)}, u32[]{:S(2)}) collective-permute-start(bf16[8,272,128]{2,1,0:T(8,128)(2,1)S(1)} %all-to-all-done.refs_0_), channel_id=1, source_target_pairs={{0,1},{1,0},{2,3},{3,2},{4,5},{5,4},{6,7},{7,6},{8,9},{9,8},{10,11... | collective-permute-start | bytes 1671176 | tf_op jit(solution)/shard_map/ppermute | solution.py:146
  50.3 2.3 %collective-permute-start.2 = (bf16[8,272,128]{2,1,0:T(8,128)(2,1)}, bf16[8,272,128]{2,1,0:T(8,128)(2,1)}, u32[]{:S(2)}, u32[]{:S(2)}) collective-permute-start(bf16[8,272,128]{2,1,0:T(8,128)(2,1)} %collective-permute-done.refs_1_), channel_id=1, source_target_pairs={{0,1},{1,0},{2,3},{3,2},{4,5},{5,4},{6,7},{7,6},{8,9},{9,8},{10,11... | collective-permute-start | bytes 1671176 | tf_op jit(solution)/shard_map/ppermute | solution.py:147
  64.4 7.9 %copy-start = (bf16[512,1024]{1,0:T(8,128)(2,1)}, bf16[512,1024]{1,0:T(8,128)(2,1)S(1)}, u32[]{:S(2)}) copy-start(bf16[512,1024]{1,0:T(8,128)(2,1)S(1)} %collective-permute-done.5.refs_7_) | copy-start | bytes 3145732
  65.6 22.4 %collective-permute-start.7 = (bf16[256,1024]{1,0:T(8,128)(2,1)}, bf16[256,1024]{1,0:T(8,128)(2,1)}, u32[]{:S(2)}, u32[]{:S(2)}) collective-permute-start(bf16[256,1024]{1,0:T(8,128)(2,1)} %get-tuple-element.12), channel_id=1, source_target_pairs={{0,8},{8,16},{16,24},{24,28},{28,20},{20,12},{12,4},{4,0},{1,9},{9... | collective-permute-start | bytes 1572872 | tf_op jit(solution)/shard_map/ppermute | solution.py:169
  71.2 5.9 %copy-start.1 = (bf16[512,1024]{1,0:T(8,128)(2,1)}, bf16[512,1024]{1,0:T(8,128)(2,1)S(1)}, u32[]{:S(2)}) copy-start(bf16[512,1024]{1,0:T(8,128)(2,1)S(1)} %collective-permute-done.6.refs_8_) | copy-start | bytes 3145732
  72.4 15.1 %collective-permute-start.9 = (bf16[256,1024]{1,0:T(8,128)(2,1)}, bf16[256,1024]{1,0:T(8,128)(2,1)S(1)}, u32[]{:S(2)}, u32[]{:S(2)}) collective-permute-start(bf16[256,1024]{1,0:T(8,128)(2,1)} %get-tuple-element.10), channel_id=1, source_target_pairs={{8,0},{16,8},{24,16},{28,24},{20,28},{12,20},{4,12},{0,4},{9,1},{1... | collective-permute-start | bytes 1572872 | tf_op jit(solution)/shard_map/ppermute | solution.py:170
  73.7 27.0 %collective-permute-start.11 = (bf16[256,1024]{1,0:T(8,128)(2,1)}, bf16[256,1024]{1,0:T(8,128)(2,1)}, u32[]{:S(2)}, u32[]{:S(2)}) collective-permute-start(bf16[256,1024]{1,0:T(8,128)(2,1)} %get-tuple-element.11), channel_id=1, source_target_pairs={{0,8},{8,16},{16,24},{24,28},{28,20},{20,12},{12,4},{4,0},{1,9},{9... | collective-permute-start | bytes 1572872 | tf_op jit(solution)/shard_map/ppermute | solution.py:171
  75.4 25.3 %collective-permute-start.12 = (bf16[256,1024]{1,0:T(8,128)(2,1)}, bf16[256,1024]{1,0:T(8,128)(2,1)}, u32[]{:S(2)}, u32[]{:S(2)}) collective-permute-start(bf16[256,1024]{1,0:T(8,128)(2,1)} %get-tuple-element.9), channel_id=1, source_target_pairs={{8,0},{16,8},{24,16},{28,24},{20,28},{12,20},{4,12},{0,4},{9,1},{1... | collective-permute-start | bytes 1572872 | tf_op jit(solution)/shard_map/ppermute | solution.py:172
  87.5 13.2 %copy-start.5 = (bf16[256,1024]{1,0:T(8,128)(2,1)}, bf16[256,1024]{1,0:T(8,128)(2,1)S(1)}, u32[]{:S(2)}) copy-start(bf16[256,1024]{1,0:T(8,128)(2,1)S(1)} %collective-permute-done.9.refs_3_) | copy-start | bytes 1572868
  87.5 20.9 %collective-permute-start.10 = (bf16[256,1024]{1,0:T(8,128)(2,1)S(1)}, bf16[256,1024]{1,0:T(8,128)(2,1)S(1)}, u32[]{:S(2)}, u32[]{:S(2)}) collective-permute-start(bf16[256,1024]{1,0:T(8,128)(2,1)S(1)} %collective-permute-done.9.refs_3_), channel_id=1, source_target_pairs={{8,0},{16,8},{24,16},{28,24},{20,28},{12,20},{4,12},{0,4},{9,1},{1... | collective-permute-start | bytes 1572872 | tf_op jit(solution)/shard_map/ppermute | solution.py:174
  88.0 20.4 %collective-permute-start.8 = (bf16[256,1024]{1,0:T(8,128)(2,1)}, bf16[256,1024]{1,0:T(8,128)(2,1)S(1)}, u32[]{:S(2)}, u32[]{:S(2)}) collective-permute-start(bf16[256,1024]{1,0:T(8,128)(2,1)} %collective-permute-done.7.refs_0_), channel_id=1, source_target_pairs={{0,8},{8,16},{16,24},{24,28},{28,20},{20,12},{12,4},{4,0},{1,9},{9... | collective-permute-start | bytes 1572872 | tf_op jit(solution)/shard_map/ppermute | solution.py:173
  108.4 0.8 copy-start.3
  109.2 0.8 copy-start.4

commit v8 on v7

--- a/solution.py
+++ b/solution.py
@@ -17,6 +17,51 @@
 
 def ring_place(g, n):
     return jnp.where(g % 2 == 0, g // 2, n - 1 - g // 2)
+
+
+def pack_kernel(slots_hbm, meta_hbm, message_hbm, sems):
+    rows = slots_hbm.shape[1]
+    copies = [
+        pltpu.make_async_copy(slots_hbm, message_hbm.at[:, pl.ds(0, rows)], sems.at[0]),
+        pltpu.make_async_copy(meta_hbm, message_hbm.at[:, pl.ds(rows, META)], sems.at[1]),
+    ]
+    for copy in copies:
+        copy.start()
+    for copy in copies:
+        copy.wait()
+
+
+def pack(slots, meta):
+    groups, rows, width = slots.shape
+    anywhere = pl.BlockSpec(memory_space=pl.ANY)
+    return pl.pallas_call(
+        pack_kernel,
+        out_shape=jax.ShapeDtypeStruct((groups, rows + META, width), slots.dtype),
+        in_specs=[anywhere] * 2,
+        out_specs=anywhere,
+        scratch_shapes=[pltpu.SemaphoreType.DMA((2,))],
+        compiler_params=pltpu.CompilerParams(vmem_limit_bytes=VMEM_BYTES),
+        cost_estimate=pl.CostEstimate(
+            flops=0, bytes_accessed=slots.size * 4, transcendentals=0
+        ),
+    )(slots, meta)
+
+
+def after_kernel(*refs):
+    pass
+
+
+def after(values, others):
+    anywhere = pl.BlockSpec(memory_space=pl.ANY)
+    return pl.pallas_call(
+        after_kernel,
+        out_shape=[jax.ShapeDtypeStruct(v.shape, v.dtype) for v in values],
+        in_specs=[anywhere] * (len(values) + len(others)),
+        out_specs=[anywhere] * len(values),
+        input_output_aliases={i: i for i in range(len(values))},
+        compiler_params=pltpu.CompilerParams(vmem_limit_bytes=VMEM_BYTES),
+        cost_estimate=pl.CostEstimate(flops=0, bytes_accessed=0, transcendentals=0),
+    )(*values, *others)
 
 
 def first_kernel(dims, dest_ref, *refs):
@@ -170,15 +215,14 @@
     right_high = lax.ppermute(from_right[split:], "grid", to_left)
     left_high = lax.ppermute(from_left[split:], "grid", to_right)
     right_low = lax.ppermute(from_right[:split], "grid", to_left)
-    low = lax.ppermute(left_low, "grid", to_right)
-    high = lax.ppermute(right_high, "grid", to_left)
 
     live = jnp.arange(cap, dtype=jnp.int32)[None, :] < a_count.reshape(groups, 1)
     row_code = jnp.where(live, a_rows.reshape(groups, cap) + 1, 0)
     meta = jnp.concatenate([row_code, a_cols.reshape(groups, cap)], axis=1)
     meta = jnp.pad(meta.astype(jnp.bfloat16)[:, None, :], ((0, 0), (0, META - 1), (0, bs - 2 * cap)))
-    message = jnp.concatenate([a_slots.reshape(groups, cap * bs, bs), meta], axis=1)
+    message = pack(a_slots.reshape(groups, cap * bs, bs), meta)
     landed = lax.all_to_all(message, "grid", split_axis=0, concat_axis=0, tiled=True)
+    (landed,) = after([landed], early[1:3])
     parts = across_row(landed, columns)
 
     metas = jnp.stack([p[:, cap * bs, : 2 * cap] for p in parts]).astype(jnp.int32)
@@ -193,6 +237,9 @@
     dest = jnp.where(jnp.any(hit, axis=-1), dest, -1)
 
     acc, late = first_product(dest, parts, early, rb * bs, 3 * k_local, bs, cap, n_local // 4)
+    left_low, right_high = after([left_low, right_high], [acc])
+    low = lax.ppermute(left_low, "grid", to_right)
+    high = lax.ppermute(right_high, "grid", to_left)
     acc = add_product(late, 0, [left_low, left_high, right_low, right_high], acc, False)
     return add_product(late, 2, [low, high], acc, True)
 

time: 116 us -> 113 us (0.974)
  waiting for transfers between devices: 59.9 us -> 33.1 us
  Pallas kernels: 24.5 us -> 42.5 us
  local copies, waits for them, and re-layouts: 7.29 us -> 11.1 us
  starting transfers between devices: 19.3 us -> 23.1 us
  other arithmetic: 4.61 us -> 2.72 us
    pallas_call x0 -> x3, Pallas kernels: none -> 18 us  [the longest x1 18 us: pack(): pl.pallas_call(pack_kernel, out_shape=jax.ShapeDtypeStruct((groups, rows...]
    ppermute x1, waiting for transfers between devices: 10.3 us -> 0.01 us  [body(): right_high = lax.ppermute(from_right[split:], 'grid', to_left)]
    all_to_all x1, waiting for transfers between devices: 24.5 us -> 14.3 us  [body(): lax.all_to_all(message, 'grid', split_axis=0, concat_axis=0, tiled=True)]
    ppermute x2, waiting for transfers between devices: 8.37 us -> 0.01 us  [body(): from_right = lax.ppermute(from_right, 'grid', to_left)]
    ppermute x2, waiting for transfers between devices: 10.9 us -> 2.62 us  [body(): from_left = lax.ppermute(from_left, 'grid', to_right)]
    ppermute x1, waiting for transfers between devices: 0.01 us -> 6.38 us  [body(): right_low = lax.ppermute(from_right[:split], 'grid', to_left)]
    ppermute x1, starting transfers between devices: 0.28 us -> 4.36 us  [body(): left_low = lax.ppermute(from_left[:split], 'grid', to_right)]
    ppermute x1, waiting for transfers between devices: 5.47 us -> 8.25 us  [across_row(): across = lax.ppermute(landed, 'blk', swap_chip)]
  transfers between devices with their start and end apart: 14 -> 14, of which waited for: 7 -> 5; matrix products, arithmetic and copies ran while one was open for 9% -> 9% of each run, Pallas kernels for 16% -> 33%
where the time goes in v8:
time: 113 us
  Pallas kernels  42.5 us (38%)
  waiting for transfers between devices  33.1 us (29%)
  starting transfers between devices  23.1 us (20%)
  local copies, waits for them, and re-layouts  11.1 us (10%)
  other arithmetic  2.72 us (2%)
    pallas_call x1, Pallas kernels, pack(): pl.pallas_call(pack_kernel, out_shape=jax.ShapeDtypeStruct((groups, rows...  18 us
    all_to_all x1, waiting for transfers between devices, body(): lax.all_to_all(message, 'grid', split_axis=0, concat_axis=0, tiled=True)  14.3 us
    pallas_call x2, Pallas kernels, add_product(): pl.pallas_call(add_kernel, out_shape=out_shape if last else jax.ShapeDtyp...  13.4 us
    pallas_call x1, Pallas kernels, first_product(): pl.pallas_call(functools.partial(first_kernel, dims), out_shape=[jax.Shap...  11.2 us
    ppermute x1, waiting for transfers between devices, across_row(): across = lax.ppermute(landed, 'blk', swap_chip)  8.25 us
    ppermute x1, waiting for transfers between devices, body(): right_low = lax.ppermute(from_right[:split], 'grid', to_left)  6.38 us
    all_to_all x1, starting transfers between devices, body(): lax.all_to_all(message, 'grid', split_axis=0, concat_axis=0, tiled=True)  6.29 us
    ppermute x2, starting transfers between devices, body(): from_left = lax.ppermute(from_left, 'grid', to_right)  5.09 us
  transfers between devices with their start and end apart: 14, of which 5 were waited for; matrix products, arithmetic and copies ran while one was open for 9% of the time, Pallas kernels for 33%

profile of v8, /device:TPU:0, one launch (start us, length us, event | category | flops | bytes accessed | tf_op | source)
XLA Modules:
  0.0 112.8 jit_solution(17201627600540723643)
XLA Ops:
  0.0 3.0 %collective-permute-start = (bf16[512,1024]{1,0:T(8,128)(2,1)}, bf16[512,1024]{1,0:T(8,128)(2,1)S(1)}, u32[]{:S(2)}, u32[]{:S(2)}) collective-permute-start(bf16[512,1024]{1,0:T(8,128)(2,1)} %refs_4_.1), channel_id=1, source_target_pairs={{0,8},{8,16},{16,24},{24,28},{28,20},{20,12},{12,4},{4,0},{1,9},{9... | collective-permute-start | bytes 3145736 | tf_op jit(solution)/shard_map/ppermute | solution.py:210
  3.0 0.7 convert_bitcast_fusion
  3.7 0.7 fusion.11
  4.4 0.1 copy.29
  4.5 0.6 pad.4.meta_hbm
  5.1 18.0 %shard_map.64 = bf16[8,272,128]{2,1,0:T(8,128)(2,1)} custom-call(bf16[8,256,128]{2,1,0:T(8,128)(2,1)} %bitcast.17, bf16[8,16,128]{2,1,0:T(8,128)(2,1)} %pad.4.meta_hbm), custom_call_target="tpu_custom_call" | custom-call | bytes 1048576 | tf_op jit(solution)/shard_map/pallas_call | solution.py:37
  23.1 6.3 %all-to-all-start = ((bf16[8,272,128]{2,1,0:T(8,128)(2,1)}), bf16[8,272,128]{2,1,0:T(8,128)(2,1)S(1)}, u32[]{:S(2)}, u32[]{:S(2)}) async-start(bf16[8,272,128]{2,1,0:T(8,128)(2,1)} %shard_map.64), calls=%async_computation | async-start | bytes 1114112 | tf_op jit(solution)/shard_map/all_to_all | solution.py:224
  29.4 0.0 collective-permute-done.refs_1_.refs_5_
  29.4 0.0 copy-start.3
  29.4 2.1 %collective-permute-start.5 = (bf16[512,1024]{1,0:T(8,128)(2,1)S(1)}, bf16[512,1024]{1,0:T(8,128)(2,1)}, u32[]{:S(2)}, u32[]{:S(2)}) collective-permute-start(bf16[512,1024]{1,0:T(8,128)(2,1)S(1)} %collective-permute-done.refs_1_.refs_5_), channel_id=1, source_target_pairs={{0,8},{8,16},{16,24},{24,28},{28,20},{20,12},{12,4},{4,0},{1,9},{9... | collective-permute-start | bytes 3145736 | tf_op jit(solution)/shard_map/ppermute | solution.py:210
  31.5 0.1 collective-permute-start.6
  31.6 14.3 %all-to-all-done.refs_0_ = bf16[8,272,128]{2,1,0:T(8,128)(2,1)S(1)} async-done(((bf16[8,272,128]{2,1,0:T(8,128)(2,1)}), bf16[8,272,128]{2,1,0:T(8,128)(2,1)S(1)}, u32[]{:S(2)}, u32[]{:S(2)}) %all-to-all-start) | async-done | bytes 557088 | tf_op jit(solution)/shard_map/all_to_all | solution.py:224
  45.9 0.8 copy-done
  46.7 1.5 %collective-permute-start.2 = (bf16[8,272,128]{2,1,0:T(8,128)(2,1)}, bf16[8,272,128]{2,1,0:T(8,128)(2,1)S(1)}, u32[]{:S(2)}, u32[]{:S(2)}) collective-permute-start(bf16[8,272,128]{2,1,0:T(8,128)(2,1)} %shard_map.65.refs_0_), channel_id=1, source_target_pairs={{0,2},{1,3},{2,0},{3,1},{4,6},{5,7},{6,4},{7,5},{8,10},{9,11},{10,... | collective-permute-start | bytes 1671176 | tf_op jit(solution)/shard_map/ppermute | solution.py:190
  48.2 8.2 %collective-permute-done.2.refs_1_ = bf16[8,272,128]{2,1,0:T(8,128)(2,1)S(1)} collective-permute-done((bf16[8,272,128]{2,1,0:T(8,128)(2,1)}, bf16[8,272,128]{2,1,0:T(8,128)(2,1)S(1)}, u32[]{:S(2)}, u32[]{:S(2)}) %collective-permute-start.2) | collective-permute-done | bytes 557088 | tf_op jit(solution)/shard_map/ppermute | solution.py:190
  56.5 0.8 slice.40
  57.3 0.1 copy.30
  57.4 0.1 copy.34
  57.5 0.1 copy.31
  57.6 0.1 copy.35
  57.7 0.1 copy.32
  57.8 0.1 copy.36
  57.9 2.6 %collective-permute-done.5.refs_7_ = bf16[512,1024]{1,0:T(8,128)(2,1)} collective-permute-done((bf16[512,1024]{1,0:T(8,128)(2,1)S(1)}, bf16[512,1024]{1,0:T(8,128)(2,1)}, u32[]{:S(2)}, u32[]{:S(2)}) %collective-permute-start.5) | collective-permute-done | bytes 1048608 | tf_op jit(solution)/shard_map/ppermute | solution.py:210
  60.5 2.1 %fusion.13 = (bf16[256,1024]{1,0:T(8,128)(2,1)S(1)}, bf16[256,1024]{1,0:T(8,128)(2,1)}) fusion(bf16[512,1024]{1,0:T(8,128)(2,1)} %collective-permute-done.5.refs_7_), kind=kLoop, calls=%fused_computation.37 | loop fusion | bytes 2097152 | tf_op jit(solution)/shard_map/slice | solution.py:216
  62.6 4.4 %collective-permute-start.7 = (bf16[256,1024]{1,0:T(8,128)(2,1)}, bf16[256,1024]{1,0:T(8,128)(2,1)S(1)}, u32[]{:S(2)}, u32[]{:S(2)}) collective-permute-start(bf16[256,1024]{1,0:T(8,128)(2,1)} %get-tuple-element.16), channel_id=1, source_target_pairs={{0,8},{8,16},{16,24},{24,28},{28,20},{20,12},{12,4},{4,0},{1,9},{9... | collective-permute-start | bytes 1572872 | tf_op jit(solution)/shard_map/ppermute | solution.py:214
  67.0 2.3 %fusion.12 = (bf16[256,1024]{1,0:T(8,128)(2,1)}, bf16[256,1024]{1,0:T(8,128)(2,1)}) fusion(bf16[512,1024]{1,0:T(8,128)(2,1)} %collective-permute-done.6.refs_8_), kind=kLoop, calls=%fused_computation.36 | loop fusion | bytes 2097152 | tf_op jit(solution)/shard_map/slice | solution.py:217
  69.3 2.6 %collective-permute-start.11 = (bf16[256,1024]{1,0:T(8,128)(2,1)S(1)}, bf16[256,1024]{1,0:T(8,128)(2,1)}, u32[]{:S(2)}, u32[]{:S(2)}) collective-permute-start(bf16[256,1024]{1,0:T(8,128)(2,1)S(1)} %get-tuple-element.15), channel_id=1, source_target_pairs={{0,8},{8,16},{16,24},{24,28},{28,20},{20,12},{12,4},{4,0},{1,9},{9... | collective-permute-start | bytes 1572872 | tf_op jit(solution)/shard_map/ppermute | solution.py:216
  71.9 1.2 %collective-permute-start.12 = (bf16[256,1024]{1,0:T(8,128)(2,1)}, bf16[256,1024]{1,0:T(8,128)(2,1)}, u32[]{:S(2)}, u32[]{:S(2)}) collective-permute-start(bf16[256,1024]{1,0:T(8,128)(2,1)} %get-tuple-element.13), channel_id=1, source_target_pairs={{8,0},{16,8},{24,16},{28,24},{20,28},{12,20},{4,12},{0,4},{9,1},{1... | collective-permute-start | bytes 1572872 | tf_op jit(solution)/shard_map/ppermute | solution.py:217
  73.1 0.7 slice.43
  73.8 0.1 copy.33
  73.9 0.1 copy.37
  74.0 0.1 copy.38
  74.1 0.3 fusion
  74.4 0.3 compare_reduce_fusion
  74.7 0.1 copy.39
  74.8 0.1 copy.40
  74.9 0.7 fusion.6.dest_ref
  75.7 11.2 %shard_map.66 = (f32[4,1024,256]{2,1,0:T(8,128)}, bf16[1024,1536]{1,0:T(8,128)(2,1)}) custom-call(s32[4,8,2]{2,1,0:T(8,128)} %fusion.6.dest_ref, bf16[8,272,128]{2,1,0:T(8,128)(2,1)} %shard_map.65.refs_0_, bf16[8,272,128]{2,1,0:T(8,128)(2,1)} %copy-done.6, bf16[8,272,128]{2,1,0:T(8,128)(2,1)} %copy-done.7, ...), custom_call_target="tpu_custom_call" | custom-call | flops 5368709120 | bytes 9437184 | tf_op jit(solution)/shard_map/pallas_call | solution.py:127
  86.8 0.0 copy-start.1
  86.9 0.8 copy-done.1
  87.6 0.2 copy-done.2
  87.8 2.0 %collective-permute-start.10 = (bf16[256,1024]{1,0:T(8,128)(2,1)}, bf16[256,1024]{1,0:T(8,128)(2,1)S(1)}, u32[]{:S(2)}, u32[]{:S(2)}) collective-permute-start(bf16[256,1024]{1,0:T(8,128)(2,1)} %get-tuple-element.12.refs_3_), channel_id=1, source_target_pairs={{8,0},{16,8},{24,16},{28,24},{20,28},{12,20},{4,12},{0,4},{9,1},{1... | collective-permute-start | bytes 1572872 | tf_op jit(solution)/shard_map/ppermute | solution.py:242
  89.9 6.4 %collective-permute-done.12.refs_2_ = bf16[256,1024]{1,0:T(8,128)(2,1)} collective-permute-done((bf16[256,1024]{1,0:T(8,128)(2,1)}, bf16[256,1024]{1,0:T(8,128)(2,1)}, u32[]{:S(2)}, u32[]{:S(2)}) %collective-permute-start.12) | collective-permute-done | bytes 524320 | tf_op jit(solution)/shard_map/ppermute | solution.py:217
  96.3 7.8 %shard_map.68.refs_2_ = f32[4,1024,256]{2,1,0:T(8,128)} custom-call(bf16[1024,1536]{1,0:T(8,128)(2,1)} %get-tuple-element.9.left_ref, bf16[256,1024]{1,0:T(8,128)(2,1)} %get-tuple-element.11.refs_0_, bf16[256,1024]{1,0:T(8,128)(2,1)} %collective-permute-done.11.refs_1_, bf16[256,1024]{1,0:T(8,128)(2,1)} %collective-permute-done.12.refs_2_, ...), custom_call_target="tpu_custom_call" | custom-call | flops 2147483648 | bytes 12582912 | tf_op jit(solution)/shard_map/pallas_call | solution.py:167
  104.0 1.5 %collective-permute-done.10.refs_1_ = bf16[256,1024]{1,0:T(8,128)(2,1)S(1)} collective-permute-done((bf16[256,1024]{1,0:T(8,128)(2,1)}, bf16[256,1024]{1,0:T(8,128)(2,1)S(1)}, u32[]{:S(2)}, u32[]{:S(2)}) %collective-permute-start.10) | collective-permute-done | bytes 524320 | tf_op jit(solution)/shard_map/ppermute | solution.py:242
  105.6 0.8 copy-done.4
  106.4 0.8 copy-done.5
  107.2 5.6 %shard_map.69 = bf16[1024,1024]{1,0:T(8,128)(2,1)} custom-call(bf16[1024,1536]{1,0:T(8,128)(2,1)} %get-tuple-element.9.left_ref, bf16[256,1024]{1,0:T(8,128)(2,1)} %copy-done.5, bf16[256,1024]{1,0:T(8,128)(2,1)} %copy-done.4, f32[4,1024,256]{2,1,0:T(8,128)} %shard_map.68.refs_2_), custom_call_target="tpu_custom_call" | custom-call | flops 1073741824 | bytes 10485760 | tf_op jit(solution)/shard_map/pallas_call | solution.py:167
  (31 shorter events, 0.1 us)
Async XLA Ops:
  0.0 56.5 %copy-start.8 = (s32[1,8]{1,0:T(1,128)S(1)}, s32[1,8]{1,0:T(1,128)}, u32[]{:S(2)}) copy-start(s32[1,8]{1,0:T(1,128)} %param.10) | copy-start | bytes 100
  0.0 29.4 %collective-permute-start = (bf16[512,1024]{1,0:T(8,128)(2,1)}, bf16[512,1024]{1,0:T(8,128)(2,1)S(1)}, u32[]{:S(2)}, u32[]{:S(2)}) collective-permute-start(bf16[512,1024]{1,0:T(8,128)(2,1)} %refs_4_.1), channel_id=1, source_target_pairs={{0,8},{8,16},{16,24},{24,28},{28,20},{20,12},{12,4},{4,0},{1,9},{9... | collective-permute-start | bytes 3145736 | tf_op jit(solution)/shard_map/ppermute | solution.py:210
  3.0 28.5 %collective-permute-start.1 = (bf16[512,1024]{1,0:T(8,128)(2,1)}, bf16[512,1024]{1,0:T(8,128)(2,1)}, u32[]{:S(2)}, u32[]{:S(2)}) collective-permute-start(bf16[512,1024]{1,0:T(8,128)(2,1)} %refs_4_.1), channel_id=1, source_target_pairs={{8,0},{16,8},{24,16},{28,24},{20,28},{12,20},{4,12},{0,4},{9,1},{1... | collective-permute-start | bytes 3145736 | tf_op jit(solution)/shard_map/ppermute | solution.py:211
  23.1 22.8 %all-to-all-start = ((bf16[8,272,128]{2,1,0:T(8,128)(2,1)}), bf16[8,272,128]{2,1,0:T(8,128)(2,1)S(1)}, u32[]{:S(2)}, u32[]{:S(2)}) async-start(bf16[8,272,128]{2,1,0:T(8,128)(2,1)} %shard_map.64), calls=%async_computation | async-start | bytes 1114112 | tf_op jit(solution)/shard_map/all_to_all | solution.py:224
  29.4 16.5 %copy-start.3 = (bf16[512,1024]{1,0:T(8,128)(2,1)}, bf16[512,1024]{1,0:T(8,128)(2,1)S(1)}, u32[]{:S(2)}) copy-start(bf16[512,1024]{1,0:T(8,128)(2,1)S(1)} %collective-permute-done.refs_1_.refs_5_) | copy-start | bytes 3145732
  29.4 31.1 %collective-permute-start.5 = (bf16[512,1024]{1,0:T(8,128)(2,1)S(1)}, bf16[512,1024]{1,0:T(8,128)(2,1)}, u32[]{:S(2)}, u32[]{:S(2)}) collective-permute-start(bf16[512,1024]{1,0:T(8,128)(2,1)S(1)} %collective-permute-done.refs_1_.refs_5_), channel_id=1, source_target_pairs={{0,8},{8,16},{16,24},{24,28},{28,20},{20,12},{12,4},{4,0},{1,9},{9... | collective-permute-start | bytes 3145736 | tf_op jit(solution)/shard_map/ppermute | solution.py:210
  31.5 35.5 %collective-permute-start.6 = (bf16[512,1024]{1,0:T(8,128)(2,1)}, bf16[512,1024]{1,0:T(8,128)(2,1)}, u32[]{:S(2)}, u32[]{:S(2)}) collective-permute-start(bf16[512,1024]{1,0:T(8,128)(2,1)} %collective-permute-done.1.refs_2_.refs_6_), channel_id=1, source_target_pairs={{8,0},{16,8},{24,16},{28,24},{20,28},{12,20},{4,12},{0,4},{9,1},{1... | collective-permute-start | bytes 3145736 | tf_op jit(solution)/shard_map/ppermute | solution.py:211
  45.9 0.8 copy-start
  46.7 9.7 %collective-permute-start.2 = (bf16[8,272,128]{2,1,0:T(8,128)(2,1)}, bf16[8,272,128]{2,1,0:T(8,128)(2,1)S(1)}, u32[]{:S(2)}, u32[]{:S(2)}) collective-permute-start(bf16[8,272,128]{2,1,0:T(8,128)(2,1)} %shard_map.65.refs_0_), channel_id=1, source_target_pairs={{0,2},{1,3},{2,0},{3,1},{4,6},{5,7},{6,4},{7,5},{8,10},{9,11},{10,... | collective-permute-start | bytes 1671176 | tf_op jit(solution)/shard_map/ppermute | solution.py:190
  48.2 9.5 %collective-permute-start.3 = (bf16[8,272,128]{2,1,0:T(8,128)(2,1)}, bf16[8,272,128]{2,1,0:T(8,128)(2,1)S(1)}, u32[]{:S(2)}, u32[]{:S(2)}) collective-permute-start(bf16[8,272,128]{2,1,0:T(8,128)(2,1)} %shard_map.65.refs_0_), channel_id=1, source_target_pairs={{0,1},{1,0},{2,3},{3,2},{4,5},{5,4},{6,7},{7,6},{8,9},{9,8},{10,11... | collective-permute-start | bytes 1671176 | tf_op jit(solution)/shard_map/ppermute | solution.py:191
  56.5 18.4 %copy-start.6 = (bf16[8,272,128]{2,1,0:T(8,128)(2,1)}, bf16[8,272,128]{2,1,0:T(8,128)(2,1)S(1)}, u32[]{:S(2)}) copy-start(bf16[8,272,128]{2,1,0:T(8,128)(2,1)S(1)} %collective-permute-done.2.refs_1_) | copy-start | bytes 1671172
  56.5 16.6 %collective-permute-start.4 = (bf16[8,272,128]{2,1,0:T(8,128)(2,1)S(1)}, bf16[8,272,128]{2,1,0:T(8,128)(2,1)}, u32[]{:S(2)}, u32[]{:S(2)}) collective-permute-start(bf16[8,272,128]{2,1,0:T(8,128)(2,1)S(1)} %collective-permute-done.2.refs_1_), channel_id=1, source_target_pairs={{0,1},{1,0},{2,3},{3,2},{4,5},{5,4},{6,7},{7,6},{8,9},{9,8},{10,11... | collective-permute-start | bytes 1671176 | tf_op jit(solution)/shard_map/ppermute | solution.py:192
  57.7 17.2 %copy-start.7 = (bf16[8,272,128]{2,1,0:T(8,128)(2,1)}, bf16[8,272,128]{2,1,0:T(8,128)(2,1)S(1)}, u32[]{:S(2)}) copy-start(bf16[8,272,128]{2,1,0:T(8,128)(2,1)S(1)} %collective-permute-done.3.refs_2_) | copy-start | bytes 1671172
  62.6 24.2 %collective-permute-start.7 = (bf16[256,1024]{1,0:T(8,128)(2,1)}, bf16[256,1024]{1,0:T(8,128)(2,1)S(1)}, u32[]{:S(2)}, u32[]{:S(2)}) collective-permute-start(bf16[256,1024]{1,0:T(8,128)(2,1)} %get-tuple-element.16), channel_id=1, source_target_pairs={{0,8},{8,16},{16,24},{24,28},{28,20},{20,12},{12,4},{4,0},{1,9},{9... | collective-permute-start | bytes 1572872 | tf_op jit(solution)/shard_map/ppermute | solution.py:214
  69.3 17.6 %collective-permute-start.8 = (bf16[256,1024]{1,0:T(8,128)(2,1)}, bf16[256,1024]{1,0:T(8,128)(2,1)S(1)}, u32[]{:S(2)}, u32[]{:S(2)}) collective-permute-start(bf16[256,1024]{1,0:T(8,128)(2,1)} %get-tuple-element.14), channel_id=1, source_target_pairs={{8,0},{16,8},{24,16},{28,24},{20,28},{12,20},{4,12},{0,4},{9,1},{1... | collective-permute-start | bytes 1572872 | tf_op jit(solution)/shard_map/ppermute | solution.py:215
  69.3 20.6 %collective-permute-start.11 = (bf16[256,1024]{1,0:T(8,128)(2,1)S(1)}, bf16[256,1024]{1,0:T(8,128)(2,1)}, u32[]{:S(2)}, u32[]{:S(2)}) collective-permute-start(bf16[256,1024]{1,0:T(8,128)(2,1)S(1)} %get-tuple-element.15), channel_id=1, source_target_pairs={{0,8},{8,16},{16,24},{24,28},{28,20},{20,12},{12,4},{4,0},{1,9},{9... | collective-permute-start | bytes 1572872 | tf_op jit(solution)/shard_map/ppermute | solution.py:216
  71.9 24.4 %collective-permute-start.12 = (bf16[256,1024]{1,0:T(8,128)(2,1)}, bf16[256,1024]{1,0:T(8,128)(2,1)}, u32[]{:S(2)}, u32[]{:S(2)}) collective-permute-start(bf16[256,1024]{1,0:T(8,128)(2,1)} %get-tuple-element.13), channel_id=1, source_target_pairs={{8,0},{16,8},{24,16},{28,24},{20,28},{12,20},{4,12},{0,4},{9,1},{1... | collective-permute-start | bytes 1572872 | tf_op jit(solution)/shard_map/ppermute | solution.py:217
  86.8 0.8 copy-start.1
  86.8 1.0 copy-start.2
  87.8 17.7 %collective-permute-start.10 = (bf16[256,1024]{1,0:T(8,128)(2,1)}, bf16[256,1024]{1,0:T(8,128)(2,1)S(1)}, u32[]{:S(2)}, u32[]{:S(2)}) collective-permute-start(bf16[256,1024]{1,0:T(8,128)(2,1)} %get-tuple-element.12.refs_3_), channel_id=1, source_target_pairs={{8,0},{16,8},{24,16},{28,24},{20,28},{12,20},{4,12},{0,4},{9,1},{1... | collective-permute-start | bytes 1572872 | tf_op jit(solution)/shard_map/ppermute | solution.py:242
  89.9 15.7 %collective-permute-start.9 = (bf16[256,1024]{1,0:T(8,128)(2,1)}, bf16[256,1024]{1,0:T(8,128)(2,1)S(1)}, u32[]{:S(2)}, u32[]{:S(2)}) collective-permute-start(bf16[256,1024]{1,0:T(8,128)(2,1)} %get-tuple-element.11.refs_0_), channel_id=1, source_target_pairs={{0,8},{8,16},{16,24},{24,28},{28,20},{20,12},{12,4},{4,0},{1,9},{9... | collective-permute-start | bytes 1572872 | tf_op jit(solution)/shard_map/ppermute | solution.py:241
  105.6 0.8 copy-start.4
  106.4 0.8 copy-start.5

commit v9 on v8

--- a/solution.py
+++ b/solution.py
@@ -19,27 +19,24 @@
     return jnp.where(g % 2 == 0, g // 2, n - 1 - g // 2)
 
 
-def pack_kernel(slots_hbm, meta_hbm, message_hbm, sems):
-    rows = slots_hbm.shape[1]
-    copies = [
-        pltpu.make_async_copy(slots_hbm, message_hbm.at[:, pl.ds(0, rows)], sems.at[0]),
-        pltpu.make_async_copy(meta_hbm, message_hbm.at[:, pl.ds(rows, META)], sems.at[1]),
-    ]
-    for copy in copies:
-        copy.start()
-    for copy in copies:
-        copy.wait()
+def pack_kernel(slots_ref, meta_ref, message_ref):
+    rows = slots_ref.shape[1]
+    message_ref[:, :rows] = slots_ref[...]
+    message_ref[:, rows:] = meta_ref[...]
 
 
 def pack(slots, meta):
     groups, rows, width = slots.shape
-    anywhere = pl.BlockSpec(memory_space=pl.ANY)
+    part = groups // 4
     return pl.pallas_call(
         pack_kernel,
         out_shape=jax.ShapeDtypeStruct((groups, rows + META, width), slots.dtype),
-        in_specs=[anywhere] * 2,
-        out_specs=anywhere,
-        scratch_shapes=[pltpu.SemaphoreType.DMA((2,))],
+        grid=(groups // part,),
+        in_specs=[
+            pl.BlockSpec((part, rows, width), lambda i: (i, 0, 0)),
+            pl.BlockSpec((part, META, width), lambda i: (i, 0, 0)),
+        ],
+        out_specs=pl.BlockSpec((part, rows + META, width), lambda i: (i, 0, 0)),
         compiler_params=pltpu.CompilerParams(vmem_limit_bytes=VMEM_BYTES),
         cost_estimate=pl.CostEstimate(
             flops=0, bytes_accessed=slots.size * 4, transcendentals=0
@@ -151,34 +148,68 @@
     )(dest, *parts, *rights)
 
 
-def add_kernel(left_ref, *refs):
-    right = jnp.concatenate([piece[...] for piece in refs[:-2]], axis=0)
-    total = jnp.dot(left_ref[...], right, preferred_element_type=jnp.float32)
-    out_ref = refs[-1]
-    out_ref[...] = (refs[-2][0] + total).astype(out_ref.dtype).reshape(out_ref.shape)
+def add_kernel(depths, left_ref, acc_ref, *refs):
+    pieces = refs[: len(depths)]
+    out_ref, right, sems = refs[len(depths) :]
+    j = pl.program_id(0)
+    steps, _, bn = right.shape
+
+    def fetch(chunk):
+        at = 0
+        copies = []
+        for i, (depth, piece) in enumerate(zip(depths, pieces)):
+            copies.append(
+                pltpu.make_async_copy(
+                    piece.at[:, pl.ds(chunk * bn, bn)],
+                    right.at[chunk, pl.ds(at, depth)],
+                    sems.at[chunk, i],
+                )
+            )
+            at += depth
+        return copies
+
+    @pl.when(j == 0)
+    def _():
+        for chunk in range(steps):
+            for copy in fetch(chunk):
+                copy.start()
+
+    for chunk in range(steps):
+
+        @pl.when(j == chunk)
+        def _():
+            for copy in fetch(chunk):
+                copy.wait()
+
+    total = jnp.dot(left_ref[...], right[j], preferred_element_type=jnp.float32)
+    out_ref[...] = (acc_ref[0] + total).astype(out_ref.dtype).reshape(out_ref.shape)
 
 
 def add_product(left, place, pieces, acc, last):
     steps, rows, bn = acc.shape
-    inner = sum(piece.shape[0] for piece in pieces)
+    depths = [piece.shape[0] for piece in pieces]
+    inner = sum(depths)
     acc_spec = pl.BlockSpec((1, rows, bn), lambda j: (j, 0, 0))
     out_spec = pl.BlockSpec((rows, bn), lambda j: (0, j))
     out_shape = jax.ShapeDtypeStruct((rows, steps * bn), jnp.bfloat16)
     return pl.pallas_call(
-        add_kernel,
+        functools.partial(add_kernel, depths),
         out_shape=out_shape if last else jax.ShapeDtypeStruct(acc.shape, acc.dtype),
         grid=(steps,),
-        in_specs=[pl.BlockSpec((rows, inner), lambda j: (0, place))]
-        + [pl.BlockSpec((piece.shape[0], bn), lambda j: (0, j)) for piece in pieces]
-        + [acc_spec],
+        in_specs=[pl.BlockSpec((rows, inner), lambda j: (0, place)), acc_spec]
+        + [pl.BlockSpec(memory_space=pl.ANY)] * len(pieces),
         out_specs=out_spec if last else acc_spec,
+        scratch_shapes=[
+            pltpu.VMEM((steps, inner, bn), jnp.bfloat16),
+            pltpu.SemaphoreType.DMA((steps, len(pieces))),
+        ],
         compiler_params=pltpu.CompilerParams(vmem_limit_bytes=VMEM_BYTES),
         cost_estimate=pl.CostEstimate(
             flops=2 * rows * inner * steps * bn,
             bytes_accessed=(rows + steps * bn) * inner * 2 + rows * steps * bn * 8,
             transcendentals=0,
         ),
-    )(left, *pieces, acc)
+    )(left, acc, *pieces)
 
 
 def across_row(landed, columns):

time: 113 us -> 110 us (0.973)
  Pallas kernels: 42.5 us -> 28.8 us
  waiting for transfers between devices: 33.1 us -> 43.9 us
    pallas_call x1, Pallas kernels: 18 us -> 3.17 us  [pack(): pl.pallas_call(pack_kernel, out_shape=jax.ShapeDtypeStruct((groups, rows...]
    ppermute x2, waiting for transfers between devices: 2.62 us -> 14.3 us  [body(): from_left = lax.ppermute(from_left, 'grid', to_right)]
    ppermute x1, starting transfers between devices: 2.59 us -> 0.11 us  [body(): left_high = lax.ppermute(from_left[split:], 'grid', to_right)]
    all_to_all x1, waiting for transfers between devices: 14.3 us -> 11.9 us  [body(): lax.all_to_all(message, 'grid', split_axis=0, concat_axis=0, tiled=True)]
    ppermute x1, starting transfers between devices: 2.02 us -> 0.01 us  [body(): high = lax.ppermute(right_high, 'grid', to_left)]
    ppermute x1, starting transfers between devices: 0.01 us -> 2.02 us  [body(): low = lax.ppermute(left_low, 'grid', to_right)]
    ppermute x1, starting transfers between devices: 1.18 us -> 2.53 us  [body(): right_low = lax.ppermute(from_right[:split], 'grid', to_left)]
    ppermute x2, starting transfers between devices: 5.09 us -> 6.33 us  [body(): from_left = lax.ppermute(from_left, 'grid', to_right)]
  transfers between devices with their start and end apart: 14 -> 14, of which waited for: 5 -> 6; matrix products, arithmetic and copies ran while one was open for 9% -> 10% of each run, Pallas kernels for 33% -> 20%
where the time goes in v9:
time: 110 us; the launch traced here: 109 us
  waiting for transfers between devices  43.9 us (40%)
  Pallas kernels  28.8 us (26%)
  starting transfers between devices  23.3 us (21%)
  local copies, waits for them, and re-layouts  10.4 us (9%)
  other arithmetic  2.72 us (2%)
    pallas_call x2, Pallas kernels, add_product(): pl.pallas_call(functools.partial(add_kernel, depths), out_shape=out_shape...  14.5 us
    ppermute x2, waiting for transfers between devices, body(): from_left = lax.ppermute(from_left, 'grid', to_right)  14.3 us
    all_to_all x1, waiting for transfers between devices, body(): lax.all_to_all(message, 'grid', split_axis=0, concat_axis=0, tiled=True)  11.9 us
    pallas_call x1, Pallas kernels, first_product(): pl.pallas_call(functools.partial(first_kernel, dims), out_shape=[jax.Shap...  11.2 us
    ppermute x1, waiting for transfers between devices, across_row(): across = lax.ppermute(landed, 'blk', swap_chip)  9.24 us
    ppermute x1, waiting for transfers between devices, body(): right_low = lax.ppermute(from_right[:split], 'grid', to_left)  7.51 us
    ppermute x2, starting transfers between devices, body(): from_left = lax.ppermute(from_left, 'grid', to_right)  6.33 us
    all_to_all x1, starting transfers between devices, body(): lax.all_to_all(message, 'grid', split_axis=0, concat_axis=0, tiled=True)  6.28 us
  transfers between devices with their start and end apart: 14, of which 6 were waited for; matrix products, arithmetic and copies ran while one was open for 10% of the time, Pallas kernels for 20%

profile of v9, /device:TPU:0, one launch (start us, length us, event | category | flops | bytes accessed | tf_op | source)
XLA Modules:
  0.0 109.3 jit_solution(16613493966867992966)
XLA Ops:
  0.0 3.0 %collective-permute-start = (bf16[512,1024]{1,0:T(8,128)(2,1)}, bf16[512,1024]{1,0:T(8,128)(2,1)S(1)}, u32[]{:S(2)}, u32[]{:S(2)}) collective-permute-start(bf16[512,1024]{1,0:T(8,128)(2,1)} %refs_4_.1), channel_id=1, source_target_pairs={{0,8},{8,16},{16,24},{24,28},{28,20},{20,12},{12,4},{4,0},{1,9},{9... | collective-permute-start | bytes 3145736 | tf_op jit(solution)/shard_map/ppermute | solution.py:241
  3.0 0.7 convert_bitcast_fusion
  3.7 0.7 fusion.11
  4.4 0.1 copy.29
  4.5 0.6 pad.4.meta_ref
  5.1 3.2 %shard_map.64 = bf16[8,272,128]{2,1,0:T(8,128)(2,1)} custom-call(bf16[8,256,128]{2,1,0:T(8,128)(2,1)} %bitcast.17, bf16[8,16,128]{2,1,0:T(8,128)(2,1)} %pad.4.meta_ref), custom_call_target="tpu_custom_call" | custom-call | bytes 1048576 | tf_op jit(solution)/shard_map/pallas_call | solution.py:31
  8.3 6.3 %all-to-all-start = ((bf16[8,272,128]{2,1,0:T(8,128)(2,1)}), bf16[8,272,128]{2,1,0:T(8,128)(2,1)S(1)}, u32[]{:S(2)}, u32[]{:S(2)}) async-start(bf16[8,272,128]{2,1,0:T(8,128)(2,1)} %shard_map.64), calls=%async_computation | async-start | bytes 1114112 | tf_op jit(solution)/shard_map/all_to_all | solution.py:255
  14.6 12.5 %collective-permute-done.refs_1_.refs_5_ = bf16[512,1024]{1,0:T(8,128)(2,1)S(1)} collective-permute-done((bf16[512,1024]{1,0:T(8,128)(2,1)}, bf16[512,1024]{1,0:T(8,128)(2,1)S(1)}, u32[]{:S(2)}, u32[]{:S(2)}) %collective-permute-start) | collective-permute-done | bytes 1048608 | tf_op jit(solution)/shard_map/ppermute | solution.py:241
  27.1 3.3 %collective-permute-start.5 = (bf16[512,1024]{1,0:T(8,128)(2,1)S(1)}, bf16[512,1024]{1,0:T(8,128)(2,1)}, u32[]{:S(2)}, u32[]{:S(2)}) collective-permute-start(bf16[512,1024]{1,0:T(8,128)(2,1)S(1)} %collective-permute-done.refs_1_.refs_5_), channel_id=1, source_target_pairs={{0,8},{8,16},{16,24},{24,28},{28,20},{20,12},{12,4},{4,0},{1,9},{9... | collective-permute-start | bytes 3145736 | tf_op jit(solution)/shard_map/ppermute | solution.py:241
  30.4 11.9 %all-to-all-done.refs_0_ = bf16[8,272,128]{2,1,0:T(8,128)(2,1)S(1)} async-done(((bf16[8,272,128]{2,1,0:T(8,128)(2,1)}), bf16[8,272,128]{2,1,0:T(8,128)(2,1)S(1)}, u32[]{:S(2)}, u32[]{:S(2)}) %all-to-all-start) | async-done | bytes 557088 | tf_op jit(solution)/shard_map/all_to_all | solution.py:255
  42.3 0.8 copy-done
  43.1 1.5 %collective-permute-start.2 = (bf16[8,272,128]{2,1,0:T(8,128)(2,1)}, bf16[8,272,128]{2,1,0:T(8,128)(2,1)S(1)}, u32[]{:S(2)}, u32[]{:S(2)}) collective-permute-start(bf16[8,272,128]{2,1,0:T(8,128)(2,1)} %shard_map.65.refs_0_), channel_id=1, source_target_pairs={{0,2},{1,3},{2,0},{3,1},{4,6},{5,7},{6,4},{7,5},{8,10},{9,11},{10,... | collective-permute-start | bytes 1671176 | tf_op jit(solution)/shard_map/ppermute | solution.py:221
  44.6 0.0 collective-permute-start.3
  44.6 9.2 %collective-permute-done.2.refs_1_ = bf16[8,272,128]{2,1,0:T(8,128)(2,1)S(1)} collective-permute-done((bf16[8,272,128]{2,1,0:T(8,128)(2,1)}, bf16[8,272,128]{2,1,0:T(8,128)(2,1)S(1)}, u32[]{:S(2)}, u32[]{:S(2)}) %collective-permute-start.2) | collective-permute-done | bytes 557088 | tf_op jit(solution)/shard_map/ppermute | solution.py:221
  53.8 0.0 collective-permute-start.4
  53.9 0.8 slice.40
  54.7 0.1 copy.30
  54.7 0.1 copy.34
  54.9 0.1 copy.31
  55.0 0.1 copy.35
  55.1 0.1 copy.32
  55.2 0.1 copy.36
  55.3 1.8 %collective-permute-done.5.refs_7_ = bf16[512,1024]{1,0:T(8,128)(2,1)} collective-permute-done((bf16[512,1024]{1,0:T(8,128)(2,1)S(1)}, bf16[512,1024]{1,0:T(8,128)(2,1)}, u32[]{:S(2)}, u32[]{:S(2)}) %collective-permute-start.5) | collective-permute-done | bytes 1048608 | tf_op jit(solution)/shard_map/ppermute | solution.py:241
  57.1 2.1 %fusion.13 = (bf16[256,1024]{1,0:T(8,128)(2,1)S(1)}, bf16[256,1024]{1,0:T(8,128)(2,1)}) fusion(bf16[512,1024]{1,0:T(8,128)(2,1)} %collective-permute-done.5.refs_7_), kind=kLoop, calls=%fused_computation.37 | loop fusion | bytes 2097152 | tf_op jit(solution)/shard_map/slice | solution.py:247
  59.2 4.6 %collective-permute-start.7 = (bf16[256,1024]{1,0:T(8,128)(2,1)}, bf16[256,1024]{1,0:T(8,128)(2,1)S(1)}, u32[]{:S(2)}, u32[]{:S(2)}) collective-permute-start(bf16[256,1024]{1,0:T(8,128)(2,1)} %get-tuple-element.16), channel_id=1, source_target_pairs={{0,8},{8,16},{16,24},{24,28},{28,20},{20,12},{12,4},{4,0},{1,9},{9... | collective-permute-start | bytes 1572872 | tf_op jit(solution)/shard_map/ppermute | solution.py:245
  63.8 2.3 %fusion.12 = (bf16[256,1024]{1,0:T(8,128)(2,1)}, bf16[256,1024]{1,0:T(8,128)(2,1)}) fusion(bf16[512,1024]{1,0:T(8,128)(2,1)} %collective-permute-done.6.refs_8_), kind=kLoop, calls=%fused_computation.36 | loop fusion | bytes 2097152 | tf_op jit(solution)/shard_map/slice | solution.py:248
  66.0 2.5 %collective-permute-start.10 = (bf16[256,1024]{1,0:T(8,128)(2,1)}, bf16[256,1024]{1,0:T(8,128)(2,1)}, u32[]{:S(2)}, u32[]{:S(2)}) collective-permute-start(bf16[256,1024]{1,0:T(8,128)(2,1)} %get-tuple-element.13), channel_id=1, source_target_pairs={{8,0},{16,8},{24,16},{28,24},{20,28},{12,20},{4,12},{0,4},{9,1},{1... | collective-permute-start | bytes 1572872 | tf_op jit(solution)/shard_map/ppermute | solution.py:248
  68.6 0.1 collective-permute-start.9
  68.7 0.7 slice.43
  69.4 0.1 copy.33
  69.5 0.1 copy.37
  69.6 0.1 copy.38
  69.7 0.3 fusion
  70.0 0.3 compare_reduce_fusion
  70.3 0.1 copy.39
  70.4 0.1 copy.40
  70.5 0.7 fusion.6.dest_ref
  71.3 11.2 %shard_map.66 = (f32[4,1024,256]{2,1,0:T(8,128)}, bf16[1024,1536]{1,0:T(8,128)(2,1)}) custom-call(s32[4,8,2]{2,1,0:T(8,128)} %fusion.6.dest_ref, bf16[8,272,128]{2,1,0:T(8,128)(2,1)} %shard_map.65.refs_0_, bf16[8,272,128]{2,1,0:T(8,128)(2,1)} %copy-done.6, bf16[8,272,128]{2,1,0:T(8,128)(2,1)} %copy-done.7, ...), custom_call_target="tpu_custom_call" | custom-call | flops 5368709120 | bytes 9437184 | tf_op jit(solution)/shard_map/pallas_call | solution.py:124
  82.4 0.0 copy-start.1
  82.5 0.8 copy-done.1
  83.2 0.2 copy-done.2
  83.5 2.0 %collective-permute-start.11 = (bf16[256,1024]{1,0:T(8,128)(2,1)}, bf16[256,1024]{1,0:T(8,128)(2,1)S(1)}, u32[]{:S(2)}, u32[]{:S(2)}) collective-permute-start(bf16[256,1024]{1,0:T(8,128)(2,1)} %get-tuple-element.11.refs_0_), channel_id=1, source_target_pairs={{0,8},{8,16},{16,24},{24,28},{28,20},{20,12},{12,4},{4,0},{1,9},{9... | collective-permute-start | bytes 1572872 | tf_op jit(solution)/shard_map/ppermute | solution.py:272
  85.5 0.0 collective-permute-start.12
  85.5 7.5 %collective-permute-done.10.refs_2_ = bf16[256,1024]{1,0:T(8,128)(2,1)} collective-permute-done((bf16[256,1024]{1,0:T(8,128)(2,1)}, bf16[256,1024]{1,0:T(8,128)(2,1)}, u32[]{:S(2)}, u32[]{:S(2)}) %collective-permute-start.10) | collective-permute-done | bytes 524320 | tf_op jit(solution)/shard_map/ppermute | solution.py:248
  93.0 8.1 %shard_map.68.acc_ref = f32[4,1024,256]{2,1,0:T(8,128)} custom-call(bf16[1024,1536]{1,0:T(8,128)(2,1)} %get-tuple-element.9.left_ref, f32[4,1024,256]{2,1,0:T(8,128)} %get-tuple-element.10.refs_2_.acc_ref, bf16[256,1024]{1,0:T(8,128)(2,1)} %get-tuple-element.11.refs_0_, bf16[256,1024]{1,0:T(8,128)(2,1)} %collective-permute-done.9.refs_1_, ...), custom_call_target="tpu_custom_call" | custom-call | flops 2147483648 | bytes 12582912 | tf_op jit(solution)/shard_map/pallas_call | solution.py:195
  101.1 0.9 collective-permute-done.12.refs_1_
  102.1 0.8 copy-done.5
  102.9 6.4 %shard_map.69 = bf16[1024,1024]{1,0:T(8,128)(2,1)} custom-call(bf16[1024,1536]{1,0:T(8,128)(2,1)} %get-tuple-element.9.left_ref, f32[4,1024,256]{2,1,0:T(8,128)} %shard_map.68.acc_ref, bf16[256,1024]{1,0:T(8,128)(2,1)} %copy-done.4, bf16[256,1024]{1,0:T(8,128)(2,1)} %copy-done.5), custom_call_target="tpu_custom_call" | custom-call | flops 1073741824 | bytes 10485760 | tf_op jit(solution)/shard_map/pallas_call | solution.py:195
  (31 shorter events, 0.1 us)
Async XLA Ops:
  0.0 53.8 %copy-start.8 = (s32[1,8]{1,0:T(1,128)S(1)}, s32[1,8]{1,0:T(1,128)}, u32[]{:S(2)}) copy-start(s32[1,8]{1,0:T(1,128)} %param.10) | copy-start | bytes 100
  0.0 27.1 %collective-permute-start = (bf16[512,1024]{1,0:T(8,128)(2,1)}, bf16[512,1024]{1,0:T(8,128)(2,1)S(1)}, u32[]{:S(2)}, u32[]{:S(2)}) collective-permute-start(bf16[512,1024]{1,0:T(8,128)(2,1)} %refs_4_.1), channel_id=1, source_target_pairs={{0,8},{8,16},{16,24},{24,28},{28,20},{20,12},{12,4},{4,0},{1,9},{9... | collective-permute-start | bytes 3145736 | tf_op jit(solution)/shard_map/ppermute | solution.py:241
  3.0 27.4 %collective-permute-start.1 = (bf16[512,1024]{1,0:T(8,128)(2,1)}, bf16[512,1024]{1,0:T(8,128)(2,1)}, u32[]{:S(2)}, u32[]{:S(2)}) collective-permute-start(bf16[512,1024]{1,0:T(8,128)(2,1)} %refs_4_.1), channel_id=1, source_target_pairs={{8,0},{16,8},{24,16},{28,24},{20,28},{12,20},{4,12},{0,4},{9,1},{1... | collective-permute-start | bytes 3145736 | tf_op jit(solution)/shard_map/ppermute | solution.py:242
  8.3 34.0 %all-to-all-start = ((bf16[8,272,128]{2,1,0:T(8,128)(2,1)}), bf16[8,272,128]{2,1,0:T(8,128)(2,1)S(1)}, u32[]{:S(2)}, u32[]{:S(2)}) async-start(bf16[8,272,128]{2,1,0:T(8,128)(2,1)} %shard_map.64), calls=%async_computation | async-start | bytes 1114112 | tf_op jit(solution)/shard_map/all_to_all | solution.py:255
  27.1 15.2 %copy-start.3 = (bf16[512,1024]{1,0:T(8,128)(2,1)}, bf16[512,1024]{1,0:T(8,128)(2,1)S(1)}, u32[]{:S(2)}) copy-start(bf16[512,1024]{1,0:T(8,128)(2,1)S(1)} %collective-permute-done.refs_1_.refs_5_) | copy-start | bytes 3145732
  27.1 30.0 %collective-permute-start.5 = (bf16[512,1024]{1,0:T(8,128)(2,1)S(1)}, bf16[512,1024]{1,0:T(8,128)(2,1)}, u32[]{:S(2)}, u32[]{:S(2)}) collective-permute-start(bf16[512,1024]{1,0:T(8,128)(2,1)S(1)} %collective-permute-done.refs_1_.refs_5_), channel_id=1, source_target_pairs={{0,8},{8,16},{16,24},{24,28},{28,20},{20,12},{12,4},{4,0},{1,9},{9... | collective-permute-start | bytes 3145736 | tf_op jit(solution)/shard_map/ppermute | solution.py:241
  30.4 33.4 %collective-permute-start.6 = (bf16[512,1024]{1,0:T(8,128)(2,1)}, bf16[512,1024]{1,0:T(8,128)(2,1)}, u32[]{:S(2)}, u32[]{:S(2)}) collective-permute-start(bf16[512,1024]{1,0:T(8,128)(2,1)} %collective-permute-done.1.refs_2_.refs_6_), channel_id=1, source_target_pairs={{8,0},{16,8},{24,16},{28,24},{20,28},{12,20},{4,12},{0,4},{9,1},{1... | collective-permute-start | bytes 3145736 | tf_op jit(solution)/shard_map/ppermute | solution.py:242
  42.3 0.8 copy-start
  43.1 10.7 %collective-permute-start.2 = (bf16[8,272,128]{2,1,0:T(8,128)(2,1)}, bf16[8,272,128]{2,1,0:T(8,128)(2,1)S(1)}, u32[]{:S(2)}, u32[]{:S(2)}) collective-permute-start(bf16[8,272,128]{2,1,0:T(8,128)(2,1)} %shard_map.65.refs_0_), channel_id=1, source_target_pairs={{0,2},{1,3},{2,0},{3,1},{4,6},{5,7},{6,4},{7,5},{8,10},{9,11},{10,... | collective-permute-start | bytes 1671176 | tf_op jit(solution)/shard_map/ppermute | solution.py:221
  44.6 10.5 %collective-permute-start.3 = (bf16[8,272,128]{2,1,0:T(8,128)(2,1)}, bf16[8,272,128]{2,1,0:T(8,128)(2,1)S(1)}, u32[]{:S(2)}, u32[]{:S(2)}) collective-permute-start(bf16[8,272,128]{2,1,0:T(8,128)(2,1)} %shard_map.65.refs_0_), channel_id=1, source_target_pairs={{0,1},{1,0},{2,3},{3,2},{4,5},{5,4},{6,7},{7,6},{8,9},{9,8},{10,11... | collective-permute-start | bytes 1671176 | tf_op jit(solution)/shard_map/ppermute | solution.py:222
  53.8 16.7 %copy-start.6 = (bf16[8,272,128]{2,1,0:T(8,128)(2,1)}, bf16[8,272,128]{2,1,0:T(8,128)(2,1)S(1)}, u32[]{:S(2)}) copy-start(bf16[8,272,128]{2,1,0:T(8,128)(2,1)S(1)} %collective-permute-done.2.refs_1_) | copy-start | bytes 1671172
  53.8 14.8 %collective-permute-start.4 = (bf16[8,272,128]{2,1,0:T(8,128)(2,1)S(1)}, bf16[8,272,128]{2,1,0:T(8,128)(2,1)}, u32[]{:S(2)}, u32[]{:S(2)}) collective-permute-start(bf16[8,272,128]{2,1,0:T(8,128)(2,1)S(1)} %collective-permute-done.2.refs_1_), channel_id=1, source_target_pairs={{0,1},{1,0},{2,3},{3,2},{4,5},{5,4},{6,7},{7,6},{8,9},{9,8},{10,11... | collective-permute-start | bytes 1671176 | tf_op jit(solution)/shard_map/ppermute | solution.py:223
  55.1 15.5 %copy-start.7 = (bf16[8,272,128]{2,1,0:T(8,128)(2,1)}, bf16[8,272,128]{2,1,0:T(8,128)(2,1)S(1)}, u32[]{:S(2)}) copy-start(bf16[8,272,128]{2,1,0:T(8,128)(2,1)S(1)} %collective-permute-done.3.refs_2_) | copy-start | bytes 1671172
  59.2 23.2 %collective-permute-start.7 = (bf16[256,1024]{1,0:T(8,128)(2,1)}, bf16[256,1024]{1,0:T(8,128)(2,1)S(1)}, u32[]{:S(2)}, u32[]{:S(2)}) collective-permute-start(bf16[256,1024]{1,0:T(8,128)(2,1)} %get-tuple-element.16), channel_id=1, source_target_pairs={{0,8},{8,16},{16,24},{24,28},{28,20},{20,12},{12,4},{4,0},{1,9},{9... | collective-permute-start | bytes 1572872 | tf_op jit(solution)/shard_map/ppermute | solution.py:245
  66.0 16.4 %collective-permute-start.8 = (bf16[256,1024]{1,0:T(8,128)(2,1)}, bf16[256,1024]{1,0:T(8,128)(2,1)S(1)}, u32[]{:S(2)}, u32[]{:S(2)}) collective-permute-start(bf16[256,1024]{1,0:T(8,128)(2,1)} %get-tuple-element.14), channel_id=1, source_target_pairs={{8,0},{16,8},{24,16},{28,24},{20,28},{12,20},{4,12},{0,4},{9,1},{1... | collective-permute-start | bytes 1572872 | tf_op jit(solution)/shard_map/ppermute | solution.py:246
  66.0 27.0 %collective-permute-start.10 = (bf16[256,1024]{1,0:T(8,128)(2,1)}, bf16[256,1024]{1,0:T(8,128)(2,1)}, u32[]{:S(2)}, u32[]{:S(2)}) collective-permute-start(bf16[256,1024]{1,0:T(8,128)(2,1)} %get-tuple-element.13), channel_id=1, source_target_pairs={{8,0},{16,8},{24,16},{28,24},{20,28},{12,20},{4,12},{0,4},{9,1},{1... | collective-permute-start | bytes 1572872 | tf_op jit(solution)/shard_map/ppermute | solution.py:248
  68.6 24.4 %collective-permute-start.9 = (bf16[256,1024]{1,0:T(8,128)(2,1)S(1)}, bf16[256,1024]{1,0:T(8,128)(2,1)}, u32[]{:S(2)}, u32[]{:S(2)}) collective-permute-start(bf16[256,1024]{1,0:T(8,128)(2,1)S(1)} %get-tuple-element.15), channel_id=1, source_target_pairs={{0,8},{8,16},{16,24},{24,28},{28,20},{20,12},{12,4},{4,0},{1,9},{9... | collective-permute-start | bytes 1572872 | tf_op jit(solution)/shard_map/ppermute | solution.py:247
  82.4 0.8 copy-start.1
  82.5 1.0 copy-start.2
  83.5 17.6 %collective-permute-start.11 = (bf16[256,1024]{1,0:T(8,128)(2,1)}, bf16[256,1024]{1,0:T(8,128)(2,1)S(1)}, u32[]{:S(2)}, u32[]{:S(2)}) collective-permute-start(bf16[256,1024]{1,0:T(8,128)(2,1)} %get-tuple-element.11.refs_0_), channel_id=1, source_target_pairs={{0,8},{8,16},{16,24},{24,28},{28,20},{20,12},{12,4},{4,0},{1,9},{9... | collective-permute-start | bytes 1572872 | tf_op jit(solution)/shard_map/ppermute | solution.py:272
  85.5 16.6 %collective-permute-start.12 = (bf16[256,1024]{1,0:T(8,128)(2,1)}, bf16[256,1024]{1,0:T(8,128)(2,1)S(1)}, u32[]{:S(2)}, u32[]{:S(2)}) collective-permute-start(bf16[256,1024]{1,0:T(8,128)(2,1)} %get-tuple-element.12.refs_3_), channel_id=1, source_target_pairs={{8,0},{16,8},{24,16},{28,24},{20,28},{12,20},{4,12},{0,4},{9,1},{1... | collective-permute-start | bytes 1572872 | tf_op jit(solution)/shard_map/ppermute | solution.py:273
  101.1 1.0 copy-start.4
  102.1 0.8 copy-start.5

commit v10 on v9

--- a/solution.py
+++ b/solution.py
@@ -8,6 +8,7 @@
 from jax.sharding import PartitionSpec as P
 
 META = 16
+QUARTERS = 4
 VMEM_BYTES = 62 << 20
 
 
@@ -61,18 +62,19 @@
     )(*values, *others)
 
 
-def first_kernel(dims, dest_ref, *refs):
-    n_parts, n_right, per_part, cap, bs, blocks = dims
+def first_kernel(depths, per_part, cap, bs, n_parts, dest_ref, *refs):
     parts = refs[:n_parts]
-    rights = refs[n_parts : n_parts + n_right]
-    acc_hbm, late_hbm, left, right, acc, right_sem, acc_sem, late_sem = refs[n_parts + n_right :]
-    depth = blocks * bs
-    inner = n_right * depth
-    bn = acc.shape[-1]
-    fetches = [
-        pltpu.make_async_copy(source, right.at[pl.ds(i * depth, depth)], right_sem.at[i])
-        for i, source in enumerate(rights)
-    ]
+    rights = refs[n_parts : n_parts + len(depths)]
+    refs = refs[n_parts + len(depths) :]
+    accs_hbm, late_hbm = refs[:QUARTERS], refs[QUARTERS]
+    left, right, acc, right_sem, acc_sem, late_sem = refs[QUARTERS + 1 :]
+    inner, bn = right.shape[0], acc.shape[-1]
+    at, fetches = 0, []
+    for i, (depth, source) in enumerate(zip(depths, rights)):
+        fetches.append(
+            pltpu.make_async_copy(source, right.at[pl.ds(at, depth)], right_sem.at[i])
+        )
+        at += depth
     for fetch in fetches:
         fetch.start()
     left[...] = jnp.zeros_like(left)
@@ -94,50 +96,55 @@
             return carry
 
         lax.fori_loop(0, per_part, place, 0)
-    late = pltpu.make_async_copy(
-        left.at[:, pl.ds(inner, late_hbm.shape[1])], late_hbm, late_sem
-    )
-    late.start()
+    some = left.shape[0] // QUARTERS
+    stores = [
+        pltpu.make_async_copy(
+            left.at[pl.ds(q * some, some), pl.ds(inner, late_hbm.shape[1])],
+            late_hbm.at[pl.ds(q * some, some)],
+            late_sem.at[q],
+        )
+        for q in range(QUARTERS)
+    ]
+    for store in stores:
+        store.start()
     for fetch in fetches:
         fetch.wait()
-    stores = []
     for j in range(acc.shape[0]):
         acc[j] = jnp.dot(
             left[:, :inner],
             right[:, j * bn : (j + 1) * bn],
             preferred_element_type=jnp.float32,
         )
-        store = pltpu.make_async_copy(acc.at[j], acc_hbm.at[j], acc_sem.at[j])
-        store.start()
-        stores.append(store)
-    late.wait()
+        for q in range(QUARTERS):
+            store = pltpu.make_async_copy(
+                acc.at[j, pl.ds(q * some, some)], accs_hbm[q].at[j], acc_sem.at[j, q]
+            )
+            store.start()
+            stores.append(store)
     for store in stores:
         store.wait()
 
 
 def first_product(dest, parts, rights, rows, late_width, bs, cap, bn):
-    n_parts, n_right = len(parts), len(rights)
-    depth, cols = rights[0].shape
-    inner = n_right * depth
+    depths = [right.shape[0] for right in rights]
+    cols = rights[0].shape[1]
+    inner, steps = sum(depths), cols // bn
     anywhere = pl.BlockSpec(memory_space=pl.ANY)
-    dims = (n_parts, n_right, parts[0].shape[0], cap, bs, depth // bs)
-    return pl.pallas_call(
-        functools.partial(first_kernel, dims),
-        out_shape=[
-            jax.ShapeDtypeStruct((cols // bn, rows, bn), jnp.float32),
-            jax.ShapeDtypeStruct((rows, late_width), jnp.bfloat16),
-        ],
+    out = pl.pallas_call(
+        functools.partial(first_kernel, depths, parts[0].shape[0], cap, bs, len(parts)),
+        out_shape=[jax.ShapeDtypeStruct((steps, rows // QUARTERS, bn), jnp.float32)] * QUARTERS
+        + [jax.ShapeDtypeStruct((rows, late_width), jnp.bfloat16)],
         in_specs=[pl.BlockSpec(memory_space=pltpu.SMEM)]
-        + [pl.BlockSpec(memory_space=pltpu.VMEM)] * n_parts
-        + [anywhere] * n_right,
-        out_specs=[anywhere] * 2,
+        + [pl.BlockSpec(memory_space=pltpu.VMEM)] * len(parts)
+        + [anywhere] * len(rights),
+        out_specs=[anywhere] * (QUARTERS + 1),
         scratch_shapes=[
             pltpu.VMEM((rows, inner + late_width), jnp.bfloat16),
             pltpu.VMEM((inner, cols), jnp.bfloat16),
-            pltpu.VMEM((cols // bn, rows, bn), jnp.float32),
-            pltpu.SemaphoreType.DMA((n_right,)),
-            pltpu.SemaphoreType.DMA((cols // bn,)),
-            pltpu.SemaphoreType.DMA,
+            pltpu.VMEM((steps, rows, bn), jnp.float32),
+            pltpu.SemaphoreType.DMA((len(rights),)),
+            pltpu.SemaphoreType.DMA((steps, QUARTERS)),
+            pltpu.SemaphoreType.DMA((QUARTERS,)),
         ],
         compiler_params=pltpu.CompilerParams(vmem_limit_bytes=VMEM_BYTES),
         cost_estimate=pl.CostEstimate(
@@ -146,11 +153,13 @@
             transcendentals=0,
         ),
     )(dest, *parts, *rights)
-
-
-def add_kernel(depths, left_ref, acc_ref, *refs):
-    pieces = refs[: len(depths)]
-    out_ref, right, sems = refs[len(depths) :]
+    return list(out[:QUARTERS]), out[QUARTERS]
+
+
+def add_kernel(depths, *refs):
+    lefts, accs = refs[:QUARTERS], refs[QUARTERS : 2 * QUARTERS]
+    refs = refs[2 * QUARTERS :]
+    pieces, outs, (right, sems) = refs[: len(depths)], refs[len(depths) : -2], refs[-2:]
     j = pl.program_id(0)
     steps, _, bn = right.shape
 
@@ -181,24 +190,40 @@
             for copy in fetch(chunk):
                 copy.wait()
 
-    total = jnp.dot(left_ref[...], right[j], preferred_element_type=jnp.float32)
-    out_ref[...] = (acc_ref[0] + total).astype(out_ref.dtype).reshape(out_ref.shape)
-
-
-def add_product(left, place, pieces, acc, last):
-    steps, rows, bn = acc.shape
+    left = jnp.concatenate([ref[...] for ref in lefts], axis=0)
+    total = jnp.dot(left, right[j], preferred_element_type=jnp.float32)
+    some = total.shape[0] // QUARTERS
+    for q, acc in enumerate(accs):
+        part = acc[0] + total[q * some : (q + 1) * some]
+        if len(outs) == 1:
+            outs[0][q * some : (q + 1) * some] = part.astype(outs[0].dtype)
+        else:
+            outs[q][0] = part
+
+
+def add_product(left, place, pieces, accs, last):
+    steps, some, bn = accs[0].shape
+    rows = some * QUARTERS
     depths = [piece.shape[0] for piece in pieces]
     inner = sum(depths)
-    acc_spec = pl.BlockSpec((1, rows, bn), lambda j: (j, 0, 0))
-    out_spec = pl.BlockSpec((rows, bn), lambda j: (0, j))
-    out_shape = jax.ShapeDtypeStruct((rows, steps * bn), jnp.bfloat16)
+    acc_spec = pl.BlockSpec((1, some, bn), lambda j: (j, 0, 0))
+    if last:
+        out_specs = pl.BlockSpec((rows, bn), lambda j: (0, j))
+        out_shape = jax.ShapeDtypeStruct((rows, steps * bn), jnp.bfloat16)
+    else:
+        out_specs = [acc_spec] * QUARTERS
+        out_shape = [jax.ShapeDtypeStruct(accs[0].shape, accs[0].dtype)] * QUARTERS
     return pl.pallas_call(
         functools.partial(add_kernel, depths),
-        out_shape=out_shape if last else jax.ShapeDtypeStruct(acc.shape, acc.dtype),
+        out_shape=out_shape,
         grid=(steps,),
-        in_specs=[pl.BlockSpec((rows, inner), lambda j: (0, place)), acc_spec]
+        in_specs=[
+            pl.BlockSpec((some, inner), functools.partial(lambda q, j: (q, place), q))
+            for q in range(QUARTERS)
+        ]
+        + [acc_spec] * QUARTERS
         + [pl.BlockSpec(memory_space=pl.ANY)] * len(pieces),
-        out_specs=out_spec if last else acc_spec,
+        out_specs=out_specs,
         scratch_shapes=[
             pltpu.VMEM((steps, inner, bn), jnp.bfloat16),
             pltpu.SemaphoreType.DMA((steps, len(pieces))),
@@ -209,7 +234,7 @@
             bytes_accessed=(rows + steps * bn) * inner * 2 + rows * steps * bn * 8,
             transcendentals=0,
         ),
-    )(left, acc, *pieces)
+    )(*[left] * QUARTERS, *accs, *pieces)
 
 
 def across_row(landed, columns):
@@ -236,16 +261,19 @@
     order = ring_order(groups)
     to_right = [(order[i], order[(i + 1) % groups]) for i in range(groups)]
     to_left = [(order[(i + 1) % groups], order[i]) for i in range(groups)]
-    from_left, from_right, early = b_matrix, b_matrix, [b_matrix]
-    for s in range(1, half - 1):
-        from_left = lax.ppermute(from_left, "grid", to_right)
-        from_right = lax.ppermute(from_right, "grid", to_left)
-        early += [from_left, from_right]
     split = k_local // 2
-    left_low = lax.ppermute(from_left[:split], "grid", to_right)
-    right_high = lax.ppermute(from_right[split:], "grid", to_left)
-    left_high = lax.ppermute(from_left[split:], "grid", to_right)
-    right_low = lax.ppermute(from_right[:split], "grid", to_left)
+    from_left = lax.ppermute(b_matrix, "grid", to_right)
+    from_right = lax.ppermute(b_matrix, "grid", to_left)
+    steps = [[b_matrix], [from_left, from_right]]
+    left_low, left_high = from_left[:split], from_left[split:]
+    right_low, right_high = from_right[:split], from_right[split:]
+    for s in range(2, half):
+        left_low = lax.ppermute(left_low, "grid", to_right)
+        right_high = lax.ppermute(right_high, "grid", to_left)
+        left_high = lax.ppermute(left_high, "grid", to_right)
+        right_low = lax.ppermute(right_low, "grid", to_left)
+        steps.append([left_low, left_high, right_low, right_high])
+    early = sum(steps[:-1], [])
 
     live = jnp.arange(cap, dtype=jnp.int32)[None, :] < a_count.reshape(groups, 1)
     row_code = jnp.where(live, a_rows.reshape(groups, cap) + 1, 0)
@@ -253,7 +281,7 @@
     meta = jnp.pad(meta.astype(jnp.bfloat16)[:, None, :], ((0, 0), (0, META - 1), (0, bs - 2 * cap)))
     message = pack(a_slots.reshape(groups, cap * bs, bs), meta)
     landed = lax.all_to_all(message, "grid", split_axis=0, concat_axis=0, tiled=True)
-    (landed,) = after([landed], early[1:3])
+    (landed,) = after([landed], [steps[2][0], steps[2][3]])
     parts = across_row(landed, columns)
 
     metas = jnp.stack([p[:, cap * bs, : 2 * cap] for p in parts]).astype(jnp.int32)
@@ -267,12 +295,12 @@
     dest = row * (blocks * groups) + first * blocks + col % blocks
     dest = jnp.where(jnp.any(hit, axis=-1), dest, -1)
 
-    acc, late = first_product(dest, parts, early, rb * bs, 3 * k_local, bs, cap, n_local // 4)
-    left_low, right_high = after([left_low, right_high], [acc])
+    accs, late = first_product(dest, parts, early, rb * bs, 3 * k_local, bs, cap, n_local // 4)
+    left_low, right_high = after([left_low, right_high], [late])
     low = lax.ppermute(left_low, "grid", to_right)
     high = lax.ppermute(right_high, "grid", to_left)
-    acc = add_product(late, 0, [left_low, left_high, right_low, right_high], acc, False)
-    return add_product(late, 2, [low, high], acc, True)
+    accs = add_product(late, 0, [left_low, left_high, right_low, right_high], accs, False)
+    return add_product(late, 2, [low, high], accs, True)
 
 
 def solution(mesh):

time: 110 us -> 123 us (1.12)
  waiting for transfers between devices: 43.9 us -> 55.2 us
  starting transfers between devices: 23.3 us -> 26.4 us
  local copies, waits for them, and re-layouts: 10.4 us -> 9.03 us
    ppermute x8 -> x10, waiting for transfers between devices: 21.8 us -> 33.8 us  [the longest x2 14.7 us: body(): left_high = lax.ppermute(left_high, 'grid', to_right)]
    ppermute x8 -> x10, starting transfers between devices: 13.5 us -> 16.6 us  [the longest x2 5.84 us: body(): left_high = lax.ppermute(left_high, 'grid', to_right)]
    all_to_all x1, waiting for transfers between devices: 11.9 us -> 8.84 us  [body(): lax.all_to_all(message, 'grid', split_axis=0, concat_axis=0, tiled=True)]
    ppermute x1, waiting for transfers between devices: 9.24 us -> 11 us  [across_row(): across = lax.ppermute(landed, 'blk', swap_chip)]
    ppermute x1, waiting for transfers between devices: 0.01 us -> 1.48 us  [body(): low = lax.ppermute(left_low, 'grid', to_right)]
    slice x2, local copies, waits for them, and re-layouts: 4.39 us -> 3.03 us  [the longest x1 2.08 us: body(): right_low, right_high = (from_right[:split], from_right[split:])]
    ppermute x1, starting transfers between devices: 2.02 us -> 0.67 us  [body(): low = lax.ppermute(left_low, 'grid', to_right)]
    ppermute x1, starting transfers between devices: 0.01 us -> 1.36 us  [body(): high = lax.ppermute(right_high, 'grid', to_left)]
  transfers between devices with their start and end apart: 14 -> 16, of which waited for: 6 -> 9; matrix products, arithmetic and copies ran while one was open for 10% -> 7% of each run, Pallas kernels for 20% -> 18%
where the time goes in v10:
time: 123 us; the launch traced here: 122 us
  waiting for transfers between devices  55.2 us (45%)
  Pallas kernels  28.6 us (23%)
  starting transfers between devices  26.4 us (21%)
  local copies, waits for them, and re-layouts  9.03 us (7%)
  other arithmetic  2.72 us (2%)
    ppermute x2, waiting for transfers between devices, body(): left_high = lax.ppermute(left_high, 'grid', to_right)  14.7 us
    pallas_call x2, Pallas kernels, add_product(): pl.pallas_call(functools.partial(add_kernel, depths), out_shape=out_shape...  14.2 us
    ppermute x1, waiting for transfers between devices, body(): from_left = lax.ppermute(b_matrix, 'grid', to_right)  12.5 us
    pallas_call x1, Pallas kernels, first_product(): pl.pallas_call(functools.partial(first_kernel, depths, parts[0].shape[0],...  11.2 us
    ppermute x1, waiting for transfers between devices, across_row(): across = lax.ppermute(landed, 'blk', swap_chip)  11 us
    all_to_all x1, waiting for transfers between devices, body(): lax.all_to_all(message, 'grid', split_axis=0, concat_axis=0, tiled=True)  8.84 us
    all_to_all x1, starting transfers between devices, body(): lax.all_to_all(message, 'grid', split_axis=0, concat_axis=0, tiled=True)  6.28 us
    ppermute x2, starting transfers between devices, body(): left_high = lax.ppermute(left_high, 'grid', to_right)  5.84 us
  transfers between devices with their start and end apart: 16, of which 9 were waited for; matrix products, arithmetic and copies ran while one was open for 7% of the time, Pallas kernels for 18%

profile of v10, /device:TPU:0, one launch (start us, length us, event | category | flops | bytes accessed | tf_op | source)
XLA Modules:
  0.0 122.0 jit_solution(13419466099266938327)
XLA Ops:
  0.0 3.0 %collective-permute-start = (bf16[512,1024]{1,0:T(8,128)(2,1)}, bf16[512,1024]{1,0:T(8,128)(2,1)S(1)}, u32[]{:S(2)}, u32[]{:S(2)}) collective-permute-start(bf16[512,1024]{1,0:T(8,128)(2,1)} %refs_4_.1), channel_id=1, source_target_pairs={{0,8},{8,16},{16,24},{24,28},{28,20},{20,12},{12,4},{4,0},{1,9},{9... | collective-permute-start | bytes 3145736 | tf_op jit(solution)/shard_map/ppermute | solution.py:265
  3.0 0.7 convert_bitcast_fusion
  3.7 0.7 fusion.11
  4.4 0.1 copy.29
  4.5 0.6 pad.4.meta_ref
  5.1 3.2 %shard_map.64 = bf16[8,272,128]{2,1,0:T(8,128)(2,1)} custom-call(bf16[8,256,128]{2,1,0:T(8,128)(2,1)} %bitcast.17, bf16[8,16,128]{2,1,0:T(8,128)(2,1)} %pad.4.meta_ref), custom_call_target="tpu_custom_call" | custom-call | bytes 1048576 | tf_op jit(solution)/shard_map/pallas_call | solution.py:32
  8.3 6.3 %all-to-all-start = ((bf16[8,272,128]{2,1,0:T(8,128)(2,1)}), bf16[8,272,128]{2,1,0:T(8,128)(2,1)S(1)}, u32[]{:S(2)}, u32[]{:S(2)}) async-start(bf16[8,272,128]{2,1,0:T(8,128)(2,1)} %shard_map.64), calls=%async_computation | async-start | bytes 1114112 | tf_op jit(solution)/shard_map/all_to_all | solution.py:283
  14.6 12.5 %collective-permute-done.refs_5_ = bf16[512,1024]{1,0:T(8,128)(2,1)S(1)} collective-permute-done((bf16[512,1024]{1,0:T(8,128)(2,1)}, bf16[512,1024]{1,0:T(8,128)(2,1)S(1)}, u32[]{:S(2)}, u32[]{:S(2)}) %collective-permute-start) | collective-permute-done | bytes 1048608 | tf_op jit(solution)/shard_map/ppermute | solution.py:265
  27.1 1.0 fusion.13
  28.0 3.3 %collective-permute-start.1 = (bf16[256,1024]{1,0:T(8,128)(2,1)S(1)}, bf16[256,1024]{1,0:T(8,128)(2,1)}, u32[]{:S(2)}, u32[]{:S(2)}) collective-permute-start(bf16[256,1024]{1,0:T(8,128)(2,1)S(1)} %get-tuple-element.30), channel_id=1, source_target_pairs={{0,8},{8,16},{16,24},{24,28},{28,20},{20,12},{12,4},{4,0},{1,9},{9... | collective-permute-start | bytes 1572872 | tf_op jit(solution)/shard_map/ppermute | solution.py:271
  31.3 2.1 %fusion.12 = (bf16[256,1024]{1,0:T(8,128)(2,1)}, bf16[256,1024]{1,0:T(8,128)(2,1)S(1)}) fusion(bf16[512,1024]{1,0:T(8,128)(2,1)} %collective-permute-done.2.refs_6_), kind=kLoop, calls=%fused_computation.36 | loop fusion | bytes 2097152 | tf_op jit(solution)/shard_map/slice | solution.py:269
  33.4 8.8 %all-to-all-done.refs_0_ = bf16[8,272,128]{2,1,0:T(8,128)(2,1)S(1)} async-done(((bf16[8,272,128]{2,1,0:T(8,128)(2,1)}), bf16[8,272,128]{2,1,0:T(8,128)(2,1)S(1)}, u32[]{:S(2)}, u32[]{:S(2)}) %all-to-all-start) | async-done | bytes 557088 | tf_op jit(solution)/shard_map/all_to_all | solution.py:283
  42.3 3.6 %collective-permute-done.1.refs_1_.refs_7_ = bf16[256,1024]{1,0:T(8,128)(2,1)} collective-permute-done((bf16[256,1024]{1,0:T(8,128)(2,1)S(1)}, bf16[256,1024]{1,0:T(8,128)(2,1)}, u32[]{:S(2)}, u32[]{:S(2)}) %collective-permute-start.1) | collective-permute-done | bytes 524320 | tf_op jit(solution)/shard_map/ppermute | solution.py:271
  45.8 2.6 %collective-permute-done.3.refs_2_.refs_10_ = bf16[256,1024]{1,0:T(8,128)(2,1)} collective-permute-done((bf16[256,1024]{1,0:T(8,128)(2,1)S(1)}, bf16[256,1024]{1,0:T(8,128)(2,1)}, u32[]{:S(2)}, u32[]{:S(2)}) %collective-permute-start.3) | collective-permute-done | bytes 524320 | tf_op jit(solution)/shard_map/ppermute | solution.py:272
  48.4 1.5 %collective-permute-start.4 = (bf16[8,272,128]{2,1,0:T(8,128)(2,1)}, bf16[8,272,128]{2,1,0:T(8,128)(2,1)S(1)}, u32[]{:S(2)}, u32[]{:S(2)}) collective-permute-start(bf16[8,272,128]{2,1,0:T(8,128)(2,1)} %shard_map.65.refs_0_), channel_id=1, source_target_pairs={{0,2},{1,3},{2,0},{3,1},{4,6},{5,7},{6,4},{7,5},{8,10},{9,11},{10,... | collective-permute-start | bytes 1671176 | tf_op jit(solution)/shard_map/ppermute | solution.py:246
  49.9 11.0 %collective-permute-done.4.refs_1_ = bf16[8,272,128]{2,1,0:T(8,128)(2,1)S(1)} collective-permute-done((bf16[8,272,128]{2,1,0:T(8,128)(2,1)}, bf16[8,272,128]{2,1,0:T(8,128)(2,1)S(1)}, u32[]{:S(2)}, u32[]{:S(2)}) %collective-permute-start.4) | collective-permute-done | bytes 557088 | tf_op jit(solution)/shard_map/ppermute | solution.py:246
  60.9 5.2 %collective-permute-start.7 = (bf16[256,1024]{1,0:T(8,128)(2,1)}, bf16[256,1024]{1,0:T(8,128)(2,1)S(1)}, u32[]{:S(2)}, u32[]{:S(2)}) collective-permute-start(bf16[256,1024]{1,0:T(8,128)(2,1)} %get-tuple-element.29), channel_id=1, source_target_pairs={{0,8},{8,16},{16,24},{24,28},{28,20},{20,12},{12,4},{4,0},{1,9},{9... | collective-permute-start | bytes 1572872 | tf_op jit(solution)/shard_map/ppermute | solution.py:273
  66.1 0.7 slice.42
  66.9 0.1 copy.34
  67.0 0.7 collective-permute-start.10
  67.7 0.1 copy.31
  67.8 0.1 copy.35
  67.9 10.4 %collective-permute-done.7.refs_8_ = bf16[256,1024]{1,0:T(8,128)(2,1)S(1)} collective-permute-done((bf16[256,1024]{1,0:T(8,128)(2,1)}, bf16[256,1024]{1,0:T(8,128)(2,1)S(1)}, u32[]{:S(2)}, u32[]{:S(2)}) %collective-permute-start.7) | collective-permute-done | bytes 524320 | tf_op jit(solution)/shard_map/ppermute | solution.py:273
  78.3 2.4 %collective-permute-start.9 = (bf16[256,1024]{1,0:T(8,128)(2,1)}, bf16[256,1024]{1,0:T(8,128)(2,1)S(1)}, u32[]{:S(2)}, u32[]{:S(2)}) collective-permute-start(bf16[256,1024]{1,0:T(8,128)(2,1)} %collective-permute-done.1.refs_1_.refs_7_), channel_id=1, source_target_pairs={{0,8},{8,16},{16,24},{24,28},{28,20},{20,12},{12,4},{4,0},{1,9},{9... | collective-permute-start | bytes 1572872 | tf_op jit(solution)/shard_map/ppermute | solution.py:271
  80.7 0.5 collective-permute-done.8.refs_9_
  81.2 0.7 collective-permute-start.11
  81.9 1.4 %collective-permute-start.12 = (bf16[256,1024]{1,0:T(8,128)(2,1)}, bf16[256,1024]{1,0:T(8,128)(2,1)}, u32[]{:S(2)}, u32[]{:S(2)}) collective-permute-start(bf16[256,1024]{1,0:T(8,128)(2,1)} %collective-permute-done.8.refs_9_), channel_id=1, source_target_pairs={{8,0},{16,8},{24,16},{28,24},{20,28},{12,20},{4,12},{0,4},{9,1},{1... | collective-permute-start | bytes 1572872 | tf_op jit(solution)/shard_map/ppermute | solution.py:274
  83.2 0.1 copy.32
  83.3 0.1 copy.36
  83.4 0.7 slice.45
  84.4 0.1 copy.38
  84.5 0.3 fusion
  84.8 0.3 compare_reduce_fusion
  85.1 0.1 copy.39
  85.2 0.1 copy.40
  85.3 0.7 fusion.6.dest_ref
  86.0 11.2 %shard_map.66 = (f32[4,256,256]{2,1,0:T(8,128)}, f32[4,256,256]{2,1,0:T(8,128)}, f32[4,256,256]{2,1,0:T(8,128)}, f32[4,256,256]{2,1,0:T(8,128)}, bf16[1024,1536]{1,0:T(8,128)(2,1)}) custom-call(s32[4,8,2]{2,1,0:T(8,128)} %fusion.6.dest_ref, bf16[8,272,128]{2,1,0:T(8,128)(2,1)} %shard_map.65.refs_0_, bf16[8,272,128]{2,1,0:T(8,128)(2,1)} %copy-done.7, ...), custom_call_target="tpu_custom_call" | custom-call | flops 5368709120 | bytes 9437184 | tf_op jit(solution)/shard_map/pallas_call | solution.py:133
  97.3 0.8 copy-done.1
  98.1 0.2 copy-done.2
  98.2 0.7 collective-permute-start.13
  98.9 1.4 %collective-permute-start.14 = (bf16[256,1024]{1,0:T(8,128)(2,1)}, bf16[256,1024]{1,0:T(8,128)(2,1)S(1)}, u32[]{:S(2)}, u32[]{:S(2)}) collective-permute-start(bf16[256,1024]{1,0:T(8,128)(2,1)} %get-tuple-element.22.refs_11_), channel_id=1, source_target_pairs={{8,0},{16,8},{24,16},{28,24},{20,28},{12,20},{4,12},{0,4},{9,1},{1... | collective-permute-start | bytes 1572872 | tf_op jit(solution)/shard_map/ppermute | solution.py:301
  100.3 4.3 %collective-permute-done.11.refs_9_ = bf16[256,1024]{1,0:T(8,128)(2,1)S(1)} collective-permute-done((bf16[256,1024]{1,0:T(8,128)(2,1)}, bf16[256,1024]{1,0:T(8,128)(2,1)S(1)}, u32[]{:S(2)}, u32[]{:S(2)}) %collective-permute-start.11) | collective-permute-done | bytes 524320 | tf_op jit(solution)/shard_map/ppermute | solution.py:273
  104.6 0.8 copy-done.4
  105.4 7.8 %shard_map.68 = (f32[4,256,256]{2,1,0:T(8,128)}, f32[4,256,256]{2,1,0:T(8,128)}, f32[4,256,256]{2,1,0:T(8,128)}, f32[4,256,256]{2,1,0:T(8,128)}) custom-call(bf16[1024,1536]{1,0:T(8,128)(2,1)} %get-tuple-element.16.refs_2_.refs_0_.refs_1_.refs_3_, bf16[1024,1536]{1,0:T(8,128)(2,1)} %get-tuple-element.16.refs_2_.refs_0_.refs_1_.refs_3_, ...), custom_call_target="tpu_custom_call" | custom-call | flops 2147483648 | bytes 12582912 | tf_op jit(solution)/shard_map/pallas_call | solution.py:216
  113.1 1.5 %collective-permute-done.13.refs_8_ = bf16[256,1024]{1,0:T(8,128)(2,1)S(1)} collective-permute-done((bf16[256,1024]{1,0:T(8,128)(2,1)}, bf16[256,1024]{1,0:T(8,128)(2,1)S(1)}, u32[]{:S(2)}, u32[]{:S(2)}) %collective-permute-start.13) | collective-permute-done | bytes 524320 | tf_op jit(solution)/shard_map/ppermute | solution.py:300
  114.6 0.8 copy-done.5
  115.4 0.1 copy-done.6
  115.6 6.4 %shard_map.69 = bf16[1024,1024]{1,0:T(8,128)(2,1)} custom-call(bf16[1024,1536]{1,0:T(8,128)(2,1)} %get-tuple-element.16.refs_2_.refs_0_.refs_1_.refs_3_, bf16[1024,1536]{1,0:T(8,128)(2,1)} %get-tuple-element.16.refs_2_.refs_0_.refs_1_.refs_3_, bf16[1024,1536]{1,0:T(8,128)(2,1)} %get-tuple-element.16.refs_2_.refs_0_.refs_1_.refs_3_, ...), custom_call_target="tpu_custom_call" | custom-call | flops 1073741824 | bytes 10485760 | tf_op jit(solution)/shard_map/pallas_call | solution.py:216
  (39 shorter events, 0.4 us)
Async XLA Ops:
  0.0 27.1 %collective-permute-start = (bf16[512,1024]{1,0:T(8,128)(2,1)}, bf16[512,1024]{1,0:T(8,128)(2,1)S(1)}, u32[]{:S(2)}, u32[]{:S(2)}) collective-permute-start(bf16[512,1024]{1,0:T(8,128)(2,1)} %refs_4_.1), channel_id=1, source_target_pairs={{0,8},{8,16},{16,24},{24,28},{28,20},{20,12},{12,4},{4,0},{1,9},{9... | collective-permute-start | bytes 3145736 | tf_op jit(solution)/shard_map/ppermute | solution.py:265
  3.0 28.3 %collective-permute-start.2 = (bf16[512,1024]{1,0:T(8,128)(2,1)}, bf16[512,1024]{1,0:T(8,128)(2,1)}, u32[]{:S(2)}, u32[]{:S(2)}) collective-permute-start(bf16[512,1024]{1,0:T(8,128)(2,1)} %refs_4_.1), channel_id=1, source_target_pairs={{8,0},{16,8},{24,16},{28,24},{20,28},{12,20},{4,12},{0,4},{9,1},{1... | collective-permute-start | bytes 3145736 | tf_op jit(solution)/shard_map/ppermute | solution.py:266
  8.3 34.0 %all-to-all-start = ((bf16[8,272,128]{2,1,0:T(8,128)(2,1)}), bf16[8,272,128]{2,1,0:T(8,128)(2,1)S(1)}, u32[]{:S(2)}, u32[]{:S(2)}) async-start(bf16[8,272,128]{2,1,0:T(8,128)(2,1)} %shard_map.64), calls=%async_computation | async-start | bytes 1114112 | tf_op jit(solution)/shard_map/all_to_all | solution.py:283
  14.6 51.5 %copy-start.10 = (s32[1,8]{1,0:T(1,128)S(1)}, s32[1,8]{1,0:T(1,128)}, u32[]{:S(2)}) copy-start(s32[1,8]{1,0:T(1,128)} %param.10) | copy-start | bytes 100
  27.1 21.3 %copy-start.3 = (bf16[512,1024]{1,0:T(8,128)(2,1)}, bf16[512,1024]{1,0:T(8,128)(2,1)S(1)}, u32[]{:S(2)}) copy-start(bf16[512,1024]{1,0:T(8,128)(2,1)S(1)} %collective-permute-done.refs_5_) | copy-start | bytes 3145732
  28.0 17.8 %collective-permute-start.1 = (bf16[256,1024]{1,0:T(8,128)(2,1)S(1)}, bf16[256,1024]{1,0:T(8,128)(2,1)}, u32[]{:S(2)}, u32[]{:S(2)}) collective-permute-start(bf16[256,1024]{1,0:T(8,128)(2,1)S(1)} %get-tuple-element.30), channel_id=1, source_target_pairs={{0,8},{8,16},{16,24},{24,28},{28,20},{20,12},{12,4},{4,0},{1,9},{9... | collective-permute-start | bytes 1572872 | tf_op jit(solution)/shard_map/ppermute | solution.py:271
  33.4 15.0 %collective-permute-start.3 = (bf16[256,1024]{1,0:T(8,128)(2,1)S(1)}, bf16[256,1024]{1,0:T(8,128)(2,1)}, u32[]{:S(2)}, u32[]{:S(2)}) collective-permute-start(bf16[256,1024]{1,0:T(8,128)(2,1)S(1)} %get-tuple-element.28), channel_id=1, source_target_pairs={{8,0},{16,8},{24,16},{28,24},{20,28},{12,20},{4,12},{0,4},{9,1},{1... | collective-permute-start | bytes 1572872 | tf_op jit(solution)/shard_map/ppermute | solution.py:272
  42.3 6.1 %copy-start = (bf16[8,272,128]{2,1,0:T(8,128)(2,1)}, bf16[8,272,128]{2,1,0:T(8,128)(2,1)S(1)}, u32[]{:S(2)}) copy-start(bf16[8,272,128]{2,1,0:T(8,128)(2,1)S(1)} %all-to-all-done.refs_0_) | copy-start | bytes 1671172
  48.4 12.5 %collective-permute-start.4 = (bf16[8,272,128]{2,1,0:T(8,128)(2,1)}, bf16[8,272,128]{2,1,0:T(8,128)(2,1)S(1)}, u32[]{:S(2)}, u32[]{:S(2)}) collective-permute-start(bf16[8,272,128]{2,1,0:T(8,128)(2,1)} %shard_map.65.refs_0_), channel_id=1, source_target_pairs={{0,2},{1,3},{2,0},{3,1},{4,6},{5,7},{6,4},{7,5},{8,10},{9,11},{10,... | collective-permute-start | bytes 1671176 | tf_op jit(solution)/shard_map/ppermute | solution.py:246
  49.9 32.0 %collective-permute-start.5 = (bf16[8,272,128]{2,1,0:T(8,128)(2,1)}, bf16[8,272,128]{2,1,0:T(8,128)(2,1)S(1)}, u32[]{:S(2)}, u32[]{:S(2)}) collective-permute-start(bf16[8,272,128]{2,1,0:T(8,128)(2,1)} %shard_map.65.refs_0_), channel_id=1, source_target_pairs={{0,1},{1,0},{2,3},{3,2},{4,5},{5,4},{6,7},{7,6},{8,9},{9,8},{10,11... | collective-permute-start | bytes 1671176 | tf_op jit(solution)/shard_map/ppermute | solution.py:247
  60.9 24.3 %copy-start.7 = (bf16[8,272,128]{2,1,0:T(8,128)(2,1)}, bf16[8,272,128]{2,1,0:T(8,128)(2,1)S(1)}, u32[]{:S(2)}) copy-start(bf16[8,272,128]{2,1,0:T(8,128)(2,1)S(1)} %collective-permute-done.4.refs_1_) | copy-start | bytes 1671172
  60.9 22.5 %collective-permute-start.6 = (bf16[8,272,128]{2,1,0:T(8,128)(2,1)S(1)}, bf16[8,272,128]{2,1,0:T(8,128)(2,1)}, u32[]{:S(2)}, u32[]{:S(2)}) collective-permute-start(bf16[8,272,128]{2,1,0:T(8,128)(2,1)S(1)} %collective-permute-done.4.refs_1_), channel_id=1, source_target_pairs={{0,1},{1,0},{2,3},{3,2},{4,5},{5,4},{6,7},{7,6},{8,9},{9,8},{10,11... | collective-permute-start | bytes 1671176 | tf_op jit(solution)/shard_map/ppermute | solution.py:248
  60.9 17.3 %collective-permute-start.7 = (bf16[256,1024]{1,0:T(8,128)(2,1)}, bf16[256,1024]{1,0:T(8,128)(2,1)S(1)}, u32[]{:S(2)}, u32[]{:S(2)}) collective-permute-start(bf16[256,1024]{1,0:T(8,128)(2,1)} %get-tuple-element.29), channel_id=1, source_target_pairs={{0,8},{8,16},{16,24},{24,28},{28,20},{20,12},{12,4},{4,0},{1,9},{9... | collective-permute-start | bytes 1572872 | tf_op jit(solution)/shard_map/ppermute | solution.py:273
  66.1 15.1 %collective-permute-start.8 = (bf16[256,1024]{1,0:T(8,128)(2,1)}, bf16[256,1024]{1,0:T(8,128)(2,1)}, u32[]{:S(2)}, u32[]{:S(2)}) collective-permute-start(bf16[256,1024]{1,0:T(8,128)(2,1)} %get-tuple-element.27), channel_id=1, source_target_pairs={{8,0},{16,8},{24,16},{28,24},{20,28},{12,20},{4,12},{0,4},{9,1},{1... | collective-permute-start | bytes 1572872 | tf_op jit(solution)/shard_map/ppermute | solution.py:274
  67.0 30.2 %collective-permute-start.10 = (bf16[256,1024]{1,0:T(8,128)(2,1)}, bf16[256,1024]{1,0:T(8,128)(2,1)S(1)}, u32[]{:S(2)}, u32[]{:S(2)}) collective-permute-start(bf16[256,1024]{1,0:T(8,128)(2,1)} %collective-permute-done.3.refs_2_.refs_10_), channel_id=1, source_target_pairs={{8,0},{16,8},{24,16},{28,24},{20,28},{12,20},{4,12},{0,4},{9,1},{1... | collective-permute-start | bytes 1572872 | tf_op jit(solution)/shard_map/ppermute | solution.py:272
  78.3 2.4 %copy-start.9 = (bf16[256,1024]{1,0:T(8,128)(2,1)}, bf16[256,1024]{1,0:T(8,128)(2,1)S(1)}, u32[]{:S(2)}) copy-start(bf16[256,1024]{1,0:T(8,128)(2,1)S(1)} %collective-permute-done.7.refs_8_) | copy-start | bytes 1572868
  78.3 19.0 %collective-permute-start.9 = (bf16[256,1024]{1,0:T(8,128)(2,1)}, bf16[256,1024]{1,0:T(8,128)(2,1)S(1)}, u32[]{:S(2)}, u32[]{:S(2)}) collective-permute-start(bf16[256,1024]{1,0:T(8,128)(2,1)} %collective-permute-done.1.refs_1_.refs_7_), channel_id=1, source_target_pairs={{0,8},{8,16},{16,24},{24,28},{28,20},{20,12},{12,4},{4,0},{1,9},{9... | collective-permute-start | bytes 1572872 | tf_op jit(solution)/shard_map/ppermute | solution.py:271
  81.2 23.4 %collective-permute-start.11 = (bf16[256,1024]{1,0:T(8,128)(2,1)}, bf16[256,1024]{1,0:T(8,128)(2,1)S(1)}, u32[]{:S(2)}, u32[]{:S(2)}) collective-permute-start(bf16[256,1024]{1,0:T(8,128)(2,1)} %copy-done.9), channel_id=1, source_target_pairs={{0,8},{8,16},{16,24},{24,28},{28,20},{20,12},{12,4},{4,0},{1,9},{9... | collective-permute-start | bytes 1572872 | tf_op jit(solution)/shard_map/ppermute | solution.py:273
  81.9 3.4 %copy-start.8 = (bf16[8,272,128]{2,1,0:T(8,128)(2,1)}, bf16[8,272,128]{2,1,0:T(8,128)(2,1)S(1)}, u32[]{:S(2)}) copy-start(bf16[8,272,128]{2,1,0:T(8,128)(2,1)S(1)} %collective-permute-done.5.refs_2_) | copy-start | bytes 1671172
  81.9 22.7 %collective-permute-start.12 = (bf16[256,1024]{1,0:T(8,128)(2,1)}, bf16[256,1024]{1,0:T(8,128)(2,1)}, u32[]{:S(2)}, u32[]{:S(2)}) collective-permute-start(bf16[256,1024]{1,0:T(8,128)(2,1)} %collective-permute-done.8.refs_9_), channel_id=1, source_target_pairs={{8,0},{16,8},{24,16},{28,24},{20,28},{12,20},{4,12},{0,4},{9,1},{1... | collective-permute-start | bytes 1572872 | tf_op jit(solution)/shard_map/ppermute | solution.py:274
  97.3 0.8 copy-start.1
  97.3 0.9 copy-start.2
  98.2 16.4 %collective-permute-start.13 = (bf16[256,1024]{1,0:T(8,128)(2,1)}, bf16[256,1024]{1,0:T(8,128)(2,1)S(1)}, u32[]{:S(2)}, u32[]{:S(2)}) collective-permute-start(bf16[256,1024]{1,0:T(8,128)(2,1)} %get-tuple-element.21.refs_8_), channel_id=1, source_target_pairs={{0,8},{8,16},{16,24},{24,28},{28,20},{20,12},{12,4},{4,0},{1,9},{9... | collective-permute-start | bytes 1572872 | tf_op jit(solution)/shard_map/ppermute | solution.py:300
  98.9 15.7 %collective-permute-start.14 = (bf16[256,1024]{1,0:T(8,128)(2,1)}, bf16[256,1024]{1,0:T(8,128)(2,1)S(1)}, u32[]{:S(2)}, u32[]{:S(2)}) collective-permute-start(bf16[256,1024]{1,0:T(8,128)(2,1)} %get-tuple-element.22.refs_11_), channel_id=1, source_target_pairs={{8,0},{16,8},{24,16},{28,24},{20,28},{12,20},{4,12},{0,4},{9,1},{1... | collective-permute-start | bytes 1572872 | tf_op jit(solution)/shard_map/ppermute | solution.py:301
  104.6 0.8 copy-start.4
  114.6 0.8 copy-start.5
  114.6 1.0 copy-start.6

commit v11 on v10

--- a/solution.py
+++ b/solution.py
@@ -8,7 +8,7 @@
 from jax.sharding import PartitionSpec as P
 
 META = 16
-QUARTERS = 4
+PARTS = 4
 VMEM_BYTES = 62 << 20
 
 
@@ -66,8 +66,7 @@
     parts = refs[:n_parts]
     rights = refs[n_parts : n_parts + len(depths)]
     refs = refs[n_parts + len(depths) :]
-    accs_hbm, late_hbm = refs[:QUARTERS], refs[QUARTERS]
-    left, right, acc, right_sem, acc_sem, late_sem = refs[QUARTERS + 1 :]
+    acc_hbm, late_hbm, left, right, acc, right_sem, acc_sem, late_sem = refs
     inner, bn = right.shape[0], acc.shape[-1]
     at, fetches = 0, []
     for i, (depth, source) in enumerate(zip(depths, rights)):
@@ -96,14 +95,14 @@
             return carry
 
         lax.fori_loop(0, per_part, place, 0)
-    some = left.shape[0] // QUARTERS
+    some = left.shape[0] // PARTS
     stores = [
         pltpu.make_async_copy(
             left.at[pl.ds(q * some, some), pl.ds(inner, late_hbm.shape[1])],
             late_hbm.at[pl.ds(q * some, some)],
             late_sem.at[q],
         )
-        for q in range(QUARTERS)
+        for q in range(PARTS)
     ]
     for store in stores:
         store.start()
@@ -115,12 +114,9 @@
             right[:, j * bn : (j + 1) * bn],
             preferred_element_type=jnp.float32,
         )
-        for q in range(QUARTERS):
-            store = pltpu.make_async_copy(
-                acc.at[j, pl.ds(q * some, some)], accs_hbm[q].at[j], acc_sem.at[j, q]
-            )
-            store.start()
-            stores.append(store)
+        store = pltpu.make_async_copy(acc.at[j], acc_hbm.at[j], acc_sem.at[j])
+        store.start()
+        stores.append(store)
     for store in stores:
         store.wait()
 
@@ -130,21 +126,23 @@
     cols = rights[0].shape[1]
     inner, steps = sum(depths), cols // bn
     anywhere = pl.BlockSpec(memory_space=pl.ANY)
-    out = pl.pallas_call(
+    return pl.pallas_call(
         functools.partial(first_kernel, depths, parts[0].shape[0], cap, bs, len(parts)),
-        out_shape=[jax.ShapeDtypeStruct((steps, rows // QUARTERS, bn), jnp.float32)] * QUARTERS
-        + [jax.ShapeDtypeStruct((rows, late_width), jnp.bfloat16)],
+        out_shape=[
+            jax.ShapeDtypeStruct((steps, rows, bn), jnp.float32),
+            jax.ShapeDtypeStruct((rows, late_width), jnp.bfloat16),
+        ],
         in_specs=[pl.BlockSpec(memory_space=pltpu.SMEM)]
         + [pl.BlockSpec(memory_space=pltpu.VMEM)] * len(parts)
         + [anywhere] * len(rights),
-        out_specs=[anywhere] * (QUARTERS + 1),
+        out_specs=[anywhere] * 2,
         scratch_shapes=[
             pltpu.VMEM((rows, inner + late_width), jnp.bfloat16),
             pltpu.VMEM((inner, cols), jnp.bfloat16),
             pltpu.VMEM((steps, rows, bn), jnp.float32),
             pltpu.SemaphoreType.DMA((len(rights),)),
-            pltpu.SemaphoreType.DMA((steps, QUARTERS)),
-            pltpu.SemaphoreType.DMA((QUARTERS,)),
+            pltpu.SemaphoreType.DMA((steps,)),
+            pltpu.SemaphoreType.DMA((PARTS,)),
         ],
         compiler_params=pltpu.CompilerParams(vmem_limit_bytes=VMEM_BYTES),
         cost_estimate=pl.CostEstimate(
@@ -153,80 +151,82 @@
             transcendentals=0,
         ),
     )(dest, *parts, *rights)
-    return list(out[:QUARTERS]), out[QUARTERS]
-
-
-def add_kernel(depths, *refs):
-    lefts, accs = refs[:QUARTERS], refs[QUARTERS : 2 * QUARTERS]
-    refs = refs[2 * QUARTERS :]
-    pieces, outs, (right, sems) = refs[: len(depths)], refs[len(depths) : -2], refs[-2:]
-    j = pl.program_id(0)
-    steps, _, bn = right.shape
-
-    def fetch(chunk):
-        at = 0
-        copies = []
+
+
+def add_kernel(depths, place, late_hbm, acc_hbm, *refs):
+    pieces = refs[: len(depths)]
+    out_hbm, left, right, acc, out, left_sem, right_sem, acc_sem, out_sem = refs[len(depths) :]
+    steps, rows, bn = acc.shape
+    inner = left.shape[1]
+    some = rows // PARTS
+    left_copies = [
+        pltpu.make_async_copy(
+            late_hbm.at[pl.ds(q * some, some), pl.ds(place, inner)],
+            left.at[pl.ds(q * some, some)],
+            left_sem.at[q],
+        )
+        for q in range(PARTS)
+    ]
+    for copy in left_copies:
+        copy.start()
+    chunks = []
+    for j in range(steps):
+        copies, at = [], 0
         for i, (depth, piece) in enumerate(zip(depths, pieces)):
             copies.append(
                 pltpu.make_async_copy(
-                    piece.at[:, pl.ds(chunk * bn, bn)],
-                    right.at[chunk, pl.ds(at, depth)],
-                    sems.at[chunk, i],
+                    piece.at[:, pl.ds(j * bn, bn)],
+                    right.at[j, pl.ds(at, depth)],
+                    right_sem.at[j, i],
                 )
             )
             at += depth
-        return copies
-
-    @pl.when(j == 0)
-    def _():
-        for chunk in range(steps):
-            for copy in fetch(chunk):
-                copy.start()
-
-    for chunk in range(steps):
-
-        @pl.when(j == chunk)
-        def _():
-            for copy in fetch(chunk):
-                copy.wait()
-
-    left = jnp.concatenate([ref[...] for ref in lefts], axis=0)
-    total = jnp.dot(left, right[j], preferred_element_type=jnp.float32)
-    some = total.shape[0] // QUARTERS
-    for q, acc in enumerate(accs):
-        part = acc[0] + total[q * some : (q + 1) * some]
-        if len(outs) == 1:
-            outs[0][q * some : (q + 1) * some] = part.astype(outs[0].dtype)
+        copies.append(pltpu.make_async_copy(acc_hbm.at[j], acc.at[j], acc_sem.at[j]))
+        for copy in copies:
+            copy.start()
+        chunks.append(copies)
+    for copy in left_copies:
+        copy.wait()
+    stores = []
+    for j in range(steps):
+        for copy in chunks[j]:
+            copy.wait()
+        total = jnp.dot(left[...], right[j], preferred_element_type=jnp.float32)
+        out[j] = (acc[j] + total).astype(out.dtype)
+        if len(out_hbm.shape) == 2:
+            target = out_hbm.at[:, pl.ds(j * bn, bn)]
         else:
-            outs[q][0] = part
-
-
-def add_product(left, place, pieces, accs, last):
-    steps, some, bn = accs[0].shape
-    rows = some * QUARTERS
+            target = out_hbm.at[j]
+        store = pltpu.make_async_copy(out.at[j], target, out_sem.at[j])
+        store.start()
+        stores.append(store)
+    for store in stores:
+        store.wait()
+
+
+def add_product(late, place, pieces, acc, last):
+    steps, rows, bn = acc.shape
     depths = [piece.shape[0] for piece in pieces]
     inner = sum(depths)
-    acc_spec = pl.BlockSpec((1, some, bn), lambda j: (j, 0, 0))
+    anywhere = pl.BlockSpec(memory_space=pl.ANY)
     if last:
-        out_specs = pl.BlockSpec((rows, bn), lambda j: (0, j))
         out_shape = jax.ShapeDtypeStruct((rows, steps * bn), jnp.bfloat16)
     else:
-        out_specs = [acc_spec] * QUARTERS
-        out_shape = [jax.ShapeDtypeStruct(accs[0].shape, accs[0].dtype)] * QUARTERS
-    return pl.pallas_call(
-        functools.partial(add_kernel, depths),
+        out_shape = jax.ShapeDtypeStruct(acc.shape, acc.dtype)
+    return pl.pallas_call(
+        functools.partial(add_kernel, depths, place),
         out_shape=out_shape,
-        grid=(steps,),
-        in_specs=[
-            pl.BlockSpec((some, inner), functools.partial(lambda q, j: (q, place), q))
-            for q in range(QUARTERS)
-        ]
-        + [acc_spec] * QUARTERS
-        + [pl.BlockSpec(memory_space=pl.ANY)] * len(pieces),
-        out_specs=out_specs,
+        in_specs=[anywhere] * (2 + len(pieces)),
+        out_specs=anywhere,
         scratch_shapes=[
+            pltpu.VMEM((rows, inner), jnp.bfloat16),
             pltpu.VMEM((steps, inner, bn), jnp.bfloat16),
+            pltpu.VMEM((steps, rows, bn), jnp.float32),
+            pltpu.VMEM((steps, rows, bn), out_shape.dtype),
+            pltpu.SemaphoreType.DMA((PARTS,)),
             pltpu.SemaphoreType.DMA((steps, len(pieces))),
+            pltpu.SemaphoreType.DMA((steps,)),
+            pltpu.SemaphoreType.DMA((steps,)),
         ],
         compiler_params=pltpu.CompilerParams(vmem_limit_bytes=VMEM_BYTES),
         cost_estimate=pl.CostEstimate(
@@ -234,7 +234,44 @@
             bytes_accessed=(rows + steps * bn) * inner * 2 + rows * steps * bn * 8,
             transcendentals=0,
         ),
-    )(*[left] * QUARTERS, *accs, *pieces)
+    )(late, acc, *pieces)
+
+
+def rest_kernel(start, block_hbm, _, out_hbm, held, in_sem, out_sem):
+    some = held.shape[0] // PARTS
+    loads, stores = [], []
+    for q in range(PARTS):
+        rows = pl.ds(q * some, some)
+        source = block_hbm.at[pl.ds(start + q * some, some)]
+        loads.append(pltpu.make_async_copy(source, held.at[rows], in_sem.at[q]))
+        stores.append(pltpu.make_async_copy(held.at[rows], out_hbm.at[rows], out_sem.at[q]))
+    for load in loads:
+        load.start()
+    for load, store in zip(loads, stores):
+        load.wait()
+        store.start()
+    for store in stores:
+        store.wait()
+
+
+def rest(block, start, size, ahead):
+    anywhere = pl.BlockSpec(memory_space=pl.ANY)
+    shape = (size, block.shape[1])
+    return pl.pallas_call(
+        functools.partial(rest_kernel, start),
+        out_shape=jax.ShapeDtypeStruct(shape, block.dtype),
+        in_specs=[anywhere] * 2,
+        out_specs=anywhere,
+        scratch_shapes=[
+            pltpu.VMEM(shape, block.dtype),
+            pltpu.SemaphoreType.DMA((PARTS,)),
+            pltpu.SemaphoreType.DMA((PARTS,)),
+        ],
+        compiler_params=pltpu.CompilerParams(vmem_limit_bytes=VMEM_BYTES),
+        cost_estimate=pl.CostEstimate(
+            flops=0, bytes_accessed=size * block.shape[1] * 4, transcendentals=0
+        ),
+    )(block, ahead)
 
 
 def across_row(landed, columns):
@@ -261,19 +298,19 @@
     order = ring_order(groups)
     to_right = [(order[i], order[(i + 1) % groups]) for i in range(groups)]
     to_left = [(order[(i + 1) % groups], order[i]) for i in range(groups)]
+    from_left, from_right, early = b_matrix, b_matrix, [b_matrix]
+    for s in range(1, half - 1):
+        from_left = lax.ppermute(from_left, "grid", to_right)
+        from_right = lax.ppermute(from_right, "grid", to_left)
+        early += [from_left, from_right]
     split = k_local // 2
-    from_left = lax.ppermute(b_matrix, "grid", to_right)
-    from_right = lax.ppermute(b_matrix, "grid", to_left)
-    steps = [[b_matrix], [from_left, from_right]]
-    left_low, left_high = from_left[:split], from_left[split:]
-    right_low, right_high = from_right[:split], from_right[split:]
-    for s in range(2, half):
-        left_low = lax.ppermute(left_low, "grid", to_right)
-        right_high = lax.ppermute(right_high, "grid", to_left)
-        left_high = lax.ppermute(left_high, "grid", to_right)
-        right_low = lax.ppermute(right_low, "grid", to_left)
-        steps.append([left_low, left_high, right_low, right_high])
-    early = sum(steps[:-1], [])
+    left_low, right_high = from_left[:split], from_right[split:]
+    left_high = rest(from_left, split, split, left_low)
+    right_low = rest(from_right, 0, split, right_high)
+    left_low = lax.ppermute(left_low, "grid", to_right)
+    right_high = lax.ppermute(right_high, "grid", to_left)
+    left_high = lax.ppermute(left_high, "grid", to_right)
+    right_low = lax.ppermute(right_low, "grid", to_left)
 
     live = jnp.arange(cap, dtype=jnp.int32)[None, :] < a_count.reshape(groups, 1)
     row_code = jnp.where(live, a_rows.reshape(groups, cap) + 1, 0)
@@ -281,7 +318,7 @@
     meta = jnp.pad(meta.astype(jnp.bfloat16)[:, None, :], ((0, 0), (0, META - 1), (0, bs - 2 * cap)))
     message = pack(a_slots.reshape(groups, cap * bs, bs), meta)
     landed = lax.all_to_all(message, "grid", split_axis=0, concat_axis=0, tiled=True)
-    (landed,) = after([landed], [steps[2][0], steps[2][3]])
+    (landed,) = after([landed], early[1:3])
     parts = across_row(landed, columns)
 
     metas = jnp.stack([p[:, cap * bs, : 2 * cap] for p in parts]).astype(jnp.int32)
@@ -295,12 +332,12 @@
     dest = row * (blocks * groups) + first * blocks + col % blocks
     dest = jnp.where(jnp.any(hit, axis=-1), dest, -1)
 
-    accs, late = first_product(dest, parts, early, rb * bs, 3 * k_local, bs, cap, n_local // 4)
+    acc, late = first_product(dest, parts, early, rb * bs, 3 * k_local, bs, cap, n_local // 4)
     left_low, right_high = after([left_low, right_high], [late])
     low = lax.ppermute(left_low, "grid", to_right)
     high = lax.ppermute(right_high, "grid", to_left)
-    accs = add_product(late, 0, [left_low, left_high, right_low, right_high], accs, False)
-    return add_product(late, 2, [low, high], accs, True)
+    acc = add_product(late, 0, [left_low, left_high, right_low, right_high], acc, False)
+    return add_product(late, 2 * k_local, [low, high], acc, True)
 
 
 def solution(mesh):

time: 123 us -> 111 us (0.902)
  waiting for transfers between devices: 55.2 us -> 19.7 us
  blocking collectives: 0 us -> 32.6 us
  starting transfers between devices: 26.4 us -> 12.8 us
  Pallas kernels: 28.6 us -> 33.6 us
    all_to_all x0 -> x1, blocking collectives: none -> 32.6 us  [body(): lax.all_to_all(message, 'grid', split_axis=0, concat_axis=0, tiled=True)]
    ppermute x2 -> x1, waiting for transfers between devices: 14.7 us -> 0.01 us  [body(): left_high = lax.ppermute(left_high, 'grid', to_right)]
    all_to_all x1 -> x0, waiting for transfers between devices: 8.84 us -> none  [body(): lax.all_to_all(message, 'grid', split_axis=0, concat_axis=0, tiled=True)]
    all_to_all x1 -> x0, starting transfers between devices: 6.28 us -> none  [body(): lax.all_to_all(message, 'grid', split_axis=0, concat_axis=0, tiled=True)]
    ppermute x2 -> x1, starting transfers between devices: 5.69 us -> 0.42 us  [body(): left_low = lax.ppermute(left_low, 'grid', to_right)]
    ppermute x2 -> x1, starting transfers between devices: 5.84 us -> 0.68 us  [body(): left_high = lax.ppermute(left_high, 'grid', to_right)]
    pallas_call x2 -> x4, Pallas kernels: 14.2 us -> 19.3 us  [the longest x2 15.6 us: add_product(): pl.pallas_call(functools.partial(add_kernel, depths, place), out_shape=ou...]
    ppermute x2 -> x4, waiting for transfers between devices: 12.5 us -> 8.84 us  [the longest x2 8.84 us: body(): from_left = lax.ppermute(from_left, 'grid', to_right)]
  transfers between devices with their start and end apart: 16 -> 13, of which waited for: 9 -> 3; matrix products, arithmetic and copies ran while one was open for 7% -> 8% of each run, Pallas kernels for 18% -> 25%
where the time goes in v11:
time: 111 us
  Pallas kernels  33.6 us (30%)
  blocking collectives  32.6 us (29%)
  waiting for transfers between devices  19.7 us (18%)
  starting transfers between devices  12.8 us (12%)
  local copies, waits for them, and re-layouts  9.18 us (8%)
  other arithmetic  2.72 us (2%)
    all_to_all x1, blocking collectives, body(): lax.all_to_all(message, 'grid', split_axis=0, concat_axis=0, tiled=True)  32.6 us
    pallas_call x2, Pallas kernels, add_product(): pl.pallas_call(functools.partial(add_kernel, depths, place), out_shape=ou...  15.6 us
    pallas_call x1, Pallas kernels, first_product(): pl.pallas_call(functools.partial(first_kernel, depths, parts[0].shape[0],...  11.1 us
    ppermute x1, waiting for transfers between devices, across_row(): across = lax.ppermute(landed, 'blk', swap_chip)  9.79 us
    ppermute x2, waiting for transfers between devices, body(): from_left = lax.ppermute(from_left, 'grid', to_right)  8.84 us
    pallas_call x2, Pallas kernels, rest(): pl.pallas_call(functools.partial(rest_kernel, start), out_shape=jax.Shape...  3.63 us
    unnamed x14, local copies, waits for them, and re-layouts  3.59 us
    ppermute x2, starting transfers between devices, body(): from_left = lax.ppermute(from_left, 'grid', to_right)  3.5 us
  transfers between devices with their start and end apart: 13, of which 3 were waited for; matrix products, arithmetic and copies ran while one was open for 8% of the time, Pallas kernels for 25%

profile of v11, /device:TPU:0, one launch (start us, length us, event | category | flops | bytes accessed | tf_op | source)
XLA Modules:
  0.0 110.7 jit_solution(9143109368378196469)
XLA Ops:
  0.0 3.0 %collective-permute-start = (bf16[512,1024]{1,0:T(8,128)(2,1)}, bf16[512,1024]{1,0:T(8,128)(2,1)S(1)}, u32[]{:S(2)}, u32[]{:S(2)}) collective-permute-start(bf16[512,1024]{1,0:T(8,128)(2,1)} %refs_4_.1), channel_id=1, source_target_pairs={{0,8},{8,16},{16,24},{24,28},{28,20},{20,12},{12,4},{4,0},{1,9},{9... | collective-permute-start | bytes 3145736 | tf_op jit(solution)/shard_map/ppermute | solution.py:303
  3.0 0.7 convert_bitcast_fusion
  3.7 0.7 fusion.11
  4.4 0.1 copy.29
  4.5 0.6 pad.4.meta_ref
  5.1 3.2 %shard_map.64 = bf16[8,272,128]{2,1,0:T(8,128)(2,1)} custom-call(bf16[8,256,128]{2,1,0:T(8,128)(2,1)} %bitcast.17, bf16[8,16,128]{2,1,0:T(8,128)(2,1)} %pad.4.meta_ref), custom_call_target="tpu_custom_call" | custom-call | bytes 1048576 | tf_op jit(solution)/shard_map/pallas_call | solution.py:32
  8.3 32.6 %all_to_all.5.refs_0_ = bf16[8,272,128]{2,1,0:T(8,128)(2,1)} all-to-all(bf16[8,272,128]{2,1,0:T(8,128)(2,1)} %shard_map.64), channel_id=1, replica_groups=mesh['grid'=8,'blk'=4] {'grid'}, dimensions={0} | all-to-all | bytes 1114112 | tf_op jit(solution)/shard_map/all_to_all | solution.py:320
  40.9 0.0 collective-permute-done.refs_1_.refs_5_
  40.9 1.0 copy-done.3
  41.9 1.5 %collective-permute-start.2 = (bf16[8,272,128]{2,1,0:T(8,128)(2,1)}, bf16[8,272,128]{2,1,0:T(8,128)(2,1)}, u32[]{:S(2)}, u32[]{:S(2)}) collective-permute-start(bf16[8,272,128]{2,1,0:T(8,128)(2,1)} %shard_map.65.refs_0_), channel_id=1, source_target_pairs={{0,2},{1,3},{2,0},{3,1},{4,6},{5,7},{6,4},{7,5},{8,10},{9,11},{10,... | collective-permute-start | bytes 1671176 | tf_op jit(solution)/shard_map/ppermute | solution.py:283
  43.4 0.5 collective-permute-start.5
  43.9 1.5 %collective-permute-start.6 = (bf16[512,1024]{1,0:T(8,128)(2,1)}, bf16[512,1024]{1,0:T(8,128)(2,1)S(1)}, u32[]{:S(2)}, u32[]{:S(2)}) collective-permute-start(bf16[512,1024]{1,0:T(8,128)(2,1)} %collective-permute-done.1.refs_2_.refs_6_), channel_id=1, source_target_pairs={{8,0},{16,8},{24,16},{28,24},{20,28},{12,20},{4,12},{0,4},{9,1},{1... | collective-permute-start | bytes 3145736 | tf_op jit(solution)/shard_map/ppermute | solution.py:304
  45.4 9.8 %collective-permute-done.2.refs_1_ = bf16[8,272,128]{2,1,0:T(8,128)(2,1)} collective-permute-done((bf16[8,272,128]{2,1,0:T(8,128)(2,1)}, bf16[8,272,128]{2,1,0:T(8,128)(2,1)}, u32[]{:S(2)}, u32[]{:S(2)}) %collective-permute-start.2) | collective-permute-done | bytes 557088 | tf_op jit(solution)/shard_map/ppermute | solution.py:283
  55.2 0.7 slice.32
  55.9 0.1 copy.30
  56.0 0.1 copy.34
  56.1 0.8 slice.33
  56.9 0.1 copy.31
  57.0 0.1 copy.35
  57.1 0.7 slice.34
  57.8 0.1 copy.32
  57.9 0.1 copy.36
  58.0 8.8 %collective-permute-done.5.refs_7_.block_hbm = bf16[512,1024]{1,0:T(8,128)(2,1)S(1)} collective-permute-done((bf16[512,1024]{1,0:T(8,128)(2,1)}, bf16[512,1024]{1,0:T(8,128)(2,1)S(1)}, u32[]{:S(2)}, u32[]{:S(2)}) %collective-permute-start.5) | collective-permute-done | bytes 1048608 | tf_op jit(solution)/shard_map/ppermute | solution.py:303
  66.9 0.4 collective-permute-start.7
  67.3 1.0 copy-done.1
  68.3 0.8 slice.39._
  69.2 1.6 %collective-permute-start.8 = (bf16[256,1024]{1,0:T(8,128)(2,1)}, bf16[256,1024]{1,0:T(8,128)(2,1)}, u32[]{:S(2)}, u32[]{:S(2)}) collective-permute-start(bf16[256,1024]{1,0:T(8,128)(2,1)} %slice.39._), channel_id=1, source_target_pairs={{8,0},{16,8},{24,16},{28,24},{20,28},{12,20},{4,12},{0,4},{9,1},{1... | collective-permute-start | bytes 1572872 | tf_op jit(solution)/shard_map/ppermute | solution.py:311
  70.8 1.8 %shard_map.69 = bf16[256,1024]{1,0:T(8,128)(2,1)} custom-call(bf16[512,1024]{1,0:T(8,128)(2,1)} %copy-done.1, bf16[256,1024]{1,0:T(8,128)(2,1)} %slice.39._), custom_call_target="tpu_custom_call" | custom-call | bytes 1048576 | tf_op jit(solution)/shard_map/pallas_call | solution.py:260
  72.6 1.4 %collective-permute-start.10 = (bf16[256,1024]{1,0:T(8,128)(2,1)}, bf16[256,1024]{1,0:T(8,128)(2,1)}, u32[]{:S(2)}, u32[]{:S(2)}) collective-permute-start(bf16[256,1024]{1,0:T(8,128)(2,1)} %shard_map.69), channel_id=1, source_target_pairs={{8,0},{16,8},{24,16},{28,24},{20,28},{12,20},{4,12},{0,4},{9,1},{1... | collective-permute-start | bytes 1572872 | tf_op jit(solution)/shard_map/ppermute | solution.py:313
  74.1 1.8 %shard_map.68 = bf16[256,1024]{1,0:T(8,128)(2,1)} custom-call(bf16[512,1024]{1,0:T(8,128)(2,1)} %copy-done, bf16[256,1024]{1,0:T(8,128)(2,1)} %copy-done.2), custom_call_target="tpu_custom_call" | custom-call | bytes 1048576 | tf_op jit(solution)/shard_map/pallas_call | solution.py:260
  75.9 0.7 collective-permute-start.9
  76.6 0.7 slice.35
  77.3 0.1 copy.33
  77.4 0.1 copy.37
  77.5 0.1 copy.38
  77.6 0.3 fusion
  77.9 0.3 compare_reduce_fusion
  78.2 0.1 copy.39
  78.3 0.1 copy.40
  78.4 0.7 fusion.6.dest_ref
  79.2 11.1 %shard_map.66 = (f32[4,1024,256]{2,1,0:T(8,128)}, bf16[1024,1536]{1,0:T(8,128)(2,1)}) custom-call(s32[4,8,2]{2,1,0:T(8,128)} %fusion.6.dest_ref, bf16[8,272,128]{2,1,0:T(8,128)(2,1)} %shard_map.65.refs_0_, bf16[8,272,128]{2,1,0:T(8,128)(2,1)} %collective-permute-done.2.refs_1_, bf16[8,272,128]{2,1,0:T(8,128)(2,1)} %collective-permute-done.3.refs_2_, ...), custom_call_target="tpu_custom_call" | custom-call | flops 5368709120 | bytes 9437184 | tf_op jit(solution)/shard_map/pallas_call | solution.py:129
  90.3 0.5 collective-permute-start.11
  90.8 1.6 %collective-permute-start.12 = (bf16[256,1024]{1,0:T(8,128)(2,1)}, bf16[256,1024]{1,0:T(8,128)(2,1)S(1)}, u32[]{:S(2)}, u32[]{:S(2)}) collective-permute-start(bf16[256,1024]{1,0:T(8,128)(2,1)} %get-tuple-element.12.refs_3_), channel_id=1, source_target_pairs={{8,0},{16,8},{24,16},{28,24},{20,28},{12,20},{4,12},{0,4},{9,1},{1... | collective-permute-start | bytes 1572872 | tf_op jit(solution)/shard_map/ppermute | solution.py:338
  92.4 1.0 collective-permute-done.10.refs_2_
  93.4 9.4 %shard_map.70.acc_hbm = f32[4,1024,256]{2,1,0:T(8,128)} custom-call(bf16[1024,1536]{1,0:T(8,128)(2,1)} %get-tuple-element.9.refs_2_.late_hbm, f32[4,1024,256]{2,1,0:T(8,128)} %get-tuple-element.10.acc_hbm, bf16[256,1024]{1,0:T(8,128)(2,1)} %get-tuple-element.11.refs_0_, bf16[256,1024]{1,0:T(8,128)(2,1)} %collective-permute-done.9.refs_1_, ...), custom_call_target="tpu_custom_call" | custom-call | flops 2147483648 | bytes 12582912 | tf_op jit(solution)/shard_map/pallas_call | solution.py:216
  102.8 0.8 copy-done.4
  103.6 0.8 copy-done.5
  104.4 6.3 %shard_map.71 = bf16[1024,1024]{1,0:T(8,128)(2,1)} custom-call(bf16[1024,1536]{1,0:T(8,128)(2,1)} %get-tuple-element.9.refs_2_.late_hbm, f32[4,1024,256]{2,1,0:T(8,128)} %shard_map.70.acc_hbm, bf16[256,1024]{1,0:T(8,128)(2,1)} %copy-done.4, bf16[256,1024]{1,0:T(8,128)(2,1)} %copy-done.5), custom_call_target="tpu_custom_call" | custom-call | flops 1073741824 | bytes 10485760 | tf_op jit(solution)/shard_map/pallas_call | solution.py:216
  (28 shorter events, 0.1 us)
Async XLA Ops:
  0.0 55.2 %copy-start.6 = (s32[1,8]{1,0:T(1,128)S(1)}, s32[1,8]{1,0:T(1,128)}, u32[]{:S(2)}) copy-start(s32[1,8]{1,0:T(1,128)} %param.10) | copy-start | bytes 100
  0.0 40.9 %collective-permute-start = (bf16[512,1024]{1,0:T(8,128)(2,1)}, bf16[512,1024]{1,0:T(8,128)(2,1)S(1)}, u32[]{:S(2)}, u32[]{:S(2)}) collective-permute-start(bf16[512,1024]{1,0:T(8,128)(2,1)} %refs_4_.1), channel_id=1, source_target_pairs={{0,8},{8,16},{16,24},{24,28},{28,20},{20,12},{12,4},{4,0},{1,9},{9... | collective-permute-start | bytes 3145736 | tf_op jit(solution)/shard_map/ppermute | solution.py:303
  3.0 37.9 %collective-permute-start.1 = (bf16[512,1024]{1,0:T(8,128)(2,1)}, bf16[512,1024]{1,0:T(8,128)(2,1)}, u32[]{:S(2)}, u32[]{:S(2)}) collective-permute-start(bf16[512,1024]{1,0:T(8,128)(2,1)} %refs_4_.1), channel_id=1, source_target_pairs={{8,0},{16,8},{24,16},{28,24},{20,28},{12,20},{4,12},{0,4},{9,1},{1... | collective-permute-start | bytes 3145736 | tf_op jit(solution)/shard_map/ppermute | solution.py:304
  40.9 1.0 copy-start.3
  41.9 13.3 %collective-permute-start.2 = (bf16[8,272,128]{2,1,0:T(8,128)(2,1)}, bf16[8,272,128]{2,1,0:T(8,128)(2,1)}, u32[]{:S(2)}, u32[]{:S(2)}) collective-permute-start(bf16[8,272,128]{2,1,0:T(8,128)(2,1)} %shard_map.65.refs_0_), channel_id=1, source_target_pairs={{0,2},{1,3},{2,0},{3,1},{4,6},{5,7},{6,4},{7,5},{8,10},{9,11},{10,... | collective-permute-start | bytes 1671176 | tf_op jit(solution)/shard_map/ppermute | solution.py:283
  43.4 23.5 %collective-permute-start.5 = (bf16[512,1024]{1,0:T(8,128)(2,1)}, bf16[512,1024]{1,0:T(8,128)(2,1)S(1)}, u32[]{:S(2)}, u32[]{:S(2)}) collective-permute-start(bf16[512,1024]{1,0:T(8,128)(2,1)} %copy-done.3), channel_id=1, source_target_pairs={{0,8},{8,16},{16,24},{24,28},{28,20},{20,12},{12,4},{4,0},{1,9},{9... | collective-permute-start | bytes 3145736 | tf_op jit(solution)/shard_map/ppermute | solution.py:303
  43.9 23.5 %collective-permute-start.6 = (bf16[512,1024]{1,0:T(8,128)(2,1)}, bf16[512,1024]{1,0:T(8,128)(2,1)S(1)}, u32[]{:S(2)}, u32[]{:S(2)}) collective-permute-start(bf16[512,1024]{1,0:T(8,128)(2,1)} %collective-permute-done.1.refs_2_.refs_6_), channel_id=1, source_target_pairs={{8,0},{16,8},{24,16},{28,24},{20,28},{12,20},{4,12},{0,4},{9,1},{1... | collective-permute-start | bytes 3145736 | tf_op jit(solution)/shard_map/ppermute | solution.py:304
  45.4 11.7 %collective-permute-start.3 = (bf16[8,272,128]{2,1,0:T(8,128)(2,1)}, bf16[8,272,128]{2,1,0:T(8,128)(2,1)}, u32[]{:S(2)}, u32[]{:S(2)}) collective-permute-start(bf16[8,272,128]{2,1,0:T(8,128)(2,1)} %shard_map.65.refs_0_), channel_id=1, source_target_pairs={{0,1},{1,0},{2,3},{3,2},{4,5},{5,4},{6,7},{7,6},{8,9},{9,8},{10,11... | collective-permute-start | bytes 1671176 | tf_op jit(solution)/shard_map/ppermute | solution.py:284
  55.2 21.4 %collective-permute-start.4 = (bf16[8,272,128]{2,1,0:T(8,128)(2,1)}, bf16[8,272,128]{2,1,0:T(8,128)(2,1)}, u32[]{:S(2)}, u32[]{:S(2)}) collective-permute-start(bf16[8,272,128]{2,1,0:T(8,128)(2,1)} %collective-permute-done.2.refs_1_), channel_id=1, source_target_pairs={{0,1},{1,0},{2,3},{3,2},{4,5},{5,4},{6,7},{7,6},{8,9},{9,8},{10,11... | collective-permute-start | bytes 1671176 | tf_op jit(solution)/shard_map/ppermute | solution.py:285
  66.8 7.2 %copy-start = (bf16[512,1024]{1,0:T(8,128)(2,1)}, bf16[512,1024]{1,0:T(8,128)(2,1)S(1)}, u32[]{:S(2)}) copy-start(bf16[512,1024]{1,0:T(8,128)(2,1)S(1)} %collective-permute-done.5.refs_7_.block_hbm) | copy-start | bytes 3145732
  66.9 7.2 %copy-start.2 = (bf16[256,1024]{1,0:T(8,128)(2,1)}, bf16[256,1024]{1,0:T(8,128)(2,1)S(1)}, u32[]{:S(2)}) copy-start(bf16[256,1024]{1,0:T(8,128)(2,1)S(1)} %slice.38._) | copy-start | bytes 1572868
  66.9 23.4 %collective-permute-start.7 = (bf16[256,1024]{1,0:T(8,128)(2,1)S(1)}, bf16[256,1024]{1,0:T(8,128)(2,1)}, u32[]{:S(2)}, u32[]{:S(2)}) collective-permute-start(bf16[256,1024]{1,0:T(8,128)(2,1)S(1)} %slice.38._), channel_id=1, source_target_pairs={{0,8},{8,16},{16,24},{24,28},{28,20},{20,12},{12,4},{4,0},{1,9},{9... | collective-permute-start | bytes 1572872 | tf_op jit(solution)/shard_map/ppermute | solution.py:310
  67.3 1.0 copy-start.1
  69.2 21.1 %collective-permute-start.8 = (bf16[256,1024]{1,0:T(8,128)(2,1)}, bf16[256,1024]{1,0:T(8,128)(2,1)}, u32[]{:S(2)}, u32[]{:S(2)}) collective-permute-start(bf16[256,1024]{1,0:T(8,128)(2,1)} %slice.39._), channel_id=1, source_target_pairs={{8,0},{16,8},{24,16},{28,24},{20,28},{12,20},{4,12},{0,4},{9,1},{1... | collective-permute-start | bytes 1572872 | tf_op jit(solution)/shard_map/ppermute | solution.py:311
  72.6 20.8 %collective-permute-start.10 = (bf16[256,1024]{1,0:T(8,128)(2,1)}, bf16[256,1024]{1,0:T(8,128)(2,1)}, u32[]{:S(2)}, u32[]{:S(2)}) collective-permute-start(bf16[256,1024]{1,0:T(8,128)(2,1)} %shard_map.69), channel_id=1, source_target_pairs={{8,0},{16,8},{24,16},{28,24},{20,28},{12,20},{4,12},{0,4},{9,1},{1... | collective-permute-start | bytes 1572872 | tf_op jit(solution)/shard_map/ppermute | solution.py:313
  75.9 17.5 %collective-permute-start.9 = (bf16[256,1024]{1,0:T(8,128)(2,1)}, bf16[256,1024]{1,0:T(8,128)(2,1)}, u32[]{:S(2)}, u32[]{:S(2)}) collective-permute-start(bf16[256,1024]{1,0:T(8,128)(2,1)} %shard_map.68), channel_id=1, source_target_pairs={{0,8},{8,16},{16,24},{24,28},{28,20},{20,12},{12,4},{4,0},{1,9},{9... | collective-permute-start | bytes 1572872 | tf_op jit(solution)/shard_map/ppermute | solution.py:312
  90.3 12.5 %collective-permute-start.11 = (bf16[256,1024]{1,0:T(8,128)(2,1)}, bf16[256,1024]{1,0:T(8,128)(2,1)S(1)}, u32[]{:S(2)}, u32[]{:S(2)}) collective-permute-start(bf16[256,1024]{1,0:T(8,128)(2,1)} %get-tuple-element.11.refs_0_), channel_id=1, source_target_pairs={{0,8},{8,16},{16,24},{24,28},{28,20},{20,12},{12,4},{4,0},{1,9},{9... | collective-permute-start | bytes 1572872 | tf_op jit(solution)/shard_map/ppermute | solution.py:337
  90.8 12.0 %collective-permute-start.12 = (bf16[256,1024]{1,0:T(8,128)(2,1)}, bf16[256,1024]{1,0:T(8,128)(2,1)S(1)}, u32[]{:S(2)}, u32[]{:S(2)}) collective-permute-start(bf16[256,1024]{1,0:T(8,128)(2,1)} %get-tuple-element.12.refs_3_), channel_id=1, source_target_pairs={{8,0},{16,8},{24,16},{28,24},{20,28},{12,20},{4,12},{0,4},{9,1},{1... | collective-permute-start | bytes 1572872 | tf_op jit(solution)/shard_map/ppermute | solution.py:338
  102.8 0.8 copy-start.4
  103.6 0.8 copy-start.5

commit v12 on v11

--- a/solution.py
+++ b/solution.py
@@ -9,6 +9,7 @@
 
 META = 16
 PARTS = 4
+CLEAR = 32
 VMEM_BYTES = 62 << 20
 
 
@@ -76,7 +77,14 @@
         at += depth
     for fetch in fetches:
         fetch.start()
-    left[...] = jnp.zeros_like(left)
+    some = left.shape[0] // PARTS
+
+    def clear(i, carry):
+        rows = pl.ds(pl.multiple_of(i * CLEAR, CLEAR), CLEAR)
+        left[rows] = jnp.zeros((CLEAR, left.shape[1]), left.dtype)
+        return carry
+
+    lax.fori_loop(0, left.shape[0] // CLEAR, clear, 0)
     k_blocks = left.shape[1] // bs
     for q, part in enumerate(parts):
 
@@ -95,7 +103,6 @@
             return carry
 
         lax.fori_loop(0, per_part, place, 0)
-    some = left.shape[0] // PARTS
     stores = [
         pltpu.make_async_copy(
             left.at[pl.ds(q * some, some), pl.ds(inner, late_hbm.shape[1])],
@@ -108,15 +115,24 @@
         store.start()
     for fetch in fetches:
         fetch.wait()
+
+    def multiply(j, carry):
+        cols = pl.ds(pl.multiple_of(j * bn, bn), bn)
+
+        def turn(q, inner_carry):
+            rows = pl.ds(pl.multiple_of(q * some, some), some)
+            acc[j, rows] = jnp.dot(
+                left[rows, :inner], right[:, cols], preferred_element_type=jnp.float32
+            )
+            return inner_carry
+
+        lax.fori_loop(0, PARTS, turn, 0)
+        pltpu.make_async_copy(acc.at[j], acc_hbm.at[j], acc_sem.at[j]).start()
+        return carry
+
+    lax.fori_loop(0, acc.shape[0], multiply, 0)
     for j in range(acc.shape[0]):
-        acc[j] = jnp.dot(
-            left[:, :inner],
-            right[:, j * bn : (j + 1) * bn],
-            preferred_element_type=jnp.float32,
-        )
-        store = pltpu.make_async_copy(acc.at[j], acc_hbm.at[j], acc_sem.at[j])
-        store.start()
-        stores.append(store)
+        pltpu.make_async_copy(acc.at[j], acc_hbm.at[j], acc_sem.at[j]).wait()
     for store in stores:
         store.wait()
 
@@ -159,49 +175,53 @@
     steps, rows, bn = acc.shape
     inner = left.shape[1]
     some = rows // PARTS
-    left_copies = [
-        pltpu.make_async_copy(
-            late_hbm.at[pl.ds(q * some, some), pl.ds(place, inner)],
-            left.at[pl.ds(q * some, some)],
-            left_sem.at[q],
-        )
-        for q in range(PARTS)
-    ]
-    for copy in left_copies:
-        copy.start()
-    chunks = []
-    for j in range(steps):
-        copies, at = [], 0
+
+    def fetch_left(q):
+        part = pl.ds(pl.multiple_of(q * some, some), some)
+        source = late_hbm.at[part, pl.ds(place, inner)]
+        return pltpu.make_async_copy(source, left.at[part], left_sem.at[q])
+
+    def fetch(j):
+        cols = pl.ds(pl.multiple_of(j * bn, bn), bn)
+        copies, at = [pltpu.make_async_copy(acc_hbm.at[j], acc.at[j], acc_sem.at[j])], 0
         for i, (depth, piece) in enumerate(zip(depths, pieces)):
-            copies.append(
-                pltpu.make_async_copy(
-                    piece.at[:, pl.ds(j * bn, bn)],
-                    right.at[j, pl.ds(at, depth)],
-                    right_sem.at[j, i],
-                )
-            )
+            target = right.at[j, pl.ds(at, depth)]
+            copies.append(pltpu.make_async_copy(piece.at[:, cols], target, right_sem.at[j, i]))
             at += depth
-        copies.append(pltpu.make_async_copy(acc_hbm.at[j], acc.at[j], acc_sem.at[j]))
-        for copy in copies:
-            copy.start()
-        chunks.append(copies)
-    for copy in left_copies:
-        copy.wait()
-    stores = []
-    for j in range(steps):
-        for copy in chunks[j]:
-            copy.wait()
-        total = jnp.dot(left[...], right[j], preferred_element_type=jnp.float32)
-        out[j] = (acc[j] + total).astype(out.dtype)
+        return copies
+
+    def store(j):
         if len(out_hbm.shape) == 2:
-            target = out_hbm.at[:, pl.ds(j * bn, bn)]
+            target = out_hbm.at[:, pl.ds(pl.multiple_of(j * bn, bn), bn)]
         else:
             target = out_hbm.at[j]
-        store = pltpu.make_async_copy(out.at[j], target, out_sem.at[j])
-        store.start()
-        stores.append(store)
-    for store in stores:
-        store.wait()
+        return pltpu.make_async_copy(out.at[j], target, out_sem.at[j])
+
+    def each(count, act):
+        def step(i, carry):
+            act(i)
+            return carry
+
+        lax.fori_loop(0, count, step, 0)
+
+    each(PARTS, lambda q: fetch_left(q).start())
+    each(steps, lambda j: [copy.start() for copy in fetch(j)])
+    each(PARTS, lambda q: fetch_left(q).wait())
+
+    def multiply(j):
+        for copy in fetch(j):
+            copy.wait()
+
+        def turn(q):
+            part = pl.ds(pl.multiple_of(q * some, some), some)
+            total = jnp.dot(left[part], right[j], preferred_element_type=jnp.float32)
+            out[j, part] = (acc[j, part] + total).astype(out.dtype)
+
+        each(PARTS, turn)
+        store(j).start()
+
+    each(steps, multiply)
+    each(steps, lambda j: store(j).wait())
 
 
 def add_product(late, place, pieces, acc, last):
@@ -237,43 +257,6 @@
     )(late, acc, *pieces)
 
 
-def rest_kernel(start, block_hbm, _, out_hbm, held, in_sem, out_sem):
-    some = held.shape[0] // PARTS
-    loads, stores = [], []
-    for q in range(PARTS):
-        rows = pl.ds(q * some, some)
-        source = block_hbm.at[pl.ds(start + q * some, some)]
-        loads.append(pltpu.make_async_copy(source, held.at[rows], in_sem.at[q]))
-        stores.append(pltpu.make_async_copy(held.at[rows], out_hbm.at[rows], out_sem.at[q]))
-    for load in loads:
-        load.start()
-    for load, store in zip(loads, stores):
-        load.wait()
-        store.start()
-    for store in stores:
-        store.wait()
-
-
-def rest(block, start, size, ahead):
-    anywhere = pl.BlockSpec(memory_space=pl.ANY)
-    shape = (size, block.shape[1])
-    return pl.pallas_call(
-        functools.partial(rest_kernel, start),
-        out_shape=jax.ShapeDtypeStruct(shape, block.dtype),
-        in_specs=[anywhere] * 2,
-        out_specs=anywhere,
-        scratch_shapes=[
-            pltpu.VMEM(shape, block.dtype),
-            pltpu.SemaphoreType.DMA((PARTS,)),
-            pltpu.SemaphoreType.DMA((PARTS,)),
-        ],
-        compiler_params=pltpu.CompilerParams(vmem_limit_bytes=VMEM_BYTES),
-        cost_estimate=pl.CostEstimate(
-            flops=0, bytes_accessed=size * block.shape[1] * 4, transcendentals=0
-        ),
-    )(block, ahead)
-
-
 def across_row(landed, columns):
     if columns != 4:
         gathered = lax.all_gather(landed, "blk", axis=0)
@@ -305,8 +288,7 @@
         early += [from_left, from_right]
     split = k_local // 2
     left_low, right_high = from_left[:split], from_right[split:]
-    left_high = rest(from_left, split, split, left_low)
-    right_low = rest(from_right, 0, split, right_high)
+    left_high, right_low = from_left[split:], from_right[:split]
     left_low = lax.ppermute(left_low, "grid", to_right)
     right_high = lax.ppermute(right_high, "grid", to_left)
     left_high = lax.ppermute(left_high, "grid", to_right)

time: 111 us -> 110 us (level)
  blocking collectives: 32.6 us -> 0 us
  waiting for transfers between devices: 19.7 us -> 41.2 us
  starting transfers between devices: 12.8 us -> 23.3 us
  Pallas kernels: 33.6 us -> 31.4 us
  local copies, waits for them, and re-layouts: 9.18 us -> 10.4 us
    all_to_all x1 -> x0, blocking collectives: 32.6 us -> none  [body(): lax.all_to_all(message, 'grid', split_axis=0, concat_axis=0, tiled=True)]
    all_to_all x0 -> x1, waiting for transfers between devices: none -> 11.9 us  [body(): lax.all_to_all(message, 'grid', split_axis=0, concat_axis=0, tiled=True)]
    all_to_all x0 -> x1, starting transfers between devices: none -> 6.28 us  [body(): lax.all_to_all(message, 'grid', split_axis=0, concat_axis=0, tiled=True)]
    ppermute x2, waiting for transfers between devices: 8.84 us -> 14.3 us  [body(): from_left = lax.ppermute(from_left, 'grid', to_right)]
    ppermute x1, starting transfers between devices: 0.42 us -> 4.56 us  [body(): left_low = lax.ppermute(left_low, 'grid', to_right)]
    ppermute x1, waiting for transfers between devices: 1.01 us -> 4.94 us  [body(): right_low = lax.ppermute(right_low, 'grid', to_left)]
    pallas_call x2 -> x0, Pallas kernels: 3.63 us -> none  [rest(): pl.pallas_call(functools.partial(rest_kernel, start), out_shape=jax.Shape...]
    slice x2, local copies, waits for them, and re-layouts: 0.86 us -> 4.39 us  [body(): left_high, right_low = (from_left[split:], from_right[:split])]
  transfers between devices with their start and end apart: 13 -> 14, of which waited for: 3 -> 6; matrix products, arithmetic and copies ran while one was open for 8% -> 10% of each run, Pallas kernels for 25% -> 23%
where the time goes in v12:
time: 110 us; the launch traced here: 109 us
  waiting for transfers between devices  41.2 us (37%)
  Pallas kernels  31.4 us (29%)
  starting transfers between devices  23.3 us (21%)
  local copies, waits for them, and re-layouts  10.4 us (9%)
  other arithmetic  2.72 us (2%)
    pallas_call x2, Pallas kernels, add_product(): pl.pallas_call(functools.partial(add_kernel, depths, place), out_shape=ou...  14.5 us
    ppermute x2, waiting for transfers between devices, body(): from_left = lax.ppermute(from_left, 'grid', to_right)  14.3 us
    pallas_call x1, Pallas kernels, first_product(): pl.pallas_call(functools.partial(first_kernel, depths, parts[0].shape[0],...  13.7 us
    all_to_all x1, waiting for transfers between devices, body(): lax.all_to_all(message, 'grid', split_axis=0, concat_axis=0, tiled=True)  11.9 us
    ppermute x1, waiting for transfers between devices, across_row(): across = lax.ppermute(landed, 'blk', swap_chip)  9.24 us
    ppermute x2, starting transfers between devices, body(): from_left = lax.ppermute(from_left, 'grid', to_right)  6.33 us
    all_to_all x1, starting transfers between devices, body(): lax.all_to_all(message, 'grid', split_axis=0, concat_axis=0, tiled=True)  6.28 us
    ppermute x1, waiting for transfers between devices, body(): right_low = lax.ppermute(right_low, 'grid', to_left)  4.94 us
  transfers between devices with their start and end apart: 14, of which 6 were waited for; matrix products, arithmetic and copies ran while one was open for 10% of the time, Pallas kernels for 23%

profile of v12, /device:TPU:0, one launch (start us, length us, event | category | flops | bytes accessed | tf_op | source)
XLA Modules:
  0.0 109.1 jit_solution(689095739466976370)
XLA Ops:
  0.0 3.0 %collective-permute-start = (bf16[512,1024]{1,0:T(8,128)(2,1)}, bf16[512,1024]{1,0:T(8,128)(2,1)S(1)}, u32[]{:S(2)}, u32[]{:S(2)}) collective-permute-start(bf16[512,1024]{1,0:T(8,128)(2,1)} %refs_4_.1), channel_id=1, source_target_pairs={{0,8},{8,16},{16,24},{24,28},{28,20},{20,12},{12,4},{4,0},{1,9},{9... | collective-permute-start | bytes 3145736 | tf_op jit(solution)/shard_map/ppermute | solution.py:286
  3.0 0.0 collective-permute-start.1
  3.0 0.7 convert_bitcast_fusion
  3.7 0.7 fusion.11
  4.4 0.1 copy.29
  4.5 0.6 pad.4.meta_ref
  5.1 3.2 %shard_map.64 = bf16[8,272,128]{2,1,0:T(8,128)(2,1)} custom-call(bf16[8,256,128]{2,1,0:T(8,128)(2,1)} %bitcast.17, bf16[8,16,128]{2,1,0:T(8,128)(2,1)} %pad.4.meta_ref), custom_call_target="tpu_custom_call" | custom-call | bytes 1048576 | tf_op jit(solution)/shard_map/pallas_call | solution.py:33
  8.3 6.3 %all-to-all-start = ((bf16[8,272,128]{2,1,0:T(8,128)(2,1)}), bf16[8,272,128]{2,1,0:T(8,128)(2,1)S(1)}, u32[]{:S(2)}, u32[]{:S(2)}) async-start(bf16[8,272,128]{2,1,0:T(8,128)(2,1)} %shard_map.64), calls=%async_computation | async-start | bytes 1114112 | tf_op jit(solution)/shard_map/all_to_all | solution.py:302
  14.6 12.5 %collective-permute-done.refs_1_.refs_5_ = bf16[512,1024]{1,0:T(8,128)(2,1)S(1)} collective-permute-done((bf16[512,1024]{1,0:T(8,128)(2,1)}, bf16[512,1024]{1,0:T(8,128)(2,1)S(1)}, u32[]{:S(2)}, u32[]{:S(2)}) %collective-permute-start) | collective-permute-done | bytes 1048608 | tf_op jit(solution)/shard_map/ppermute | solution.py:286
  27.1 3.3 %collective-permute-start.5 = (bf16[512,1024]{1,0:T(8,128)(2,1)S(1)}, bf16[512,1024]{1,0:T(8,128)(2,1)}, u32[]{:S(2)}, u32[]{:S(2)}) collective-permute-start(bf16[512,1024]{1,0:T(8,128)(2,1)S(1)} %collective-permute-done.refs_1_.refs_5_), channel_id=1, source_target_pairs={{0,8},{8,16},{16,24},{24,28},{28,20},{20,12},{12,4},{4,0},{1,9},{9... | collective-permute-start | bytes 3145736 | tf_op jit(solution)/shard_map/ppermute | solution.py:286
  30.4 0.0 collective-permute-done.1.refs_2_.refs_6_
  30.4 11.9 %all-to-all-done.refs_0_ = bf16[8,272,128]{2,1,0:T(8,128)(2,1)S(1)} async-done(((bf16[8,272,128]{2,1,0:T(8,128)(2,1)}), bf16[8,272,128]{2,1,0:T(8,128)(2,1)S(1)}, u32[]{:S(2)}, u32[]{:S(2)}) %all-to-all-start) | async-done | bytes 557088 | tf_op jit(solution)/shard_map/all_to_all | solution.py:302
  42.3 0.8 copy-done
  43.1 1.5 %collective-permute-start.2 = (bf16[8,272,128]{2,1,0:T(8,128)(2,1)}, bf16[8,272,128]{2,1,0:T(8,128)(2,1)S(1)}, u32[]{:S(2)}, u32[]{:S(2)}) collective-permute-start(bf16[8,272,128]{2,1,0:T(8,128)(2,1)} %shard_map.65.refs_0_), channel_id=1, source_target_pairs={{0,2},{1,3},{2,0},{3,1},{4,6},{5,7},{6,4},{7,5},{8,10},{9,11},{10,... | collective-permute-start | bytes 1671176 | tf_op jit(solution)/shard_map/ppermute | solution.py:266
  44.6 9.2 %collective-permute-done.2.refs_1_ = bf16[8,272,128]{2,1,0:T(8,128)(2,1)S(1)} collective-permute-done((bf16[8,272,128]{2,1,0:T(8,128)(2,1)}, bf16[8,272,128]{2,1,0:T(8,128)(2,1)S(1)}, u32[]{:S(2)}, u32[]{:S(2)}) %collective-permute-start.2) | collective-permute-done | bytes 557088 | tf_op jit(solution)/shard_map/ppermute | solution.py:266
  53.9 0.8 slice.40
  54.7 0.1 copy.30
  54.7 0.1 copy.34
  54.9 0.1 copy.31
  55.0 0.1 copy.35
  55.1 0.1 copy.32
  55.2 0.1 copy.36
  55.3 1.8 %collective-permute-done.5.refs_7_ = bf16[512,1024]{1,0:T(8,128)(2,1)} collective-permute-done((bf16[512,1024]{1,0:T(8,128)(2,1)S(1)}, bf16[512,1024]{1,0:T(8,128)(2,1)}, u32[]{:S(2)}, u32[]{:S(2)}) %collective-permute-start.5) | collective-permute-done | bytes 1048608 | tf_op jit(solution)/shard_map/ppermute | solution.py:286
  57.1 2.1 %fusion.13 = (bf16[256,1024]{1,0:T(8,128)(2,1)S(1)}, bf16[256,1024]{1,0:T(8,128)(2,1)}) fusion(bf16[512,1024]{1,0:T(8,128)(2,1)} %collective-permute-done.5.refs_7_), kind=kLoop, calls=%fused_computation.37 | loop fusion | bytes 2097152 | tf_op jit(solution)/shard_map/slice | solution.py:291
  59.2 4.6 %collective-permute-start.7 = (bf16[256,1024]{1,0:T(8,128)(2,1)}, bf16[256,1024]{1,0:T(8,128)(2,1)S(1)}, u32[]{:S(2)}, u32[]{:S(2)}) collective-permute-start(bf16[256,1024]{1,0:T(8,128)(2,1)} %get-tuple-element.16), channel_id=1, source_target_pairs={{0,8},{8,16},{16,24},{24,28},{28,20},{20,12},{12,4},{4,0},{1,9},{9... | collective-permute-start | bytes 1572872 | tf_op jit(solution)/shard_map/ppermute | solution.py:292
  63.8 2.3 %fusion.12 = (bf16[256,1024]{1,0:T(8,128)(2,1)}, bf16[256,1024]{1,0:T(8,128)(2,1)}) fusion(bf16[512,1024]{1,0:T(8,128)(2,1)} %collective-permute-done.6.refs_8_), kind=kLoop, calls=%fused_computation.36 | loop fusion | bytes 2097152 | tf_op jit(solution)/shard_map/slice | solution.py:291
  66.0 2.5 %collective-permute-start.10 = (bf16[256,1024]{1,0:T(8,128)(2,1)}, bf16[256,1024]{1,0:T(8,128)(2,1)}, u32[]{:S(2)}, u32[]{:S(2)}) collective-permute-start(bf16[256,1024]{1,0:T(8,128)(2,1)} %get-tuple-element.13), channel_id=1, source_target_pairs={{8,0},{16,8},{24,16},{28,24},{20,28},{12,20},{4,12},{0,4},{9,1},{1... | collective-permute-start | bytes 1572872 | tf_op jit(solution)/shard_map/ppermute | solution.py:295
  68.6 0.1 collective-permute-start.9
  68.7 0.7 slice.43
  69.4 0.1 copy.33
  69.5 0.1 copy.37
  69.6 0.1 copy.38
  69.7 0.3 fusion
  70.0 0.3 compare_reduce_fusion
  70.3 0.1 copy.39
  70.4 0.1 copy.40
  70.5 0.7 fusion.6.dest_ref
  71.3 13.7 %shard_map.66 = (f32[4,1024,256]{2,1,0:T(8,128)}, bf16[1024,1536]{1,0:T(8,128)(2,1)}) custom-call(s32[4,8,2]{2,1,0:T(8,128)} %fusion.6.dest_ref, bf16[8,272,128]{2,1,0:T(8,128)(2,1)} %shard_map.65.refs_0_, bf16[8,272,128]{2,1,0:T(8,128)(2,1)} %copy-done.6, bf16[8,272,128]{2,1,0:T(8,128)(2,1)} %copy-done.7, ...), custom_call_target="tpu_custom_call" | custom-call | flops 5368709120 | bytes 9437184 | tf_op jit(solution)/shard_map/pallas_call | solution.py:145
  85.0 0.0 copy-start.1
  85.0 0.8 copy-done.1
  85.8 0.2 copy-done.2
  86.0 2.0 %collective-permute-start.11 = (bf16[256,1024]{1,0:T(8,128)(2,1)}, bf16[256,1024]{1,0:T(8,128)(2,1)S(1)}, u32[]{:S(2)}, u32[]{:S(2)}) collective-permute-start(bf16[256,1024]{1,0:T(8,128)(2,1)} %get-tuple-element.11.refs_0_), channel_id=1, source_target_pairs={{0,8},{8,16},{16,24},{24,28},{28,20},{20,12},{12,4},{4,0},{1,9},{9... | collective-permute-start | bytes 1572872 | tf_op jit(solution)/shard_map/ppermute | solution.py:319
  88.0 0.0 collective-permute-start.12
  88.1 4.9 %collective-permute-done.10.refs_2_ = bf16[256,1024]{1,0:T(8,128)(2,1)} collective-permute-done((bf16[256,1024]{1,0:T(8,128)(2,1)}, bf16[256,1024]{1,0:T(8,128)(2,1)}, u32[]{:S(2)}, u32[]{:S(2)}) %collective-permute-start.10) | collective-permute-done | bytes 524320 | tf_op jit(solution)/shard_map/ppermute | solution.py:295
  93.0 8.2 %shard_map.68.acc_hbm = f32[4,1024,256]{2,1,0:T(8,128)} custom-call(bf16[1024,1536]{1,0:T(8,128)(2,1)} %get-tuple-element.9.refs_2_.late_hbm, f32[4,1024,256]{2,1,0:T(8,128)} %get-tuple-element.10.acc_hbm, bf16[256,1024]{1,0:T(8,128)(2,1)} %get-tuple-element.11.refs_0_, bf16[256,1024]{1,0:T(8,128)(2,1)} %collective-permute-done.9.refs_1_, ...), custom_call_target="tpu_custom_call" | custom-call | flops 2147483648 | bytes 12582912 | tf_op jit(solution)/shard_map/pallas_call | solution.py:236
  101.2 0.8 collective-permute-done.12.refs_1_
  102.1 0.8 copy-done.5
  102.9 6.3 %shard_map.69 = bf16[1024,1024]{1,0:T(8,128)(2,1)} custom-call(bf16[1024,1536]{1,0:T(8,128)(2,1)} %get-tuple-element.9.refs_2_.late_hbm, f32[4,1024,256]{2,1,0:T(8,128)} %shard_map.68.acc_hbm, bf16[256,1024]{1,0:T(8,128)(2,1)} %copy-done.4, bf16[256,1024]{1,0:T(8,128)(2,1)} %copy-done.5), custom_call_target="tpu_custom_call" | custom-call | flops 1073741824 | bytes 10485760 | tf_op jit(solution)/shard_map/pallas_call | solution.py:236
  (31 shorter events, 0.1 us)
Async XLA Ops:
  0.0 53.8 %copy-start.8 = (s32[1,8]{1,0:T(1,128)S(1)}, s32[1,8]{1,0:T(1,128)}, u32[]{:S(2)}) copy-start(s32[1,8]{1,0:T(1,128)} %param.10) | copy-start | bytes 100
  0.0 27.1 %collective-permute-start = (bf16[512,1024]{1,0:T(8,128)(2,1)}, bf16[512,1024]{1,0:T(8,128)(2,1)S(1)}, u32[]{:S(2)}, u32[]{:S(2)}) collective-permute-start(bf16[512,1024]{1,0:T(8,128)(2,1)} %refs_4_.1), channel_id=1, source_target_pairs={{0,8},{8,16},{16,24},{24,28},{28,20},{20,12},{12,4},{4,0},{1,9},{9... | collective-permute-start | bytes 3145736 | tf_op jit(solution)/shard_map/ppermute | solution.py:286
  3.0 27.4 %collective-permute-start.1 = (bf16[512,1024]{1,0:T(8,128)(2,1)}, bf16[512,1024]{1,0:T(8,128)(2,1)}, u32[]{:S(2)}, u32[]{:S(2)}) collective-permute-start(bf16[512,1024]{1,0:T(8,128)(2,1)} %refs_4_.1), channel_id=1, source_target_pairs={{8,0},{16,8},{24,16},{28,24},{20,28},{12,20},{4,12},{0,4},{9,1},{1... | collective-permute-start | bytes 3145736 | tf_op jit(solution)/shard_map/ppermute | solution.py:287
  8.3 34.0 %all-to-all-start = ((bf16[8,272,128]{2,1,0:T(8,128)(2,1)}), bf16[8,272,128]{2,1,0:T(8,128)(2,1)S(1)}, u32[]{:S(2)}, u32[]{:S(2)}) async-start(bf16[8,272,128]{2,1,0:T(8,128)(2,1)} %shard_map.64), calls=%async_computation | async-start | bytes 1114112 | tf_op jit(solution)/shard_map/all_to_all | solution.py:302
  27.1 15.2 %copy-start.3 = (bf16[512,1024]{1,0:T(8,128)(2,1)}, bf16[512,1024]{1,0:T(8,128)(2,1)S(1)}, u32[]{:S(2)}) copy-start(bf16[512,1024]{1,0:T(8,128)(2,1)S(1)} %collective-permute-done.refs_1_.refs_5_) | copy-start | bytes 3145732
  27.1 30.0 %collective-permute-start.5 = (bf16[512,1024]{1,0:T(8,128)(2,1)S(1)}, bf16[512,1024]{1,0:T(8,128)(2,1)}, u32[]{:S(2)}, u32[]{:S(2)}) collective-permute-start(bf16[512,1024]{1,0:T(8,128)(2,1)S(1)} %collective-permute-done.refs_1_.refs_5_), channel_id=1, source_target_pairs={{0,8},{8,16},{16,24},{24,28},{28,20},{20,12},{12,4},{4,0},{1,9},{9... | collective-permute-start | bytes 3145736 | tf_op jit(solution)/shard_map/ppermute | solution.py:286
  30.4 33.4 %collective-permute-start.6 = (bf16[512,1024]{1,0:T(8,128)(2,1)}, bf16[512,1024]{1,0:T(8,128)(2,1)}, u32[]{:S(2)}, u32[]{:S(2)}) collective-permute-start(bf16[512,1024]{1,0:T(8,128)(2,1)} %collective-permute-done.1.refs_2_.refs_6_), channel_id=1, source_target_pairs={{8,0},{16,8},{24,16},{28,24},{20,28},{12,20},{4,12},{0,4},{9,1},{1... | collective-permute-start | bytes 3145736 | tf_op jit(solution)/shard_map/ppermute | solution.py:287
  42.3 0.8 copy-start
  43.1 10.7 %collective-permute-start.2 = (bf16[8,272,128]{2,1,0:T(8,128)(2,1)}, bf16[8,272,128]{2,1,0:T(8,128)(2,1)S(1)}, u32[]{:S(2)}, u32[]{:S(2)}) collective-permute-start(bf16[8,272,128]{2,1,0:T(8,128)(2,1)} %shard_map.65.refs_0_), channel_id=1, source_target_pairs={{0,2},{1,3},{2,0},{3,1},{4,6},{5,7},{6,4},{7,5},{8,10},{9,11},{10,... | collective-permute-start | bytes 1671176 | tf_op jit(solution)/shard_map/ppermute | solution.py:266
  44.6 10.5 %collective-permute-start.3 = (bf16[8,272,128]{2,1,0:T(8,128)(2,1)}, bf16[8,272,128]{2,1,0:T(8,128)(2,1)S(1)}, u32[]{:S(2)}, u32[]{:S(2)}) collective-permute-start(bf16[8,272,128]{2,1,0:T(8,128)(2,1)} %shard_map.65.refs_0_), channel_id=1, source_target_pairs={{0,1},{1,0},{2,3},{3,2},{4,5},{5,4},{6,7},{7,6},{8,9},{9,8},{10,11... | collective-permute-start | bytes 1671176 | tf_op jit(solution)/shard_map/ppermute | solution.py:267
  53.8 16.7 %copy-start.6 = (bf16[8,272,128]{2,1,0:T(8,128)(2,1)}, bf16[8,272,128]{2,1,0:T(8,128)(2,1)S(1)}, u32[]{:S(2)}) copy-start(bf16[8,272,128]{2,1,0:T(8,128)(2,1)S(1)} %collective-permute-done.2.refs_1_) | copy-start | bytes 1671172
  53.8 14.8 %collective-permute-start.4 = (bf16[8,272,128]{2,1,0:T(8,128)(2,1)S(1)}, bf16[8,272,128]{2,1,0:T(8,128)(2,1)}, u32[]{:S(2)}, u32[]{:S(2)}) collective-permute-start(bf16[8,272,128]{2,1,0:T(8,128)(2,1)S(1)} %collective-permute-done.2.refs_1_), channel_id=1, source_target_pairs={{0,1},{1,0},{2,3},{3,2},{4,5},{5,4},{6,7},{7,6},{8,9},{9,8},{10,11... | collective-permute-start | bytes 1671176 | tf_op jit(solution)/shard_map/ppermute | solution.py:268
  55.1 15.5 %copy-start.7 = (bf16[8,272,128]{2,1,0:T(8,128)(2,1)}, bf16[8,272,128]{2,1,0:T(8,128)(2,1)S(1)}, u32[]{:S(2)}) copy-start(bf16[8,272,128]{2,1,0:T(8,128)(2,1)S(1)} %collective-permute-done.3.refs_2_) | copy-start | bytes 1671172
  59.2 25.8 %collective-permute-start.7 = (bf16[256,1024]{1,0:T(8,128)(2,1)}, bf16[256,1024]{1,0:T(8,128)(2,1)S(1)}, u32[]{:S(2)}, u32[]{:S(2)}) collective-permute-start(bf16[256,1024]{1,0:T(8,128)(2,1)} %get-tuple-element.16), channel_id=1, source_target_pairs={{0,8},{8,16},{16,24},{24,28},{28,20},{20,12},{12,4},{4,0},{1,9},{9... | collective-permute-start | bytes 1572872 | tf_op jit(solution)/shard_map/ppermute | solution.py:292
  66.0 19.0 %collective-permute-start.8 = (bf16[256,1024]{1,0:T(8,128)(2,1)}, bf16[256,1024]{1,0:T(8,128)(2,1)S(1)}, u32[]{:S(2)}, u32[]{:S(2)}) collective-permute-start(bf16[256,1024]{1,0:T(8,128)(2,1)} %get-tuple-element.14), channel_id=1, source_target_pairs={{8,0},{16,8},{24,16},{28,24},{20,28},{12,20},{4,12},{0,4},{9,1},{1... | collective-permute-start | bytes 1572872 | tf_op jit(solution)/shard_map/ppermute | solution.py:293
  66.0 27.0 %collective-permute-start.10 = (bf16[256,1024]{1,0:T(8,128)(2,1)}, bf16[256,1024]{1,0:T(8,128)(2,1)}, u32[]{:S(2)}, u32[]{:S(2)}) collective-permute-start(bf16[256,1024]{1,0:T(8,128)(2,1)} %get-tuple-element.13), channel_id=1, source_target_pairs={{8,0},{16,8},{24,16},{28,24},{20,28},{12,20},{4,12},{0,4},{9,1},{1... | collective-permute-start | bytes 1572872 | tf_op jit(solution)/shard_map/ppermute | solution.py:295
  68.6 24.4 %collective-permute-start.9 = (bf16[256,1024]{1,0:T(8,128)(2,1)S(1)}, bf16[256,1024]{1,0:T(8,128)(2,1)}, u32[]{:S(2)}, u32[]{:S(2)}) collective-permute-start(bf16[256,1024]{1,0:T(8,128)(2,1)S(1)} %get-tuple-element.15), channel_id=1, source_target_pairs={{0,8},{8,16},{16,24},{24,28},{28,20},{20,12},{12,4},{4,0},{1,9},{9... | collective-permute-start | bytes 1572872 | tf_op jit(solution)/shard_map/ppermute | solution.py:294
  85.0 0.8 copy-start.1
  85.0 1.0 copy-start.2
  86.0 15.2 %collective-permute-start.11 = (bf16[256,1024]{1,0:T(8,128)(2,1)}, bf16[256,1024]{1,0:T(8,128)(2,1)S(1)}, u32[]{:S(2)}, u32[]{:S(2)}) collective-permute-start(bf16[256,1024]{1,0:T(8,128)(2,1)} %get-tuple-element.11.refs_0_), channel_id=1, source_target_pairs={{0,8},{8,16},{16,24},{24,28},{28,20},{20,12},{12,4},{4,0},{1,9},{9... | collective-permute-start | bytes 1572872 | tf_op jit(solution)/shard_map/ppermute | solution.py:319
  88.0 14.0 %collective-permute-start.12 = (bf16[256,1024]{1,0:T(8,128)(2,1)}, bf16[256,1024]{1,0:T(8,128)(2,1)S(1)}, u32[]{:S(2)}, u32[]{:S(2)}) collective-permute-start(bf16[256,1024]{1,0:T(8,128)(2,1)} %get-tuple-element.12.refs_3_), channel_id=1, source_target_pairs={{8,0},{16,8},{24,16},{28,24},{20,28},{12,20},{4,12},{0,4},{9,1},{1... | collective-permute-start | bytes 1572872 | tf_op jit(solution)/shard_map/ppermute | solution.py:320
  101.2 0.8 copy-start.4
  102.1 0.8 copy-start.5

commit v13 on v12

--- a/solution.py
+++ b/solution.py
@@ -11,6 +11,7 @@
 PARTS = 4
 CLEAR = 32
 VMEM_BYTES = 62 << 20
+SPARE_BYTES = 4 << 20
 
 
 def ring_order(n):
@@ -50,7 +51,7 @@
     pass
 
 
-def after(values, others):
+def after(values, others, claim):
     anywhere = pl.BlockSpec(memory_space=pl.ANY)
     return pl.pallas_call(
         after_kernel,
@@ -58,7 +59,7 @@
         in_specs=[anywhere] * (len(values) + len(others)),
         out_specs=[anywhere] * len(values),
         input_output_aliases={i: i for i in range(len(values))},
-        compiler_params=pltpu.CompilerParams(vmem_limit_bytes=VMEM_BYTES),
+        compiler_params=pltpu.CompilerParams(vmem_limit_bytes=claim),
         cost_estimate=pl.CostEstimate(flops=0, bytes_accessed=0, transcendentals=0),
     )(*values, *others)
 
@@ -118,15 +119,7 @@
 
     def multiply(j, carry):
         cols = pl.ds(pl.multiple_of(j * bn, bn), bn)
-
-        def turn(q, inner_carry):
-            rows = pl.ds(pl.multiple_of(q * some, some), some)
-            acc[j, rows] = jnp.dot(
-                left[rows, :inner], right[:, cols], preferred_element_type=jnp.float32
-            )
-            return inner_carry
-
-        lax.fori_loop(0, PARTS, turn, 0)
+        acc[j] = jnp.dot(left[:, :inner], right[:, cols], preferred_element_type=jnp.float32)
         pltpu.make_async_copy(acc.at[j], acc_hbm.at[j], acc_sem.at[j]).start()
         return carry
 
@@ -160,7 +153,11 @@
             pltpu.SemaphoreType.DMA((steps,)),
             pltpu.SemaphoreType.DMA((PARTS,)),
         ],
-        compiler_params=pltpu.CompilerParams(vmem_limit_bytes=VMEM_BYTES),
+        compiler_params=pltpu.CompilerParams(
+            vmem_limit_bytes=SPARE_BYTES
+            + 2 * (rows * (inner + late_width) + inner * cols + 2 * rows * cols)
+            + 2 * sum(part.size for part in parts)
+        ),
         cost_estimate=pl.CostEstimate(
             flops=2 * rows * inner * cols,
             bytes_accessed=inner * cols * 2 + rows * cols * 4,
@@ -248,13 +245,50 @@
             pltpu.SemaphoreType.DMA((steps,)),
             pltpu.SemaphoreType.DMA((steps,)),
         ],
-        compiler_params=pltpu.CompilerParams(vmem_limit_bytes=VMEM_BYTES),
+        compiler_params=pltpu.CompilerParams(
+            vmem_limit_bytes=SPARE_BYTES + 2 * inner * (rows + steps * bn) + 8 * rows * steps * bn
+        ),
         cost_estimate=pl.CostEstimate(
             flops=2 * rows * inner * steps * bn,
             bytes_accessed=(rows + steps * bn) * inner * 2 + rows * steps * bn * 8,
             transcendentals=0,
         ),
     )(late, acc, *pieces)
+
+
+def halve_kernel(block_hbm, _, low_hbm, high_hbm, held, in_sem, out_sem):
+    some = held.shape[0] // PARTS
+    loads, stores = [], []
+    for q in range(PARTS):
+        rows = pl.ds(q * some, some)
+        out_hbm = low_hbm if q < PARTS // 2 else high_hbm
+        target = out_hbm.at[pl.ds(q % (PARTS // 2) * some, some)]
+        loads.append(pltpu.make_async_copy(block_hbm.at[rows], held.at[rows], in_sem.at[q]))
+        stores.append(pltpu.make_async_copy(held.at[rows], target, out_sem.at[q]))
+    for load in loads:
+        load.start()
+    for load, store in zip(loads, stores):
+        load.wait()
+        store.start()
+    for store in stores:
+        store.wait()
+
+
+def halve(block, ahead):
+    anywhere = pl.BlockSpec(memory_space=pl.ANY)
+    rows, cols = block.shape
+    return pl.pallas_call(
+        halve_kernel,
+        out_shape=[jax.ShapeDtypeStruct((rows // 2, cols), block.dtype)] * 2,
+        in_specs=[anywhere] * 2,
+        out_specs=[anywhere] * 2,
+        scratch_shapes=[
+            pltpu.VMEM(block.shape, block.dtype),
+            pltpu.SemaphoreType.DMA((PARTS,)),
+            pltpu.SemaphoreType.DMA((PARTS,)),
+        ],
+        cost_estimate=pl.CostEstimate(flops=0, bytes_accessed=rows * cols * 4, transcendentals=0),
+    )(block, ahead)
 
 
 def across_row(landed, columns):
@@ -286,13 +320,6 @@
         from_left = lax.ppermute(from_left, "grid", to_right)
         from_right = lax.ppermute(from_right, "grid", to_left)
         early += [from_left, from_right]
-    split = k_local // 2
-    left_low, right_high = from_left[:split], from_right[split:]
-    left_high, right_low = from_left[split:], from_right[:split]
-    left_low = lax.ppermute(left_low, "grid", to_right)
-    right_high = lax.ppermute(right_high, "grid", to_left)
-    left_high = lax.ppermute(left_high, "grid", to_right)
-    right_low = lax.ppermute(right_low, "grid", to_left)
 
     live = jnp.arange(cap, dtype=jnp.int32)[None, :] < a_count.reshape(groups, 1)
     row_code = jnp.where(live, a_rows.reshape(groups, cap) + 1, 0)
@@ -300,7 +327,7 @@
     meta = jnp.pad(meta.astype(jnp.bfloat16)[:, None, :], ((0, 0), (0, META - 1), (0, bs - 2 * cap)))
     message = pack(a_slots.reshape(groups, cap * bs, bs), meta)
     landed = lax.all_to_all(message, "grid", split_axis=0, concat_axis=0, tiled=True)
-    (landed,) = after([landed], early[1:3])
+    (landed,) = after([landed], early[1:3], VMEM_BYTES)
     parts = across_row(landed, columns)
 
     metas = jnp.stack([p[:, cap * bs, : 2 * cap] for p in parts]).astype(jnp.int32)
@@ -314,8 +341,15 @@
     dest = row * (blocks * groups) + first * blocks + col % blocks
     dest = jnp.where(jnp.any(hit, axis=-1), dest, -1)
 
+    left_low, left_high = halve(from_left, dest)
+    right_low, right_high = halve(from_right, dest)
+    left_low = lax.ppermute(left_low, "grid", to_right)
+    right_high = lax.ppermute(right_high, "grid", to_left)
+    left_high = lax.ppermute(left_high, "grid", to_right)
+    right_low = lax.ppermute(right_low, "grid", to_left)
+
     acc, late = first_product(dest, parts, early, rb * bs, 3 * k_local, bs, cap, n_local // 4)
-    left_low, right_high = after([left_low, right_high], [late])
+    left_low, right_high = after([left_low, right_high], [late], SPARE_BYTES)
     low = lax.ppermute(left_low, "grid", to_right)
     high = lax.ppermute(right_high, "grid", to_left)
     acc = add_product(late, 0, [left_low, left_high, right_low, right_high], acc, False)

time: 110 us -> 129 us (1.17)
  blocking collectives: 0 us -> 32.6 us
  starting transfers between devices: 23.3 us -> 12.8 us
  waiting for transfers between devices: 41.2 us -> 37.8 us
  local copies, waits for them, and re-layouts: 10.4 us -> 13.6 us
  Pallas kernels: 31.4 us -> 28.9 us
    all_to_all x0 -> x1, blocking collectives: none -> 32.6 us  [body(): lax.all_to_all(message, 'grid', split_axis=0, concat_axis=0, tiled=True)]
    all_to_all x1 -> x0, waiting for transfers between devices: 11.9 us -> none  [body(): lax.all_to_all(message, 'grid', split_axis=0, concat_axis=0, tiled=True)]
    unnamed x18 -> x20, local copies, waits for them, and re-layouts: 2.65 us -> 9.59 us
    all_to_all x1 -> x0, starting transfers between devices: 6.28 us -> none  [body(): lax.all_to_all(message, 'grid', split_axis=0, concat_axis=0, tiled=True)]
    ppermute x2, waiting for transfers between devices: 14.3 us -> 19.1 us  [body(): from_left = lax.ppermute(from_left, 'grid', to_right)]
    slice x2 -> x0, local copies, waits for them, and re-layouts: 4.39 us -> none  [body(): left_high, right_low = (from_left[split:], from_right[:split])]
    ppermute x1, starting transfers between devices: 4.56 us -> 0.39 us  [body(): left_low = lax.ppermute(left_low, 'grid', to_right)]
    pallas_call x0 -> x2, Pallas kernels: none -> 3.99 us  [halve(): pl.pallas_call(halve_kernel, out_shape=[jax.ShapeDtypeStruct((rows // 2,...]
  transfers between devices with their start and end apart: 14 -> 13, of which waited for: 6 -> 5; matrix products, arithmetic and copies ran while one was open for 10% -> 5% of each run, Pallas kernels for 23% -> 18%
where the time goes in v13:
time: 129 us
  waiting for transfers between devices  37.8 us (29%)
  blocking collectives  32.6 us (25%)
  Pallas kernels  28.9 us (22%)
  local copies, waits for them, and re-layouts  13.6 us (11%)
  starting transfers between devices  12.8 us (10%)
  other arithmetic  2.72 us (2%)
    all_to_all x1, blocking collectives, body(): lax.all_to_all(message, 'grid', split_axis=0, concat_axis=0, tiled=True)  32.6 us
    ppermute x2, waiting for transfers between devices, body(): from_left = lax.ppermute(from_left, 'grid', to_right)  19.1 us
    ppermute x1, waiting for transfers between devices, across_row(): across = lax.ppermute(landed, 'blk', swap_chip)  11.7 us
    pallas_call x2, Pallas kernels, add_product(): pl.pallas_call(functools.partial(add_kernel, depths, place), out_shape=ou...  11.6 us
    pallas_call x1, Pallas kernels, first_product(): pl.pallas_call(functools.partial(first_kernel, depths, parts[0].shape[0],...  10.1 us
    unnamed x20, local copies, waits for them, and re-layouts  9.59 us
    pallas_call x2, Pallas kernels, halve(): pl.pallas_call(halve_kernel, out_shape=[jax.ShapeDtypeStruct((rows // 2,...  3.99 us
    ppermute x1, waiting for transfers between devices, body(): right_low = lax.ppermute(right_low, 'grid', to_left)  3.72 us
  transfers between devices with their start and end apart: 13, of which 5 were waited for; matrix products, arithmetic and copies ran while one was open for 5% of the time, Pallas kernels for 18%

profile of v13, /device:TPU:0, one launch (start us, length us, event | category | flops | bytes accessed | tf_op | source)
XLA Modules:
  0.0 128.5 jit_solution(1293377744425353963)
XLA Ops:
  0.0 3.0 %collective-permute-start = (bf16[512,1024]{1,0:T(8,128)(2,1)}, bf16[512,1024]{1,0:T(8,128)(2,1)S(1)}, u32[]{:S(2)}, u32[]{:S(2)}) collective-permute-start(bf16[512,1024]{1,0:T(8,128)(2,1)} %refs_4_.1), channel_id=1, source_target_pairs={{0,8},{8,16},{16,24},{24,28},{28,20},{20,12},{12,4},{4,0},{1,9},{9... | collective-permute-start | bytes 3145736 | tf_op jit(solution)/shard_map/ppermute | solution.py:320
  3.0 0.7 convert_bitcast_fusion
  3.7 0.7 fusion.11
  4.4 0.1 copy.29
  4.5 0.6 pad.4.meta_ref
  5.1 3.2 %shard_map.64 = bf16[8,272,128]{2,1,0:T(8,128)(2,1)} custom-call(bf16[8,256,128]{2,1,0:T(8,128)(2,1)} %bitcast.17, bf16[8,16,128]{2,1,0:T(8,128)(2,1)} %pad.4.meta_ref), custom_call_target="tpu_custom_call" | custom-call | bytes 1048576 | tf_op jit(solution)/shard_map/pallas_call | solution.py:34
  8.3 32.6 %all_to_all.5.refs_0_ = bf16[8,272,128]{2,1,0:T(8,128)(2,1)} all-to-all(bf16[8,272,128]{2,1,0:T(8,128)(2,1)} %shard_map.64), channel_id=1, replica_groups=mesh['grid'=8,'blk'=4] {'grid'}, dimensions={0} | all-to-all | bytes 1114112 | tf_op jit(solution)/shard_map/all_to_all | solution.py:329
  40.9 1.0 copy-done.1
  41.9 1.5 %collective-permute-start.2 = (bf16[8,272,128]{2,1,0:T(8,128)(2,1)}, bf16[8,272,128]{2,1,0:T(8,128)(2,1)S(1)}, u32[]{:S(2)}, u32[]{:S(2)}) collective-permute-start(bf16[8,272,128]{2,1,0:T(8,128)(2,1)} %shard_map.65.refs_0_), channel_id=1, source_target_pairs={{0,2},{1,3},{2,0},{3,1},{4,6},{5,7},{6,4},{7,5},{8,10},{9,11},{10,... | collective-permute-start | bytes 1671176 | tf_op jit(solution)/shard_map/ppermute | solution.py:300
  43.4 11.7 %collective-permute-done.2.refs_1_ = bf16[8,272,128]{2,1,0:T(8,128)(2,1)S(1)} collective-permute-done((bf16[8,272,128]{2,1,0:T(8,128)(2,1)}, bf16[8,272,128]{2,1,0:T(8,128)(2,1)S(1)}, u32[]{:S(2)}, u32[]{:S(2)}) %collective-permute-start.2) | collective-permute-done | bytes 557088 | tf_op jit(solution)/shard_map/ppermute | solution.py:300
  55.1 0.3 collective-permute-start.5
  55.4 1.7 %collective-permute-start.6 = (bf16[512,1024]{1,0:T(8,128)(2,1)}, bf16[512,1024]{1,0:T(8,128)(2,1)S(1)}, u32[]{:S(2)}, u32[]{:S(2)}) collective-permute-start(bf16[512,1024]{1,0:T(8,128)(2,1)} %collective-permute-done.1.refs_2_.refs_6_), channel_id=1, source_target_pairs={{8,0},{16,8},{24,16},{28,24},{20,28},{12,20},{4,12},{0,4},{9,1},{1... | collective-permute-start | bytes 3145736 | tf_op jit(solution)/shard_map/ppermute | solution.py:321
  57.1 0.7 slice.24
  58.1 0.1 copy.31
  58.2 0.1 copy.35
  58.3 0.7 slice.26
  59.1 0.1 copy.36
  59.2 0.7 slice.27
  60.0 0.1 copy.37
  60.1 0.1 copy.38
  60.2 0.3 fusion
  60.5 0.1 copy.39
  60.6 0.3 compare_reduce_fusion
  60.9 0.1 copy.40
  61.0 0.7 fusion.6.dest_ref._
  61.8 19.1 %collective-permute-done.5.refs_7_.block_hbm = bf16[512,1024]{1,0:T(8,128)(2,1)S(1)} collective-permute-done((bf16[512,1024]{1,0:T(8,128)(2,1)}, bf16[512,1024]{1,0:T(8,128)(2,1)S(1)}, u32[]{:S(2)}, u32[]{:S(2)}) %collective-permute-start.5) | collective-permute-done | bytes 1048608 | tf_op jit(solution)/shard_map/ppermute | solution.py:320
  80.9 1.0 copy-done.3
  81.9 2.0 %shard_map.67 = (bf16[256,1024]{1,0:T(8,128)(2,1)}, bf16[256,1024]{1,0:T(8,128)(2,1)}) custom-call(bf16[512,1024]{1,0:T(8,128)(2,1)} %copy-done.3, s32[4,8,2]{2,1,0:T(8,128)} %fusion.6.dest_ref._), custom_call_target="tpu_custom_call" | custom-call | bytes 2097152 | tf_op jit(solution)/shard_map/pallas_call | solution.py:280
  83.8 0.4 collective-permute-start.7
  84.2 1.0 copy-done.5
  85.2 2.0 %shard_map.68 = (bf16[256,1024]{1,0:T(8,128)(2,1)}, bf16[256,1024]{1,0:T(8,128)(2,1)}) custom-call(bf16[512,1024]{1,0:T(8,128)(2,1)} %copy-done.5, s32[4,8,2]{2,1,0:T(8,128)} %fusion.6.dest_ref._), custom_call_target="tpu_custom_call" | custom-call | bytes 2097152 | tf_op jit(solution)/shard_map/pallas_call | solution.py:280
  87.2 1.7 %collective-permute-start.8 = (bf16[256,1024]{1,0:T(8,128)(2,1)}, bf16[256,1024]{1,0:T(8,128)(2,1)S(1)}, u32[]{:S(2)}, u32[]{:S(2)}) collective-permute-start(bf16[256,1024]{1,0:T(8,128)(2,1)} %get-tuple-element.16), channel_id=1, source_target_pairs={{8,0},{16,8},{24,16},{28,24},{20,28},{12,20},{4,12},{0,4},{9,1},{1... | collective-permute-start | bytes 1572872 | tf_op jit(solution)/shard_map/ppermute | solution.py:347
  89.0 1.3 collective-permute-start.10
  90.2 0.8 collective-permute-start.9
  91.0 1.1 copy-done
  92.1 1.2 copy-done.2
  93.3 1.2 copy-done.4
  94.5 1.2 copy-done.6
  95.7 0.7 copy-done.7
  96.4 1.2 copy-done.8
  97.7 10.1 %shard_map.66 = (f32[4,1024,256]{2,1,0:T(8,128)S(1)}, bf16[1024,1536]{1,0:T(8,128)(2,1)S(1)}) custom-call(s32[4,8,2]{2,1,0:T(8,128)S(1)} %copy-done.7, bf16[8,272,128]{2,1,0:T(8,128)(2,1)S(1)} %copy-done, bf16[8,272,128]{2,1,0:T(8,128)(2,1)S(1)} %collective-permute-done.2.refs_1_, bf16[8,272,128]{2,1,0:T(8,128)(2,1)} %collective-permute-done.3.refs_2_, ...), custom_call_target="tpu_custom_call" | custom-call | flops 5368709120 | bytes 9437184 | tf_op jit(solution)/shard_map/pallas_call | solution.py:138
  107.8 0.4 collective-permute-start.11
  108.2 1.7 %collective-permute-start.12 = (bf16[256,1024]{1,0:T(8,128)(2,1)S(1)}, bf16[256,1024]{1,0:T(8,128)(2,1)S(1)}, u32[]{:S(2)}, u32[]{:S(2)}) collective-permute-start(bf16[256,1024]{1,0:T(8,128)(2,1)S(1)} %get-tuple-element.20.refs_3_), channel_id=1, source_target_pairs={{8,0},{16,8},{24,16},{28,24},{20,28},{12,20},{4,12},{0,4},{9,1},{1... | collective-permute-start | bytes 1572872 | tf_op jit(solution)/shard_map/ppermute | solution.py:354
  109.9 3.7 %collective-permute-done.10.refs_2_ = bf16[256,1024]{1,0:T(8,128)(2,1)S(1)} collective-permute-done((bf16[256,1024]{1,0:T(8,128)(2,1)}, bf16[256,1024]{1,0:T(8,128)(2,1)S(1)}, u32[]{:S(2)}, u32[]{:S(2)}) %collective-permute-start.10) | collective-permute-done | bytes 524320 | tf_op jit(solution)/shard_map/ppermute | solution.py:349
  113.6 6.3 %shard_map.70.acc_hbm = f32[4,1024,256]{2,1,0:T(8,128)S(1)} custom-call(bf16[1024,1536]{1,0:T(8,128)(2,1)S(1)} %get-tuple-element.13.refs_2_.late_hbm, f32[4,1024,256]{2,1,0:T(8,128)S(1)} %get-tuple-element.14.acc_hbm, bf16[256,1024]{1,0:T(8,128)(2,1)S(1)} %get-tuple-element.17.refs_0_, bf16[256,1024]{1,0:T(8,128)(2,1)S(1)} %collective-permute-done.9.refs_1_, ...), custom_call_target="tpu_custom_call" | custom-call | flops 2147483648 | bytes 12582912 | tf_op jit(solution)/shard_map/pallas_call | solution.py:233
  119.9 0.3 collective-permute-done.11.refs_0_
  120.3 3.0 %collective-permute-done.12.refs_1_ = bf16[256,1024]{1,0:T(8,128)(2,1)S(1)} collective-permute-done((bf16[256,1024]{1,0:T(8,128)(2,1)S(1)}, bf16[256,1024]{1,0:T(8,128)(2,1)S(1)}, u32[]{:S(2)}, u32[]{:S(2)}) %collective-permute-start.12) | collective-permute-done | bytes 524320 | tf_op jit(solution)/shard_map/ppermute | solution.py:354
  123.2 5.3 %shard_map.71 = bf16[1024,1024]{1,0:T(8,128)(2,1)} custom-call(bf16[1024,1536]{1,0:T(8,128)(2,1)S(1)} %get-tuple-element.13.refs_2_.late_hbm, f32[4,1024,256]{2,1,0:T(8,128)S(1)} %shard_map.70.acc_hbm, bf16[256,1024]{1,0:T(8,128)(2,1)S(1)} %collective-permute-done.11.refs_0_, bf16[256,1024]{1,0:T(8,128)(2,1)S(1)} %collective-permute-done.12.refs_1_), custom_call_target="tpu_custom_call" | custom-call | flops 1073741824 | bytes 10485760 | tf_op jit(solution)/shard_map/pallas_call | solution.py:233
  (32 shorter events, 0.5 us)
Async XLA Ops:
  0.0 57.1 %copy-start.9 = (s32[1,8]{1,0:T(1,128)S(1)}, s32[1,8]{1,0:T(1,128)}, u32[]{:S(2)}) copy-start(s32[1,8]{1,0:T(1,128)} %param.10) | copy-start | bytes 100
  0.0 40.9 %collective-permute-start = (bf16[512,1024]{1,0:T(8,128)(2,1)}, bf16[512,1024]{1,0:T(8,128)(2,1)S(1)}, u32[]{:S(2)}, u32[]{:S(2)}) collective-permute-start(bf16[512,1024]{1,0:T(8,128)(2,1)} %refs_4_.1), channel_id=1, source_target_pairs={{0,8},{8,16},{16,24},{24,28},{28,20},{20,12},{12,4},{4,0},{1,9},{9... | collective-permute-start | bytes 3145736 | tf_op jit(solution)/shard_map/ppermute | solution.py:320
  3.0 37.9 %collective-permute-start.1 = (bf16[512,1024]{1,0:T(8,128)(2,1)}, bf16[512,1024]{1,0:T(8,128)(2,1)}, u32[]{:S(2)}, u32[]{:S(2)}) collective-permute-start(bf16[512,1024]{1,0:T(8,128)(2,1)} %refs_4_.1), channel_id=1, source_target_pairs={{8,0},{16,8},{24,16},{28,24},{20,28},{12,20},{4,12},{0,4},{9,1},{1... | collective-permute-start | bytes 3145736 | tf_op jit(solution)/shard_map/ppermute | solution.py:321
  40.9 1.0 copy-start.1
  41.9 13.2 %collective-permute-start.2 = (bf16[8,272,128]{2,1,0:T(8,128)(2,1)}, bf16[8,272,128]{2,1,0:T(8,128)(2,1)S(1)}, u32[]{:S(2)}, u32[]{:S(2)}) collective-permute-start(bf16[8,272,128]{2,1,0:T(8,128)(2,1)} %shard_map.65.refs_0_), channel_id=1, source_target_pairs={{0,2},{1,3},{2,0},{3,1},{4,6},{5,7},{6,4},{7,5},{8,10},{9,11},{10,... | collective-permute-start | bytes 1671176 | tf_op jit(solution)/shard_map/ppermute | solution.py:300
  43.4 14.9 %collective-permute-start.3 = (bf16[8,272,128]{2,1,0:T(8,128)(2,1)}, bf16[8,272,128]{2,1,0:T(8,128)(2,1)}, u32[]{:S(2)}, u32[]{:S(2)}) collective-permute-start(bf16[8,272,128]{2,1,0:T(8,128)(2,1)} %shard_map.65.refs_0_), channel_id=1, source_target_pairs={{0,1},{1,0},{2,3},{3,2},{4,5},{5,4},{6,7},{7,6},{8,9},{9,8},{10,11... | collective-permute-start | bytes 1671176 | tf_op jit(solution)/shard_map/ppermute | solution.py:301
  55.1 4.1 %collective-permute-start.4 = (bf16[8,272,128]{2,1,0:T(8,128)(2,1)S(1)}, bf16[8,272,128]{2,1,0:T(8,128)(2,1)}, u32[]{:S(2)}, u32[]{:S(2)}) collective-permute-start(bf16[8,272,128]{2,1,0:T(8,128)(2,1)S(1)} %collective-permute-done.2.refs_1_), channel_id=1, source_target_pairs={{0,1},{1,0},{2,3},{3,2},{4,5},{5,4},{6,7},{7,6},{8,9},{9,8},{10,11... | collective-permute-start | bytes 1671176 | tf_op jit(solution)/shard_map/ppermute | solution.py:302
  55.1 25.8 %collective-permute-start.5 = (bf16[512,1024]{1,0:T(8,128)(2,1)}, bf16[512,1024]{1,0:T(8,128)(2,1)S(1)}, u32[]{:S(2)}, u32[]{:S(2)}) collective-permute-start(bf16[512,1024]{1,0:T(8,128)(2,1)} %copy-done.1), channel_id=1, source_target_pairs={{0,8},{8,16},{16,24},{24,28},{28,20},{20,12},{12,4},{4,0},{1,9},{9... | collective-permute-start | bytes 3145736 | tf_op jit(solution)/shard_map/ppermute | solution.py:320
  55.4 28.8 %collective-permute-start.6 = (bf16[512,1024]{1,0:T(8,128)(2,1)}, bf16[512,1024]{1,0:T(8,128)(2,1)S(1)}, u32[]{:S(2)}, u32[]{:S(2)}) collective-permute-start(bf16[512,1024]{1,0:T(8,128)(2,1)} %collective-permute-done.1.refs_2_.refs_6_), channel_id=1, source_target_pairs={{8,0},{16,8},{24,16},{28,24},{20,28},{12,20},{4,12},{0,4},{9,1},{1... | collective-permute-start | bytes 3145736 | tf_op jit(solution)/shard_map/ppermute | solution.py:321
  80.9 1.0 copy-start.3
  83.8 23.9 %collective-permute-start.7 = (bf16[256,1024]{1,0:T(8,128)(2,1)}, bf16[256,1024]{1,0:T(8,128)(2,1)S(1)}, u32[]{:S(2)}, u32[]{:S(2)}) collective-permute-start(bf16[256,1024]{1,0:T(8,128)(2,1)} %get-tuple-element.15), channel_id=1, source_target_pairs={{0,8},{8,16},{16,24},{24,28},{28,20},{20,12},{12,4},{4,0},{1,9},{9... | collective-permute-start | bytes 1572872 | tf_op jit(solution)/shard_map/ppermute | solution.py:346
  84.2 1.0 copy-start.5
  87.2 20.5 %collective-permute-start.8 = (bf16[256,1024]{1,0:T(8,128)(2,1)}, bf16[256,1024]{1,0:T(8,128)(2,1)S(1)}, u32[]{:S(2)}, u32[]{:S(2)}) collective-permute-start(bf16[256,1024]{1,0:T(8,128)(2,1)} %get-tuple-element.16), channel_id=1, source_target_pairs={{8,0},{16,8},{24,16},{28,24},{20,28},{12,20},{4,12},{0,4},{9,1},{1... | collective-permute-start | bytes 1572872 | tf_op jit(solution)/shard_map/ppermute | solution.py:347
  89.0 24.6 %collective-permute-start.10 = (bf16[256,1024]{1,0:T(8,128)(2,1)}, bf16[256,1024]{1,0:T(8,128)(2,1)S(1)}, u32[]{:S(2)}, u32[]{:S(2)}) collective-permute-start(bf16[256,1024]{1,0:T(8,128)(2,1)} %get-tuple-element.19), channel_id=1, source_target_pairs={{8,0},{16,8},{24,16},{28,24},{20,28},{12,20},{4,12},{0,4},{9,1},{1... | collective-permute-start | bytes 1572872 | tf_op jit(solution)/shard_map/ppermute | solution.py:349
  90.2 23.4 %collective-permute-start.9 = (bf16[256,1024]{1,0:T(8,128)(2,1)}, bf16[256,1024]{1,0:T(8,128)(2,1)S(1)}, u32[]{:S(2)}, u32[]{:S(2)}) collective-permute-start(bf16[256,1024]{1,0:T(8,128)(2,1)} %get-tuple-element.18), channel_id=1, source_target_pairs={{0,8},{8,16},{16,24},{24,28},{28,20},{20,12},{12,4},{4,0},{1,9},{9... | collective-permute-start | bytes 1572872 | tf_op jit(solution)/shard_map/ppermute | solution.py:348
  91.0 1.1 copy-start
  92.1 1.2 copy-start.2
  93.3 1.2 copy-start.4
  94.5 1.2 copy-start.6
  95.7 0.7 copy-start.7
  96.4 1.2 copy-start.8
  107.8 12.5 %collective-permute-start.11 = (bf16[256,1024]{1,0:T(8,128)(2,1)S(1)}, bf16[256,1024]{1,0:T(8,128)(2,1)S(1)}, u32[]{:S(2)}, u32[]{:S(2)}) collective-permute-start(bf16[256,1024]{1,0:T(8,128)(2,1)S(1)} %get-tuple-element.17.refs_0_), channel_id=1, source_target_pairs={{0,8},{8,16},{16,24},{24,28},{28,20},{20,12},{12,4},{4,0},{1,9},{9... | collective-permute-start | bytes 1572872 | tf_op jit(solution)/shard_map/ppermute | solution.py:353
  108.2 15.1 %collective-permute-start.12 = (bf16[256,1024]{1,0:T(8,128)(2,1)S(1)}, bf16[256,1024]{1,0:T(8,128)(2,1)S(1)}, u32[]{:S(2)}, u32[]{:S(2)}) collective-permute-start(bf16[256,1024]{1,0:T(8,128)(2,1)S(1)} %get-tuple-element.20.refs_3_), channel_id=1, source_target_pairs={{8,0},{16,8},{24,16},{28,24},{20,28},{12,20},{4,12},{0,4},{9,1},{1... | collective-permute-start | bytes 1572872 | tf_op jit(solution)/shard_map/ppermute | solution.py:354

commit v14 on v12

--- a/solution.py
+++ b/solution.py
@@ -11,6 +11,8 @@
 PARTS = 4
 CLEAR = 32
 VMEM_BYTES = 62 << 20
+FIRST_BYTES = 255 << 18
+SPARE_BYTES = 4 << 20
 
 
 def ring_order(n):
@@ -58,7 +60,7 @@
         in_specs=[anywhere] * (len(values) + len(others)),
         out_specs=[anywhere] * len(values),
         input_output_aliases={i: i for i in range(len(values))},
-        compiler_params=pltpu.CompilerParams(vmem_limit_bytes=VMEM_BYTES),
+        compiler_params=pltpu.CompilerParams(vmem_limit_bytes=SPARE_BYTES),
         cost_estimate=pl.CostEstimate(flops=0, bytes_accessed=0, transcendentals=0),
     )(*values, *others)
 
@@ -67,7 +69,8 @@
     parts = refs[:n_parts]
     rights = refs[n_parts : n_parts + len(depths)]
     refs = refs[n_parts + len(depths) :]
-    acc_hbm, late_hbm, left, right, acc, right_sem, acc_sem, late_sem = refs
+    acc_hbm, late_hbm, mark, left, right, acc, right_sem, acc_sem, late_sem = refs
+    mark[...] = jnp.zeros_like(mark)
     inner, bn = right.shape[0], acc.shape[-1]
     at, fetches = 0, []
     for i, (depth, source) in enumerate(zip(depths, rights)):
@@ -118,15 +121,7 @@
 
     def multiply(j, carry):
         cols = pl.ds(pl.multiple_of(j * bn, bn), bn)
-
-        def turn(q, inner_carry):
-            rows = pl.ds(pl.multiple_of(q * some, some), some)
-            acc[j, rows] = jnp.dot(
-                left[rows, :inner], right[:, cols], preferred_element_type=jnp.float32
-            )
-            return inner_carry
-
-        lax.fori_loop(0, PARTS, turn, 0)
+        acc[j] = jnp.dot(left[:, :inner], right[:, cols], preferred_element_type=jnp.float32)
         pltpu.make_async_copy(acc.at[j], acc_hbm.at[j], acc_sem.at[j]).start()
         return carry
 
@@ -147,11 +142,12 @@
         out_shape=[
             jax.ShapeDtypeStruct((steps, rows, bn), jnp.float32),
             jax.ShapeDtypeStruct((rows, late_width), jnp.bfloat16),
+            jax.ShapeDtypeStruct((8, bs), jnp.float32),
         ],
         in_specs=[pl.BlockSpec(memory_space=pltpu.SMEM)]
         + [pl.BlockSpec(memory_space=pltpu.VMEM)] * len(parts)
         + [anywhere] * len(rights),
-        out_specs=[anywhere] * 2,
+        out_specs=[anywhere] * 2 + [pl.BlockSpec(memory_space=pltpu.VMEM)],
         scratch_shapes=[
             pltpu.VMEM((rows, inner + late_width), jnp.bfloat16),
             pltpu.VMEM((inner, cols), jnp.bfloat16),
@@ -160,7 +156,7 @@
             pltpu.SemaphoreType.DMA((steps,)),
             pltpu.SemaphoreType.DMA((PARTS,)),
         ],
-        compiler_params=pltpu.CompilerParams(vmem_limit_bytes=VMEM_BYTES),
+        compiler_params=pltpu.CompilerParams(vmem_limit_bytes=FIRST_BYTES),
         cost_estimate=pl.CostEstimate(
             flops=2 * rows * inner * cols,
             bytes_accessed=inner * cols * 2 + rows * cols * 4,
@@ -248,7 +244,9 @@
             pltpu.SemaphoreType.DMA((steps,)),
             pltpu.SemaphoreType.DMA((steps,)),
         ],
-        compiler_params=pltpu.CompilerParams(vmem_limit_bytes=VMEM_BYTES),
+        compiler_params=pltpu.CompilerParams(
+            vmem_limit_bytes=SPARE_BYTES + 2 * inner * (rows + steps * bn) + 8 * rows * steps * bn
+        ),
         cost_estimate=pl.CostEstimate(
             flops=2 * rows * inner * steps * bn,
             bytes_accessed=(rows + steps * bn) * inner * 2 + rows * steps * bn * 8,
@@ -314,8 +312,8 @@
     dest = row * (blocks * groups) + first * blocks + col % blocks
     dest = jnp.where(jnp.any(hit, axis=-1), dest, -1)
 
-    acc, late = first_product(dest, parts, early, rb * bs, 3 * k_local, bs, cap, n_local // 4)
-    left_low, right_high = after([left_low, right_high], [late])
+    acc, late, mark = first_product(dest, parts, early, rb * bs, 3 * k_local, bs, cap, n_local // 4)
+    left_low, right_high = after([left_low, right_high], [mark])
     low = lax.ppermute(left_low, "grid", to_right)
     high = lax.ppermute(right_high, "grid", to_left)
     acc = add_product(late, 0, [left_low, left_high, right_low, right_high], acc, False)

time: 110 us -> 110 us (level)
  Pallas kernels: 31.4 us -> 27.3 us
  waiting for transfers between devices: 41.2 us -> 44.1 us
  local copies, waits for them, and re-layouts: 10.4 us -> 11.8 us
    ppermute x1, waiting for transfers between devices: 4.94 us -> 7.13 us  [body(): right_low = lax.ppermute(right_low, 'grid', to_left)]
    pallas_call x2, Pallas kernels: 14.5 us -> 12.3 us  [add_product(): pl.pallas_call(functools.partial(add_kernel, depths, place), out_shape=ou...]
    unnamed x18, local copies, waits for them, and re-layouts: 2.65 us -> 4.77 us
    pallas_call x1, Pallas kernels: 13.7 us -> 11.9 us  [first_product(): pl.pallas_call(functools.partial(first_kernel, depths, parts[0].shape[0],...]
    ppermute x2, waiting for transfers between devices: 14.3 us -> 16.1 us  [body(): from_left = lax.ppermute(from_left, 'grid', to_right)]
  transfers between devices with their start and end apart: 14 -> 14, of which waited for: 6 -> 5; matrix products, arithmetic and copies ran while one was open for 10% -> 9% of each run, Pallas kernels for 23% -> 20%
where the time goes in v14:
time: 110 us
  waiting for transfers between devices  44.1 us (40%)
  Pallas kernels  27.3 us (25%)
  starting transfers between devices  23.3 us (21%)
  local copies, waits for them, and re-layouts  11.8 us (11%)
  other arithmetic  2.72 us (2%)
    ppermute x2, waiting for transfers between devices, body(): from_left = lax.ppermute(from_left, 'grid', to_right)  16.1 us
    pallas_call x2, Pallas kernels, add_product(): pl.pallas_call(functools.partial(add_kernel, depths, place), out_shape=ou...  12.3 us
    pallas_call x1, Pallas kernels, first_product(): pl.pallas_call(functools.partial(first_kernel, depths, parts[0].shape[0],...  11.9 us
    all_to_all x1, waiting for transfers between devices, body(): lax.all_to_all(message, 'grid', split_axis=0, concat_axis=0, tiled=True)  11.9 us
    ppermute x1, waiting for transfers between devices, across_row(): across = lax.ppermute(landed, 'blk', swap_chip)  9.03 us
    ppermute x1, waiting for transfers between devices, body(): right_low = lax.ppermute(right_low, 'grid', to_left)  7.13 us
    ppermute x2, starting transfers between devices, body(): from_left = lax.ppermute(from_left, 'grid', to_right)  6.33 us
    all_to_all x1, starting transfers between devices, body(): lax.all_to_all(message, 'grid', split_axis=0, concat_axis=0, tiled=True)  6.28 us
  transfers between devices with their start and end apart: 14, of which 5 were waited for; matrix products, arithmetic and copies ran while one was open for 9% of the time, Pallas kernels for 20%

profile of v14, /device:TPU:0, one launch (start us, length us, event | category | flops | bytes accessed | tf_op | source)
XLA Modules:
  0.0 109.5 jit_solution(9767199448581753487)
XLA Ops:
  0.0 3.0 %collective-permute-start = (bf16[512,1024]{1,0:T(8,128)(2,1)}, bf16[512,1024]{1,0:T(8,128)(2,1)S(1)}, u32[]{:S(2)}, u32[]{:S(2)}) collective-permute-start(bf16[512,1024]{1,0:T(8,128)(2,1)} %refs_4_.1), channel_id=1, source_target_pairs={{0,8},{8,16},{16,24},{24,28},{28,20},{20,12},{12,4},{4,0},{1,9},{9... | collective-permute-start | bytes 3145736 | tf_op jit(solution)/shard_map/ppermute | solution.py:284
  3.0 0.7 convert_bitcast_fusion
  3.7 0.7 fusion.11
  4.4 0.1 copy.29
  4.5 0.6 pad.4.meta_ref
  5.1 3.2 %shard_map.64 = bf16[8,272,128]{2,1,0:T(8,128)(2,1)} custom-call(bf16[8,256,128]{2,1,0:T(8,128)(2,1)} %bitcast.17, bf16[8,16,128]{2,1,0:T(8,128)(2,1)} %pad.4.meta_ref), custom_call_target="tpu_custom_call" | custom-call | bytes 1048576 | tf_op jit(solution)/shard_map/pallas_call | solution.py:35
  8.3 6.3 %all-to-all-start = ((bf16[8,272,128]{2,1,0:T(8,128)(2,1)}), bf16[8,272,128]{2,1,0:T(8,128)(2,1)S(1)}, u32[]{:S(2)}, u32[]{:S(2)}) async-start(bf16[8,272,128]{2,1,0:T(8,128)(2,1)} %shard_map.64), calls=%async_computation | async-start | bytes 1114112 | tf_op jit(solution)/shard_map/all_to_all | solution.py:300
  14.6 12.5 %collective-permute-done.refs_1_.refs_5_ = bf16[512,1024]{1,0:T(8,128)(2,1)S(1)} collective-permute-done((bf16[512,1024]{1,0:T(8,128)(2,1)}, bf16[512,1024]{1,0:T(8,128)(2,1)S(1)}, u32[]{:S(2)}, u32[]{:S(2)}) %collective-permute-start) | collective-permute-done | bytes 1048608 | tf_op jit(solution)/shard_map/ppermute | solution.py:284
  27.1 3.3 %collective-permute-start.5 = (bf16[512,1024]{1,0:T(8,128)(2,1)S(1)}, bf16[512,1024]{1,0:T(8,128)(2,1)}, u32[]{:S(2)}, u32[]{:S(2)}) collective-permute-start(bf16[512,1024]{1,0:T(8,128)(2,1)S(1)} %collective-permute-done.refs_1_.refs_5_), channel_id=1, source_target_pairs={{0,8},{8,16},{16,24},{24,28},{28,20},{20,12},{12,4},{4,0},{1,9},{9... | collective-permute-start | bytes 3145736 | tf_op jit(solution)/shard_map/ppermute | solution.py:284
  30.4 11.9 %all-to-all-done.refs_0_ = bf16[8,272,128]{2,1,0:T(8,128)(2,1)S(1)} async-done(((bf16[8,272,128]{2,1,0:T(8,128)(2,1)}), bf16[8,272,128]{2,1,0:T(8,128)(2,1)S(1)}, u32[]{:S(2)}, u32[]{:S(2)}) %all-to-all-start) | async-done | bytes 557088 | tf_op jit(solution)/shard_map/all_to_all | solution.py:300
  42.3 1.5 %collective-permute-start.2 = (bf16[8,272,128]{2,1,0:T(8,128)(2,1)S(1)}, bf16[8,272,128]{2,1,0:T(8,128)(2,1)S(1)}, u32[]{:S(2)}, u32[]{:S(2)}) collective-permute-start(bf16[8,272,128]{2,1,0:T(8,128)(2,1)S(1)} %shard_map.65.refs_0_), channel_id=1, source_target_pairs={{0,2},{1,3},{2,0},{3,1},{4,6},{5,7},{6,4},{7,5},{8,10},{9,11},{10,... | collective-permute-start | bytes 1671176 | tf_op jit(solution)/shard_map/ppermute | solution.py:264
  43.8 0.0 collective-permute-start.3
  43.8 9.0 %collective-permute-done.2.refs_1_ = bf16[8,272,128]{2,1,0:T(8,128)(2,1)S(1)} collective-permute-done((bf16[8,272,128]{2,1,0:T(8,128)(2,1)S(1)}, bf16[8,272,128]{2,1,0:T(8,128)(2,1)S(1)}, u32[]{:S(2)}, u32[]{:S(2)}) %collective-permute-start.2) | collective-permute-done | bytes 557088 | tf_op jit(solution)/shard_map/ppermute | solution.py:264
  52.8 0.0 collective-permute-start.4
  52.9 0.1 copy.30
  53.0 0.1 copy.34
  53.1 0.1 copy.31
  53.2 0.1 copy.35
  53.3 0.1 copy.32
  53.4 0.1 copy.36
  53.5 3.6 %collective-permute-done.5.refs_7_ = bf16[512,1024]{1,0:T(8,128)(2,1)} collective-permute-done((bf16[512,1024]{1,0:T(8,128)(2,1)S(1)}, bf16[512,1024]{1,0:T(8,128)(2,1)}, u32[]{:S(2)}, u32[]{:S(2)}) %collective-permute-start.5) | collective-permute-done | bytes 1048608 | tf_op jit(solution)/shard_map/ppermute | solution.py:284
  57.1 2.2 %fusion.13 = (bf16[256,1024]{1,0:T(8,128)(2,1)}, bf16[256,1024]{1,0:T(8,128)(2,1)}) fusion(bf16[512,1024]{1,0:T(8,128)(2,1)} %collective-permute-done.5.refs_7_), kind=kLoop, calls=%fused_computation.37 | loop fusion | bytes 2097152 | tf_op jit(solution)/shard_map/slice | solution.py:289
  59.3 4.6 %collective-permute-start.7 = (bf16[256,1024]{1,0:T(8,128)(2,1)}, bf16[256,1024]{1,0:T(8,128)(2,1)}, u32[]{:S(2)}, u32[]{:S(2)}) collective-permute-start(bf16[256,1024]{1,0:T(8,128)(2,1)} %get-tuple-element.18), channel_id=1, source_target_pairs={{0,8},{8,16},{16,24},{24,28},{28,20},{20,12},{12,4},{4,0},{1,9},{9... | collective-permute-start | bytes 1572872 | tf_op jit(solution)/shard_map/ppermute | solution.py:290
  63.9 0.0 collective-permute-done.6.refs_8_
  63.9 2.2 %fusion.12 = (bf16[256,1024]{1,0:T(8,128)(2,1)}, bf16[256,1024]{1,0:T(8,128)(2,1)}) fusion(bf16[512,1024]{1,0:T(8,128)(2,1)} %collective-permute-done.6.refs_8_), kind=kLoop, calls=%fused_computation.36 | loop fusion | bytes 2097152 | tf_op jit(solution)/shard_map/slice | solution.py:289
  66.1 2.5 %collective-permute-start.10 = (bf16[256,1024]{1,0:T(8,128)(2,1)}, bf16[256,1024]{1,0:T(8,128)(2,1)}, u32[]{:S(2)}, u32[]{:S(2)}) collective-permute-start(bf16[256,1024]{1,0:T(8,128)(2,1)} %get-tuple-element.15), channel_id=1, source_target_pairs={{8,0},{16,8},{24,16},{28,24},{20,28},{12,20},{4,12},{0,4},{9,1},{1... | collective-permute-start | bytes 1572872 | tf_op jit(solution)/shard_map/ppermute | solution.py:293
  68.7 0.1 collective-permute-start.9
  68.8 0.0 collective-permute-done.4.refs_3_
  68.8 0.7 slice.43
  69.5 0.1 copy.33
  69.6 0.1 copy.37
  69.7 0.1 copy.38
  69.8 0.3 fusion
  70.1 0.3 compare_reduce_fusion
  70.4 0.1 copy.39
  70.5 0.1 copy.40
  70.6 0.7 fusion.6.dest_ref
  71.4 11.9 %shard_map.66 = (f32[4,1024,256]{2,1,0:T(8,128)}, bf16[1024,1536]{1,0:T(8,128)(2,1)}, f32[8,128]{1,0:T(8,128)}) custom-call(s32[4,8,2]{2,1,0:T(8,128)} %fusion.6.dest_ref, bf16[8,272,128]{2,1,0:T(8,128)(2,1)} %copy-done.3, bf16[8,272,128]{2,1,0:T(8,128)(2,1)} %copy-done.6, bf16[8,272,128]{2,1,0:T(8,128)(2,1)} %copy-done.7, ...), custom_call_target="tpu_custom_call" | custom-call | flops 5368709120 | bytes 9437184 | tf_op jit(solution)/shard_map/pallas_call | solution.py:140
  83.3 0.0 collective-permute-done.7.refs_0_
  83.3 0.0 collective-permute-done.8.refs_1_
  83.3 0.7 copy-done.5
  84.0 2.0 %collective-permute-start.11 = (bf16[256,1024]{1,0:T(8,128)(2,1)}, bf16[256,1024]{1,0:T(8,128)(2,1)S(1)}, u32[]{:S(2)}, u32[]{:S(2)}) collective-permute-start(bf16[256,1024]{1,0:T(8,128)(2,1)} %get-tuple-element.13.refs_0_), channel_id=1, source_target_pairs={{0,8},{8,16},{16,24},{24,28},{28,20},{20,12},{12,4},{4,0},{1,9},{9... | collective-permute-start | bytes 1572872 | tf_op jit(solution)/shard_map/ppermute | solution.py:317
  86.0 0.0 collective-permute-start.12
  86.0 7.1 %collective-permute-done.10.refs_2_ = bf16[256,1024]{1,0:T(8,128)(2,1)} collective-permute-done((bf16[256,1024]{1,0:T(8,128)(2,1)}, bf16[256,1024]{1,0:T(8,128)(2,1)}, u32[]{:S(2)}, u32[]{:S(2)}) %collective-permute-start.10) | collective-permute-done | bytes 524320 | tf_op jit(solution)/shard_map/ppermute | solution.py:293
  93.1 1.9 %copy-done = bf16[1024,1536]{1,0:T(8,128)(2,1)S(1)} copy-done((bf16[1024,1536]{1,0:T(8,128)(2,1)S(1)}, bf16[1024,1536]{1,0:T(8,128)(2,1)}, u32[]{:S(2)}) %copy-start) | copy-done | bytes 3145752
  95.0 2.2 %copy-done.2 = f32[4,1024,256]{2,1,0:T(8,128)S(1)} copy-done((f32[4,1024,256]{2,1,0:T(8,128)S(1)}, f32[4,1024,256]{2,1,0:T(8,128)}, u32[]{:S(2)}) %copy-start.2) | copy-done | bytes 4194328
  97.2 7.0 %shard_map.68.acc_hbm = f32[4,1024,256]{2,1,0:T(8,128)S(1)} custom-call(bf16[1024,1536]{1,0:T(8,128)(2,1)S(1)} %copy-done, f32[4,1024,256]{2,1,0:T(8,128)S(1)} %copy-done.2, bf16[256,1024]{1,0:T(8,128)(2,1)} %get-tuple-element.13.refs_0_, bf16[256,1024]{1,0:T(8,128)(2,1)} %collective-permute-done.9.refs_1_, ...), custom_call_target="tpu_custom_call" | custom-call | flops 2147483648 | bytes 12582912 | tf_op jit(solution)/shard_map/pallas_call | solution.py:232
  104.2 5.3 %shard_map.69 = bf16[1024,1024]{1,0:T(8,128)(2,1)} custom-call(bf16[1024,1536]{1,0:T(8,128)(2,1)S(1)} %copy-done.1, f32[4,1024,256]{2,1,0:T(8,128)S(1)} %shard_map.68.acc_hbm, bf16[256,1024]{1,0:T(8,128)(2,1)S(1)} %collective-permute-done.11.refs_0_, bf16[256,1024]{1,0:T(8,128)(2,1)S(1)} %collective-permute-done.12.refs_1_), custom_call_target="tpu_custom_call" | custom-call | flops 1073741824 | bytes 10485760 | tf_op jit(solution)/shard_map/pallas_call | solution.py:232
  (31 shorter events, 0.1 us)
Async XLA Ops:
  0.0 52.8 %copy-start.8 = (s32[1,8]{1,0:T(1,128)S(1)}, s32[1,8]{1,0:T(1,128)}, u32[]{:S(2)}) copy-start(s32[1,8]{1,0:T(1,128)} %param.10) | copy-start | bytes 100
  0.0 27.1 %collective-permute-start = (bf16[512,1024]{1,0:T(8,128)(2,1)}, bf16[512,1024]{1,0:T(8,128)(2,1)S(1)}, u32[]{:S(2)}, u32[]{:S(2)}) collective-permute-start(bf16[512,1024]{1,0:T(8,128)(2,1)} %refs_4_.1), channel_id=1, source_target_pairs={{0,8},{8,16},{16,24},{24,28},{28,20},{20,12},{12,4},{4,0},{1,9},{9... | collective-permute-start | bytes 3145736 | tf_op jit(solution)/shard_map/ppermute | solution.py:284
  3.0 27.4 %collective-permute-start.1 = (bf16[512,1024]{1,0:T(8,128)(2,1)}, bf16[512,1024]{1,0:T(8,128)(2,1)}, u32[]{:S(2)}, u32[]{:S(2)}) collective-permute-start(bf16[512,1024]{1,0:T(8,128)(2,1)} %refs_4_.1), channel_id=1, source_target_pairs={{8,0},{16,8},{24,16},{28,24},{20,28},{12,20},{4,12},{0,4},{9,1},{1... | collective-permute-start | bytes 3145736 | tf_op jit(solution)/shard_map/ppermute | solution.py:285
  8.3 34.0 %all-to-all-start = ((bf16[8,272,128]{2,1,0:T(8,128)(2,1)}), bf16[8,272,128]{2,1,0:T(8,128)(2,1)S(1)}, u32[]{:S(2)}, u32[]{:S(2)}) async-start(bf16[8,272,128]{2,1,0:T(8,128)(2,1)} %shard_map.64), calls=%async_computation | async-start | bytes 1114112 | tf_op jit(solution)/shard_map/all_to_all | solution.py:300
  27.1 26.2 %copy-start.4 = (bf16[512,1024]{1,0:T(8,128)(2,1)}, bf16[512,1024]{1,0:T(8,128)(2,1)S(1)}, u32[]{:S(2)}) copy-start(bf16[512,1024]{1,0:T(8,128)(2,1)S(1)} %collective-permute-done.refs_1_.refs_5_) | copy-start | bytes 3145732
  27.1 30.0 %collective-permute-start.5 = (bf16[512,1024]{1,0:T(8,128)(2,1)S(1)}, bf16[512,1024]{1,0:T(8,128)(2,1)}, u32[]{:S(2)}, u32[]{:S(2)}) collective-permute-start(bf16[512,1024]{1,0:T(8,128)(2,1)S(1)} %collective-permute-done.refs_1_.refs_5_), channel_id=1, source_target_pairs={{0,8},{8,16},{16,24},{24,28},{28,20},{20,12},{12,4},{4,0},{1,9},{9... | collective-permute-start | bytes 3145736 | tf_op jit(solution)/shard_map/ppermute | solution.py:284
  30.4 33.5 %collective-permute-start.6 = (bf16[512,1024]{1,0:T(8,128)(2,1)}, bf16[512,1024]{1,0:T(8,128)(2,1)}, u32[]{:S(2)}, u32[]{:S(2)}) collective-permute-start(bf16[512,1024]{1,0:T(8,128)(2,1)} %collective-permute-done.1.refs_2_.refs_6_), channel_id=1, source_target_pairs={{8,0},{16,8},{24,16},{28,24},{20,28},{12,20},{4,12},{0,4},{9,1},{1... | collective-permute-start | bytes 3145736 | tf_op jit(solution)/shard_map/ppermute | solution.py:285
  42.3 10.6 %copy-start.3 = (bf16[8,272,128]{2,1,0:T(8,128)(2,1)}, bf16[8,272,128]{2,1,0:T(8,128)(2,1)S(1)}, u32[]{:S(2)}) copy-start(bf16[8,272,128]{2,1,0:T(8,128)(2,1)S(1)} %shard_map.65.refs_0_) | copy-start | bytes 1671172
  42.3 10.5 %collective-permute-start.2 = (bf16[8,272,128]{2,1,0:T(8,128)(2,1)S(1)}, bf16[8,272,128]{2,1,0:T(8,128)(2,1)S(1)}, u32[]{:S(2)}, u32[]{:S(2)}) collective-permute-start(bf16[8,272,128]{2,1,0:T(8,128)(2,1)S(1)} %shard_map.65.refs_0_), channel_id=1, source_target_pairs={{0,2},{1,3},{2,0},{3,1},{4,6},{5,7},{6,4},{7,5},{8,10},{9,11},{10,... | collective-permute-start | bytes 1671176 | tf_op jit(solution)/shard_map/ppermute | solution.py:264
  43.8 9.5 %collective-permute-start.3 = (bf16[8,272,128]{2,1,0:T(8,128)(2,1)S(1)}, bf16[8,272,128]{2,1,0:T(8,128)(2,1)S(1)}, u32[]{:S(2)}, u32[]{:S(2)}) collective-permute-start(bf16[8,272,128]{2,1,0:T(8,128)(2,1)S(1)} %shard_map.65.refs_0_), channel_id=1, source_target_pairs={{0,1},{1,0},{2,3},{3,2},{4,5},{5,4},{6,7},{7,6},{8,9},{9,8},{10,11... | collective-permute-start | bytes 1671176 | tf_op jit(solution)/shard_map/ppermute | solution.py:265
  52.8 17.8 %copy-start.6 = (bf16[8,272,128]{2,1,0:T(8,128)(2,1)}, bf16[8,272,128]{2,1,0:T(8,128)(2,1)S(1)}, u32[]{:S(2)}) copy-start(bf16[8,272,128]{2,1,0:T(8,128)(2,1)S(1)} %collective-permute-done.2.refs_1_) | copy-start | bytes 1671172
  52.8 16.0 %collective-permute-start.4 = (bf16[8,272,128]{2,1,0:T(8,128)(2,1)S(1)}, bf16[8,272,128]{2,1,0:T(8,128)(2,1)}, u32[]{:S(2)}, u32[]{:S(2)}) collective-permute-start(bf16[8,272,128]{2,1,0:T(8,128)(2,1)S(1)} %collective-permute-done.2.refs_1_), channel_id=1, source_target_pairs={{0,1},{1,0},{2,3},{3,2},{4,5},{5,4},{6,7},{7,6},{8,9},{9,8},{10,11... | collective-permute-start | bytes 1671176 | tf_op jit(solution)/shard_map/ppermute | solution.py:266
  53.3 17.4 %copy-start.7 = (bf16[8,272,128]{2,1,0:T(8,128)(2,1)}, bf16[8,272,128]{2,1,0:T(8,128)(2,1)S(1)}, u32[]{:S(2)}) copy-start(bf16[8,272,128]{2,1,0:T(8,128)(2,1)S(1)} %collective-permute-done.3.refs_2_) | copy-start | bytes 1671172
  59.3 23.9 %collective-permute-start.7 = (bf16[256,1024]{1,0:T(8,128)(2,1)}, bf16[256,1024]{1,0:T(8,128)(2,1)}, u32[]{:S(2)}, u32[]{:S(2)}) collective-permute-start(bf16[256,1024]{1,0:T(8,128)(2,1)} %get-tuple-element.18), channel_id=1, source_target_pairs={{0,8},{8,16},{16,24},{24,28},{28,20},{20,12},{12,4},{4,0},{1,9},{9... | collective-permute-start | bytes 1572872 | tf_op jit(solution)/shard_map/ppermute | solution.py:290
  66.1 17.1 %collective-permute-start.8 = (bf16[256,1024]{1,0:T(8,128)(2,1)}, bf16[256,1024]{1,0:T(8,128)(2,1)}, u32[]{:S(2)}, u32[]{:S(2)}) collective-permute-start(bf16[256,1024]{1,0:T(8,128)(2,1)} %get-tuple-element.16), channel_id=1, source_target_pairs={{8,0},{16,8},{24,16},{28,24},{20,28},{12,20},{4,12},{0,4},{9,1},{1... | collective-permute-start | bytes 1572872 | tf_op jit(solution)/shard_map/ppermute | solution.py:291
  66.1 27.0 %collective-permute-start.10 = (bf16[256,1024]{1,0:T(8,128)(2,1)}, bf16[256,1024]{1,0:T(8,128)(2,1)}, u32[]{:S(2)}, u32[]{:S(2)}) collective-permute-start(bf16[256,1024]{1,0:T(8,128)(2,1)} %get-tuple-element.15), channel_id=1, source_target_pairs={{8,0},{16,8},{24,16},{28,24},{20,28},{12,20},{4,12},{0,4},{9,1},{1... | collective-permute-start | bytes 1572872 | tf_op jit(solution)/shard_map/ppermute | solution.py:293
  68.7 24.4 %collective-permute-start.9 = (bf16[256,1024]{1,0:T(8,128)(2,1)}, bf16[256,1024]{1,0:T(8,128)(2,1)}, u32[]{:S(2)}, u32[]{:S(2)}) collective-permute-start(bf16[256,1024]{1,0:T(8,128)(2,1)} %get-tuple-element.17), channel_id=1, source_target_pairs={{0,8},{8,16},{16,24},{24,28},{28,20},{20,12},{12,4},{4,0},{1,9},{9... | collective-permute-start | bytes 1572872 | tf_op jit(solution)/shard_map/ppermute | solution.py:292
  83.3 0.7 copy-start.5
  84.0 20.3 %collective-permute-start.11 = (bf16[256,1024]{1,0:T(8,128)(2,1)}, bf16[256,1024]{1,0:T(8,128)(2,1)S(1)}, u32[]{:S(2)}, u32[]{:S(2)}) collective-permute-start(bf16[256,1024]{1,0:T(8,128)(2,1)} %get-tuple-element.13.refs_0_), channel_id=1, source_target_pairs={{0,8},{8,16},{16,24},{24,28},{28,20},{20,12},{12,4},{4,0},{1,9},{9... | collective-permute-start | bytes 1572872 | tf_op jit(solution)/shard_map/ppermute | solution.py:317
  86.0 18.3 %collective-permute-start.12 = (bf16[256,1024]{1,0:T(8,128)(2,1)}, bf16[256,1024]{1,0:T(8,128)(2,1)S(1)}, u32[]{:S(2)}, u32[]{:S(2)}) collective-permute-start(bf16[256,1024]{1,0:T(8,128)(2,1)} %get-tuple-element.14.refs_3_), channel_id=1, source_target_pairs={{8,0},{16,8},{24,16},{28,24},{20,28},{12,20},{4,12},{0,4},{9,1},{1... | collective-permute-start | bytes 1572872 | tf_op jit(solution)/shard_map/ppermute | solution.py:318
  93.1 1.9 %copy-start = (bf16[1024,1536]{1,0:T(8,128)(2,1)S(1)}, bf16[1024,1536]{1,0:T(8,128)(2,1)}, u32[]{:S(2)}) copy-start(bf16[1024,1536]{1,0:T(8,128)(2,1)} %get-tuple-element.10.late_hbm) | copy-start | bytes 9437188
  95.0 2.2 %copy-start.2 = (f32[4,1024,256]{2,1,0:T(8,128)S(1)}, f32[4,1024,256]{2,1,0:T(8,128)}, u32[]{:S(2)}) copy-start(f32[4,1024,256]{2,1,0:T(8,128)} %get-tuple-element.11.acc_hbm) | copy-start | bytes 12582916
  97.2 7.0 %copy-start.1 = (bf16[1024,1536]{1,0:T(8,128)(2,1)S(1)}, bf16[1024,1536]{1,0:T(8,128)(2,1)}, u32[]{:S(2)}) copy-start(bf16[1024,1536]{1,0:T(8,128)(2,1)} %get-tuple-element.10.late_hbm) | copy-start | bytes 9437188

commit v15 on v14

--- a/solution.py
+++ b/solution.py
@@ -11,7 +11,9 @@
 PARTS = 4
 CLEAR = 32
 VMEM_BYTES = 62 << 20
-FIRST_BYTES = 255 << 18
+FIRST_BYTES = 26 << 20
+ADD_BYTES = 18 << 20
+LARGE = 4 << 20
 SPARE_BYTES = 4 << 20
 
 
@@ -69,9 +71,14 @@
     parts = refs[:n_parts]
     rights = refs[n_parts : n_parts + len(depths)]
     refs = refs[n_parts + len(depths) :]
-    acc_hbm, late_hbm, mark, left, right, acc, right_sem, acc_sem, late_sem = refs
+    acc_hbm, late_hbm, mark, left, right, acc, held, right_sem, acc_sem, late_sem, part_sem = refs
     mark[...] = jnp.zeros_like(mark)
     inner, bn = right.shape[0], acc.shape[-1]
+    part_copies = [
+        pltpu.make_async_copy(part, held.at[q], part_sem.at[q]) for q, part in enumerate(parts)
+    ]
+    for copy in part_copies:
+        copy.start()
     at, fetches = 0, []
     for i, (depth, source) in enumerate(zip(depths, rights)):
         fetches.append(
@@ -89,7 +96,8 @@
 
     lax.fori_loop(0, left.shape[0] // CLEAR, clear, 0)
     k_blocks = left.shape[1] // bs
-    for q, part in enumerate(parts):
+    for q in range(n_parts):
+        part_copies[q].wait()
 
         def place(i, carry):
             for c in range(cap):
@@ -101,7 +109,7 @@
                     left[
                         pl.ds(pl.multiple_of(row * bs, bs), bs),
                         pl.ds(pl.multiple_of(col * bs, bs), bs),
-                    ] = part[i, pl.ds(c * bs, bs), :]
+                    ] = held[q, i, pl.ds(c * bs, bs), :]
 
             return carry
 
@@ -145,18 +153,19 @@
             jax.ShapeDtypeStruct((8, bs), jnp.float32),
         ],
         in_specs=[pl.BlockSpec(memory_space=pltpu.SMEM)]
-        + [pl.BlockSpec(memory_space=pltpu.VMEM)] * len(parts)
-        + [anywhere] * len(rights),
+        + [pl.BlockSpec(memory_space=pltpu.HBM)] * (len(parts) + len(rights)),
         out_specs=[anywhere] * 2 + [pl.BlockSpec(memory_space=pltpu.VMEM)],
         scratch_shapes=[
             pltpu.VMEM((rows, inner + late_width), jnp.bfloat16),
             pltpu.VMEM((inner, cols), jnp.bfloat16),
             pltpu.VMEM((steps, rows, bn), jnp.float32),
+            pltpu.VMEM((len(parts),) + parts[0].shape, parts[0].dtype),
             pltpu.SemaphoreType.DMA((len(rights),)),
             pltpu.SemaphoreType.DMA((steps,)),
             pltpu.SemaphoreType.DMA((PARTS,)),
+            pltpu.SemaphoreType.DMA((len(parts),)),
         ],
-        compiler_params=pltpu.CompilerParams(vmem_limit_bytes=FIRST_BYTES),
+        compiler_params=pltpu.CompilerParams(vmem_limit_bytes=FIRST_BYTES if cols * inner < LARGE else VMEM_BYTES),
         cost_estimate=pl.CostEstimate(
             flops=2 * rows * inner * cols,
             bytes_accessed=inner * cols * 2 + rows * cols * 4,
@@ -245,7 +254,7 @@
             pltpu.SemaphoreType.DMA((steps,)),
         ],
         compiler_params=pltpu.CompilerParams(
-            vmem_limit_bytes=SPARE_BYTES + 2 * inner * (rows + steps * bn) + 8 * rows * steps * bn
+            vmem_limit_bytes=ADD_BYTES
         ),
         cost_estimate=pl.CostEstimate(
             flops=2 * rows * inner * steps * bn,

time: 110 us -> 107 us (0.973)
  Pallas kernels: 27.3 us -> 24.9 us
  local copies, waits for them, and re-layouts: 11.8 us -> 10.3 us
  waiting for transfers between devices: 44.1 us -> 45.6 us
    ppermute x1, waiting for transfers between devices: 0.01 us -> 2.46 us  [body(): high = lax.ppermute(right_high, 'grid', to_left)]
    pallas_call x1, Pallas kernels: 11.9 us -> 9.78 us  [first_product(): pl.pallas_call(functools.partial(first_kernel, depths, parts[0].shape[0],...]
    slice x2, local copies, waits for them, and re-layouts: 4.49 us -> 3.38 us  [body(): left_high, right_low = (from_left[split:], from_right[:split])]
    unnamed x18 -> x12, local copies, waits for them, and re-layouts: 4.77 us -> 3.7 us
  transfers between devices with their start and end apart: 14 -> 14, of which waited for: 5 -> 6; matrix products, arithmetic and copies ran while one was open for 9% -> 8% of each run, Pallas kernels for 20% -> 18%
where the time goes in v15:
time: 107 us; the launch traced here: 106 us
  waiting for transfers between devices  45.6 us (43%)
  Pallas kernels  24.9 us (23%)
  starting transfers between devices  23.3 us (22%)
  local copies, waits for them, and re-layouts  10.3 us (10%)
  other arithmetic  2.12 us (2%)
    ppermute x2, waiting for transfers between devices, body(): from_left = lax.ppermute(from_left, 'grid', to_right)  15.3 us
    pallas_call x2, Pallas kernels, add_product(): pl.pallas_call(functools.partial(add_kernel, depths, place), out_shape=ou...  12 us
    all_to_all x1, waiting for transfers between devices, body(): lax.all_to_all(message, 'grid', split_axis=0, concat_axis=0, tiled=True)  11.9 us
    pallas_call x1, Pallas kernels, first_product(): pl.pallas_call(functools.partial(first_kernel, depths, parts[0].shape[0],...  9.78 us
    ppermute x1, waiting for transfers between devices, across_row(): across = lax.ppermute(landed, 'blk', swap_chip)  9.13 us
    ppermute x1, waiting for transfers between devices, body(): right_low = lax.ppermute(right_low, 'grid', to_left)  6.82 us
    ppermute x2, starting transfers between devices, body(): from_left = lax.ppermute(from_left, 'grid', to_right)  6.33 us
    all_to_all x1, starting transfers between devices, body(): lax.all_to_all(message, 'grid', split_axis=0, concat_axis=0, tiled=True)  6.28 us
  transfers between devices with their start and end apart: 14, of which 6 were waited for; matrix products, arithmetic and copies ran while one was open for 8% of the time, Pallas kernels for 18%

profile of v15, /device:TPU:0, one launch (start us, length us, event | category | flops | bytes accessed | tf_op | source)
XLA Modules:
  0.0 106.4 jit_solution(12101730573788148587)
XLA Ops:
  0.0 3.0 %collective-permute-start = (bf16[512,1024]{1,0:T(8,128)(2,1)}, bf16[512,1024]{1,0:T(8,128)(2,1)S(1)}, u32[]{:S(2)}, u32[]{:S(2)}) collective-permute-start(bf16[512,1024]{1,0:T(8,128)(2,1)} %refs_4_.1), channel_id=1, source_target_pairs={{0,8},{8,16},{16,24},{24,28},{28,20},{20,12},{12,4},{4,0},{1,9},{9... | collective-permute-start | bytes 3145736 | tf_op jit(solution)/shard_map/ppermute | solution.py:293
  3.0 0.0 collective-permute-start.1
  3.0 0.7 convert_bitcast_fusion
  3.7 0.7 fusion.11
  4.4 0.1 copy.29
  4.5 0.6 pad.4.meta_ref
  5.1 3.2 %shard_map.64 = bf16[8,272,128]{2,1,0:T(8,128)(2,1)} custom-call(bf16[8,256,128]{2,1,0:T(8,128)(2,1)} %bitcast.17, bf16[8,16,128]{2,1,0:T(8,128)(2,1)} %pad.4.meta_ref), custom_call_target="tpu_custom_call" | custom-call | bytes 1048576 | tf_op jit(solution)/shard_map/pallas_call | solution.py:37
  8.3 6.3 %all-to-all-start = ((bf16[8,272,128]{2,1,0:T(8,128)(2,1)}), bf16[8,272,128]{2,1,0:T(8,128)(2,1)S(1)}, u32[]{:S(2)}, u32[]{:S(2)}) async-start(bf16[8,272,128]{2,1,0:T(8,128)(2,1)} %shard_map.64), calls=%async_computation | async-start | bytes 1114112 | tf_op jit(solution)/shard_map/all_to_all | solution.py:309
  14.6 12.5 %collective-permute-done.refs_1_.refs_5_ = bf16[512,1024]{1,0:T(8,128)(2,1)S(1)} collective-permute-done((bf16[512,1024]{1,0:T(8,128)(2,1)}, bf16[512,1024]{1,0:T(8,128)(2,1)S(1)}, u32[]{:S(2)}, u32[]{:S(2)}) %collective-permute-start) | collective-permute-done | bytes 1048608 | tf_op jit(solution)/shard_map/ppermute | solution.py:293
  27.1 3.3 %collective-permute-start.5 = (bf16[512,1024]{1,0:T(8,128)(2,1)S(1)}, bf16[512,1024]{1,0:T(8,128)(2,1)S(1)}, u32[]{:S(2)}, u32[]{:S(2)}) collective-permute-start(bf16[512,1024]{1,0:T(8,128)(2,1)S(1)} %collective-permute-done.refs_1_.refs_5_), channel_id=1, source_target_pairs={{0,8},{8,16},{16,24},{24,28},{28,20},{20,12},{12,4},{4,0},{1,9},{9... | collective-permute-start | bytes 3145736 | tf_op jit(solution)/shard_map/ppermute | solution.py:293
  30.4 0.0 collective-permute-done.1.refs_2_.refs_6_
  30.4 11.9 %all-to-all-done.refs_0_ = bf16[8,272,128]{2,1,0:T(8,128)(2,1)S(1)} async-done(((bf16[8,272,128]{2,1,0:T(8,128)(2,1)}), bf16[8,272,128]{2,1,0:T(8,128)(2,1)S(1)}, u32[]{:S(2)}, u32[]{:S(2)}) %all-to-all-start) | async-done | bytes 557088 | tf_op jit(solution)/shard_map/all_to_all | solution.py:309
  42.3 1.5 %collective-permute-start.2 = (bf16[8,272,128]{2,1,0:T(8,128)(2,1)S(1)}, bf16[8,272,128]{2,1,0:T(8,128)(2,1)}, u32[]{:S(2)}, u32[]{:S(2)}) collective-permute-start(bf16[8,272,128]{2,1,0:T(8,128)(2,1)S(1)} %shard_map.65.refs_0_), channel_id=1, source_target_pairs={{0,2},{1,3},{2,0},{3,1},{4,6},{5,7},{6,4},{7,5},{8,10},{9,11},{10,... | collective-permute-start | bytes 1671176 | tf_op jit(solution)/shard_map/ppermute | solution.py:273
  43.8 9.1 %collective-permute-done.2.refs_1_ = bf16[8,272,128]{2,1,0:T(8,128)(2,1)} collective-permute-done((bf16[8,272,128]{2,1,0:T(8,128)(2,1)S(1)}, bf16[8,272,128]{2,1,0:T(8,128)(2,1)}, u32[]{:S(2)}, u32[]{:S(2)}) %collective-permute-start.2) | collective-permute-done | bytes 557088 | tf_op jit(solution)/shard_map/ppermute | solution.py:273
  53.0 0.1 copy.30
  53.0 0.1 copy.34
  53.1 0.7 slice.41
  53.9 0.1 copy.31
  54.0 0.1 copy.35
  54.1 0.1 copy.32
  54.2 0.1 copy.36
  54.3 2.8 %collective-permute-done.5.refs_7_ = bf16[512,1024]{1,0:T(8,128)(2,1)S(1)} collective-permute-done((bf16[512,1024]{1,0:T(8,128)(2,1)S(1)}, bf16[512,1024]{1,0:T(8,128)(2,1)S(1)}, u32[]{:S(2)}, u32[]{:S(2)}) %collective-permute-start.5) | collective-permute-done | bytes 1048608 | tf_op jit(solution)/shard_map/ppermute | solution.py:293
  57.1 1.1 %fusion.13 = (bf16[256,1024]{1,0:T(8,128)(2,1)}, bf16[256,1024]{1,0:T(8,128)(2,1)}) fusion(bf16[512,1024]{1,0:T(8,128)(2,1)S(1)} %collective-permute-done.5.refs_7_), kind=kLoop, calls=%fused_computation.37 | loop fusion | bytes 2097152 | tf_op jit(solution)/shard_map/slice | solution.py:298
  58.2 0.2 copy-done
  58.4 4.6 %collective-permute-start.7 = (bf16[256,1024]{1,0:T(8,128)(2,1)}, bf16[256,1024]{1,0:T(8,128)(2,1)S(1)}, u32[]{:S(2)}, u32[]{:S(2)}) collective-permute-start(bf16[256,1024]{1,0:T(8,128)(2,1)} %get-tuple-element.18), channel_id=1, source_target_pairs={{0,8},{8,16},{16,24},{24,28},{28,20},{20,12},{12,4},{4,0},{1,9},{9... | collective-permute-start | bytes 1572872 | tf_op jit(solution)/shard_map/ppermute | solution.py:299
  63.0 2.3 %fusion.12 = (bf16[256,1024]{1,0:T(8,128)(2,1)}, bf16[256,1024]{1,0:T(8,128)(2,1)}) fusion(bf16[512,1024]{1,0:T(8,128)(2,1)} %collective-permute-done.6.refs_8_), kind=kLoop, calls=%fused_computation.36 | loop fusion | bytes 2097152 | tf_op jit(solution)/shard_map/slice | solution.py:298
  65.2 2.4 %collective-permute-start.10 = (bf16[256,1024]{1,0:T(8,128)(2,1)}, bf16[256,1024]{1,0:T(8,128)(2,1)S(1)}, u32[]{:S(2)}, u32[]{:S(2)}) collective-permute-start(bf16[256,1024]{1,0:T(8,128)(2,1)} %get-tuple-element.15), channel_id=1, source_target_pairs={{8,0},{16,8},{24,16},{28,24},{20,28},{12,20},{4,12},{0,4},{9,1},{1... | collective-permute-start | bytes 1572872 | tf_op jit(solution)/shard_map/ppermute | solution.py:302
  67.6 0.1 collective-permute-start.9
  67.8 0.7 slice.43
  68.5 0.1 copy.33
  68.6 0.1 copy.37
  68.7 0.1 copy.38
  68.8 0.3 fusion
  69.1 0.3 compare_reduce_fusion
  69.4 0.1 copy.39
  69.5 0.1 copy.40
  69.6 0.1 fusion.6.dest_ref
  69.8 0.0 copy-start.1
  69.8 1.2 %copy-done.1 = bf16[512,1024]{1,0:T(8,128)(2,1)S(1)} copy-done((bf16[512,1024]{1,0:T(8,128)(2,1)S(1)}, bf16[512,1024]{1,0:T(8,128)(2,1)}, u32[]{:S(2)}) %copy-start.1) | copy-done | bytes 1048600
  71.0 1.1 copy-done.3
  72.0 1.2 %copy-done.4 = bf16[512,1024]{1,0:T(8,128)(2,1)S(1)} copy-done((bf16[512,1024]{1,0:T(8,128)(2,1)S(1)}, bf16[512,1024]{1,0:T(8,128)(2,1)}, u32[]{:S(2)}) %copy-start.4) | copy-done | bytes 1048600
  73.3 9.8 %shard_map.66 = (f32[4,1024,256]{2,1,0:T(8,128)S(1)}, bf16[1024,1536]{1,0:T(8,128)(2,1)S(1)}, f32[8,128]{1,0:T(8,128)S(1)}) custom-call(s32[4,8,2]{2,1,0:T(8,128)S(1)} %fusion.6.dest_ref, bf16[8,272,128]{2,1,0:T(8,128)(2,1)S(1)} %shard_map.65.refs_0_, bf16[8,272,128]{2,1,0:T(8,128)(2,1)} %collective-permute-done.2.refs_1_, ...), custom_call_target="tpu_custom_call" | custom-call | flops 5368709120 | bytes 9437184 | tf_op jit(solution)/shard_map/pallas_call | solution.py:148
  83.1 2.0 %collective-permute-start.11 = (bf16[256,1024]{1,0:T(8,128)(2,1)S(1)}, bf16[256,1024]{1,0:T(8,128)(2,1)S(1)}, u32[]{:S(2)}, u32[]{:S(2)}) collective-permute-start(bf16[256,1024]{1,0:T(8,128)(2,1)S(1)} %get-tuple-element.13.refs_0_), channel_id=1, source_target_pairs={{0,8},{8,16},{16,24},{24,28},{28,20},{20,12},{12,4},{4,0},{1,9},{9... | collective-permute-start | bytes 1572872 | tf_op jit(solution)/shard_map/ppermute | solution.py:326
  85.1 0.0 collective-permute-start.12
  85.2 6.8 %collective-permute-done.10.refs_2_ = bf16[256,1024]{1,0:T(8,128)(2,1)S(1)} collective-permute-done((bf16[256,1024]{1,0:T(8,128)(2,1)}, bf16[256,1024]{1,0:T(8,128)(2,1)S(1)}, u32[]{:S(2)}, u32[]{:S(2)}) %collective-permute-start.10) | collective-permute-done | bytes 524320 | tf_op jit(solution)/shard_map/ppermute | solution.py:302
  92.0 6.7 %shard_map.68.acc_hbm = f32[4,1024,256]{2,1,0:T(8,128)S(1)} custom-call(bf16[1024,1536]{1,0:T(8,128)(2,1)S(1)} %get-tuple-element.10.late_hbm, f32[4,1024,256]{2,1,0:T(8,128)S(1)} %get-tuple-element.11.acc_hbm, bf16[256,1024]{1,0:T(8,128)(2,1)S(1)} %get-tuple-element.13.refs_0_, bf16[256,1024]{1,0:T(8,128)(2,1)} %collective-permute-done.9.refs_1_, ...), custom_call_target="tpu_custom_call" | custom-call | flops 2147483648 | bytes 12582912 | tf_op jit(solution)/shard_map/pallas_call | solution.py:241
  98.7 2.5 %collective-permute-done.12.refs_1_ = bf16[256,1024]{1,0:T(8,128)(2,1)S(1)} collective-permute-done((bf16[256,1024]{1,0:T(8,128)(2,1)S(1)}, bf16[256,1024]{1,0:T(8,128)(2,1)S(1)}, u32[]{:S(2)}, u32[]{:S(2)}) %collective-permute-start.12) | collective-permute-done | bytes 524320 | tf_op jit(solution)/shard_map/ppermute | solution.py:327
  101.2 5.3 %shard_map.69 = bf16[1024,1024]{1,0:T(8,128)(2,1)} custom-call(bf16[1024,1536]{1,0:T(8,128)(2,1)S(1)} %get-tuple-element.10.late_hbm, f32[4,1024,256]{2,1,0:T(8,128)S(1)} %shard_map.68.acc_hbm, bf16[256,1024]{1,0:T(8,128)(2,1)S(1)} %collective-permute-done.11.refs_0_, bf16[256,1024]{1,0:T(8,128)(2,1)S(1)} %collective-permute-done.12.refs_1_), custom_call_target="tpu_custom_call" | custom-call | flops 1073741824 | bytes 10485760 | tf_op jit(solution)/shard_map/pallas_call | solution.py:241
  (25 shorter events, 0.1 us)
Async XLA Ops:
  0.0 52.9 %copy-start.5 = (s32[1,8]{1,0:T(1,128)S(1)}, s32[1,8]{1,0:T(1,128)}, u32[]{:S(2)}) copy-start(s32[1,8]{1,0:T(1,128)} %param.10) | copy-start | bytes 100
  0.0 27.1 %collective-permute-start = (bf16[512,1024]{1,0:T(8,128)(2,1)}, bf16[512,1024]{1,0:T(8,128)(2,1)S(1)}, u32[]{:S(2)}, u32[]{:S(2)}) collective-permute-start(bf16[512,1024]{1,0:T(8,128)(2,1)} %refs_4_.1), channel_id=1, source_target_pairs={{0,8},{8,16},{16,24},{24,28},{28,20},{20,12},{12,4},{4,0},{1,9},{9... | collective-permute-start | bytes 3145736 | tf_op jit(solution)/shard_map/ppermute | solution.py:293
  3.0 27.4 %collective-permute-start.1 = (bf16[512,1024]{1,0:T(8,128)(2,1)}, bf16[512,1024]{1,0:T(8,128)(2,1)}, u32[]{:S(2)}, u32[]{:S(2)}) collective-permute-start(bf16[512,1024]{1,0:T(8,128)(2,1)} %refs_4_.1), channel_id=1, source_target_pairs={{8,0},{16,8},{24,16},{28,24},{20,28},{12,20},{4,12},{0,4},{9,1},{1... | collective-permute-start | bytes 3145736 | tf_op jit(solution)/shard_map/ppermute | solution.py:294
  8.3 34.0 %all-to-all-start = ((bf16[8,272,128]{2,1,0:T(8,128)(2,1)}), bf16[8,272,128]{2,1,0:T(8,128)(2,1)S(1)}, u32[]{:S(2)}, u32[]{:S(2)}) async-start(bf16[8,272,128]{2,1,0:T(8,128)(2,1)} %shard_map.64), calls=%async_computation | async-start | bytes 1114112 | tf_op jit(solution)/shard_map/all_to_all | solution.py:309
  27.1 30.0 %collective-permute-start.5 = (bf16[512,1024]{1,0:T(8,128)(2,1)S(1)}, bf16[512,1024]{1,0:T(8,128)(2,1)S(1)}, u32[]{:S(2)}, u32[]{:S(2)}) collective-permute-start(bf16[512,1024]{1,0:T(8,128)(2,1)S(1)} %collective-permute-done.refs_1_.refs_5_), channel_id=1, source_target_pairs={{0,8},{8,16},{16,24},{24,28},{28,20},{20,12},{12,4},{4,0},{1,9},{9... | collective-permute-start | bytes 3145736 | tf_op jit(solution)/shard_map/ppermute | solution.py:293
  30.4 32.6 %collective-permute-start.6 = (bf16[512,1024]{1,0:T(8,128)(2,1)}, bf16[512,1024]{1,0:T(8,128)(2,1)}, u32[]{:S(2)}, u32[]{:S(2)}) collective-permute-start(bf16[512,1024]{1,0:T(8,128)(2,1)} %collective-permute-done.1.refs_2_.refs_6_), channel_id=1, source_target_pairs={{8,0},{16,8},{24,16},{28,24},{20,28},{12,20},{4,12},{0,4},{9,1},{1... | collective-permute-start | bytes 3145736 | tf_op jit(solution)/shard_map/ppermute | solution.py:294
  42.3 10.6 %collective-permute-start.2 = (bf16[8,272,128]{2,1,0:T(8,128)(2,1)S(1)}, bf16[8,272,128]{2,1,0:T(8,128)(2,1)}, u32[]{:S(2)}, u32[]{:S(2)}) collective-permute-start(bf16[8,272,128]{2,1,0:T(8,128)(2,1)S(1)} %shard_map.65.refs_0_), channel_id=1, source_target_pairs={{0,2},{1,3},{2,0},{3,1},{4,6},{5,7},{6,4},{7,5},{8,10},{9,11},{10,... | collective-permute-start | bytes 1671176 | tf_op jit(solution)/shard_map/ppermute | solution.py:273
  43.8 10.3 %collective-permute-start.3 = (bf16[8,272,128]{2,1,0:T(8,128)(2,1)S(1)}, bf16[8,272,128]{2,1,0:T(8,128)(2,1)S(1)}, u32[]{:S(2)}, u32[]{:S(2)}) collective-permute-start(bf16[8,272,128]{2,1,0:T(8,128)(2,1)S(1)} %shard_map.65.refs_0_), channel_id=1, source_target_pairs={{0,1},{1,0},{2,3},{3,2},{4,5},{5,4},{6,7},{7,6},{8,9},{9,8},{10,11... | collective-permute-start | bytes 1671176 | tf_op jit(solution)/shard_map/ppermute | solution.py:274
  52.9 14.9 %collective-permute-start.4 = (bf16[8,272,128]{2,1,0:T(8,128)(2,1)}, bf16[8,272,128]{2,1,0:T(8,128)(2,1)}, u32[]{:S(2)}, u32[]{:S(2)}) collective-permute-start(bf16[8,272,128]{2,1,0:T(8,128)(2,1)} %collective-permute-done.2.refs_1_), channel_id=1, source_target_pairs={{0,1},{1,0},{2,3},{3,2},{4,5},{5,4},{6,7},{7,6},{8,9},{9,8},{10,11... | collective-permute-start | bytes 1671176 | tf_op jit(solution)/shard_map/ppermute | solution.py:275
  54.1 11.2 %copy-start.2 = (bf16[8,272,128]{2,1,0:T(8,128)(2,1)}, bf16[8,272,128]{2,1,0:T(8,128)(2,1)S(1)}, u32[]{:S(2)}) copy-start(bf16[8,272,128]{2,1,0:T(8,128)(2,1)S(1)} %collective-permute-done.3.refs_2_) | copy-start | bytes 1671172
  57.1 1.3 %copy-start = (bf16[512,1024]{1,0:T(8,128)(2,1)}, bf16[512,1024]{1,0:T(8,128)(2,1)S(1)}, u32[]{:S(2)}) copy-start(bf16[512,1024]{1,0:T(8,128)(2,1)S(1)} %collective-permute-done.5.refs_7_) | copy-start | bytes 3145732
  58.4 24.7 %collective-permute-start.7 = (bf16[256,1024]{1,0:T(8,128)(2,1)}, bf16[256,1024]{1,0:T(8,128)(2,1)S(1)}, u32[]{:S(2)}, u32[]{:S(2)}) collective-permute-start(bf16[256,1024]{1,0:T(8,128)(2,1)} %get-tuple-element.18), channel_id=1, source_target_pairs={{0,8},{8,16},{16,24},{24,28},{28,20},{20,12},{12,4},{4,0},{1,9},{9... | collective-permute-start | bytes 1572872 | tf_op jit(solution)/shard_map/ppermute | solution.py:299
  65.2 17.8 %collective-permute-start.8 = (bf16[256,1024]{1,0:T(8,128)(2,1)}, bf16[256,1024]{1,0:T(8,128)(2,1)S(1)}, u32[]{:S(2)}, u32[]{:S(2)}) collective-permute-start(bf16[256,1024]{1,0:T(8,128)(2,1)} %get-tuple-element.16), channel_id=1, source_target_pairs={{8,0},{16,8},{24,16},{28,24},{20,28},{12,20},{4,12},{0,4},{9,1},{1... | collective-permute-start | bytes 1572872 | tf_op jit(solution)/shard_map/ppermute | solution.py:300
  65.2 26.8 %collective-permute-start.10 = (bf16[256,1024]{1,0:T(8,128)(2,1)}, bf16[256,1024]{1,0:T(8,128)(2,1)S(1)}, u32[]{:S(2)}, u32[]{:S(2)}) collective-permute-start(bf16[256,1024]{1,0:T(8,128)(2,1)} %get-tuple-element.15), channel_id=1, source_target_pairs={{8,0},{16,8},{24,16},{28,24},{20,28},{12,20},{4,12},{0,4},{9,1},{1... | collective-permute-start | bytes 1572872 | tf_op jit(solution)/shard_map/ppermute | solution.py:302
  67.6 24.3 %collective-permute-start.9 = (bf16[256,1024]{1,0:T(8,128)(2,1)}, bf16[256,1024]{1,0:T(8,128)(2,1)}, u32[]{:S(2)}, u32[]{:S(2)}) collective-permute-start(bf16[256,1024]{1,0:T(8,128)(2,1)} %get-tuple-element.17), channel_id=1, source_target_pairs={{0,8},{8,16},{16,24},{24,28},{28,20},{20,12},{12,4},{4,0},{1,9},{9... | collective-permute-start | bytes 1572872 | tf_op jit(solution)/shard_map/ppermute | solution.py:301
  69.8 1.2 %copy-start.1 = (bf16[512,1024]{1,0:T(8,128)(2,1)S(1)}, bf16[512,1024]{1,0:T(8,128)(2,1)}, u32[]{:S(2)}) copy-start(bf16[512,1024]{1,0:T(8,128)(2,1)} %copy-done) | copy-start | bytes 3145732
  71.0 1.1 copy-start.3
  72.0 1.2 %copy-start.4 = (bf16[512,1024]{1,0:T(8,128)(2,1)S(1)}, bf16[512,1024]{1,0:T(8,128)(2,1)}, u32[]{:S(2)}) copy-start(bf16[512,1024]{1,0:T(8,128)(2,1)} %refs_4_.1) | copy-start | bytes 3145732
  83.1 15.6 %collective-permute-start.11 = (bf16[256,1024]{1,0:T(8,128)(2,1)S(1)}, bf16[256,1024]{1,0:T(8,128)(2,1)S(1)}, u32[]{:S(2)}, u32[]{:S(2)}) collective-permute-start(bf16[256,1024]{1,0:T(8,128)(2,1)S(1)} %get-tuple-element.13.refs_0_), channel_id=1, source_target_pairs={{0,8},{8,16},{16,24},{24,28},{28,20},{20,12},{12,4},{4,0},{1,9},{9... | collective-permute-start | bytes 1572872 | tf_op jit(solution)/shard_map/ppermute | solution.py:326
  85.1 16.0 %collective-permute-start.12 = (bf16[256,1024]{1,0:T(8,128)(2,1)S(1)}, bf16[256,1024]{1,0:T(8,128)(2,1)S(1)}, u32[]{:S(2)}, u32[]{:S(2)}) collective-permute-start(bf16[256,1024]{1,0:T(8,128)(2,1)S(1)} %get-tuple-element.14.refs_3_), channel_id=1, source_target_pairs={{8,0},{16,8},{24,16},{28,24},{20,28},{12,20},{4,12},{0,4},{9,1},{1... | collective-permute-start | bytes 1572872 | tf_op jit(solution)/shard_map/ppermute | solution.py:327

commit v16 on v15

--- a/solution.py
+++ b/solution.py
@@ -54,7 +54,7 @@
     pass
 
 
-def after(values, others):
+def after(values, others, claim):
     anywhere = pl.BlockSpec(memory_space=pl.ANY)
     return pl.pallas_call(
         after_kernel,
@@ -62,7 +62,7 @@
         in_specs=[anywhere] * (len(values) + len(others)),
         out_specs=[anywhere] * len(values),
         input_output_aliases={i: i for i in range(len(values))},
-        compiler_params=pltpu.CompilerParams(vmem_limit_bytes=SPARE_BYTES),
+        compiler_params=pltpu.CompilerParams(vmem_limit_bytes=claim),
         cost_estimate=pl.CostEstimate(flops=0, bytes_accessed=0, transcendentals=0),
     )(*values, *others)
 
@@ -217,12 +217,8 @@
         for copy in fetch(j):
             copy.wait()
 
-        def turn(q):
-            part = pl.ds(pl.multiple_of(q * some, some), some)
-            total = jnp.dot(left[part], right[j], preferred_element_type=jnp.float32)
-            out[j, part] = (acc[j, part] + total).astype(out.dtype)
-
-        each(PARTS, turn)
+        total = jnp.dot(left[...], right[j], preferred_element_type=jnp.float32)
+        out[j] = (acc[j] + total).astype(out.dtype)
         store(j).start()
 
     each(steps, multiply)
@@ -307,7 +303,7 @@
     meta = jnp.pad(meta.astype(jnp.bfloat16)[:, None, :], ((0, 0), (0, META - 1), (0, bs - 2 * cap)))
     message = pack(a_slots.reshape(groups, cap * bs, bs), meta)
     landed = lax.all_to_all(message, "grid", split_axis=0, concat_axis=0, tiled=True)
-    (landed,) = after([landed], early[1:3])
+    (landed,) = after([landed], early[1:3], VMEM_BYTES)
     parts = across_row(landed, columns)
 
     metas = jnp.stack([p[:, cap * bs, : 2 * cap] for p in parts]).astype(jnp.int32)
@@ -322,7 +318,7 @@
     dest = jnp.where(jnp.any(hit, axis=-1), dest, -1)
 
     acc, late, mark = first_product(dest, parts, early, rb * bs, 3 * k_local, bs, cap, n_local // 4)
-    left_low, right_high = after([left_low, right_high], [mark])
+    left_low, right_high = after([left_low, right_high], [mark], SPARE_BYTES)
     low = lax.ppermute(left_low, "grid", to_right)
     high = lax.ppermute(right_high, "grid", to_left)
     acc = add_product(late, 0, [left_low, left_high, right_low, right_high], acc, False)

time: 107 us -> 105 us (0.981)
  Pallas kernels: 24.9 us -> 21 us
  waiting for transfers between devices: 45.6 us -> 47.3 us
    pallas_call x2, Pallas kernels: 12 us -> 8.03 us  [add_product(): pl.pallas_call(functools.partial(add_kernel, depths, place), out_shape=ou...]
    ppermute x1, waiting for transfers between devices: 2.46 us -> 4.34 us  [body(): high = lax.ppermute(right_high, 'grid', to_left)]
    ppermute x2, waiting for transfers between devices: 15.3 us -> 13.8 us  [body(): from_left = lax.ppermute(from_left, 'grid', to_right)]
    ppermute x1, waiting for transfers between devices: 6.82 us -> 7.96 us  [body(): right_low = lax.ppermute(right_low, 'grid', to_left)]
  transfers between devices with their start and end apart: 14 -> 14, of which waited for: 6 -> 6; matrix products, arithmetic and copies ran while one was open for 8% -> 9% of each run, Pallas kernels for 18% -> 17%
where the time goes in v16:
time: 105 us; the launch traced here: 104 us
  waiting for transfers between devices  47.3 us (45%)
  starting transfers between devices  23.3 us (22%)
  Pallas kernels  21 us (20%)
  local copies, waits for them, and re-layouts  10.2 us (10%)
  other arithmetic  2.12 us (2%)
    ppermute x2, waiting for transfers between devices, body(): from_left = lax.ppermute(from_left, 'grid', to_right)  13.8 us
    all_to_all x1, waiting for transfers between devices, body(): lax.all_to_all(message, 'grid', split_axis=0, concat_axis=0, tiled=True)  11.9 us
    pallas_call x1, Pallas kernels, first_product(): pl.pallas_call(functools.partial(first_kernel, depths, parts[0].shape[0],...  9.76 us
    ppermute x1, waiting for transfers between devices, across_row(): across = lax.ppermute(landed, 'blk', swap_chip)  9.34 us
    pallas_call x2, Pallas kernels, add_product(): pl.pallas_call(functools.partial(add_kernel, depths, place), out_shape=ou...  8.03 us
    ppermute x1, waiting for transfers between devices, body(): right_low = lax.ppermute(right_low, 'grid', to_left)  7.96 us
    all_to_all x1, starting transfers between devices, body(): lax.all_to_all(message, 'grid', split_axis=0, concat_axis=0, tiled=True)  6.28 us
    ppermute x2, starting transfers between devices, body(): from_left = lax.ppermute(from_left, 'grid', to_right)  6.23 us
  transfers between devices with their start and end apart: 14, of which 6 were waited for; matrix products, arithmetic and copies ran while one was open for 9% of the time, Pallas kernels for 17%

profile of v16, /device:TPU:0, one launch (start us, length us, event | category | flops | bytes accessed | tf_op | source)
XLA Modules:
  0.0 104.0 jit_solution(16564957316725307331)
XLA Ops:
  0.0 3.0 %collective-permute-start = (bf16[512,1024]{1,0:T(8,128)(2,1)}, bf16[512,1024]{1,0:T(8,128)(2,1)}, u32[]{:S(2)}, u32[]{:S(2)}) collective-permute-start(bf16[512,1024]{1,0:T(8,128)(2,1)} %refs_4_.1), channel_id=1, source_target_pairs={{0,8},{8,16},{16,24},{24,28},{28,20},{20,12},{12,4},{4,0},{1,9},{9... | collective-permute-start | bytes 3145736 | tf_op jit(solution)/shard_map/ppermute | solution.py:289
  3.0 0.7 convert_bitcast_fusion
  3.7 0.7 fusion.11
  4.4 0.1 copy.29
  4.5 0.6 pad.4.meta_ref
  5.1 3.2 %shard_map.64 = bf16[8,272,128]{2,1,0:T(8,128)(2,1)} custom-call(bf16[8,256,128]{2,1,0:T(8,128)(2,1)} %bitcast.17, bf16[8,16,128]{2,1,0:T(8,128)(2,1)} %pad.4.meta_ref), custom_call_target="tpu_custom_call" | custom-call | bytes 1048576 | tf_op jit(solution)/shard_map/pallas_call | solution.py:37
  8.3 6.3 %all-to-all-start = ((bf16[8,272,128]{2,1,0:T(8,128)(2,1)}), bf16[8,272,128]{2,1,0:T(8,128)(2,1)S(1)}, u32[]{:S(2)}, u32[]{:S(2)}) async-start(bf16[8,272,128]{2,1,0:T(8,128)(2,1)} %shard_map.64), calls=%async_computation | async-start | bytes 1114112 | tf_op jit(solution)/shard_map/all_to_all | solution.py:305
  14.6 12.6 %collective-permute-done.refs_1_.refs_5_ = bf16[512,1024]{1,0:T(8,128)(2,1)} collective-permute-done((bf16[512,1024]{1,0:T(8,128)(2,1)}, bf16[512,1024]{1,0:T(8,128)(2,1)}, u32[]{:S(2)}, u32[]{:S(2)}) %collective-permute-start) | collective-permute-done | bytes 1048608 | tf_op jit(solution)/shard_map/ppermute | solution.py:289
  27.2 3.2 %collective-permute-start.5 = (bf16[512,1024]{1,0:T(8,128)(2,1)}, bf16[512,1024]{1,0:T(8,128)(2,1)S(1)}, u32[]{:S(2)}, u32[]{:S(2)}) collective-permute-start(bf16[512,1024]{1,0:T(8,128)(2,1)} %collective-permute-done.refs_1_.refs_5_), channel_id=1, source_target_pairs={{0,8},{8,16},{16,24},{24,28},{28,20},{20,12},{12,4},{4,0},{1,9},{9... | collective-permute-start | bytes 3145736 | tf_op jit(solution)/shard_map/ppermute | solution.py:289
  30.4 0.0 collective-permute-done.1.refs_2_.refs_6_
  30.4 0.0 collective-permute-start.6
  30.4 11.9 %all-to-all-done.refs_0_ = bf16[8,272,128]{2,1,0:T(8,128)(2,1)S(1)} async-done(((bf16[8,272,128]{2,1,0:T(8,128)(2,1)}), bf16[8,272,128]{2,1,0:T(8,128)(2,1)S(1)}, u32[]{:S(2)}, u32[]{:S(2)}) %all-to-all-start) | async-done | bytes 557088 | tf_op jit(solution)/shard_map/all_to_all | solution.py:305
  42.3 0.8 copy-done
  43.1 1.5 %collective-permute-start.2 = (bf16[8,272,128]{2,1,0:T(8,128)(2,1)}, bf16[8,272,128]{2,1,0:T(8,128)(2,1)}, u32[]{:S(2)}, u32[]{:S(2)}) collective-permute-start(bf16[8,272,128]{2,1,0:T(8,128)(2,1)} %shard_map.65.refs_0_), channel_id=1, source_target_pairs={{0,2},{1,3},{2,0},{3,1},{4,6},{5,7},{6,4},{7,5},{8,10},{9,11},{10,... | collective-permute-start | bytes 1671176 | tf_op jit(solution)/shard_map/ppermute | solution.py:269
  44.6 9.3 %collective-permute-done.2.refs_1_ = bf16[8,272,128]{2,1,0:T(8,128)(2,1)} collective-permute-done((bf16[8,272,128]{2,1,0:T(8,128)(2,1)}, bf16[8,272,128]{2,1,0:T(8,128)(2,1)}, u32[]{:S(2)}, u32[]{:S(2)}) %collective-permute-start.2) | collective-permute-done | bytes 557088 | tf_op jit(solution)/shard_map/ppermute | solution.py:269
  54.0 0.7 slice.40
  54.7 0.1 copy.30
  54.8 0.1 copy.34
  54.9 0.7 slice.41
  55.6 0.1 copy.31
  55.7 0.1 copy.35
  55.8 0.0 collective-permute-done.3.refs_2_
  55.8 0.1 copy.32
  55.9 0.1 copy.36
  56.0 1.2 %collective-permute-done.5.refs_7_ = bf16[512,1024]{1,0:T(8,128)(2,1)S(1)} collective-permute-done((bf16[512,1024]{1,0:T(8,128)(2,1)}, bf16[512,1024]{1,0:T(8,128)(2,1)S(1)}, u32[]{:S(2)}, u32[]{:S(2)}) %collective-permute-start.5) | collective-permute-done | bytes 1048608 | tf_op jit(solution)/shard_map/ppermute | solution.py:289
  57.2 0.9 fusion.13
  58.1 4.6 %collective-permute-start.7 = (bf16[256,1024]{1,0:T(8,128)(2,1)}, bf16[256,1024]{1,0:T(8,128)(2,1)S(1)}, u32[]{:S(2)}, u32[]{:S(2)}) collective-permute-start(bf16[256,1024]{1,0:T(8,128)(2,1)} %get-tuple-element.18), channel_id=1, source_target_pairs={{0,8},{8,16},{16,24},{24,28},{28,20},{20,12},{12,4},{4,0},{1,9},{9... | collective-permute-start | bytes 1572872 | tf_op jit(solution)/shard_map/ppermute | solution.py:295
  62.6 2.3 %fusion.12 = (bf16[256,1024]{1,0:T(8,128)(2,1)}, bf16[256,1024]{1,0:T(8,128)(2,1)}) fusion(bf16[512,1024]{1,0:T(8,128)(2,1)} %collective-permute-done.6.refs_8_), kind=kLoop, calls=%fused_computation.36 | loop fusion | bytes 2097152 | tf_op jit(solution)/shard_map/slice | solution.py:294
  64.9 2.3 %collective-permute-start.10 = (bf16[256,1024]{1,0:T(8,128)(2,1)}, bf16[256,1024]{1,0:T(8,128)(2,1)}, u32[]{:S(2)}, u32[]{:S(2)}) collective-permute-start(bf16[256,1024]{1,0:T(8,128)(2,1)} %get-tuple-element.15), channel_id=1, source_target_pairs={{8,0},{16,8},{24,16},{28,24},{20,28},{12,20},{4,12},{0,4},{9,1},{1... | collective-permute-start | bytes 1572872 | tf_op jit(solution)/shard_map/ppermute | solution.py:298
  67.2 0.1 collective-permute-start.9
  67.3 0.7 slice.43
  68.0 0.1 copy.33
  68.1 0.1 copy.37
  68.2 0.1 copy.38
  68.3 0.3 fusion
  68.6 0.3 compare_reduce_fusion
  68.9 0.1 copy.39
  69.0 0.1 copy.40
  69.2 0.1 fusion.6.dest_ref
  69.3 1.0 %copy-done.3 = bf16[8,272,128]{2,1,0:T(8,128)(2,1)S(1)} copy-done((bf16[8,272,128]{2,1,0:T(8,128)(2,1)S(1)}, bf16[8,272,128]{2,1,0:T(8,128)(2,1)}, u32[]{:S(2)}) %copy-start.3) | copy-done | bytes 557080
  70.4 1.2 %copy-done.4 = bf16[512,1024]{1,0:T(8,128)(2,1)S(1)} copy-done((bf16[512,1024]{1,0:T(8,128)(2,1)S(1)}, bf16[512,1024]{1,0:T(8,128)(2,1)}, u32[]{:S(2)}) %copy-start.4) | copy-done | bytes 1048600
  71.6 9.8 %shard_map.66 = (f32[4,1024,256]{2,1,0:T(8,128)S(1)}, bf16[1024,1536]{1,0:T(8,128)(2,1)S(1)}, f32[8,128]{1,0:T(8,128)S(1)}) custom-call(s32[4,8,2]{2,1,0:T(8,128)S(1)} %fusion.6.dest_ref, bf16[8,272,128]{2,1,0:T(8,128)(2,1)S(1)} %copy-done.1, bf16[8,272,128]{2,1,0:T(8,128)(2,1)} %collective-permute-done.2.refs_1_, bf16[8,272,128]{2,1,0:T(8,128)(2,1)S(1)} %copy-done.3, ...), custom_call_target="tpu_custom_call" | custom-call | flops 5368709120 | bytes 9437184 | tf_op jit(solution)/shard_map/pallas_call | solution.py:148
  81.4 2.1 %collective-permute-start.11 = (bf16[256,1024]{1,0:T(8,128)(2,1)S(1)}, bf16[256,1024]{1,0:T(8,128)(2,1)S(1)}, u32[]{:S(2)}, u32[]{:S(2)}) collective-permute-start(bf16[256,1024]{1,0:T(8,128)(2,1)S(1)} %get-tuple-element.13.refs_0_), channel_id=1, source_target_pairs={{0,8},{8,16},{16,24},{24,28},{28,20},{20,12},{12,4},{4,0},{1,9},{9... | collective-permute-start | bytes 1572872 | tf_op jit(solution)/shard_map/ppermute | solution.py:322
  83.4 0.2 collective-permute-start.12
  83.7 8.0 %collective-permute-done.10.refs_2_ = bf16[256,1024]{1,0:T(8,128)(2,1)} collective-permute-done((bf16[256,1024]{1,0:T(8,128)(2,1)}, bf16[256,1024]{1,0:T(8,128)(2,1)}, u32[]{:S(2)}, u32[]{:S(2)}) %collective-permute-start.10) | collective-permute-done | bytes 524320 | tf_op jit(solution)/shard_map/ppermute | solution.py:298
  91.6 4.7 %shard_map.68.acc_hbm = f32[4,1024,256]{2,1,0:T(8,128)S(1)} custom-call(bf16[1024,1536]{1,0:T(8,128)(2,1)S(1)} %get-tuple-element.10.late_hbm, f32[4,1024,256]{2,1,0:T(8,128)S(1)} %get-tuple-element.11.acc_hbm, bf16[256,1024]{1,0:T(8,128)(2,1)S(1)} %get-tuple-element.13.refs_0_, bf16[256,1024]{1,0:T(8,128)(2,1)} %collective-permute-done.9.refs_1_, ...), custom_call_target="tpu_custom_call" | custom-call | flops 2147483648 | bytes 12582912 | tf_op jit(solution)/shard_map/pallas_call | solution.py:237
  96.4 4.3 %collective-permute-done.12.refs_1_ = bf16[256,1024]{1,0:T(8,128)(2,1)S(1)} collective-permute-done((bf16[256,1024]{1,0:T(8,128)(2,1)S(1)}, bf16[256,1024]{1,0:T(8,128)(2,1)S(1)}, u32[]{:S(2)}, u32[]{:S(2)}) %collective-permute-start.12) | collective-permute-done | bytes 524320 | tf_op jit(solution)/shard_map/ppermute | solution.py:323
  100.7 3.3 %shard_map.69 = bf16[1024,1024]{1,0:T(8,128)(2,1)} custom-call(bf16[1024,1536]{1,0:T(8,128)(2,1)S(1)} %get-tuple-element.10.late_hbm, f32[4,1024,256]{2,1,0:T(8,128)S(1)} %shard_map.68.acc_hbm, bf16[256,1024]{1,0:T(8,128)(2,1)S(1)} %collective-permute-done.11.refs_0_, bf16[256,1024]{1,0:T(8,128)(2,1)S(1)} %collective-permute-done.12.refs_1_), custom_call_target="tpu_custom_call" | custom-call | flops 1073741824 | bytes 10485760 | tf_op jit(solution)/shard_map/pallas_call | solution.py:237
  (25 shorter events, 0.1 us)
Async XLA Ops:
  0.0 53.9 %copy-start.5 = (s32[1,8]{1,0:T(1,128)S(1)}, s32[1,8]{1,0:T(1,128)}, u32[]{:S(2)}) copy-start(s32[1,8]{1,0:T(1,128)} %param.10) | copy-start | bytes 100
  0.0 27.2 %collective-permute-start = (bf16[512,1024]{1,0:T(8,128)(2,1)}, bf16[512,1024]{1,0:T(8,128)(2,1)}, u32[]{:S(2)}, u32[]{:S(2)}) collective-permute-start(bf16[512,1024]{1,0:T(8,128)(2,1)} %refs_4_.1), channel_id=1, source_target_pairs={{0,8},{8,16},{16,24},{24,28},{28,20},{20,12},{12,4},{4,0},{1,9},{9... | collective-permute-start | bytes 3145736 | tf_op jit(solution)/shard_map/ppermute | solution.py:289
  3.0 27.4 %collective-permute-start.1 = (bf16[512,1024]{1,0:T(8,128)(2,1)}, bf16[512,1024]{1,0:T(8,128)(2,1)}, u32[]{:S(2)}, u32[]{:S(2)}) collective-permute-start(bf16[512,1024]{1,0:T(8,128)(2,1)} %refs_4_.1), channel_id=1, source_target_pairs={{8,0},{16,8},{24,16},{28,24},{20,28},{12,20},{4,12},{0,4},{9,1},{1... | collective-permute-start | bytes 3145736 | tf_op jit(solution)/shard_map/ppermute | solution.py:290
  8.3 34.0 %all-to-all-start = ((bf16[8,272,128]{2,1,0:T(8,128)(2,1)}), bf16[8,272,128]{2,1,0:T(8,128)(2,1)S(1)}, u32[]{:S(2)}, u32[]{:S(2)}) async-start(bf16[8,272,128]{2,1,0:T(8,128)(2,1)} %shard_map.64), calls=%async_computation | async-start | bytes 1114112 | tf_op jit(solution)/shard_map/all_to_all | solution.py:305
  27.2 30.0 %collective-permute-start.5 = (bf16[512,1024]{1,0:T(8,128)(2,1)}, bf16[512,1024]{1,0:T(8,128)(2,1)S(1)}, u32[]{:S(2)}, u32[]{:S(2)}) collective-permute-start(bf16[512,1024]{1,0:T(8,128)(2,1)} %collective-permute-done.refs_1_.refs_5_), channel_id=1, source_target_pairs={{0,8},{8,16},{16,24},{24,28},{28,20},{20,12},{12,4},{4,0},{1,9},{9... | collective-permute-start | bytes 3145736 | tf_op jit(solution)/shard_map/ppermute | solution.py:289
  30.4 32.2 %collective-permute-start.6 = (bf16[512,1024]{1,0:T(8,128)(2,1)}, bf16[512,1024]{1,0:T(8,128)(2,1)}, u32[]{:S(2)}, u32[]{:S(2)}) collective-permute-start(bf16[512,1024]{1,0:T(8,128)(2,1)} %collective-permute-done.1.refs_2_.refs_6_), channel_id=1, source_target_pairs={{8,0},{16,8},{24,16},{28,24},{20,28},{12,20},{4,12},{0,4},{9,1},{1... | collective-permute-start | bytes 3145736 | tf_op jit(solution)/shard_map/ppermute | solution.py:290
  42.3 0.8 copy-start
  43.1 26.2 %copy-start.1 = (bf16[8,272,128]{2,1,0:T(8,128)(2,1)S(1)}, bf16[8,272,128]{2,1,0:T(8,128)(2,1)}, u32[]{:S(2)}) copy-start(bf16[8,272,128]{2,1,0:T(8,128)(2,1)} %shard_map.65.refs_0_) | copy-start | bytes 1671172
  43.1 10.8 %collective-permute-start.2 = (bf16[8,272,128]{2,1,0:T(8,128)(2,1)}, bf16[8,272,128]{2,1,0:T(8,128)(2,1)}, u32[]{:S(2)}, u32[]{:S(2)}) collective-permute-start(bf16[8,272,128]{2,1,0:T(8,128)(2,1)} %shard_map.65.refs_0_), channel_id=1, source_target_pairs={{0,2},{1,3},{2,0},{3,1},{4,6},{5,7},{6,4},{7,5},{8,10},{9,11},{10,... | collective-permute-start | bytes 1671176 | tf_op jit(solution)/shard_map/ppermute | solution.py:269
  44.6 11.2 %collective-permute-start.3 = (bf16[8,272,128]{2,1,0:T(8,128)(2,1)}, bf16[8,272,128]{2,1,0:T(8,128)(2,1)S(1)}, u32[]{:S(2)}, u32[]{:S(2)}) collective-permute-start(bf16[8,272,128]{2,1,0:T(8,128)(2,1)} %shard_map.65.refs_0_), channel_id=1, source_target_pairs={{0,1},{1,0},{2,3},{3,2},{4,5},{5,4},{6,7},{7,6},{8,9},{9,8},{10,11... | collective-permute-start | bytes 1671176 | tf_op jit(solution)/shard_map/ppermute | solution.py:270
  53.9 13.4 %collective-permute-start.4 = (bf16[8,272,128]{2,1,0:T(8,128)(2,1)}, bf16[8,272,128]{2,1,0:T(8,128)(2,1)}, u32[]{:S(2)}, u32[]{:S(2)}) collective-permute-start(bf16[8,272,128]{2,1,0:T(8,128)(2,1)} %collective-permute-done.2.refs_1_), channel_id=1, source_target_pairs={{0,1},{1,0},{2,3},{3,2},{4,5},{5,4},{6,7},{7,6},{8,9},{9,8},{10,11... | collective-permute-start | bytes 1671176 | tf_op jit(solution)/shard_map/ppermute | solution.py:271
  55.8 2.3 %copy-start.2 = (bf16[8,272,128]{2,1,0:T(8,128)(2,1)}, bf16[8,272,128]{2,1,0:T(8,128)(2,1)S(1)}, u32[]{:S(2)}) copy-start(bf16[8,272,128]{2,1,0:T(8,128)(2,1)S(1)} %collective-permute-done.3.refs_2_) | copy-start | bytes 1671172
  58.1 23.3 %collective-permute-start.7 = (bf16[256,1024]{1,0:T(8,128)(2,1)}, bf16[256,1024]{1,0:T(8,128)(2,1)S(1)}, u32[]{:S(2)}, u32[]{:S(2)}) collective-permute-start(bf16[256,1024]{1,0:T(8,128)(2,1)} %get-tuple-element.18), channel_id=1, source_target_pairs={{0,8},{8,16},{16,24},{24,28},{28,20},{20,12},{12,4},{4,0},{1,9},{9... | collective-permute-start | bytes 1572872 | tf_op jit(solution)/shard_map/ppermute | solution.py:295
  64.9 16.5 %collective-permute-start.8 = (bf16[256,1024]{1,0:T(8,128)(2,1)}, bf16[256,1024]{1,0:T(8,128)(2,1)S(1)}, u32[]{:S(2)}, u32[]{:S(2)}) collective-permute-start(bf16[256,1024]{1,0:T(8,128)(2,1)} %get-tuple-element.16), channel_id=1, source_target_pairs={{8,0},{16,8},{24,16},{28,24},{20,28},{12,20},{4,12},{0,4},{9,1},{1... | collective-permute-start | bytes 1572872 | tf_op jit(solution)/shard_map/ppermute | solution.py:296
  64.9 26.8 %collective-permute-start.10 = (bf16[256,1024]{1,0:T(8,128)(2,1)}, bf16[256,1024]{1,0:T(8,128)(2,1)}, u32[]{:S(2)}, u32[]{:S(2)}) collective-permute-start(bf16[256,1024]{1,0:T(8,128)(2,1)} %get-tuple-element.15), channel_id=1, source_target_pairs={{8,0},{16,8},{24,16},{28,24},{20,28},{12,20},{4,12},{0,4},{9,1},{1... | collective-permute-start | bytes 1572872 | tf_op jit(solution)/shard_map/ppermute | solution.py:298
  67.2 24.4 %collective-permute-start.9 = (bf16[256,1024]{1,0:T(8,128)(2,1)S(1)}, bf16[256,1024]{1,0:T(8,128)(2,1)}, u32[]{:S(2)}, u32[]{:S(2)}) collective-permute-start(bf16[256,1024]{1,0:T(8,128)(2,1)S(1)} %get-tuple-element.17), channel_id=1, source_target_pairs={{0,8},{8,16},{16,24},{24,28},{28,20},{20,12},{12,4},{4,0},{1,9},{9... | collective-permute-start | bytes 1572872 | tf_op jit(solution)/shard_map/ppermute | solution.py:297
  69.3 1.1 %copy-start.3 = (bf16[8,272,128]{2,1,0:T(8,128)(2,1)S(1)}, bf16[8,272,128]{2,1,0:T(8,128)(2,1)}, u32[]{:S(2)}) copy-start(bf16[8,272,128]{2,1,0:T(8,128)(2,1)} %copy-done.2) | copy-start | bytes 1671172
  70.4 1.2 %copy-start.4 = (bf16[512,1024]{1,0:T(8,128)(2,1)S(1)}, bf16[512,1024]{1,0:T(8,128)(2,1)}, u32[]{:S(2)}) copy-start(bf16[512,1024]{1,0:T(8,128)(2,1)} %refs_4_.1) | copy-start | bytes 3145732
  81.4 15.0 %collective-permute-start.11 = (bf16[256,1024]{1,0:T(8,128)(2,1)S(1)}, bf16[256,1024]{1,0:T(8,128)(2,1)S(1)}, u32[]{:S(2)}, u32[]{:S(2)}) collective-permute-start(bf16[256,1024]{1,0:T(8,128)(2,1)S(1)} %get-tuple-element.13.refs_0_), channel_id=1, source_target_pairs={{0,8},{8,16},{16,24},{24,28},{28,20},{20,12},{12,4},{4,0},{1,9},{9... | collective-permute-start | bytes 1572872 | tf_op jit(solution)/shard_map/ppermute | solution.py:322
  83.4 17.3 %collective-permute-start.12 = (bf16[256,1024]{1,0:T(8,128)(2,1)S(1)}, bf16[256,1024]{1,0:T(8,128)(2,1)S(1)}, u32[]{:S(2)}, u32[]{:S(2)}) collective-permute-start(bf16[256,1024]{1,0:T(8,128)(2,1)S(1)} %get-tuple-element.14.refs_3_), channel_id=1, source_target_pairs={{8,0},{16,8},{24,16},{28,24},{20,28},{12,20},{4,12},{0,4},{9,1},{1... | collective-permute-start | bytes 1572872 | tf_op jit(solution)/shard_map/ppermute | solution.py:323

commit v17 on v16

--- a/solution.py
+++ b/solution.py
@@ -289,7 +289,7 @@
         from_left = lax.ppermute(from_left, "grid", to_right)
         from_right = lax.ppermute(from_right, "grid", to_left)
         early += [from_left, from_right]
-    split = k_local // 2
+    split = k_local // 16 * 9
     left_low, right_high = from_left[:split], from_right[split:]
     left_high, right_low = from_left[split:], from_right[:split]
     left_low = lax.ppermute(left_low, "grid", to_right)

time: 105 us -> 109 us (1.038)
  blocking collectives: 0 us -> 32.6 us
  waiting for transfers between devices: 47.3 us -> 23.4 us
  starting transfers between devices: 23.3 us -> 12.7 us
  local copies, waits for them, and re-layouts: 10.2 us -> 16.6 us
    all_to_all x0 -> x1, blocking collectives: none -> 32.6 us  [body(): lax.all_to_all(message, 'grid', split_axis=0, concat_axis=0, tiled=True)]
    all_to_all x1 -> x0, waiting for transfers between devices: 11.9 us -> none  [body(): lax.all_to_all(message, 'grid', split_axis=0, concat_axis=0, tiled=True)]
    ppermute x1, waiting for transfers between devices: 7.96 us -> 0.01 us  [body(): right_low = lax.ppermute(right_low, 'grid', to_left)]
    all_to_all x1 -> x0, starting transfers between devices: 6.28 us -> none  [body(): lax.all_to_all(message, 'grid', split_axis=0, concat_axis=0, tiled=True)]
    ppermute x2, waiting for transfers between devices: 13.8 us -> 8.77 us  [body(): from_left = lax.ppermute(from_left, 'grid', to_right)]
    ppermute x1, starting transfers between devices: 4.56 us -> 0.34 us  [body(): left_low = lax.ppermute(left_low, 'grid', to_right)]
    unnamed x12 -> x18, local copies, waits for them, and re-layouts: 3.09 us -> 6.25 us
    ppermute x2, starting transfers between devices: 6.23 us -> 3.5 us  [body(): from_left = lax.ppermute(from_left, 'grid', to_right)]
  transfers between devices with their start and end apart: 14 -> 13, of which waited for: 6 -> 4; matrix products, arithmetic and copies ran while one was open for 9% -> 12% of each run, Pallas kernels for 17% -> 16%
where the time goes in v17:
time: 109 us; the launch traced here: 108 us
  blocking collectives  32.6 us (30%)
  waiting for transfers between devices  23.4 us (21%)
  Pallas kernels  20.9 us (19%)
  local copies, waits for them, and re-layouts  16.6 us (15%)
  starting transfers between devices  12.7 us (12%)
  other arithmetic  2.12 us (2%)
    all_to_all x1, blocking collectives, body(): lax.all_to_all(message, 'grid', split_axis=0, concat_axis=0, tiled=True)  32.6 us
    ppermute x1, waiting for transfers between devices, across_row(): across = lax.ppermute(landed, 'blk', swap_chip)  9.79 us
    pallas_call x1, Pallas kernels, first_product(): pl.pallas_call(functools.partial(first_kernel, depths, parts[0].shape[0],...  9.77 us
    ppermute x2, waiting for transfers between devices, body(): from_left = lax.ppermute(from_left, 'grid', to_right)  8.77 us
    pallas_call x2, Pallas kernels, add_product(): pl.pallas_call(functools.partial(add_kernel, depths, place), out_shape=ou...  7.97 us
    unnamed x18, local copies, waits for them, and re-layouts  6.25 us
    slice x2, local copies, waits for them, and re-layouts, body(): left_high, right_low = (from_left[split:], from_right[:split])  3.72 us
    ppermute x2, starting transfers between devices, body(): from_left = lax.ppermute(from_left, 'grid', to_right)  3.5 us
  transfers between devices with their start and end apart: 13, of which 4 were waited for; matrix products, arithmetic and copies ran while one was open for 12% of the time, Pallas kernels for 16%

profile of v17, /device:TPU:0, one launch (start us, length us, event | category | flops | bytes accessed | tf_op | source)
XLA Modules:
  0.0 108.5 jit_solution(15798999386764689160)
XLA Ops:
  0.0 3.0 %collective-permute-start = (bf16[512,1024]{1,0:T(8,128)(2,1)}, bf16[512,1024]{1,0:T(8,128)(2,1)S(1)}, u32[]{:S(2)}, u32[]{:S(2)}) collective-permute-start(bf16[512,1024]{1,0:T(8,128)(2,1)} %refs_4_.1), channel_id=1, source_target_pairs={{0,8},{8,16},{16,24},{24,28},{28,20},{20,12},{12,4},{4,0},{1,9},{9... | collective-permute-start | bytes 3145736 | tf_op jit(solution)/shard_map/ppermute | solution.py:289
  3.0 0.7 convert_bitcast_fusion
  3.7 0.7 fusion.11
  4.4 0.1 copy.29
  4.5 0.6 pad.4.meta_ref
  5.1 3.2 %shard_map.64 = bf16[8,272,128]{2,1,0:T(8,128)(2,1)} custom-call(bf16[8,256,128]{2,1,0:T(8,128)(2,1)} %bitcast.17, bf16[8,16,128]{2,1,0:T(8,128)(2,1)} %pad.4.meta_ref), custom_call_target="tpu_custom_call" | custom-call | bytes 1048576 | tf_op jit(solution)/shard_map/pallas_call | solution.py:37
  8.3 32.6 %all_to_all.5.refs_0_ = bf16[8,272,128]{2,1,0:T(8,128)(2,1)} all-to-all(bf16[8,272,128]{2,1,0:T(8,128)(2,1)} %shard_map.64), channel_id=1, replica_groups=mesh['grid'=8,'blk'=4] {'grid'}, dimensions={0} | all-to-all | bytes 1114112 | tf_op jit(solution)/shard_map/all_to_all | solution.py:305
  40.9 1.0 copy-done.1
  41.9 1.5 %collective-permute-start.2 = (bf16[8,272,128]{2,1,0:T(8,128)(2,1)}, bf16[8,272,128]{2,1,0:T(8,128)(2,1)}, u32[]{:S(2)}, u32[]{:S(2)}) collective-permute-start(bf16[8,272,128]{2,1,0:T(8,128)(2,1)} %shard_map.65.refs_0_), channel_id=1, source_target_pairs={{0,2},{1,3},{2,0},{3,1},{4,6},{5,7},{6,4},{7,5},{8,10},{9,11},{10,... | collective-permute-start | bytes 1671176 | tf_op jit(solution)/shard_map/ppermute | solution.py:269
  43.4 0.5 collective-permute-start.5
  43.9 1.5 %collective-permute-start.6 = (bf16[512,1024]{1,0:T(8,128)(2,1)}, bf16[512,1024]{1,0:T(8,128)(2,1)}, u32[]{:S(2)}, u32[]{:S(2)}) collective-permute-start(bf16[512,1024]{1,0:T(8,128)(2,1)} %collective-permute-done.1.refs_2_.refs_6_), channel_id=1, source_target_pairs={{8,0},{16,8},{24,16},{28,24},{20,28},{12,20},{4,12},{0,4},{9,1},{1... | collective-permute-start | bytes 3145736 | tf_op jit(solution)/shard_map/ppermute | solution.py:290
  45.4 9.8 %collective-permute-done.2.refs_1_ = bf16[8,272,128]{2,1,0:T(8,128)(2,1)} collective-permute-done((bf16[8,272,128]{2,1,0:T(8,128)(2,1)}, bf16[8,272,128]{2,1,0:T(8,128)(2,1)}, u32[]{:S(2)}, u32[]{:S(2)}) %collective-permute-start.2) | collective-permute-done | bytes 557088 | tf_op jit(solution)/shard_map/ppermute | solution.py:269
  55.2 0.7 slice.40
  55.9 0.1 copy.30
  56.0 0.1 copy.34
  56.1 0.7 slice.41
  56.9 0.1 copy.31
  57.0 0.1 copy.35
  57.1 0.8 copy-done.5
  58.0 0.1 copy.36
  58.1 8.8 %collective-permute-done.5.refs_7_ = bf16[512,1024]{1,0:T(8,128)(2,1)S(1)} collective-permute-done((bf16[512,1024]{1,0:T(8,128)(2,1)}, bf16[512,1024]{1,0:T(8,128)(2,1)S(1)}, u32[]{:S(2)}, u32[]{:S(2)}) %collective-permute-start.5) | collective-permute-done | bytes 1048608 | tf_op jit(solution)/shard_map/ppermute | solution.py:289
  66.8 1.0 copy-done.3
  67.8 0.9 slice.46
  68.7 0.3 collective-permute-start.7
  69.0 1.8 %slice.47 = bf16[224,1024]{1,0:T(8,128)(2,1)} slice(bf16[512,1024]{1,0:T(8,128)(2,1)} %collective-permute-done.6.refs_8_), slice={[288:512], [0:1024]} | slice | bytes 917504 | tf_op jit(solution)/shard_map/slice | solution.py:293
  70.8 1.7 %collective-permute-start.8 = (bf16[224,1024]{1,0:T(8,128)(2,1)}, bf16[224,1024]{1,0:T(8,128)(2,1)S(1)}, u32[]{:S(2)}, u32[]{:S(2)}) collective-permute-start(bf16[224,1024]{1,0:T(8,128)(2,1)} %slice.47), channel_id=1, source_target_pairs={{8,0},{16,8},{24,16},{28,24},{20,28},{12,20},{4,12},{0,4},{9,1},{1... | collective-permute-start | bytes 1376264 | tf_op jit(solution)/shard_map/ppermute | solution.py:296
  72.5 1.9 %slice.49 = bf16[288,1024]{1,0:T(8,128)(2,1)} slice(bf16[512,1024]{1,0:T(8,128)(2,1)} %collective-permute-done.6.refs_8_), slice={[0:288], [0:1024]} | slice | bytes 1179648 | tf_op jit(solution)/shard_map/slice | solution.py:294
  74.4 1.3 %collective-permute-start.10 = (bf16[288,1024]{1,0:T(8,128)(2,1)}, bf16[288,1024]{1,0:T(8,128)(2,1)S(1)}, u32[]{:S(2)}, u32[]{:S(2)}) collective-permute-start(bf16[288,1024]{1,0:T(8,128)(2,1)} %slice.49), channel_id=1, source_target_pairs={{8,0},{16,8},{24,16},{28,24},{20,28},{12,20},{4,12},{0,4},{9,1},{1... | collective-permute-start | bytes 1769480 | tf_op jit(solution)/shard_map/ppermute | solution.py:298
  75.7 1.8 %slice.48 = bf16[224,1024]{1,0:T(8,128)(2,1)} slice(bf16[512,1024]{1,0:T(8,128)(2,1)} %copy-done.3), slice={[288:512], [0:1024]} | slice | bytes 917504 | tf_op jit(solution)/shard_map/slice | solution.py:294
  77.5 0.8 collective-permute-start.9
  78.3 0.7 slice.43
  79.1 0.1 copy.37
  79.2 0.1 copy.38
  79.3 0.3 fusion
  79.6 0.3 compare_reduce_fusion
  79.9 0.1 copy.39
  80.0 0.1 copy.40
  80.1 0.1 fusion.6.dest_ref
  80.3 1.2 %copy-done.4 = bf16[512,1024]{1,0:T(8,128)(2,1)S(1)} copy-done((bf16[512,1024]{1,0:T(8,128)(2,1)S(1)}, bf16[512,1024]{1,0:T(8,128)(2,1)}, u32[]{:S(2)}) %copy-start.4) | copy-done | bytes 1048600
  81.5 1.1 copy-done.6
  82.6 1.2 %copy-done.7 = bf16[512,1024]{1,0:T(8,128)(2,1)S(1)} copy-done((bf16[512,1024]{1,0:T(8,128)(2,1)S(1)}, bf16[512,1024]{1,0:T(8,128)(2,1)}, u32[]{:S(2)}) %copy-start.7) | copy-done | bytes 1048600
  83.8 9.8 %shard_map.66 = (f32[4,1024,256]{2,1,0:T(8,128)S(1)}, bf16[1024,1536]{1,0:T(8,128)(2,1)S(1)}, f32[8,128]{1,0:T(8,128)S(1)}) custom-call(s32[4,8,2]{2,1,0:T(8,128)S(1)} %fusion.6.dest_ref, bf16[8,272,128]{2,1,0:T(8,128)(2,1)S(1)} %copy-done, bf16[8,272,128]{2,1,0:T(8,128)(2,1)} %collective-permute-done.2.refs_1_, bf16[8,272,128]{2,1,0:T(8,128)(2,1)S(1)} %copy-done.6, ...), custom_call_target="tpu_custom_call" | custom-call | flops 5368709120 | bytes 9437184 | tf_op jit(solution)/shard_map/pallas_call | solution.py:148
  93.6 0.7 collective-permute-start.11
  94.3 1.4 %collective-permute-start.12 = (bf16[224,1024]{1,0:T(8,128)(2,1)S(1)}, bf16[224,1024]{1,0:T(8,128)(2,1)S(1)}, u32[]{:S(2)}, u32[]{:S(2)}) collective-permute-start(bf16[224,1024]{1,0:T(8,128)(2,1)S(1)} %get-tuple-element.14.refs_3_), channel_id=1, source_target_pairs={{8,0},{16,8},{24,16},{28,24},{20,28},{12,20},{4,12},{0,4},{9,1},{1... | collective-permute-start | bytes 1376264 | tf_op jit(solution)/shard_map/ppermute | solution.py:323
  95.7 4.6 %shard_map.68.acc_hbm = f32[4,1024,256]{2,1,0:T(8,128)S(1)} custom-call(bf16[1024,1536]{1,0:T(8,128)(2,1)S(1)} %get-tuple-element.10.late_hbm, f32[4,1024,256]{2,1,0:T(8,128)S(1)} %get-tuple-element.11.acc_hbm, bf16[288,1024]{1,0:T(8,128)(2,1)S(1)} %get-tuple-element.13.refs_0_, bf16[224,1024]{1,0:T(8,128)(2,1)} %collective-permute-done.9.refs_1_, ...), custom_call_target="tpu_custom_call" | custom-call | flops 2147483648 | bytes 12582912 | tf_op jit(solution)/shard_map/pallas_call | solution.py:237
  100.3 2.7 %collective-permute-done.12.refs_1_ = bf16[224,1024]{1,0:T(8,128)(2,1)S(1)} collective-permute-done((bf16[224,1024]{1,0:T(8,128)(2,1)S(1)}, bf16[224,1024]{1,0:T(8,128)(2,1)S(1)}, u32[]{:S(2)}, u32[]{:S(2)}) %collective-permute-start.12) | collective-permute-done | bytes 458784 | tf_op jit(solution)/shard_map/ppermute | solution.py:323
  103.0 2.2 %collective-permute-done.11.refs_0_ = bf16[288,1024]{1,0:T(8,128)(2,1)S(1)} collective-permute-done((bf16[288,1024]{1,0:T(8,128)(2,1)S(1)}, bf16[288,1024]{1,0:T(8,128)(2,1)S(1)}, u32[]{:S(2)}, u32[]{:S(2)}) %collective-permute-start.11) | collective-permute-done | bytes 589856 | tf_op jit(solution)/shard_map/ppermute | solution.py:322
  105.2 3.3 %shard_map.69 = bf16[1024,1024]{1,0:T(8,128)(2,1)} custom-call(bf16[1024,1536]{1,0:T(8,128)(2,1)S(1)} %get-tuple-element.10.late_hbm, f32[4,1024,256]{2,1,0:T(8,128)S(1)} %shard_map.68.acc_hbm, bf16[288,1024]{1,0:T(8,128)(2,1)S(1)} %collective-permute-done.11.refs_0_, bf16[224,1024]{1,0:T(8,128)(2,1)S(1)} %collective-permute-done.12.refs_1_), custom_call_target="tpu_custom_call" | custom-call | flops 1073741824 | bytes 10485760 | tf_op jit(solution)/shard_map/pallas_call | solution.py:237
  (32 shorter events, 0.3 us)
Async XLA Ops:
  0.0 55.2 %copy-start.8 = (s32[1,8]{1,0:T(1,128)S(1)}, s32[1,8]{1,0:T(1,128)}, u32[]{:S(2)}) copy-start(s32[1,8]{1,0:T(1,128)} %param.10) | copy-start | bytes 100
  0.0 40.9 %collective-permute-start = (bf16[512,1024]{1,0:T(8,128)(2,1)}, bf16[512,1024]{1,0:T(8,128)(2,1)S(1)}, u32[]{:S(2)}, u32[]{:S(2)}) collective-permute-start(bf16[512,1024]{1,0:T(8,128)(2,1)} %refs_4_.1), channel_id=1, source_target_pairs={{0,8},{8,16},{16,24},{24,28},{28,20},{20,12},{12,4},{4,0},{1,9},{9... | collective-permute-start | bytes 3145736 | tf_op jit(solution)/shard_map/ppermute | solution.py:289
  3.0 37.9 %collective-permute-start.1 = (bf16[512,1024]{1,0:T(8,128)(2,1)}, bf16[512,1024]{1,0:T(8,128)(2,1)}, u32[]{:S(2)}, u32[]{:S(2)}) collective-permute-start(bf16[512,1024]{1,0:T(8,128)(2,1)} %refs_4_.1), channel_id=1, source_target_pairs={{8,0},{16,8},{24,16},{28,24},{20,28},{12,20},{4,12},{0,4},{9,1},{1... | collective-permute-start | bytes 3145736 | tf_op jit(solution)/shard_map/ppermute | solution.py:290
  40.9 1.0 copy-start.1
  41.9 38.4 %copy-start = (bf16[8,272,128]{2,1,0:T(8,128)(2,1)S(1)}, bf16[8,272,128]{2,1,0:T(8,128)(2,1)}, u32[]{:S(2)}) copy-start(bf16[8,272,128]{2,1,0:T(8,128)(2,1)} %shard_map.65.refs_0_) | copy-start | bytes 1671172
  41.9 38.4 %copy-start.2 = (bf16[512,1024]{1,0:T(8,128)(2,1)S(1)}, bf16[512,1024]{1,0:T(8,128)(2,1)}, u32[]{:S(2)}) copy-start(bf16[512,1024]{1,0:T(8,128)(2,1)} %copy-done.1) | copy-start | bytes 3145732
  41.9 13.3 %collective-permute-start.2 = (bf16[8,272,128]{2,1,0:T(8,128)(2,1)}, bf16[8,272,128]{2,1,0:T(8,128)(2,1)}, u32[]{:S(2)}, u32[]{:S(2)}) collective-permute-start(bf16[8,272,128]{2,1,0:T(8,128)(2,1)} %shard_map.65.refs_0_), channel_id=1, source_target_pairs={{0,2},{1,3},{2,0},{3,1},{4,6},{5,7},{6,4},{7,5},{8,10},{9,11},{10,... | collective-permute-start | bytes 1671176 | tf_op jit(solution)/shard_map/ppermute | solution.py:269
  43.4 23.5 %collective-permute-start.5 = (bf16[512,1024]{1,0:T(8,128)(2,1)}, bf16[512,1024]{1,0:T(8,128)(2,1)S(1)}, u32[]{:S(2)}, u32[]{:S(2)}) collective-permute-start(bf16[512,1024]{1,0:T(8,128)(2,1)} %copy-done.1), channel_id=1, source_target_pairs={{0,8},{8,16},{16,24},{24,28},{28,20},{20,12},{12,4},{4,0},{1,9},{9... | collective-permute-start | bytes 3145736 | tf_op jit(solution)/shard_map/ppermute | solution.py:289
  43.9 25.2 %collective-permute-start.6 = (bf16[512,1024]{1,0:T(8,128)(2,1)}, bf16[512,1024]{1,0:T(8,128)(2,1)}, u32[]{:S(2)}, u32[]{:S(2)}) collective-permute-start(bf16[512,1024]{1,0:T(8,128)(2,1)} %collective-permute-done.1.refs_2_.refs_6_), channel_id=1, source_target_pairs={{8,0},{16,8},{24,16},{28,24},{20,28},{12,20},{4,12},{0,4},{9,1},{1... | collective-permute-start | bytes 3145736 | tf_op jit(solution)/shard_map/ppermute | solution.py:290
  45.4 11.6 %collective-permute-start.3 = (bf16[8,272,128]{2,1,0:T(8,128)(2,1)}, bf16[8,272,128]{2,1,0:T(8,128)(2,1)S(1)}, u32[]{:S(2)}, u32[]{:S(2)}) collective-permute-start(bf16[8,272,128]{2,1,0:T(8,128)(2,1)} %shard_map.65.refs_0_), channel_id=1, source_target_pairs={{0,1},{1,0},{2,3},{3,2},{4,5},{5,4},{6,7},{7,6},{8,9},{9,8},{10,11... | collective-permute-start | bytes 1671176 | tf_op jit(solution)/shard_map/ppermute | solution.py:270
  55.2 23.1 %collective-permute-start.4 = (bf16[8,272,128]{2,1,0:T(8,128)(2,1)}, bf16[8,272,128]{2,1,0:T(8,128)(2,1)}, u32[]{:S(2)}, u32[]{:S(2)}) collective-permute-start(bf16[8,272,128]{2,1,0:T(8,128)(2,1)} %collective-permute-done.2.refs_1_), channel_id=1, source_target_pairs={{0,1},{1,0},{2,3},{3,2},{4,5},{5,4},{6,7},{7,6},{8,9},{9,8},{10,11... | collective-permute-start | bytes 1671176 | tf_op jit(solution)/shard_map/ppermute | solution.py:271
  57.1 0.8 copy-start.5
  66.8 1.0 copy-start.3
  68.7 24.9 %collective-permute-start.7 = (bf16[288,1024]{1,0:T(8,128)(2,1)}, bf16[288,1024]{1,0:T(8,128)(2,1)S(1)}, u32[]{:S(2)}, u32[]{:S(2)}) collective-permute-start(bf16[288,1024]{1,0:T(8,128)(2,1)} %slice.46), channel_id=1, source_target_pairs={{0,8},{8,16},{16,24},{24,28},{28,20},{20,12},{12,4},{4,0},{1,9},{9... | collective-permute-start | bytes 1769480 | tf_op jit(solution)/shard_map/ppermute | solution.py:295
  70.8 22.7 %collective-permute-start.8 = (bf16[224,1024]{1,0:T(8,128)(2,1)}, bf16[224,1024]{1,0:T(8,128)(2,1)S(1)}, u32[]{:S(2)}, u32[]{:S(2)}) collective-permute-start(bf16[224,1024]{1,0:T(8,128)(2,1)} %slice.47), channel_id=1, source_target_pairs={{8,0},{16,8},{24,16},{28,24},{20,28},{12,20},{4,12},{0,4},{9,1},{1... | collective-permute-start | bytes 1376264 | tf_op jit(solution)/shard_map/ppermute | solution.py:296
  74.4 21.2 %collective-permute-start.10 = (bf16[288,1024]{1,0:T(8,128)(2,1)}, bf16[288,1024]{1,0:T(8,128)(2,1)S(1)}, u32[]{:S(2)}, u32[]{:S(2)}) collective-permute-start(bf16[288,1024]{1,0:T(8,128)(2,1)} %slice.49), channel_id=1, source_target_pairs={{8,0},{16,8},{24,16},{28,24},{20,28},{12,20},{4,12},{0,4},{9,1},{1... | collective-permute-start | bytes 1769480 | tf_op jit(solution)/shard_map/ppermute | solution.py:298
  77.5 18.2 %collective-permute-start.9 = (bf16[224,1024]{1,0:T(8,128)(2,1)}, bf16[224,1024]{1,0:T(8,128)(2,1)}, u32[]{:S(2)}, u32[]{:S(2)}) collective-permute-start(bf16[224,1024]{1,0:T(8,128)(2,1)} %slice.48), channel_id=1, source_target_pairs={{0,8},{8,16},{16,24},{24,28},{28,20},{20,12},{12,4},{4,0},{1,9},{9... | collective-permute-start | bytes 1376264 | tf_op jit(solution)/shard_map/ppermute | solution.py:297
  80.3 1.2 %copy-start.4 = (bf16[512,1024]{1,0:T(8,128)(2,1)S(1)}, bf16[512,1024]{1,0:T(8,128)(2,1)}, u32[]{:S(2)}) copy-start(bf16[512,1024]{1,0:T(8,128)(2,1)} %copy-done.3) | copy-start | bytes 3145732
  81.5 1.1 copy-start.6
  82.6 1.2 %copy-start.7 = (bf16[512,1024]{1,0:T(8,128)(2,1)S(1)}, bf16[512,1024]{1,0:T(8,128)(2,1)}, u32[]{:S(2)}) copy-start(bf16[512,1024]{1,0:T(8,128)(2,1)} %refs_4_.1) | copy-start | bytes 3145732
  93.6 11.6 %collective-permute-start.11 = (bf16[288,1024]{1,0:T(8,128)(2,1)S(1)}, bf16[288,1024]{1,0:T(8,128)(2,1)S(1)}, u32[]{:S(2)}, u32[]{:S(2)}) collective-permute-start(bf16[288,1024]{1,0:T(8,128)(2,1)S(1)} %get-tuple-element.13.refs_0_), channel_id=1, source_target_pairs={{0,8},{8,16},{16,24},{24,28},{28,20},{20,12},{12,4},{4,0},{1,9},{9... | collective-permute-start | bytes 1769480 | tf_op jit(solution)/shard_map/ppermute | solution.py:322
  94.3 8.7 %collective-permute-start.12 = (bf16[224,1024]{1,0:T(8,128)(2,1)S(1)}, bf16[224,1024]{1,0:T(8,128)(2,1)S(1)}, u32[]{:S(2)}, u32[]{:S(2)}) collective-permute-start(bf16[224,1024]{1,0:T(8,128)(2,1)S(1)} %get-tuple-element.14.refs_3_), channel_id=1, source_target_pairs={{8,0},{16,8},{24,16},{28,24},{20,28},{12,20},{4,12},{0,4},{9,1},{1... | collective-permute-start | bytes 1376264 | tf_op jit(solution)/shard_map/ppermute | solution.py:323

commit v18 on v16

--- a/solution.py
+++ b/solution.py
@@ -284,7 +284,7 @@
     order = ring_order(groups)
     to_right = [(order[i], order[(i + 1) % groups]) for i in range(groups)]
     to_left = [(order[(i + 1) % groups], order[i]) for i in range(groups)]
-    from_left, from_right, early = b_matrix, b_matrix, [b_matrix]
+    from_left, from_right, early = b_matrix, b_matrix, []
     for s in range(1, half - 1):
         from_left = lax.ppermute(from_left, "grid", to_right)
         from_right = lax.ppermute(from_right, "grid", to_left)
@@ -303,7 +303,7 @@
     meta = jnp.pad(meta.astype(jnp.bfloat16)[:, None, :], ((0, 0), (0, META - 1), (0, bs - 2 * cap)))
     message = pack(a_slots.reshape(groups, cap * bs, bs), meta)
     landed = lax.all_to_all(message, "grid", split_axis=0, concat_axis=0, tiled=True)
-    (landed,) = after([landed], early[1:3], VMEM_BYTES)
+    (landed,) = after([landed], early[:2], VMEM_BYTES)
     parts = across_row(landed, columns)
 
     metas = jnp.stack([p[:, cap * bs, : 2 * cap] for p in parts]).astype(jnp.int32)
@@ -313,16 +313,18 @@
     pos = ring_place(lax.axis_index("grid"), groups)
     ahead = (ring_place(col // blocks, groups) - pos + groups) % groups
     hops = jnp.minimum(ahead, groups - ahead)
-    first = jnp.where(hops == 0, 0, 2 * hops - 1) + jnp.where((ahead > 0) & (ahead < half), 1, 0)
+    first = jnp.where(hops == 0, groups - 2, 2 * hops - 2 + jnp.where(ahead < half, 1, 0))
+    first = jnp.where(hops == half, groups - 1, first)
     dest = row * (blocks * groups) + first * blocks + col % blocks
     dest = jnp.where(jnp.any(hit, axis=-1), dest, -1)
 
-    acc, late, mark = first_product(dest, parts, early, rb * bs, 3 * k_local, bs, cap, n_local // 4)
+    acc, late, mark = first_product(dest, parts, early, rb * bs, 4 * k_local, bs, cap, n_local // 4)
     left_low, right_high = after([left_low, right_high], [mark], SPARE_BYTES)
     low = lax.ppermute(left_low, "grid", to_right)
     high = lax.ppermute(right_high, "grid", to_left)
-    acc = add_product(late, 0, [left_low, left_high, right_low, right_high], acc, False)
-    return add_product(late, 2 * k_local, [low, high], acc, True)
+    pieces = [left_low, left_high, right_low, right_high, b_matrix]
+    acc = add_product(late, 0, pieces, acc, False)
+    return add_product(late, 3 * k_local, [low, high], acc, True)
 
 
 def solution(mesh):

time: 105 us -> 105 us (level)
  waiting for transfers between devices: 47.3 us -> 48.6 us
  local copies, waits for them, and re-layouts: 10.2 us -> 8.97 us
    ppermute x1, waiting for transfers between devices: 7.96 us -> 9.31 us  [body(): right_low = lax.ppermute(right_low, 'grid', to_left)]
    unnamed x12, local copies, waits for them, and re-layouts: 3.09 us -> 1.86 us
    ppermute x1, waiting for transfers between devices: 4.34 us -> 3.13 us  [body(): high = lax.ppermute(right_high, 'grid', to_left)]
    pallas_call x2, Pallas kernels: 8.03 us -> 9.23 us  [add_product(): pl.pallas_call(functools.partial(add_kernel, depths, place), out_shape=ou...]
    ppermute x1, waiting for transfers between devices: 0.01 us -> 1.17 us  [body(): right_high = lax.ppermute(right_high, 'grid', to_left)]
  transfers between devices with their start and end apart: 14 -> 14, of which waited for: 6 -> 7; matrix products, arithmetic and copies ran while one was open for 9% -> 9% of each run, Pallas kernels for 17% -> 17%
where the time goes in v18:
time: 105 us; the launch traced here: 104 us
  waiting for transfers between devices  48.6 us (46%)
  starting transfers between devices  23 us (22%)
  Pallas kernels  21.1 us (20%)
  local copies, waits for them, and re-layouts  8.97 us (9%)
  other arithmetic  2.12 us (2%)
    ppermute x2, waiting for transfers between devices, body(): from_left = lax.ppermute(from_left, 'grid', to_right)  13.8 us
    all_to_all x1, waiting for transfers between devices, body(): lax.all_to_all(message, 'grid', split_axis=0, concat_axis=0, tiled=True)  11.9 us
    ppermute x1, waiting for transfers between devices, across_row(): across = lax.ppermute(landed, 'blk', swap_chip)  9.34 us
    ppermute x1, waiting for transfers between devices, body(): right_low = lax.ppermute(right_low, 'grid', to_left)  9.31 us
    pallas_call x2, Pallas kernels, add_product(): pl.pallas_call(functools.partial(add_kernel, depths, place), out_shape=ou...  9.23 us
    pallas_call x1, Pallas kernels, first_product(): pl.pallas_call(functools.partial(first_kernel, depths, parts[0].shape[0],...  8.75 us
    all_to_all x1, starting transfers between devices, body(): lax.all_to_all(message, 'grid', split_axis=0, concat_axis=0, tiled=True)  6.28 us
    ppermute x2, starting transfers between devices, body(): from_left = lax.ppermute(from_left, 'grid', to_right)  6.23 us
  transfers between devices with their start and end apart: 14, of which 7 were waited for; matrix products, arithmetic and copies ran while one was open for 9% of the time, Pallas kernels for 17%

profile of v18, /device:TPU:0, one launch (start us, length us, event | category | flops | bytes accessed | tf_op | source)
XLA Modules:
  0.0 104.0 jit_solution(10508546658290085313)
XLA Ops:
  0.0 3.0 %collective-permute-start = (bf16[512,1024]{1,0:T(8,128)(2,1)}, bf16[512,1024]{1,0:T(8,128)(2,1)}, u32[]{:S(2)}, u32[]{:S(2)}) collective-permute-start(bf16[512,1024]{1,0:T(8,128)(2,1)} %refs_4_.1), channel_id=1, source_target_pairs={{0,8},{8,16},{16,24},{24,28},{28,20},{20,12},{12,4},{4,0},{1,9},{9... | collective-permute-start | bytes 3145736 | tf_op jit(solution)/shard_map/ppermute | solution.py:289
  3.0 0.7 convert_bitcast_fusion
  3.7 0.7 fusion.12
  4.4 0.1 copy.29
  4.5 0.6 pad.4.meta_ref
  5.1 3.2 %shard_map.64 = bf16[8,272,128]{2,1,0:T(8,128)(2,1)} custom-call(bf16[8,256,128]{2,1,0:T(8,128)(2,1)} %bitcast.17, bf16[8,16,128]{2,1,0:T(8,128)(2,1)} %pad.4.meta_ref), custom_call_target="tpu_custom_call" | custom-call | bytes 1048576 | tf_op jit(solution)/shard_map/pallas_call | solution.py:37
  8.3 6.3 %all-to-all-start = ((bf16[8,272,128]{2,1,0:T(8,128)(2,1)}), bf16[8,272,128]{2,1,0:T(8,128)(2,1)S(1)}, u32[]{:S(2)}, u32[]{:S(2)}) async-start(bf16[8,272,128]{2,1,0:T(8,128)(2,1)} %shard_map.64), calls=%async_computation | async-start | bytes 1114112 | tf_op jit(solution)/shard_map/all_to_all | solution.py:305
  14.6 12.6 %collective-permute-done.refs_1_.refs_4_ = bf16[512,1024]{1,0:T(8,128)(2,1)} collective-permute-done((bf16[512,1024]{1,0:T(8,128)(2,1)}, bf16[512,1024]{1,0:T(8,128)(2,1)}, u32[]{:S(2)}, u32[]{:S(2)}) %collective-permute-start) | collective-permute-done | bytes 1048608 | tf_op jit(solution)/shard_map/ppermute | solution.py:289
  27.2 3.2 %collective-permute-start.5 = (bf16[512,1024]{1,0:T(8,128)(2,1)}, bf16[512,1024]{1,0:T(8,128)(2,1)S(1)}, u32[]{:S(2)}, u32[]{:S(2)}) collective-permute-start(bf16[512,1024]{1,0:T(8,128)(2,1)} %collective-permute-done.refs_1_.refs_4_), channel_id=1, source_target_pairs={{0,8},{8,16},{16,24},{24,28},{28,20},{20,12},{12,4},{4,0},{1,9},{9... | collective-permute-start | bytes 3145736 | tf_op jit(solution)/shard_map/ppermute | solution.py:289
  30.4 0.0 collective-permute-done.1.refs_2_.refs_5_
  30.4 0.0 collective-permute-start.6
  30.4 11.9 %all-to-all-done.refs_0_ = bf16[8,272,128]{2,1,0:T(8,128)(2,1)S(1)} async-done(((bf16[8,272,128]{2,1,0:T(8,128)(2,1)}), bf16[8,272,128]{2,1,0:T(8,128)(2,1)S(1)}, u32[]{:S(2)}, u32[]{:S(2)}) %all-to-all-start) | async-done | bytes 557088 | tf_op jit(solution)/shard_map/all_to_all | solution.py:305
  42.3 0.8 copy-done
  43.1 1.5 %collective-permute-start.2 = (bf16[8,272,128]{2,1,0:T(8,128)(2,1)}, bf16[8,272,128]{2,1,0:T(8,128)(2,1)}, u32[]{:S(2)}, u32[]{:S(2)}) collective-permute-start(bf16[8,272,128]{2,1,0:T(8,128)(2,1)} %shard_map.65.refs_0_), channel_id=1, source_target_pairs={{0,2},{1,3},{2,0},{3,1},{4,6},{5,7},{6,4},{7,5},{8,10},{9,11},{10,... | collective-permute-start | bytes 1671176 | tf_op jit(solution)/shard_map/ppermute | solution.py:269
  44.6 9.3 %collective-permute-done.2.refs_1_ = bf16[8,272,128]{2,1,0:T(8,128)(2,1)} collective-permute-done((bf16[8,272,128]{2,1,0:T(8,128)(2,1)}, bf16[8,272,128]{2,1,0:T(8,128)(2,1)}, u32[]{:S(2)}, u32[]{:S(2)}) %collective-permute-start.2) | collective-permute-done | bytes 557088 | tf_op jit(solution)/shard_map/ppermute | solution.py:269
  54.0 0.7 slice.40
  54.7 0.1 copy.30
  54.8 0.1 copy.34
  54.9 0.7 slice.41
  55.6 0.1 copy.31
  55.7 0.1 copy.35
  55.8 0.0 collective-permute-done.3.refs_2_
  55.8 0.1 copy.32
  55.9 0.1 copy.36
  56.0 1.2 %collective-permute-done.5.refs_6_ = bf16[512,1024]{1,0:T(8,128)(2,1)S(1)} collective-permute-done((bf16[512,1024]{1,0:T(8,128)(2,1)}, bf16[512,1024]{1,0:T(8,128)(2,1)S(1)}, u32[]{:S(2)}, u32[]{:S(2)}) %collective-permute-start.5) | collective-permute-done | bytes 1048608 | tf_op jit(solution)/shard_map/ppermute | solution.py:289
  57.2 0.9 fusion.14
  58.1 4.6 %collective-permute-start.7 = (bf16[256,1024]{1,0:T(8,128)(2,1)}, bf16[256,1024]{1,0:T(8,128)(2,1)S(1)}, u32[]{:S(2)}, u32[]{:S(2)}) collective-permute-start(bf16[256,1024]{1,0:T(8,128)(2,1)} %get-tuple-element.18), channel_id=1, source_target_pairs={{0,8},{8,16},{16,24},{24,28},{28,20},{20,12},{12,4},{4,0},{1,9},{9... | collective-permute-start | bytes 1572872 | tf_op jit(solution)/shard_map/ppermute | solution.py:295
  62.6 2.3 %fusion.13 = (bf16[256,1024]{1,0:T(8,128)(2,1)}, bf16[256,1024]{1,0:T(8,128)(2,1)}) fusion(bf16[512,1024]{1,0:T(8,128)(2,1)} %collective-permute-done.6.refs_7_), kind=kLoop, calls=%fused_computation.37 | loop fusion | bytes 2097152 | tf_op jit(solution)/shard_map/slice | solution.py:294
  64.9 2.3 %collective-permute-start.10 = (bf16[256,1024]{1,0:T(8,128)(2,1)}, bf16[256,1024]{1,0:T(8,128)(2,1)}, u32[]{:S(2)}, u32[]{:S(2)}) collective-permute-start(bf16[256,1024]{1,0:T(8,128)(2,1)} %get-tuple-element.15), channel_id=1, source_target_pairs={{8,0},{16,8},{24,16},{28,24},{20,28},{12,20},{4,12},{0,4},{9,1},{1... | collective-permute-start | bytes 1572872 | tf_op jit(solution)/shard_map/ppermute | solution.py:298
  67.2 0.1 collective-permute-start.9
  67.3 0.0 collective-permute-done.4.refs_3_
  67.3 0.7 slice.43
  68.0 0.1 copy.33
  68.1 0.1 copy.37
  68.2 0.1 copy.38
  68.3 0.3 fusion
  68.6 0.3 compare_reduce_fusion
  68.9 0.1 copy.39
  69.0 0.1 copy.40
  69.2 0.1 fusion.6.dest_ref
  69.3 1.0 %copy-done.4 = bf16[8,272,128]{2,1,0:T(8,128)(2,1)S(1)} copy-done((bf16[8,272,128]{2,1,0:T(8,128)(2,1)S(1)}, bf16[8,272,128]{2,1,0:T(8,128)(2,1)}, u32[]{:S(2)}) %copy-start.4) | copy-done | bytes 557080
  70.4 8.8 %shard_map.66 = (f32[4,1024,256]{2,1,0:T(8,128)S(1)}, bf16[1024,2048]{1,0:T(8,128)(2,1)S(1)}, f32[8,128]{1,0:T(8,128)S(1)}) custom-call(s32[4,8,2]{2,1,0:T(8,128)S(1)} %fusion.6.dest_ref, bf16[8,272,128]{2,1,0:T(8,128)(2,1)S(1)} %copy-done.1, bf16[8,272,128]{2,1,0:T(8,128)(2,1)} %collective-permute-done.2.refs_1_, bf16[8,272,128]{2,1,0:T(8,128)(2,1)S(1)} %copy-done.4, ...), custom_call_target="tpu_custom_call" | custom-call | flops 4294967296 | bytes 8388608 | tf_op jit(solution)/shard_map/pallas_call | solution.py:148
  79.1 1.2 %collective-permute-done.8.refs_1_ = bf16[256,1024]{1,0:T(8,128)(2,1)S(1)} collective-permute-done((bf16[256,1024]{1,0:T(8,128)(2,1)}, bf16[256,1024]{1,0:T(8,128)(2,1)S(1)}, u32[]{:S(2)}, u32[]{:S(2)}) %collective-permute-start.8) | collective-permute-done | bytes 524320 | tf_op jit(solution)/shard_map/ppermute | solution.py:296
  80.3 2.0 %collective-permute-start.11 = (bf16[256,1024]{1,0:T(8,128)(2,1)S(1)}, bf16[256,1024]{1,0:T(8,128)(2,1)S(1)}, u32[]{:S(2)}, u32[]{:S(2)}) collective-permute-start(bf16[256,1024]{1,0:T(8,128)(2,1)S(1)} %get-tuple-element.13.refs_0_), channel_id=1, source_target_pairs={{0,8},{8,16},{16,24},{24,28},{28,20},{20,12},{12,4},{4,0},{1,9},{9... | collective-permute-start | bytes 1572872 | tf_op jit(solution)/shard_map/ppermute | solution.py:323
  82.3 9.3 %collective-permute-done.10.refs_2_ = bf16[256,1024]{1,0:T(8,128)(2,1)} collective-permute-done((bf16[256,1024]{1,0:T(8,128)(2,1)}, bf16[256,1024]{1,0:T(8,128)(2,1)}, u32[]{:S(2)}, u32[]{:S(2)}) %collective-permute-start.10) | collective-permute-done | bytes 524320 | tf_op jit(solution)/shard_map/ppermute | solution.py:298
  91.7 5.9 %shard_map.68.acc_hbm = f32[4,1024,256]{2,1,0:T(8,128)S(1)} custom-call(bf16[1024,2048]{1,0:T(8,128)(2,1)S(1)} %get-tuple-element.10.late_hbm, f32[4,1024,256]{2,1,0:T(8,128)S(1)} %get-tuple-element.11.acc_hbm, bf16[256,1024]{1,0:T(8,128)(2,1)S(1)} %get-tuple-element.13.refs_0_, bf16[256,1024]{1,0:T(8,128)(2,1)} %collective-permute-done.9.refs_1_, ...), custom_call_target="tpu_custom_call" | custom-call | flops 3221225472 | bytes 14680064 | tf_op jit(solution)/shard_map/pallas_call | solution.py:237
  97.6 3.1 %collective-permute-done.12.refs_1_ = bf16[256,1024]{1,0:T(8,128)(2,1)S(1)} collective-permute-done((bf16[256,1024]{1,0:T(8,128)(2,1)S(1)}, bf16[256,1024]{1,0:T(8,128)(2,1)S(1)}, u32[]{:S(2)}, u32[]{:S(2)}) %collective-permute-start.12) | collective-permute-done | bytes 524320 | tf_op jit(solution)/shard_map/ppermute | solution.py:324
  100.7 3.3 %shard_map.69 = bf16[1024,1024]{1,0:T(8,128)(2,1)} custom-call(bf16[1024,2048]{1,0:T(8,128)(2,1)S(1)} %get-tuple-element.10.late_hbm, f32[4,1024,256]{2,1,0:T(8,128)S(1)} %shard_map.68.acc_hbm, bf16[256,1024]{1,0:T(8,128)(2,1)S(1)} %collective-permute-done.11.refs_0_, bf16[256,1024]{1,0:T(8,128)(2,1)S(1)} %collective-permute-done.12.refs_1_), custom_call_target="tpu_custom_call" | custom-call | flops 1073741824 | bytes 10485760 | tf_op jit(solution)/shard_map/pallas_call | solution.py:237
  (25 shorter events, 0.1 us)
Async XLA Ops:
  0.0 53.9 %copy-start.5 = (s32[1,8]{1,0:T(1,128)S(1)}, s32[1,8]{1,0:T(1,128)}, u32[]{:S(2)}) copy-start(s32[1,8]{1,0:T(1,128)} %param.10) | copy-start | bytes 100
  0.0 27.2 %collective-permute-start = (bf16[512,1024]{1,0:T(8,128)(2,1)}, bf16[512,1024]{1,0:T(8,128)(2,1)}, u32[]{:S(2)}, u32[]{:S(2)}) collective-permute-start(bf16[512,1024]{1,0:T(8,128)(2,1)} %refs_4_.1), channel_id=1, source_target_pairs={{0,8},{8,16},{16,24},{24,28},{28,20},{20,12},{12,4},{4,0},{1,9},{9... | collective-permute-start | bytes 3145736 | tf_op jit(solution)/shard_map/ppermute | solution.py:289
  3.0 27.4 %collective-permute-start.1 = (bf16[512,1024]{1,0:T(8,128)(2,1)}, bf16[512,1024]{1,0:T(8,128)(2,1)}, u32[]{:S(2)}, u32[]{:S(2)}) collective-permute-start(bf16[512,1024]{1,0:T(8,128)(2,1)} %refs_4_.1), channel_id=1, source_target_pairs={{8,0},{16,8},{24,16},{28,24},{20,28},{12,20},{4,12},{0,4},{9,1},{1... | collective-permute-start | bytes 3145736 | tf_op jit(solution)/shard_map/ppermute | solution.py:290
  8.3 34.0 %all-to-all-start = ((bf16[8,272,128]{2,1,0:T(8,128)(2,1)}), bf16[8,272,128]{2,1,0:T(8,128)(2,1)S(1)}, u32[]{:S(2)}, u32[]{:S(2)}) async-start(bf16[8,272,128]{2,1,0:T(8,128)(2,1)} %shard_map.64), calls=%async_computation | async-start | bytes 1114112 | tf_op jit(solution)/shard_map/all_to_all | solution.py:305
  27.2 30.0 %collective-permute-start.5 = (bf16[512,1024]{1,0:T(8,128)(2,1)}, bf16[512,1024]{1,0:T(8,128)(2,1)S(1)}, u32[]{:S(2)}, u32[]{:S(2)}) collective-permute-start(bf16[512,1024]{1,0:T(8,128)(2,1)} %collective-permute-done.refs_1_.refs_4_), channel_id=1, source_target_pairs={{0,8},{8,16},{16,24},{24,28},{28,20},{20,12},{12,4},{4,0},{1,9},{9... | collective-permute-start | bytes 3145736 | tf_op jit(solution)/shard_map/ppermute | solution.py:289
  30.4 32.2 %collective-permute-start.6 = (bf16[512,1024]{1,0:T(8,128)(2,1)}, bf16[512,1024]{1,0:T(8,128)(2,1)}, u32[]{:S(2)}, u32[]{:S(2)}) collective-permute-start(bf16[512,1024]{1,0:T(8,128)(2,1)} %collective-permute-done.1.refs_2_.refs_5_), channel_id=1, source_target_pairs={{8,0},{16,8},{24,16},{28,24},{20,28},{12,20},{4,12},{0,4},{9,1},{1... | collective-permute-start | bytes 3145736 | tf_op jit(solution)/shard_map/ppermute | solution.py:290
  42.3 0.8 copy-start
  43.1 26.2 %copy-start.1 = (bf16[8,272,128]{2,1,0:T(8,128)(2,1)S(1)}, bf16[8,272,128]{2,1,0:T(8,128)(2,1)}, u32[]{:S(2)}) copy-start(bf16[8,272,128]{2,1,0:T(8,128)(2,1)} %shard_map.65.refs_0_) | copy-start | bytes 1671172
  43.1 10.8 %collective-permute-start.2 = (bf16[8,272,128]{2,1,0:T(8,128)(2,1)}, bf16[8,272,128]{2,1,0:T(8,128)(2,1)}, u32[]{:S(2)}, u32[]{:S(2)}) collective-permute-start(bf16[8,272,128]{2,1,0:T(8,128)(2,1)} %shard_map.65.refs_0_), channel_id=1, source_target_pairs={{0,2},{1,3},{2,0},{3,1},{4,6},{5,7},{6,4},{7,5},{8,10},{9,11},{10,... | collective-permute-start | bytes 1671176 | tf_op jit(solution)/shard_map/ppermute | solution.py:269
  44.6 11.2 %collective-permute-start.3 = (bf16[8,272,128]{2,1,0:T(8,128)(2,1)}, bf16[8,272,128]{2,1,0:T(8,128)(2,1)S(1)}, u32[]{:S(2)}, u32[]{:S(2)}) collective-permute-start(bf16[8,272,128]{2,1,0:T(8,128)(2,1)} %shard_map.65.refs_0_), channel_id=1, source_target_pairs={{0,1},{1,0},{2,3},{3,2},{4,5},{5,4},{6,7},{7,6},{8,9},{9,8},{10,11... | collective-permute-start | bytes 1671176 | tf_op jit(solution)/shard_map/ppermute | solution.py:270
  53.9 13.4 %collective-permute-start.4 = (bf16[8,272,128]{2,1,0:T(8,128)(2,1)}, bf16[8,272,128]{2,1,0:T(8,128)(2,1)}, u32[]{:S(2)}, u32[]{:S(2)}) collective-permute-start(bf16[8,272,128]{2,1,0:T(8,128)(2,1)} %collective-permute-done.2.refs_1_), channel_id=1, source_target_pairs={{0,1},{1,0},{2,3},{3,2},{4,5},{5,4},{6,7},{7,6},{8,9},{9,8},{10,11... | collective-permute-start | bytes 1671176 | tf_op jit(solution)/shard_map/ppermute | solution.py:271
  55.8 2.3 %copy-start.3 = (bf16[8,272,128]{2,1,0:T(8,128)(2,1)}, bf16[8,272,128]{2,1,0:T(8,128)(2,1)S(1)}, u32[]{:S(2)}) copy-start(bf16[8,272,128]{2,1,0:T(8,128)(2,1)S(1)} %collective-permute-done.3.refs_2_) | copy-start | bytes 1671172
  58.1 21.1 %collective-permute-start.7 = (bf16[256,1024]{1,0:T(8,128)(2,1)}, bf16[256,1024]{1,0:T(8,128)(2,1)S(1)}, u32[]{:S(2)}, u32[]{:S(2)}) collective-permute-start(bf16[256,1024]{1,0:T(8,128)(2,1)} %get-tuple-element.18), channel_id=1, source_target_pairs={{0,8},{8,16},{16,24},{24,28},{28,20},{20,12},{12,4},{4,0},{1,9},{9... | collective-permute-start | bytes 1572872 | tf_op jit(solution)/shard_map/ppermute | solution.py:295
  64.9 15.4 %collective-permute-start.8 = (bf16[256,1024]{1,0:T(8,128)(2,1)}, bf16[256,1024]{1,0:T(8,128)(2,1)S(1)}, u32[]{:S(2)}, u32[]{:S(2)}) collective-permute-start(bf16[256,1024]{1,0:T(8,128)(2,1)} %get-tuple-element.16), channel_id=1, source_target_pairs={{8,0},{16,8},{24,16},{28,24},{20,28},{12,20},{4,12},{0,4},{9,1},{1... | collective-permute-start | bytes 1572872 | tf_op jit(solution)/shard_map/ppermute | solution.py:296
  64.9 26.8 %collective-permute-start.10 = (bf16[256,1024]{1,0:T(8,128)(2,1)}, bf16[256,1024]{1,0:T(8,128)(2,1)}, u32[]{:S(2)}, u32[]{:S(2)}) collective-permute-start(bf16[256,1024]{1,0:T(8,128)(2,1)} %get-tuple-element.15), channel_id=1, source_target_pairs={{8,0},{16,8},{24,16},{28,24},{20,28},{12,20},{4,12},{0,4},{9,1},{1... | collective-permute-start | bytes 1572872 | tf_op jit(solution)/shard_map/ppermute | solution.py:298
  67.2 24.4 %collective-permute-start.9 = (bf16[256,1024]{1,0:T(8,128)(2,1)S(1)}, bf16[256,1024]{1,0:T(8,128)(2,1)}, u32[]{:S(2)}, u32[]{:S(2)}) collective-permute-start(bf16[256,1024]{1,0:T(8,128)(2,1)S(1)} %get-tuple-element.17), channel_id=1, source_target_pairs={{0,8},{8,16},{16,24},{24,28},{28,20},{20,12},{12,4},{4,0},{1,9},{9... | collective-permute-start | bytes 1572872 | tf_op jit(solution)/shard_map/ppermute | solution.py:297
  69.3 1.1 %copy-start.4 = (bf16[8,272,128]{2,1,0:T(8,128)(2,1)S(1)}, bf16[8,272,128]{2,1,0:T(8,128)(2,1)}, u32[]{:S(2)}) copy-start(bf16[8,272,128]{2,1,0:T(8,128)(2,1)} %copy-done.3) | copy-start | bytes 1671172
  70.4 21.3 %copy-start.2 = (bf16[512,1024]{1,0:T(8,128)(2,1)S(1)}, bf16[512,1024]{1,0:T(8,128)(2,1)}, u32[]{:S(2)}) copy-start(bf16[512,1024]{1,0:T(8,128)(2,1)} %refs_4_.1) | copy-start | bytes 3145732
  80.3 17.3 %collective-permute-start.11 = (bf16[256,1024]{1,0:T(8,128)(2,1)S(1)}, bf16[256,1024]{1,0:T(8,128)(2,1)S(1)}, u32[]{:S(2)}, u32[]{:S(2)}) collective-permute-start(bf16[256,1024]{1,0:T(8,128)(2,1)S(1)} %get-tuple-element.13.refs_0_), channel_id=1, source_target_pairs={{0,8},{8,16},{16,24},{24,28},{28,20},{20,12},{12,4},{4,0},{1,9},{9... | collective-permute-start | bytes 1572872 | tf_op jit(solution)/shard_map/ppermute | solution.py:323
  82.3 18.4 %collective-permute-start.12 = (bf16[256,1024]{1,0:T(8,128)(2,1)S(1)}, bf16[256,1024]{1,0:T(8,128)(2,1)S(1)}, u32[]{:S(2)}, u32[]{:S(2)}) collective-permute-start(bf16[256,1024]{1,0:T(8,128)(2,1)S(1)} %get-tuple-element.14.refs_3_), channel_id=1, source_target_pairs={{8,0},{16,8},{24,16},{28,24},{20,28},{12,20},{4,12},{0,4},{9,1},{1... | collective-permute-start | bytes 1572872 | tf_op jit(solution)/shard_map/ppermute | solution.py:324
